TPU v7x, 128 devices: a whole 4x4x4 slice. The times are simulated.
128 devices in a mesh: lo: 8 (over y, z_hi), hi: 16 (over x, z_lo, core).
Axes of the slice: x: 4, y: 4, z: 4 (z_hi: 2, z_lo: 2; z = z_hi * 2 + z_lo), core: 2. Of those that a mesh axis runs over, the one named last changes fastest.
Arguments:
- coefficients: float32 [2, 32, 8, 131072], P(None, None, None, ('lo', 'hi')), may hold values from -6 to 6
- angle_in: float32 [7, 64, 131072], P(None, None, ('lo', 'hi')), may hold values from -3.140625 to 3.140625
- angle_out: float32 [7, 32, 131072], P(None, None, ('lo', 'hi')), may hold values from -3.140625 to 3.140625
- interp: float32 [7, 32, 64], replicated, may hold values from -0.75 to 0.75
- destination: int32 [128, 1024], P(('lo', 'hi')), may hold values from 0 to 1023, each once within a row
Outputs:
- relaid: float32 [2, 32, 8, 131072], P(None, None, None, ('lo', 'hi'))
All inputs are finite; a program needn't handle non-finite values.
Results may differ from a plain program's by a relative error of at most 0.0001.
Values sent between devices are 32-bit elements; how exact they have to be, the bound alone decides.
No kernel may reach another device: no remote copies, remote signals or barrier semaphores. Data moves between devices by JAX's collectives and lax.ppermute only.
A program may use at most 128 MiB of HBM per device.

v0:
```python
import jax
import jax.numpy as jnp
from jax import lax
from jax.sharding import PartitionSpec as P


def from_partner(x, axis, distance):
    return lax.ppermute(x, axis, [(i, i ^ 1 << distance) for i in range(lax.axis_size(axis))])


def widen(part):
    rows = part.shape[0]
    count = part.shape[1]
    half = part.shape[2]
    return jnp.broadcast_to(part[:, :, :, None], (rows, count, half, 2)).reshape(
        rows, count, 2 * half
    )


def apply_cols(matrix, real, imag, angle):
    rows = real.shape[0]
    count = real.shape[1]
    width = 2 * real.shape[2]
    cosine = jnp.cos(angle)[:, None, :]
    sine = jnp.sin(angle)[:, None, :]
    wide_re = widen(real)
    wide_im = widen(imag)
    yre = (wide_re * cosine - wide_im * sine).reshape(rows, count * width)
    yim = (wide_re * sine + wide_im * cosine).reshape(rows, count * width)
    outrows = matrix.shape[0]
    pre = jnp.dot(matrix, yre, precision=lax.Precision.HIGHEST, preferred_element_type=jnp.float32)
    pim = jnp.dot(matrix, yim, precision=lax.Precision.HIGHEST, preferred_element_type=jnp.float32)
    return (pre.reshape(outrows, count, width), pim.reshape(outrows, count, width))


def level(state, angle_in, angle_out, interp, axis, bit):
    width = state.shape[3]
    half = width // 2
    rank = state.shape[1]
    if axis == "lo":
        side = lax.axis_index("lo") // 2**bit % 2
    else:
        side = lax.axis_index("hi") // 2**bit % 2
    kept = lax.dynamic_slice_in_dim(state, side * half, half, 3)
    sent = lax.dynamic_slice_in_dim(state, (1 - side) * half, half, 3)
    if axis == "lo":
        got = from_partner(sent, "lo", bit)
    else:
        got = from_partner(sent, "hi", bit)
    shift_by = side * rank
    matrix = jnp.roll(interp, shift_by, axis=1)
    phases = jnp.roll(angle_in, shift_by, axis=0)
    real = jnp.concatenate([kept[0], got[0]], axis=0)
    imag = jnp.concatenate([kept[1], got[1]], axis=0)
    mre, mim = apply_cols(matrix, real, imag, phases)
    cosine = jnp.cos(angle_out)[:, None, :]
    sine = jnp.sin(angle_out)[:, None, :]
    zre = mre * cosine - mim * sine
    zim = mre * sine + mim * cosine
    return jnp.stack([zre, zim])


def shards(coefficients, angle_in, angle_out, interp, destination):
    state = coefficients
    lo_bits = lax.axis_size("lo").bit_length() - 1
    hi_bits = lax.axis_size("hi").bit_length() - 1
    step = 0
    for bit in range(lo_bits):
        state = level(state, angle_in[step], angle_out[step], interp[step], "lo", bit)
        step = step + 1
    for bit in range(hi_bits):
        state = level(state, angle_in[step], angle_out[step], interp[step], "hi", bit)
        step = step + 1
    taken = jnp.take(state, destination[0], axis=3)
    relaid = lax.all_to_all(taken, ("lo", "hi"), split_axis=3, concat_axis=3, tiled=True)
    return relaid


def solution(mesh):
    placed = (
        P(None, None, None, ("lo", "hi")),
        P(None, None, ("lo", "hi")),
        P(None, None, ("lo", "hi")),
        P(),
        P(("lo", "hi"), None),
    )
    return jax.shard_map(
        shards,
        mesh=mesh,
        in_specs=placed,
        out_specs=P(None, None, None, ("lo", "hi")),
        check_vma=False,
    )
```

profile of v0, /device:TPU:1, one launch (start us, length us, event | category | flops | bytes accessed | tf_op | source)
XLA Modules:
  0.0 398.6 jit_solution(4303448056122044556)
XLA Ops:
  0.0 2.4 constant_dynamic-slice_fusion
  2.4 4.4 %collective-permute-start = (f32[2,32,8,512]{3,2,1,0:T(8,128)}, f32[2,32,8,512]{3,2,1,0:T(8,128)}, u32[]{:S(2)}, u32[]{:S(2)}) collective-permute-start(f32[2,32,8,512]{3,2,1,0:T(8,128)} %constant_dynamic-slice_fusion), channel_id=1, source_target_pairs={{0,16},{16,0},{32,48},{48,32},{64,80},{80,64},{96,112},{112,96},{1... | collective-permute-start | bytes 3145736 | tf_op jit(solution)/shard_map/ppermute | solution.py:8
  6.8 2.5 slice_bitcast_fusion.26
  9.4 2.8 fusion.33
  14.9 5.1 %cosine_bitcast_fusion = (f32[32,1024]{1,0:T(8,128)S(1)}, f32[32,1024]{1,0:T(8,128)}, f32[32,1024]{1,0:T(8,128)}, f32[32,1024]{1,0:T(8,128)}, f32[32,1024]{1,0:T...) fusion(f32[7,32,1024]{2,1,0:T(8,128)} %param.11), kind=kLoop, calls=%fused_computation.166 | loop fusion | bytes 2752512 | tf_op jit(solution)/shard_map/cos | solution.py:56
  20.1 9.9 %collective-permute-done = f32[2,32,8,512]{3,2,1,0:T(8,128)} collective-permute-done((f32[2,32,8,512]{3,2,1,0:T(8,128)}, f32[2,32,8,512]{3,2,1,0:T(8,128)}, u32[]{:S(2)}, u32[]{:S(2)}) %collective-permute-start) | collective-permute-done | bytes 1048608 | tf_op jit(solution)/shard_map/ppermute | solution.py:8
  37.8 3.1 broadcast_in_dim.37
  41.9 4.4 %fusion.78 = f32[32,8,1024]{2,0,1:T(8,128)S(1)} fusion(f32[8,1024,64]{2,1,0:T(8,128)S(1)} %bitcast.378, s32[]{:T(128)S(6)} %select_n.194, f32[32,64]{1,0:T(8,128)S(1)} %copy-done.43), kind=kOutput, calls=%fused_computation.229 | convolution fusion | flops 201328640 | bytes 3153924 | tf_op jit(solution)/shard_map/dot_general | solution.py:32
  46.4 4.5 %add_bitcast_fusion.6 = (f32[1,32,8,1024]{3,1,2,0:T(8,128)S(1)}, f32[1,32,8,1024]{3,1,2,0:T(8,128)S(1)}) fusion(f32[32,8,1024]{2,0,1:T(8,128)S(1)} %fusion.78, f32[32,1024]{1,0:T(8,128)S(1)} %copy-done.36, f32[32,1024]{1,0:T(8,128)S(1)} %copy-done.37, f32[8,1024,64]{2,1,0:T(8,128)S(1)} %bitcast.363, s32[]{:T(128)S(6)} %select_n.194, ...), kind=kOutput, calls=%fused_computation.107 | convolution fusion | flops 202901504 | bytes 5513220 | tf_op jit(solution)/shard_map/dot_general | solution.py:31
  55.8 19.3 %collective-permute-done.1 = f32[2,32,8,512]{3,1,2,0:T(8,128)} collective-permute-done((f32[2,32,8,512]{3,1,2,0:T(8,128)S(1)}, f32[2,32,8,512]{3,1,2,0:T(8,128)}, u32[]{:S(2)}, u32[]{:S(2)}) %collective-permute-start.1) | collective-permute-done | bytes 1048608 | tf_op jit(solution)/shard_map/ppermute | solution.py:8
  75.1 2.1 slice_bitcast_fusion.22
  82.6 3.1 broadcast_in_dim.38
  86.6 4.4 %fusion.74 = f32[32,8,1024]{2,0,1:T(8,128)S(1)} fusion(f32[8,1024,64]{2,1,0:T(8,128)S(1)} %bitcast.380, s32[]{:T(128)S(6)} %select_n.192, f32[32,64]{1,0:T(8,128)S(1)} %copy-done.42), kind=kOutput, calls=%fused_computation.227 | convolution fusion | flops 201328640 | bytes 3153924 | tf_op jit(solution)/shard_map/dot_general | solution.py:32
  91.1 4.5 %add_bitcast_fusion.5 = (f32[1,32,8,1024]{3,1,2,0:T(8,128)S(1)}, f32[1,32,8,1024]{3,1,2,0:T(8,128)S(1)}) fusion(f32[32,8,1024]{2,0,1:T(8,128)S(1)} %fusion.74, f32[32,1024]{1,0:T(8,128)S(1)} %copy-done.34, f32[32,1024]{1,0:T(8,128)S(1)} %copy-done.35, f32[8,1024,64]{2,1,0:T(8,128)S(1)} %bitcast.364, s32[]{:T(128)S(6)} %select_n.192, ...), kind=kOutput, calls=%fused_computation.105 | convolution fusion | flops 202901504 | bytes 5513220 | tf_op jit(solution)/shard_map/dot_general | solution.py:31
  95.9 3.0 collective-permute-start.2
  98.8 3.0 fusion.37
  104.7 15.3 %collective-permute-done.2 = f32[2,32,8,512]{3,1,2,0:T(8,128)} collective-permute-done((f32[2,32,8,512]{3,1,2,0:T(8,128)S(1)}, f32[2,32,8,512]{3,1,2,0:T(8,128)}, u32[]{:S(2)}, u32[]{:S(2)}) %collective-permute-start.2) | collective-permute-done | bytes 1048608 | tf_op jit(solution)/shard_map/ppermute | solution.py:8
  120.1 2.1 slice_bitcast_fusion.18
  127.5 3.1 broadcast_in_dim.40
  131.6 4.4 %fusion.70 = f32[32,8,1024]{2,0,1:T(8,128)S(1)} fusion(f32[8,1024,64]{2,1,0:T(8,128)S(1)} %bitcast.382, s32[]{:T(128)S(6)} %select_n.190, f32[32,64]{1,0:T(8,128)S(1)} %copy-done.41), kind=kOutput, calls=%fused_computation.225 | convolution fusion | flops 201328640 | bytes 3153924 | tf_op jit(solution)/shard_map/dot_general | solution.py:32
  136.1 4.5 %add_bitcast_fusion.4 = (f32[1,32,8,1024]{3,1,2,0:T(8,128)S(1)}, f32[1,32,8,1024]{3,1,2,0:T(8,128)S(1)}) fusion(f32[32,8,1024]{2,0,1:T(8,128)S(1)} %fusion.70, f32[32,1024]{1,0:T(8,128)S(1)} %copy-done.32, f32[32,1024]{1,0:T(8,128)S(1)} %copy-done.33, f32[8,1024,64]{2,1,0:T(8,128)S(1)} %bitcast.365, s32[]{:T(128)S(6)} %select_n.190, ...), kind=kOutput, calls=%fused_computation.103 | convolution fusion | flops 202901504 | bytes 5513220 | tf_op jit(solution)/shard_map/dot_general | solution.py:31
  140.8 3.5 collective-permute-start.3
  147.3 2.1 slice_bitcast_fusion.14
  154.8 3.1 broadcast_in_dim.42
  158.8 4.4 %fusion.66 = f32[32,8,1024]{2,0,1:T(8,128)S(1)} fusion(f32[8,1024,64]{2,1,0:T(8,128)S(1)} %bitcast.384, s32[]{:T(128)S(6)} %select_n.188, f32[32,64]{1,0:T(8,128)S(1)} %copy-done.40), kind=kOutput, calls=%fused_computation.223 | convolution fusion | flops 201328640 | bytes 3153924 | tf_op jit(solution)/shard_map/dot_general | solution.py:32
  163.3 4.5 %add_bitcast_fusion.3 = (f32[1,32,8,1024]{3,1,2,0:T(8,128)S(1)}, f32[1,32,8,1024]{3,1,2,0:T(8,128)S(1)}) fusion(f32[32,8,1024]{2,0,1:T(8,128)S(1)} %fusion.66, f32[32,1024]{1,0:T(8,128)S(1)} %copy-done.30, f32[32,1024]{1,0:T(8,128)S(1)} %copy-done.31, f32[8,1024,64]{2,1,0:T(8,128)S(1)} %bitcast.366, s32[]{:T(128)S(6)} %select_n.188, ...), kind=kOutput, calls=%fused_computation.101 | convolution fusion | flops 202901504 | bytes 5513220 | tf_op jit(solution)/shard_map/dot_general | solution.py:31
  168.5 2.9 fusion.41
  174.3 18.6 %collective-permute-done.4 = f32[2,32,8,512]{3,1,2,0:T(8,128)} collective-permute-done((f32[2,32,8,512]{3,1,2,0:T(8,128)S(1)}, f32[2,32,8,512]{3,1,2,0:T(8,128)}, u32[]{:S(2)}, u32[]{:S(2)}) %collective-permute-start.4) | collective-permute-done | bytes 1048608 | tf_op jit(solution)/shard_map/ppermute | solution.py:8
  200.4 3.1 broadcast_in_dim.44
  204.5 4.4 %fusion.62 = f32[32,8,1024]{2,0,1:T(8,128)S(1)} fusion(f32[8,1024,64]{2,1,0:T(8,128)S(1)} %bitcast.386, s32[]{:T(128)S(6)} %select_n.186, f32[32,64]{1,0:T(8,128)S(1)} %copy-done.39), kind=kOutput, calls=%fused_computation.221 | convolution fusion | flops 201328640 | bytes 3153924 | tf_op jit(solution)/shard_map/dot_general | solution.py:32
  209.0 4.5 %add_bitcast_fusion.2 = (f32[1,32,8,1024]{3,1,2,0:T(8,128)S(1)}, f32[1,32,8,1024]{3,1,2,0:T(8,128)S(1)}) fusion(f32[32,8,1024]{2,0,1:T(8,128)S(1)} %fusion.62, f32[32,1024]{1,0:T(8,128)S(1)} %copy-done.28, f32[32,1024]{1,0:T(8,128)S(1)} %copy-done.29, f32[8,1024,64]{2,1,0:T(8,128)S(1)} %bitcast.367, s32[]{:T(128)S(6)} %select_n.186, f32[32,64]{1,0:T(8,128)S(1)} %copy-done.39), kind=kOutput, calls=%fused_computation.99 | convolution fusion | flops 202901504 | bytes 5513220 | tf_op jit(solution)/shard_map/dot_general | solution.py:31
  218.3 19.8 %collective-permute-done.5 = f32[2,32,8,512]{3,1,2,0:T(8,128)} collective-permute-done((f32[2,32,8,512]{3,1,2,0:T(8,128)S(1)}, f32[2,32,8,512]{3,1,2,0:T(8,128)}, u32[]{:S(2)}, u32[]{:S(2)}) %collective-permute-start.5) | collective-permute-done | bytes 1048608 | tf_op jit(solution)/shard_map/ppermute | solution.py:8
  245.6 3.1 broadcast_in_dim.46
  249.7 4.4 %fusion.58 = f32[32,8,1024]{2,0,1:T(8,128)S(1)} fusion(f32[8,1024,64]{2,1,0:T(8,128)S(1)} %bitcast.388, s32[]{:T(128)S(6)} %select_n.184, f32[32,64]{1,0:T(8,128)S(1)} %copy-done.38), kind=kOutput, calls=%fused_computation.219 | convolution fusion | flops 201328640 | bytes 3153924 | tf_op jit(solution)/shard_map/dot_general | solution.py:32
  254.1 4.5 %add_bitcast_fusion.1 = (f32[1,32,8,1024]{3,1,2,0:T(8,128)S(1)}, f32[1,32,8,1024]{3,1,2,0:T(8,128)S(1)}) fusion(f32[32,8,1024]{2,0,1:T(8,128)S(1)} %fusion.58, f32[32,1024]{1,0:T(8,128)S(1)} %copy-done.26, f32[32,1024]{1,0:T(8,128)S(1)} %copy-done.27, f32[8,1024,64]{2,1,0:T(8,128)S(1)} %bitcast.368, s32[]{:T(128)S(6)} %select_n.184, f32[32,64]{1,0:T(8,128)S(1)} %copy-done.38), kind=kOutput, calls=%fused_computation.97 | convolution fusion | flops 202901504 | bytes 5513220 | tf_op jit(solution)/shard_map/dot_general | solution.py:31
  258.9 3.0 collective-permute-start.6
  265.8 17.8 %collective-permute-done.6 = f32[2,32,8,512]{3,1,2,0:T(8,128)} collective-permute-done((f32[2,32,8,512]{3,1,2,0:T(8,128)S(1)}, f32[2,32,8,512]{3,1,2,0:T(8,128)}, u32[]{:S(2)}, u32[]{:S(2)}) %collective-permute-start.6) | collective-permute-done | bytes 1048608 | tf_op jit(solution)/shard_map/ppermute | solution.py:8
  291.1 3.1 broadcast_in_dim.48
  295.1 4.4 %fusion.54 = f32[32,8,1024]{2,0,1:T(8,128)S(1)} fusion(f32[8,1024,64]{2,1,0:T(8,128)S(1)} %bitcast.376, s32[]{:T(128)S(6)} %select_n.182, f32[32,64]{1,0:T(8,128)S(1)} %get-tuple-element.110), kind=kOutput, calls=%fused_computation.217 | convolution fusion | flops 201328640 | bytes 3153924 | tf_op jit(solution)/shard_map/dot_general | solution.py:32
  299.6 4.5 %subtract_bitcast_fusion = (f32[1,32,8,1024]{3,1,2,0:T(8,128)S(1)}, f32[1,32,8,1024]{3,1,2,0:T(8,128)S(1)}) fusion(f32[32,8,1024]{2,0,1:T(8,128)S(1)} %fusion.54, f32[32,1024]{1,0:T(8,128)S(1)} %copy-done.25, f32[32,1024]{1,0:T(8,128)S(1)} %get-tuple-element.82, f32[8,1024,64]{2,1,0:T(8,128)S(1)} %bitcast.362, s32[]{:T(128)S(6)} %select_n.182, ...), kind=kOutput, calls=%fused_computation.96 | convolution fusion | flops 202901504 | bytes 5513220 | tf_op jit(solution)/shard_map/dot_general | solution.py:31
  304.3 5.0 %copy.75 = f32[2,32,8,1024]{1,2,3,0:T(8,128)} copy(f32[2,32,8,1024]{3,1,2,0:T(8,128)S(1)} %pad_maximum_fusion) | data formatting | bytes 4194304 | tf_op jit(solution)/shard_map/stack | solution.py:60
  309.3 13.1 %gather_fusion = f32[1024,2,32,8]{2,3,1,0:T(8,128)} fusion(f32[2,32,8,1024]{1,2,3,0:T(8,128)} %copy.75, s32[1024]{0:T(1024)S(1)} %broadcast_clamp_fusion), kind=kCustom, calls=%fused_computation | custom fusion | bytes 4198400 | tf_op jit(solution)/shard_map/jit(_take)/gather | solution.py:74
  322.4 8.7 %fusion.96 = f32[1024,2,8,32]{3,2,1,0:T(8,128)} fusion(f32[1024,2,32,8]{2,3,1,0:T(8,128)} %gather_fusion, pred[1024]{0:T(1024)(128)(4,1)S(1)} %compare_and_fusion), kind=kLoop, calls=%fused_computation.247 | loop fusion | flops 524288 | bytes 4195328
  331.1 6.8 %reshape.315 = f32[128,1,4096]{2,1,0:T(1,128)S(1)} reshape(f32[1024,2,8,32]{3,2,1,0:T(8,128)} %fusion.96) | data formatting | bytes 4194304
  337.9 41.2 %all_to_all.5 = f32[128,1,4096]{2,1,0:T(1,128)} all-to-all(f32[128,1,4096]{2,1,0:T(1,128)S(1)} %reshape.315), channel_id=1, replica_groups=mesh['lo'=8,'hi'=16] {'lo','hi'}, dimensions={0} | all-to-all | bytes 4194304 | tf_op jit(solution)/shard_map/all_to_all | solution.py:75
  379.6 7.3 %reduce = f32[128,4096]{1,0:T(8,128)S(1)} reduce(f32[128,1,4096]{2,1,0:T(1,128)} %all_to_all.5, f32[]{:T(128)} %broadcast.109), dimensions={1}, to_apply=%all_to_all.3.reduce_sub_computation | reduce | bytes 4194308 | tf_op jit(solution)/shard_map/all_to_all | solution.py:75
  386.9 4.9 %reshape.316 = f32[1024,2,8,32]{3,2,1,0:T(8,128)} reshape(f32[128,4096]{1,0:T(8,128)S(1)} %reduce) | data formatting | bytes 4194304
  391.8 6.6 %copy.76 = f32[2,32,8,1024]{3,2,1,0:T(8,128)} copy(f32[2,32,8,1024]{1,2,0,3:T(8,128)} %bitcast.361) | data formatting | bytes 4194304 | tf_op jit(solution)/shard_map/all_to_all | solution.py:75
  (175 shorter events, 79.3 us)
Async XLA Ops:
  0.0 14.2 %copy-start.14 = (f32[2,32,8,1024]{3,2,1,0:T(8,128)S(1)}, f32[2,32,8,1024]{3,2,1,0:T(8,128)}, u32[]{:S(2)}) copy-start(f32[2,32,8,1024]{3,2,1,0:T(8,128)} %param.9) | copy-start | bytes 6291460
  2.4 27.6 %collective-permute-start = (f32[2,32,8,512]{3,2,1,0:T(8,128)}, f32[2,32,8,512]{3,2,1,0:T(8,128)}, u32[]{:S(2)}, u32[]{:S(2)}) collective-permute-start(f32[2,32,8,512]{3,2,1,0:T(8,128)} %constant_dynamic-slice_fusion), channel_id=1, source_target_pairs={{0,16},{16,0},{32,48},{48,32},{64,80},{80,64},{96,112},{112,96},{1... | collective-permute-start | bytes 3145736 | tf_op jit(solution)/shard_map/ppermute | solution.py:8
  6.8 7.4 %copy-start.44 = (f32[7,32,64]{2,1,0:T(8,128)S(1)}, f32[7,32,64]{2,1,0:T(8,128)}, u32[]{:S(2)}) copy-start(f32[7,32,64]{2,1,0:T(8,128)} %param.12) | copy-start | bytes 172036
  37.8 3.1 copy-start
  37.8 3.1 copy-start.1
  41.0 0.9 copy-start.43
  41.9 4.5 %copy-start.36 = (f32[32,1024]{1,0:T(8,128)S(1)}, f32[32,1024]{1,0:T(8,128)}, u32[]{:S(2)}) copy-start(f32[32,1024]{1,0:T(8,128)} %get-tuple-element.83) | copy-start | bytes 393220
  41.9 4.5 %copy-start.37 = (f32[32,1024]{1,0:T(8,128)S(1)}, f32[32,1024]{1,0:T(8,128)}, u32[]{:S(2)}) copy-start(f32[32,1024]{1,0:T(8,128)} %get-tuple-element.94) | copy-start | bytes 393220
  46.4 6.5 %copy-start.22 = (f32[64,1024]{1,0:T(8,128)S(1)}, f32[64,1024]{1,0:T(8,128)}, u32[]{:S(2)}) copy-start(f32[64,1024]{1,0:T(8,128)} %get-tuple-element.120) | copy-start | bytes 786436
  50.9 3.0 copy-start.21
  51.1 24.0 %collective-permute-start.1 = (f32[2,32,8,512]{3,1,2,0:T(8,128)S(1)}, f32[2,32,8,512]{3,1,2,0:T(8,128)}, u32[]{:S(2)}, u32[]{:S(2)}) collective-permute-start(f32[2,32,8,512]{3,1,2,0:T(8,128)S(1)} %get-tuple-element.46), channel_id=1, source_target_pairs={{0,32},{16,48},{32,0},{48,16},{64,96},{80,112},{96,64},{112,80},{1... | collective-permute-start | bytes 3145736 | tf_op jit(solution)/shard_map/ppermute | solution.py:8
  82.6 3.1 copy-start.4
  82.6 3.1 copy-start.8
  86.6 4.5 %copy-start.34 = (f32[32,1024]{1,0:T(8,128)S(1)}, f32[32,1024]{1,0:T(8,128)}, u32[]{:S(2)}) copy-start(f32[32,1024]{1,0:T(8,128)} %get-tuple-element.84) | copy-start | bytes 393220
  86.6 4.5 %copy-start.35 = (f32[32,1024]{1,0:T(8,128)S(1)}, f32[32,1024]{1,0:T(8,128)}, u32[]{:S(2)}) copy-start(f32[32,1024]{1,0:T(8,128)} %get-tuple-element.93) | copy-start | bytes 393220
  91.1 7.7 %copy-start.17 = (f32[64,1024]{1,0:T(8,128)S(1)}, f32[64,1024]{1,0:T(8,128)}, u32[]{:S(2)}) copy-start(f32[64,1024]{1,0:T(8,128)} %get-tuple-element.51) | copy-start | bytes 786436
  91.1 7.7 %copy-start.18 = (f32[64,1024]{1,0:T(8,128)S(1)}, f32[64,1024]{1,0:T(8,128)}, u32[]{:S(2)}) copy-start(f32[64,1024]{1,0:T(8,128)} %get-tuple-element.52) | copy-start | bytes 786436
  95.9 24.2 %collective-permute-start.2 = (f32[2,32,8,512]{3,1,2,0:T(8,128)S(1)}, f32[2,32,8,512]{3,1,2,0:T(8,128)}, u32[]{:S(2)}, u32[]{:S(2)}) collective-permute-start(f32[2,32,8,512]{3,1,2,0:T(8,128)S(1)} %get-tuple-element.44), channel_id=1, source_target_pairs={{0,64},{16,80},{32,96},{48,112},{64,0},{80,16},{96,32},{112,48},{1... | collective-permute-start | bytes 3145736 | tf_op jit(solution)/shard_map/ppermute | solution.py:8
  127.5 3.1 copy-start.6
  127.5 3.1 copy-start.9
  131.6 4.5 %copy-start.32 = (f32[32,1024]{1,0:T(8,128)S(1)}, f32[32,1024]{1,0:T(8,128)}, u32[]{:S(2)}) copy-start(f32[32,1024]{1,0:T(8,128)} %get-tuple-element.85) | copy-start | bytes 393220
  131.6 4.5 %copy-start.33 = (f32[32,1024]{1,0:T(8,128)S(1)}, f32[32,1024]{1,0:T(8,128)}, u32[]{:S(2)}) copy-start(f32[32,1024]{1,0:T(8,128)} %get-tuple-element.92) | copy-start | bytes 393220
  136.1 8.3 %copy-start.24 = (f32[64,1024]{1,0:T(8,128)S(1)}, f32[64,1024]{1,0:T(8,128)}, u32[]{:S(2)}) copy-start(f32[64,1024]{1,0:T(8,128)} %get-tuple-element.122) | copy-start | bytes 786436
  140.6 4.8 %copy-start.23 = (f32[64,1024]{1,0:T(8,128)S(1)}, f32[64,1024]{1,0:T(8,128)}, u32[]{:S(2)}) copy-start(f32[64,1024]{1,0:T(8,128)} %get-tuple-element.121) | copy-start | bytes 786436
  140.8 6.5 %collective-permute-start.3 = (f32[2,32,8,512]{3,1,2,0:T(8,128)S(1)}, f32[2,32,8,512]{3,1,2,0:T(8,128)}, u32[]{:S(2)}, u32[]{:S(2)}) collective-permute-start(f32[2,32,8,512]{3,1,2,0:T(8,128)S(1)} %get-tuple-element.42), channel_id=1, source_target_pairs={{0,1},{1,0},{2,3},{3,2},{4,5},{5,4},{6,7},{7,6},{8,9},{9,8},{10,11... | collective-permute-start | bytes 3145736 | tf_op jit(solution)/shard_map/ppermute | solution.py:8
  154.7 3.1 copy-start.5
  154.8 3.1 copy-start.10
  158.8 4.5 %copy-start.30 = (f32[32,1024]{1,0:T(8,128)S(1)}, f32[32,1024]{1,0:T(8,128)}, u32[]{:S(2)}) copy-start(f32[32,1024]{1,0:T(8,128)} %get-tuple-element.86) | copy-start | bytes 393220
  158.8 4.5 %copy-start.31 = (f32[32,1024]{1,0:T(8,128)S(1)}, f32[32,1024]{1,0:T(8,128)}, u32[]{:S(2)}) copy-start(f32[32,1024]{1,0:T(8,128)} %get-tuple-element.91) | copy-start | bytes 393220
  163.3 5.2 %copy-start.15 = (f32[64,1024]{1,0:T(8,128)S(1)}, f32[64,1024]{1,0:T(8,128)}, u32[]{:S(2)}) copy-start(f32[64,1024]{1,0:T(8,128)} %get-tuple-element.50) | copy-start | bytes 786436
  163.3 5.2 %copy-start.16 = (f32[64,1024]{1,0:T(8,128)S(1)}, f32[64,1024]{1,0:T(8,128)}, u32[]{:S(2)}) copy-start(f32[64,1024]{1,0:T(8,128)} %get-tuple-element.55) | copy-start | bytes 786436
  168.0 24.9 %collective-permute-start.4 = (f32[2,32,8,512]{3,1,2,0:T(8,128)S(1)}, f32[2,32,8,512]{3,1,2,0:T(8,128)}, u32[]{:S(2)}, u32[]{:S(2)}) collective-permute-start(f32[2,32,8,512]{3,1,2,0:T(8,128)S(1)} %get-tuple-element.40), channel_id=1, source_target_pairs={{0,2},{1,3},{2,0},{3,1},{4,6},{5,7},{6,4},{7,5},{8,10},{9,11},{10,... | collective-permute-start | bytes 3145736 | tf_op jit(solution)/shard_map/ppermute | solution.py:8
  200.4 3.1 copy-start.7
  200.4 3.1 copy-start.11
  204.5 4.5 %copy-start.28 = (f32[32,1024]{1,0:T(8,128)S(1)}, f32[32,1024]{1,0:T(8,128)}, u32[]{:S(2)}) copy-start(f32[32,1024]{1,0:T(8,128)} %get-tuple-element.87) | copy-start | bytes 393220
  204.5 4.5 %copy-start.29 = (f32[32,1024]{1,0:T(8,128)S(1)}, f32[32,1024]{1,0:T(8,128)}, u32[]{:S(2)}) copy-start(f32[32,1024]{1,0:T(8,128)} %get-tuple-element.90) | copy-start | bytes 393220
  209.0 6.4 %copy-start.20 = (f32[64,1024]{1,0:T(8,128)S(1)}, f32[64,1024]{1,0:T(8,128)}, u32[]{:S(2)}) copy-start(f32[64,1024]{1,0:T(8,128)} %get-tuple-element.124) | copy-start | bytes 786436
  213.5 2.9 copy-start.19
  213.7 24.4 %collective-permute-start.5 = (f32[2,32,8,512]{3,1,2,0:T(8,128)S(1)}, f32[2,32,8,512]{3,1,2,0:T(8,128)}, u32[]{:S(2)}, u32[]{:S(2)}) collective-permute-start(f32[2,32,8,512]{3,1,2,0:T(8,128)S(1)} %get-tuple-element.38), channel_id=1, source_target_pairs={{0,4},{1,5},{2,6},{3,7},{4,0},{5,1},{6,2},{7,3},{8,12},{9,13},{10,... | collective-permute-start | bytes 3145736 | tf_op jit(solution)/shard_map/ppermute | solution.py:8
  245.6 3.1 copy-start.2
  245.6 3.1 copy-start.3
  249.6 4.5 %copy-start.26 = (f32[32,1024]{1,0:T(8,128)S(1)}, f32[32,1024]{1,0:T(8,128)}, u32[]{:S(2)}) copy-start(f32[32,1024]{1,0:T(8,128)} %get-tuple-element.88) | copy-start | bytes 393220
  249.6 4.5 %copy-start.27 = (f32[32,1024]{1,0:T(8,128)S(1)}, f32[32,1024]{1,0:T(8,128)}, u32[]{:S(2)}) copy-start(f32[32,1024]{1,0:T(8,128)} %get-tuple-element.95) | copy-start | bytes 393220
  258.7 6.2 %copy-start.45 = (s32[1,1024]{1,0:T(1,128)S(1)}, s32[1,1024]{1,0:T(1,128)}, u32[]{:S(2)}) copy-start(s32[1,1024]{1,0:T(1,128)} %param.13) | copy-start | bytes 12292
  258.9 24.8 %collective-permute-start.6 = (f32[2,32,8,512]{3,1,2,0:T(8,128)S(1)}, f32[2,32,8,512]{3,1,2,0:T(8,128)}, u32[]{:S(2)}, u32[]{:S(2)}) collective-permute-start(f32[2,32,8,512]{3,1,2,0:T(8,128)S(1)} %get-tuple-element.36), channel_id=1, source_target_pairs={{0,8},{1,9},{2,10},{3,11},{4,12},{5,13},{6,14},{7,15},{8,0},{9,1},... | collective-permute-start | bytes 3145736 | tf_op jit(solution)/shard_map/ppermute | solution.py:8
  291.1 3.1 copy-start.12
  291.1 3.1 copy-start.13
  295.1 4.5 %copy-start.25 = (f32[32,1024]{1,0:T(8,128)S(1)}, f32[32,1024]{1,0:T(8,128)}, u32[]{:S(2)}) copy-start(f32[32,1024]{1,0:T(8,128)} %get-tuple-element.89) | copy-start | bytes 393220
  (5 other events, 4.5 us)
where the time goes:
time: 402 us; the launch traced here: 399 us
  local copies, waits for them, and re-layouts  132 us (33%)
  waiting for transfers between devices  101 us (25%)
  matrix products  62.7 us (16%)
  other arithmetic  42.4 us (11%)
  blocking collectives  41.2 us (10%)
  starting transfers between devices  17.8 us (4%)
    ppermute x7, waiting for transfers between devices, from_partner(): lax.ppermute(x, axis, [(i, i ^ 1 << distance) for i in range(lax.axis_siz...  101 us
    all_to_all x1, blocking collectives, shards(): lax.all_to_all(taken, ('lo', 'hi'), split_axis=3, concat_axis=3, tiled=True)  41.2 us
    broadcast_in_dim x14, local copies, waits for them, and re-layouts, widen(): jnp.broadcast_to(part[:, :, :, None], (rows, count, half, 2))  31.9 us
    dot_general x7, matrix products, apply_cols(): jnp.dot(matrix, yre, precision=lax.Precision.HIGHEST, preferred_element_t...  31.6 us
    dot_general x7, matrix products, apply_cols(): jnp.dot(matrix, yim, precision=lax.Precision.HIGHEST, preferred_element_t...  31.1 us
    squeeze x14, local copies, waits for them, and re-layouts, level(): real = jnp.concatenate([kept[0], got[0]], axis=0)  19.3 us
    ppermute x7, starting transfers between devices, from_partner(): lax.ppermute(x, axis, [(i, i ^ 1 << distance) for i in range(lax.axis_siz...  17.8 us
    concatenate x7, local copies, waits for them, and re-layouts, level(): real = jnp.concatenate([kept[0], got[0]], axis=0)  13.4 us
  transfers between devices with their start and end apart: 7, of which 6 were waited for; matrix products, arithmetic and copies ran while one was open for 9% of the time, Pallas kernels for 0%

commit v1 on v0

v1 whole, which is shorter than its diff:
```python
import functools

import jax
import jax.numpy as jnp
from jax import lax
from jax.experimental import pallas as pl
from jax.experimental.pallas import tpu as pltpu
from jax.sharding import PartitionSpec as P

F32 = jnp.float32
BF16 = jnp.bfloat16
VMEM = pl.BlockSpec(memory_space=pltpu.VMEM)
SMEM = pl.BlockSpec(memory_space=pltpu.SMEM)

SIN = (
    0.9999996039252741,
    -0.1666655344642713,
    0.008332407591595805,
    -0.00019808739967677424,
    2.699822692004479e-06,
    -2.036622659870151e-08,
)
COS = (
    0.999999989116818,
    -0.49999989185961996,
    0.04166649020175043,
    -0.0013887807832168462,
    2.476996623505445e-05,
    -2.70797756302502e-07,
    1.724760753325688e-09,
)
MIB = 1024 * 1024


def params(mib):
    return pltpu.CompilerParams(vmem_limit_bytes=mib * MIB)


def rev(value, bits):
    out = 0
    for i in range(bits):
        out = out | ((value >> i & 1) << (bits - 1 - i))
    return out


def horner(coefs, u):
    acc = jnp.full_like(u, coefs[-1])
    for c in reversed(coefs[:-1]):
        acc = acc * u + c
    return acc


def sincos(x):
    u = x * x
    return x * horner(SIN, u), horner(COS, u)


def dot(a, b, dims=((1,), (0,))):
    return lax.dot_general(a, b, (dims, ((), ())), preferred_element_type=F32)


def split(x):
    hi = x.astype(BF16)
    return hi, (x - hi.astype(F32)).astype(BF16)


def send_kernel(nv, half, x_ref, out_ref, columns):
    for kt in range(8):
        columns[kt] = x_ref[:, kt * 128 : kt * 128 + 128]
        for c in range(2):
            for v in range(nv):
                start = c * 256 + half + v
                part = columns[kt, pl.ds(start, 128, stride=2), :]
                at = (c * nv + v) * 128
                out_ref[rev(kt, 3), :, at : at + 128] = part.T


def final_kernel(nv, *refs):
    out_ref, columns = refs[-2:]
    ncv = 2 * nv
    for kt in range(8):
        for half, x_ref in enumerate(refs[:-2]):
            for c in range(2):
                for v in range(nv):
                    cv = c * nv + v
                    part = x_ref[pl.ds(kt * 128 * ncv + cv, 128, stride=ncv), :]
                    start = c * 256 + half + v
                    columns[kt, pl.ds(start, 128, stride=2), :] = part.T
        out_ref[:, kt * 128 : kt * 128 + 128] = columns[kt]


def pack_kernel(pos_ref, ain, aout, y1, y2, y3, x01, x02, x03, z0, z1, z2, z3):
    y = pos_ref[0]
    x = pos_ref[1]
    z = pos_ref[2]

    def put(dst, at, level, chunk, width):
        start = pl.multiple_of(chunk * width, width)
        dst[0:64, at : at + width] = ain[level, :, pl.ds(start, width)]
        dst[64:96, at : at + width] = aout[level, :, pl.ds(start, width)]

    ry = rev(y, 2)
    rx = rev(x, 2)
    for m, dst in ((1, y1), (2, y2), (3, y3)):
        put(dst, 0, 0, ry ^ rev(m, 2), 256)
    put(y2, 256, 1, (y >> 1) ^ 1, 512)
    for m, dst in ((1, x01), (2, x02), (3, x03)):
        put(dst, 0, 3, z * 4 + (rx ^ rev(m, 2)), 128)
        put(dst, 128, 4, rx ^ rev(m, 2), 256)
    put(x02, 384, 5, (x >> 1) ^ 1, 512)
    for m, dst in enumerate((z0, z1, z2, z3)):
        put(dst, 0, 3, (1 - z) * 4 + (rx ^ rev(m, 2)), 128)


def turned(parts, scratch, width):
    a, b = parts
    for t in range(width // 128):
        s = slice(t * 128, t * 128 + 128)
        full = jnp.concatenate([a(s), b(s), jnp.zeros((32, 128), F32)], axis=0)
        scratch[s, :] = full.T


def own(ain, aout, level, chunk, width):
    def read(ref, rows):
        def go(s):
            start = chunk * width + s.start
            return ref[level, 0:rows, pl.ds(pl.multiple_of(start, 128), 128)]

        return go

    return read(ain, 64), read(aout, 32)


def got(ref, at):
    return (
        lambda s: ref[0:64, at + s.start : at + s.stop],
        lambda s: ref[64:96, at + s.start : at + s.stop],
    )


def weights(interp_ref, w_ref, count):
    row = lax.broadcasted_iota(jnp.int32, (256, 64), 0)
    col = lax.broadcasted_iota(jnp.int32, (256, 64), 1)
    left = ((row >> 2) == col).astype(F32).astype(BF16)
    row = lax.broadcasted_iota(jnp.int32, (32, 128), 0)
    col = lax.broadcasted_iota(jnp.int32, (32, 128), 1)
    right = (row == (col >> 2)).astype(F32).astype(BF16)
    row = lax.broadcasted_iota(jnp.int32, (256, 128), 0)
    col = lax.broadcasted_iota(jnp.int32, (256, 128), 1)
    keep = (row & 3) == (col & 3)
    for level in range(count):
        for i, part in enumerate(split(interp_ref[level])):
            mid = dot(left, part, ((1,), (1,))).astype(BF16)
            full = jnp.where(keep, dot(mid, right), 0.0)
            w_ref[level, :, i * 128 : i * 128 + 128] = full.astype(BF16)


def table_lo_kernel(pos_ref, ain, aout, interp, y1, y2, y3, cos_ref, sin_ref, w_ref, scratch):
    y = pos_ref[0]
    ry = rev(y, 2)
    weights(interp, w_ref, 3)

    def emit(level, base, rows, ts):
        for t in range(ts):
            s, c = sincos(scratch[pl.ds(t, 128, stride=ts), :])
            at = pl.multiple_of((base + t) * 128, 128)
            cos_ref[level, pl.ds(at, 128), :] = c
            sin_ref[level, pl.ds(at, 128), :] = s

    for m, src in ((0, None), (1, y1), (2, y2), (3, y3)):
        parts = own(ain, aout, 0, ry, 256) if src is None else got(src, 0)
        turned(parts, scratch, 256)
        emit(0, (ry ^ rev(m, 2)) * 2, 256, 2)
    turned(own(ain, aout, 1, y >> 1, 512), scratch, 512)
    emit(1, (y >> 1) * 4, 512, 4)
    turned(got(y2, 256), scratch, 512)
    emit(1, (1 - (y >> 1)) * 4, 512, 4)
    turned(own(ain, aout, 2, 0, 1024), scratch, 1024)
    emit(2, 0, 1024, 8)


def table_hi_kernel(
    pos_ref, ain, aout, interp, x01, x02, x03, z0, z1, z2, z3, cos_ref, sin_ref, w_ref, scratch
):
    x = pos_ref[1]
    z = pos_ref[2]
    rx = rev(x, 2)
    weights(interp, w_ref, 4)

    def emit(level, base, ts):
        for t in range(ts):
            rows = [scratch[pl.ds(T * ts + t, 8, stride=8 * ts), :] for T in range(8)]
            s, c = sincos(jnp.concatenate(rows, axis=0))
            at = pl.multiple_of((base + t) * 64, 64)
            cos_ref[level, pl.ds(at, 64), :] = c
            sin_ref[level, pl.ds(at, 64), :] = s

    zs = (z0, z1, z2, z3)
    xs = (None, x01, x02, x03)
    for mz in range(2):
        for m in range(4):
            if mz == 0 and m == 0:
                parts = own(ain, aout, 0, z * 4 + rx, 128)
            else:
                parts = got(zs[m], 0) if mz else got(xs[m], 0)
            turned(parts, scratch, 128)
            emit(0, ((z ^ mz) * 4 + (rx ^ rev(m, 2))) * 2, 2)
    for m in range(4):
        parts = own(ain, aout, 1, rx, 256) if m == 0 else got(xs[m], 128)
        turned(parts, scratch, 256)
        emit(1, (rx ^ rev(m, 2)) * 4, 4)
    turned(own(ain, aout, 2, x >> 1, 512), scratch, 512)
    emit(2, (x >> 1) * 8, 8)
    turned(got(x02, 384), scratch, 512)
    emit(2, (1 - (x >> 1)) * 8, 8)
    turned(own(ain, aout, 3, 0, 1024), scratch, 1024)
    emit(3, 0, 16)


def spread(table, kind):
    lane = lax.broadcasted_iota(jnp.int32, table.shape, 1)
    return jnp.take_along_axis(table, kind * 32 + (lane >> 2), axis=1)


def step(nv, low, high, cos, sin, w):
    n = cos.shape[0]
    reals, imags = [], []
    sides = []
    for kind, src in enumerate((low, high)):
        c = spread(cos, kind)
        s = spread(sin, kind)
        re, im = [], []
        for v in range(nv):
            xr = src(v)
            xi = src(nv + v)
            re.append(xr * c - xi * s)
            im.append(xr * s + xi * c)
        sides.append(jnp.concatenate(re + im, axis=0))
    hi, lo = split(jnp.concatenate(sides, axis=1))
    first = dot(hi, w)
    out = first[:, :128] + first[:, 128:] + dot(lo, w[:, :128])
    c = spread(cos, 2)
    s = spread(sin, 2)
    re, im = [], []
    for v in range(nv):
        mr = out[v * n : v * n + n]
        mi = out[(nv + v) * n : (nv + v) * n + n]
        re.append(mr * c - mi * s)
        im.append(mr * s + mi * c)
    return re + im


def run_level(nv, level, count, rows, load_low, load_high, store, cos_ref, sin_ref, w_ref):
    group = 128 // rows
    w = w_ref[level]

    def body(i, _):
        for t in range(2):
            at = [
                pl.multiple_of((2 * (i * group + g) + t) * rows, rows) for g in range(group)
            ]
            c = jnp.concatenate([cos_ref[level, pl.ds(a, rows), :] for a in at], axis=0)
            s = jnp.concatenate([sin_ref[level, pl.ds(a, rows), :] for a in at], axis=0)
            low = lambda q: jnp.concatenate(
                [load_low(i * group + g, q) for g in range(group)], axis=0
            )
            high = lambda q: jnp.concatenate(
                [load_high(i * group + g, q) for g in range(group)], axis=0
            )
            for q, tile in enumerate(step(nv, low, high, c, s, w)):
                for g in range(group):
                    store(2 * (i * group + g) + t, q, tile[g * rows : g * rows + rows])
        return 0

    lax.fori_loop(0, count // group, body, 0)


def levels_lo_kernel(nv, x_ref, cos_ref, sin_ref, w_ref, out_ref, one, two):
    lanes = lambda q: slice(q * 128, q * 128 + 128)

    def keep(ref):
        def store(slab, q, tile):
            ref[slab, :, lanes(q)] = tile

        return store

    def last(slab, q, tile):
        for kp in range(16):
            out_ref[rev(kp, 4), pl.ds(pl.multiple_of(slab * 8, 8), 8), lanes(q)] = tile[
                kp * 8 : kp * 8 + 8
            ]

    run = functools.partial(run_level, nv)
    run(
        0, 4, 128,
        lambda m, q: x_ref[rev(m, 2) * 2, :, lanes(q)],
        lambda m, q: x_ref[rev(m, 2) * 2 + 1, :, lanes(q)],
        keep(one), cos_ref, sin_ref, w_ref,
    )
    run(
        1, 4, 128,
        lambda m, q: one[m, :, lanes(q)],
        lambda m, q: one[m + 4, :, lanes(q)],
        keep(two), cos_ref, sin_ref, w_ref,
    )
    run(
        2, 4, 128,
        lambda m, q: two[m, :, lanes(q)],
        lambda m, q: two[m + 4, :, lanes(q)],
        last, cos_ref, sin_ref, w_ref,
    )


def levels_hi_kernel(nv, where_ref, x_ref, cos_ref, sin_ref, w_ref, out_ref, one, two, last):
    lanes = lambda q: slice(q * 128, q * 128 + 128)
    ncv = 2 * nv

    def keep(ref):
        def store(slab, q, tile):
            ref[slab, :, lanes(q)] = tile

        return store

    def put(slab, q, tile):
        last[pl.ds(pl.multiple_of(slab * 64, 64), 64), q, :] = tile

    run = functools.partial(run_level, nv)
    run(
        0, 8, 64,
        lambda m, q: x_ref[rev(m, 3) * 2, :, lanes(q)],
        lambda m, q: x_ref[rev(m, 3) * 2 + 1, :, lanes(q)],
        keep(one), cos_ref, sin_ref, w_ref,
    )
    for level, src, store in ((1, one, keep(two)), (2, two, keep(one)), (3, one, put)):
        run(
            level, 8, 64,
            lambda m, q, src=src: src[m, :, lanes(q)],
            lambda m, q, src=src: src[m + 8, :, lanes(q)],
            store, cos_ref, sin_ref, w_ref,
        )

    def gather(e, _):
        for r in range(8):
            out_ref[e, r * ncv : r * ncv + ncv, :] = last[where_ref[e * 8 + r]]
        return 0

    lax.fori_loop(0, 128, gather, 0)


def shards(coefficients, angle_in, angle_out, interp, destination):
    nv = 2
    ncv = 2 * nv
    a = lax.axis_index("lo")
    c = lax.axis_index("hi")
    pos = jnp.stack([a >> 1, c >> 2, c >> 1 & 1]).astype(jnp.int32)
    shape = jax.ShapeDtypeStruct

    sends = pl.pallas_call(
        pack_kernel,
        out_shape=[shape((96, w), F32) for w in (256, 768, 256, 384, 896, 384, 128, 128, 128, 128)],
        in_specs=[SMEM, VMEM, VMEM],
        out_specs=[VMEM] * 10,
        compiler_params=params(24),
    )(pos, angle_in, angle_out)
    moved = []
    for m, s in zip((1, 2, 3), sends[:3]):
        moved.append(lax.ppermute(s, "lo", [(i, i ^ (2 * m)) for i in range(8)]))
    for m, s in zip((1, 2, 3), sends[3:6]):
        moved.append(lax.ppermute(s, "hi", [(i, i ^ (4 * m)) for i in range(16)]))
    for m, s in enumerate(sends[6:]):
        moved.append(lax.ppermute(s, "hi", [(i, i ^ (4 * m + 2)) for i in range(16)]))

    state = pl.pallas_call(
        functools.partial(send_kernel, nv, 0),
        out_shape=shape((8, 128, ncv * 128), F32),
        in_specs=[VMEM],
        out_specs=VMEM,
        scratch_shapes=[pltpu.VMEM((8, 512, 128), F32)],
        compiler_params=params(16),
    )(coefficients.reshape(512, 1024))
    state = lax.all_to_all(state, "lo", 0, 0, tiled=True)

    cos_lo, sin_lo, w_lo = pl.pallas_call(
        table_lo_kernel,
        out_shape=[shape((3, 1024, 128), F32)] * 2 + [shape((3, 256, 256), BF16)],
        in_specs=[SMEM] + [VMEM] * 6,
        out_specs=[VMEM] * 3,
        scratch_shapes=[pltpu.VMEM((1024, 128), F32)],
        compiler_params=params(24),
    )(pos, angle_in[:3], angle_out[:3], interp[:3], *moved[:3])
    cos_hi, sin_hi, w_hi = pl.pallas_call(
        table_hi_kernel,
        out_shape=[shape((4, 1024, 128), F32)] * 2 + [shape((4, 256, 256), BF16)],
        in_specs=[SMEM] + [VMEM] * 10,
        out_specs=[VMEM] * 3,
        scratch_shapes=[pltpu.VMEM((1024, 128), F32)],
        compiler_params=params(24),
    )(pos, angle_in[3:], angle_out[3:], interp[3:], *moved[3:])

    state = pl.pallas_call(
        functools.partial(levels_lo_kernel, nv),
        out_shape=shape((16, 64, ncv * 128), F32),
        in_specs=[VMEM] * 4,
        out_specs=VMEM,
        scratch_shapes=[pltpu.VMEM((8, 128, ncv * 128), F32)] * 2,
        compiler_params=params(32),
    )(state, cos_lo, sin_lo, w_lo)
    state = lax.all_to_all(state, "hi", 0, 0, tiled=True)

    wanted = destination[0]
    where = (wanted & 15) * 64 + (wanted >> 4 & 7) * 8 + (wanted >> 7)
    state = pl.pallas_call(
        functools.partial(levels_hi_kernel, nv),
        out_shape=shape((128, 8 * ncv, 128), F32),
        in_specs=[SMEM] + [VMEM] * 4,
        out_specs=VMEM,
        scratch_shapes=[pltpu.VMEM((16, 64, ncv * 128), F32)] * 2
        + [pltpu.VMEM((1024, ncv, 128), F32)],
        compiler_params=params(32),
    )(where, state, cos_hi, sin_hi, w_hi)
    state = lax.all_to_all(state, ("lo", "hi"), 0, 0, tiled=True)

    out = pl.pallas_call(
        functools.partial(final_kernel, nv),
        out_shape=shape((512, 1024), F32),
        in_specs=[VMEM],
        out_specs=VMEM,
        scratch_shapes=[pltpu.VMEM((8, 512, 128), F32)],
        compiler_params=params(16),
    )(state.reshape(1024 * ncv, 128))
    return out.reshape(2, 32, 8, 1024)


def solution(mesh):
    placed = (
        P(None, None, None, ("lo", "hi")),
        P(None, None, ("lo", "hi")),
        P(None, None, ("lo", "hi")),
        P(),
        P(("lo", "hi"), None),
    )
    return jax.shard_map(
        shards,
        mesh=mesh,
        in_specs=placed,
        out_specs=P(None, None, None, ("lo", "hi")),
        check_vma=False,
    )
```

time: 402 us -> 176 us (0.44)
  local copies, waits for them, and re-layouts: 132 us -> 21.4 us
  matrix products: 62.7 us -> 0 us
  waiting for transfers between devices: 101 us -> 51.5 us
  other arithmetic: 42.4 us -> 0.09 us
  Pallas kernels: 0 us -> 30.8 us
  starting transfers between devices: 17.8 us -> 34.2 us
    dot_general x14 -> x0, matrix products: 62.7 us -> none  [the longest x7 31.6 us: apply_cols(): jnp.dot(matrix, yre, precision=lax.Precision.HIGHEST, preferred_element_t...]
    ppermute x7 -> x10, waiting for transfers between devices: 101 us -> 51.5 us  [the longest x3 26 us: shards(): moved.append(lax.ppermute(s, 'lo', [(i, i ^ 2 * m) for i in range(8)]))]
    broadcast_in_dim x14 -> x0, local copies, waits for them, and re-layouts: 31.9 us -> none  [widen(): jnp.broadcast_to(part[:, :, :, None], (rows, count, half, 2))]
    pallas_call x0 -> x7, Pallas kernels: none -> 30.8 us  [the longest x1 13 us: shards(): pl.pallas_call(functools.partial(levels_hi_kernel, nv), out_shape=shape((...]
    squeeze x16 -> x0, local copies, waits for them, and re-layouts: 22.5 us -> none  [the longest x14 19.3 us: level(): real = jnp.concatenate([kept[0], got[0]], axis=0)]
    concatenate x14 -> x0, local copies, waits for them, and re-layouts: 19.1 us -> none  [the longest x7 13.4 us: level(): real = jnp.concatenate([kept[0], got[0]], axis=0)]
    all_to_all x0 -> x2, starting transfers between devices: none -> 16 us  [the longest x1 8.46 us: shards(): state = lax.all_to_all(state, 'lo', 0, 0, tiled=True)]
    gather x1 -> x0, local copies, waits for them, and re-layouts: 13.1 us -> none  [shards(): taken = jnp.take(state, destination[0], axis=3)]
  transfers between devices with their start and end apart: 7 -> 12, of which waited for: 6 -> 6; matrix products, arithmetic and copies ran while one was open for 9% -> 1% of each run, Pallas kernels for 0% -> 4%
where the time goes in v1:
time: 176 us
  waiting for transfers between devices  51.5 us (29%)
  blocking collectives  37.5 us (21%)
  starting transfers between devices  34.2 us (19%)
  Pallas kernels  30.8 us (18%)
  local copies, waits for them, and re-layouts  21.4 us (12%)
    all_to_all x1, blocking collectives, shards(): state = lax.all_to_all(state, ('lo', 'hi'), 0, 0, tiled=True)  37.5 us
    ppermute x3, waiting for transfers between devices, shards(): moved.append(lax.ppermute(s, 'lo', [(i, i ^ 2 * m) for i in range(8)]))  26 us
    ppermute x4, waiting for transfers between devices, shards(): moved.append(lax.ppermute(s, 'hi', [(i, i ^ 4 * m + 2) for i in range(16)]))  25.4 us
    unnamed x46, local copies, waits for them, and re-layouts  19.2 us
    pallas_call x1, Pallas kernels, shards(): pl.pallas_call(functools.partial(levels_hi_kernel, nv), out_shape=shape((...  13 us
    ppermute x4, starting transfers between devices, shards(): moved.append(lax.ppermute(s, 'hi', [(i, i ^ 4 * m + 2) for i in range(16)]))  9.27 us
    all_to_all x1, starting transfers between devices, shards(): state = lax.all_to_all(state, 'lo', 0, 0, tiled=True)  8.46 us
    all_to_all x1, starting transfers between devices, shards(): state = lax.all_to_all(state, 'hi', 0, 0, tiled=True)  7.57 us
  transfers between devices with their start and end apart: 12, of which 6 were waited for; matrix products, arithmetic and copies ran while one was open for 1% of the time, Pallas kernels for 4%

profile of v1, /device:TPU:1, one launch (start us, length us, event | category | flops | bytes accessed | tf_op | source)
XLA Modules:
  0.0 175.6 jit_solution(4015888222298494888)
XLA Ops:
  0.0 1.6 copy-done.3
  1.6 2.0 %shard_map.55 = f32[8,128,512]{2,1,0:T(8,128)} custom-call(f32[512,1024]{1,0:T(8,128)S(1)} %bitcast.8), custom_call_target="tpu_custom_call" | custom-call | tf_op jit(solution)/shard_map/pallas_call | solution.py:373
  3.6 8.5 %all-to-all-start = ((f32[8,128,512]{2,1,0:T(8,128)}), f32[8,128,512]{2,1,0:T(8,128)S(1)}, u32[]{:S(2)}, u32[]{:S(2)}) async-start(f32[8,128,512]{2,1,0:T(8,128)} %shard_map.55), calls=%async_computation | async-start | bytes 4194304 | tf_op jit(solution)/shard_map/all_to_all | solution.py:381
  12.0 0.1 pad_add_fusion.pos_ref
  12.1 1.5 copy-done.1
  13.6 0.7 shard_map.56
  14.3 0.6 copy-done.14
  14.9 0.7 copy-done.16
  15.6 0.6 copy-done.17
  16.2 0.6 copy-done.18
  16.8 0.6 copy-done.19
  17.4 0.6 copy-done.20
  18.0 3.0 %collective-permute-start.1 = (f32[96,768]{1,0:T(8,128)S(1)}, f32[96,768]{1,0:T(8,128)S(1)}, u32[]{:S(2)}, u32[]{:S(2)}) collective-permute-start(f32[96,768]{1,0:T(8,128)S(1)} %get-tuple-element.22), channel_id=1, source_target_pairs={{0,64},{16,80},{32,96},{48,112},{64,0},{80,16},{96,32},{112,48},{1... | collective-permute-start | bytes 884744 | tf_op jit(solution)/shard_map/ppermute | solution.py:367
  21.0 0.3 collective-permute-start
  21.3 0.6 collective-permute-start.2
  21.9 0.1 slice.18.ain
  22.0 0.8 slice.20.interp
  22.8 25.1 %collective-permute-done.y1 = f32[96,256]{1,0:T(8,128)S(1)} collective-permute-done((f32[96,256]{1,0:T(8,128)S(1)}, f32[96,256]{1,0:T(8,128)S(1)}, u32[]{:S(2)}, u32[]{:S(2)}) %collective-permute-start) | collective-permute-done | bytes 98336 | tf_op jit(solution)/shard_map/ppermute | solution.py:367
  47.9 0.9 collective-permute-done.1.y2
  48.8 2.1 %shard_map.57 = (f32[3,1024,128]{2,1,0:T(8,128)S(1)}, f32[3,1024,128]{2,1,0:T(8,128)S(1)}, bf16[3,256,256]{2,1,0:T(8,128)(2,1)S(1)}) custom-call(s32[3]{0:T(128)S(1)} %pad_add_fusion.pos_ref, f32[3,64,1024]{2,1,0:T(8,128)S(1)} %slice.18.ain, f32[3,32,1024]{2,1,0:T(8,128)S(1)} %slice.19.aout, f32[3,32,64]{2,1,0:T(8,128)S(1)} %slice.20.interp, ...), custom_call_target="tpu_custom_call" | custom-call | tf_op jit(solution)/shard_map/pallas_call | solution.py:383
  50.9 1.2 copy-done.8
  52.1 1.1 copy-done.10
  53.3 1.4 copy-done.9
  54.7 1.4 copy-done.11
  56.1 7.3 %shard_map.58 = f32[16,64,512]{2,1,0:T(8,128)S(1)} custom-call(f32[8,128,512]{2,1,0:T(8,128)S(1)} %all-to-all-done.x_ref, f32[3,1024,128]{2,1,0:T(8,128)S(1)} %copy-done.9, f32[3,1024,128]{2,1,0:T(8,128)S(1)} %copy-done.11, bf16[3,256,256]{2,1,0:T(8,128)(2,1)S(1)} %get-tuple-element.26.w_ref), custom_call_target="tpu_custom_call" | custom-call | tf_op jit(solution)/shard_map/pallas_call | solution.py:400
  63.4 0.0 copy-start
  63.5 1.3 copy-done
  64.8 7.6 %all-to-all-start.1 = ((f32[16,64,512]{2,1,0:T(8,128)}), f32[16,64,512]{2,1,0:T(8,128)S(1)}, u32[]{:S(2)}, u32[]{:S(2)}) async-start(f32[16,64,512]{2,1,0:T(8,128)} %copy-done), calls=%async_computation.1 | async-start | bytes 4194304 | tf_op jit(solution)/shard_map/all_to_all | solution.py:408
  72.4 3.0 %collective-permute-start.4 = (f32[96,896]{1,0:T(8,128)S(1)}, f32[96,896]{1,0:T(8,128)S(1)}, u32[]{:S(2)}, u32[]{:S(2)}) collective-permute-start(f32[96,896]{1,0:T(8,128)S(1)} %copy-done.13), channel_id=1, source_target_pairs={{0,8},{1,9},{2,10},{3,11},{4,12},{5,13},{6,14},{7,15},{8,0},{9,1},... | collective-permute-start | bytes 1032200 | tf_op jit(solution)/shard_map/ppermute | solution.py:369
  75.3 1.2 collective-permute-start.6
  76.5 0.3 collective-permute-start.7
  76.8 1.2 collective-permute-start.3
  78.0 0.9 collective-permute-start.5
  78.9 10.9 %collective-permute-done.6.z0 = f32[96,128]{1,0:T(8,128)S(1)} collective-permute-done((f32[96,128]{1,0:T(8,128)}, f32[96,128]{1,0:T(8,128)S(1)}, u32[]{:S(2)}, u32[]{:S(2)}) %collective-permute-start.6) | collective-permute-done | bytes 49184 | tf_op jit(solution)/shard_map/ppermute | solution.py:371
  89.8 5.2 %collective-permute-start.8 = (f32[96,128]{1,0:T(8,128)}, f32[96,128]{1,0:T(8,128)S(1)}, u32[]{:S(2)}, u32[]{:S(2)}) collective-permute-start(f32[96,128]{1,0:T(8,128)} %copy-done.18), channel_id=1, source_target_pairs={{0,10},{1,11},{2,8},{3,9},{4,14},{5,15},{6,12},{7,13},{8,2},{9,3},... | collective-permute-start | bytes 147464 | tf_op jit(solution)/shard_map/ppermute | solution.py:371
  95.0 13.2 %collective-permute-done.7.z1 = f32[96,128]{1,0:T(8,128)S(1)} collective-permute-done((f32[96,128]{1,0:T(8,128)}, f32[96,128]{1,0:T(8,128)S(1)}, u32[]{:S(2)}, u32[]{:S(2)}) %collective-permute-start.7) | collective-permute-done | bytes 49184 | tf_op jit(solution)/shard_map/ppermute | solution.py:371
  108.2 2.6 %collective-permute-start.9 = (f32[96,128]{1,0:T(8,128)}, f32[96,128]{1,0:T(8,128)S(1)}, u32[]{:S(2)}, u32[]{:S(2)}) collective-permute-start(f32[96,128]{1,0:T(8,128)} %copy-done.17), channel_id=1, source_target_pairs={{0,14},{1,15},{2,12},{3,13},{4,10},{5,11},{6,8},{7,9},{8,6},{9,7},... | collective-permute-start | bytes 147464 | tf_op jit(solution)/shard_map/ppermute | solution.py:371
  110.8 1.3 slice.21.ain
  112.2 0.2 collective-permute-done.8.z2
  112.4 1.1 collective-permute-done.9.z3
  113.5 3.6 %shard_map.59 = (f32[4,1024,128]{2,1,0:T(8,128)S(1)}, f32[4,1024,128]{2,1,0:T(8,128)S(1)}, bf16[4,256,256]{2,1,0:T(8,128)(2,1)S(1)}) custom-call(s32[3]{0:T(128)S(1)} %pad_add_fusion.pos_ref, f32[4,64,1024]{2,1,0:T(8,128)S(1)} %slice.21.ain, f32[4,32,1024]{2,1,0:T(8,128)S(1)} %slice.22.aout, f32[4,32,64]{2,1,0:T(8,128)S(1)} %slice.23.interp, ...), custom_call_target="tpu_custom_call" | custom-call | tf_op jit(solution)/shard_map/pallas_call | solution.py:391
  117.1 1.4 copy-done.4
  118.4 1.3 copy-done.6
  119.8 1.6 copy-done.5
  121.4 1.6 copy-done.7
  122.9 13.0 %shard_map.60 = f32[128,32,128]{2,1,0:T(8,128)S(1)} custom-call(s32[1024]{0:T(1024)S(1)} %bitcast.9, f32[16,64,512]{2,1,0:T(8,128)S(1)} %all-to-all-done.1.x_ref, f32[4,1024,128]{2,1,0:T(8,128)S(1)} %copy-done.5, f32[4,1024,128]{2,1,0:T(8,128)S(1)} %copy-done.7, bf16[4,256,256]{2,1,0:T(8,128)(2,1)S(1)} %get-tuple-element.36.w_ref), custom_call_target="tpu_custom_call" | custom-call | tf_op jit(solution)/shard_map/pallas_call | solution.py:412
  135.9 37.5 %all_to_all.15 = f32[128,32,128]{2,1,0:T(8,128)S(1)} all-to-all(f32[128,32,128]{2,1,0:T(8,128)S(1)} %shard_map.60), channel_id=1, replica_groups=mesh['lo'=8,'hi'=16] {'lo','hi'}, dimensions={0} | all-to-all | bytes 4194304 | tf_op jit(solution)/shard_map/all_to_all | solution.py:421
  173.5 2.2 %shard_map.61 = f32[512,1024]{1,0:T(8,128)} custom-call(f32[4096,128]{1,0:T(8,128)S(1)} %bitcast.7), custom_call_target="tpu_custom_call" | custom-call | tf_op jit(solution)/shard_map/pallas_call | solution.py:423
  (38 shorter events, 0.1 us)
Async XLA Ops:
  0.0 1.6 copy-start.3
  3.6 8.5 %copy-start.2 = (f32[7,32,1024]{2,1,0:T(8,128)S(1)}, f32[7,32,1024]{2,1,0:T(8,128)}, u32[]{:S(2)}) copy-start(f32[7,32,1024]{2,1,0:T(8,128)} %aout.1) | copy-start | bytes 2752516
  3.6 49.7 %all-to-all-start = ((f32[8,128,512]{2,1,0:T(8,128)}), f32[8,128,512]{2,1,0:T(8,128)S(1)}, u32[]{:S(2)}, u32[]{:S(2)}) async-start(f32[8,128,512]{2,1,0:T(8,128)} %shard_map.55), calls=%async_computation | async-start | bytes 4194304 | tf_op jit(solution)/shard_map/all_to_all | solution.py:381
  12.1 1.5 copy-start.1
  14.3 0.6 copy-start.14
  14.9 0.7 copy-start.16
  15.6 0.6 copy-start.17
  16.2 0.6 copy-start.18
  16.8 0.6 copy-start.19
  17.4 0.6 copy-start.20
  18.0 29.9 %copy-start.12 = (f32[96,896]{1,0:T(8,128)}, f32[96,896]{1,0:T(8,128)S(1)}, u32[]{:S(2)}) copy-start(f32[96,896]{1,0:T(8,128)S(1)} %get-tuple-element.28) | copy-start | bytes 1032196
  18.0 30.8 %collective-permute-start.1 = (f32[96,768]{1,0:T(8,128)S(1)}, f32[96,768]{1,0:T(8,128)S(1)}, u32[]{:S(2)}, u32[]{:S(2)}) collective-permute-start(f32[96,768]{1,0:T(8,128)S(1)} %get-tuple-element.22), channel_id=1, source_target_pairs={{0,64},{16,80},{32,96},{48,112},{64,0},{80,16},{96,32},{112,48},{1... | collective-permute-start | bytes 884744 | tf_op jit(solution)/shard_map/ppermute | solution.py:367
  21.0 26.9 %collective-permute-start = (f32[96,256]{1,0:T(8,128)S(1)}, f32[96,256]{1,0:T(8,128)S(1)}, u32[]{:S(2)}, u32[]{:S(2)}) collective-permute-start(f32[96,256]{1,0:T(8,128)S(1)} %get-tuple-element.21), channel_id=1, source_target_pairs={{0,32},{16,48},{32,0},{48,16},{64,96},{80,112},{96,64},{112,80},{1... | collective-permute-start | bytes 294920 | tf_op jit(solution)/shard_map/ppermute | solution.py:367
  21.3 26.6 %collective-permute-start.2 = (f32[96,256]{1,0:T(8,128)S(1)}, f32[96,256]{1,0:T(8,128)S(1)}, u32[]{:S(2)}, u32[]{:S(2)}) collective-permute-start(f32[96,256]{1,0:T(8,128)S(1)} %get-tuple-element.23), channel_id=1, source_target_pairs={{0,96},{16,112},{32,64},{48,80},{64,32},{80,48},{96,0},{112,16},{1... | collective-permute-start | bytes 294920 | tf_op jit(solution)/shard_map/ppermute | solution.py:367
  50.9 1.2 copy-start.8
  52.1 1.1 copy-start.10
  53.3 1.4 copy-start.9
  54.7 1.4 copy-start.11
  63.4 1.3 copy-start
  64.8 7.6 %copy-start.13 = (f32[96,896]{1,0:T(8,128)S(1)}, f32[96,896]{1,0:T(8,128)}, u32[]{:S(2)}) copy-start(f32[96,896]{1,0:T(8,128)} %copy-done.12) | copy-start | bytes 1032196
  64.8 13.2 %copy-start.15 = (f32[96,384]{1,0:T(8,128)S(1)}, f32[96,384]{1,0:T(8,128)}, u32[]{:S(2)}) copy-start(f32[96,384]{1,0:T(8,128)} %copy-done.14) | copy-start | bytes 442372
  64.8 46.0 %copy-start.22 = (s32[1,1024]{1,0:T(1,128)S(1)}, s32[1,1024]{1,0:T(1,128)}, u32[]{:S(2)}) copy-start(s32[1,1024]{1,0:T(1,128)} %param.9) | copy-start | bytes 12292
  64.8 55.0 %all-to-all-start.1 = ((f32[16,64,512]{2,1,0:T(8,128)}), f32[16,64,512]{2,1,0:T(8,128)S(1)}, u32[]{:S(2)}, u32[]{:S(2)}) async-start(f32[16,64,512]{2,1,0:T(8,128)} %copy-done), calls=%async_computation.1 | async-start | bytes 4194304 | tf_op jit(solution)/shard_map/all_to_all | solution.py:408
  72.3 39.8 %copy-start.21 = (f32[7,32,64]{2,1,0:T(8,128)S(1)}, f32[7,32,64]{2,1,0:T(8,128)}, u32[]{:S(2)}) copy-start(f32[7,32,64]{2,1,0:T(8,128)} %param.8) | copy-start | bytes 172036
  72.4 41.1 %collective-permute-start.4 = (f32[96,896]{1,0:T(8,128)S(1)}, f32[96,896]{1,0:T(8,128)S(1)}, u32[]{:S(2)}, u32[]{:S(2)}) collective-permute-start(f32[96,896]{1,0:T(8,128)S(1)} %copy-done.13), channel_id=1, source_target_pairs={{0,8},{1,9},{2,10},{3,11},{4,12},{5,13},{6,14},{7,15},{8,0},{9,1},... | collective-permute-start | bytes 1032200 | tf_op jit(solution)/shard_map/ppermute | solution.py:369
  75.3 14.5 %collective-permute-start.6 = (f32[96,128]{1,0:T(8,128)}, f32[96,128]{1,0:T(8,128)S(1)}, u32[]{:S(2)}, u32[]{:S(2)}) collective-permute-start(f32[96,128]{1,0:T(8,128)} %copy-done.20), channel_id=1, source_target_pairs={{0,2},{1,3},{2,0},{3,1},{4,6},{5,7},{6,4},{7,5},{8,10},{9,11},{10,... | collective-permute-start | bytes 147464 | tf_op jit(solution)/shard_map/ppermute | solution.py:371
  76.5 31.7 %collective-permute-start.7 = (f32[96,128]{1,0:T(8,128)}, f32[96,128]{1,0:T(8,128)S(1)}, u32[]{:S(2)}, u32[]{:S(2)}) collective-permute-start(f32[96,128]{1,0:T(8,128)} %copy-done.19), channel_id=1, source_target_pairs={{0,6},{1,7},{2,4},{3,5},{4,2},{5,3},{6,0},{7,1},{8,14},{9,15},{10,... | collective-permute-start | bytes 147464 | tf_op jit(solution)/shard_map/ppermute | solution.py:371
  76.8 36.7 %collective-permute-start.3 = (f32[96,384]{1,0:T(8,128)}, f32[96,384]{1,0:T(8,128)S(1)}, u32[]{:S(2)}, u32[]{:S(2)}) collective-permute-start(f32[96,384]{1,0:T(8,128)} %copy-done.16), channel_id=1, source_target_pairs={{0,4},{1,5},{2,6},{3,7},{4,0},{5,1},{6,2},{7,3},{8,12},{9,13},{10,... | collective-permute-start | bytes 442376 | tf_op jit(solution)/shard_map/ppermute | solution.py:369
  78.0 35.5 %collective-permute-start.5 = (f32[96,384]{1,0:T(8,128)S(1)}, f32[96,384]{1,0:T(8,128)S(1)}, u32[]{:S(2)}, u32[]{:S(2)}) collective-permute-start(f32[96,384]{1,0:T(8,128)S(1)} %copy-done.15), channel_id=1, source_target_pairs={{0,12},{1,13},{2,14},{3,15},{4,8},{5,9},{6,10},{7,11},{8,4},{9,5},... | collective-permute-start | bytes 442376 | tf_op jit(solution)/shard_map/ppermute | solution.py:369
  89.8 22.6 %collective-permute-start.8 = (f32[96,128]{1,0:T(8,128)}, f32[96,128]{1,0:T(8,128)S(1)}, u32[]{:S(2)}, u32[]{:S(2)}) collective-permute-start(f32[96,128]{1,0:T(8,128)} %copy-done.18), channel_id=1, source_target_pairs={{0,10},{1,11},{2,8},{3,9},{4,14},{5,15},{6,12},{7,13},{8,2},{9,3},... | collective-permute-start | bytes 147464 | tf_op jit(solution)/shard_map/ppermute | solution.py:371
  108.2 5.3 %collective-permute-start.9 = (f32[96,128]{1,0:T(8,128)}, f32[96,128]{1,0:T(8,128)S(1)}, u32[]{:S(2)}, u32[]{:S(2)}) collective-permute-start(f32[96,128]{1,0:T(8,128)} %copy-done.17), channel_id=1, source_target_pairs={{0,14},{1,15},{2,12},{3,13},{4,10},{5,11},{6,8},{7,9},{8,6},{9,7},... | collective-permute-start | bytes 147464 | tf_op jit(solution)/shard_map/ppermute | solution.py:371
  117.1 1.4 copy-start.4
  118.4 1.3 copy-start.6
  119.8 1.6 copy-start.5
  121.4 1.6 copy-start.7

commit v2 on v1

--- a/solution.py
+++ b/solution.py
@@ -360,7 +360,7 @@
         out_shape=[shape((96, w), F32) for w in (256, 768, 256, 384, 896, 384, 128, 128, 128, 128)],
         in_specs=[SMEM, VMEM, VMEM],
         out_specs=[VMEM] * 10,
-        compiler_params=params(24),
+        compiler_params=params(4),
     )(pos, angle_in, angle_out)
     moved = []
     for m, s in zip((1, 2, 3), sends[:3]):
@@ -376,8 +376,9 @@
         in_specs=[VMEM],
         out_specs=VMEM,
         scratch_shapes=[pltpu.VMEM((8, 512, 128), F32)],
-        compiler_params=params(16),
+        compiler_params=params(6),
     )(coefficients.reshape(512, 1024))
+    state, *moved[:3] = lax.optimization_barrier((state, *moved[:3]))
     state = lax.all_to_all(state, "lo", 0, 0, tiled=True)
 
     cos_lo, sin_lo, w_lo = pl.pallas_call(
@@ -386,7 +387,7 @@
         in_specs=[SMEM] + [VMEM] * 6,
         out_specs=[VMEM] * 3,
         scratch_shapes=[pltpu.VMEM((1024, 128), F32)],
-        compiler_params=params(24),
+        compiler_params=params(8),
     )(pos, angle_in[:3], angle_out[:3], interp[:3], *moved[:3])
     cos_hi, sin_hi, w_hi = pl.pallas_call(
         table_hi_kernel,
@@ -394,7 +395,7 @@
         in_specs=[SMEM] + [VMEM] * 10,
         out_specs=[VMEM] * 3,
         scratch_shapes=[pltpu.VMEM((1024, 128), F32)],
-        compiler_params=params(24),
+        compiler_params=params(8),
     )(pos, angle_in[3:], angle_out[3:], interp[3:], *moved[3:])
 
     state = pl.pallas_call(
@@ -403,8 +404,9 @@
         in_specs=[VMEM] * 4,
         out_specs=VMEM,
         scratch_shapes=[pltpu.VMEM((8, 128, ncv * 128), F32)] * 2,
-        compiler_params=params(32),
+        compiler_params=params(12),
     )(state, cos_lo, sin_lo, w_lo)
+    state, cos_hi, sin_hi, w_hi = lax.optimization_barrier((state, cos_hi, sin_hi, w_hi))
     state = lax.all_to_all(state, "hi", 0, 0, tiled=True)
 
     wanted = destination[0]
@@ -416,7 +418,7 @@
         out_specs=VMEM,
         scratch_shapes=[pltpu.VMEM((16, 64, ncv * 128), F32)] * 2
         + [pltpu.VMEM((1024, ncv, 128), F32)],
-        compiler_params=params(32),
+        compiler_params=params(14),
     )(where, state, cos_hi, sin_hi, w_hi)
     state = lax.all_to_all(state, ("lo", "hi"), 0, 0, tiled=True)
 
@@ -426,7 +428,7 @@
         in_specs=[VMEM],
         out_specs=VMEM,
         scratch_shapes=[pltpu.VMEM((8, 512, 128), F32)],
-        compiler_params=params(16),
+        compiler_params=params(6),
     )(state.reshape(1024 * ncv, 128))
     return out.reshape(2, 32, 8, 1024)
 

time: 176 us -> 171 us (0.972)
  blocking collectives: 37.5 us -> 43.5 us
  starting transfers between devices: 34.2 us -> 29.2 us
  waiting for transfers between devices: 51.5 us -> 48.4 us
  local copies, waits for them, and re-layouts: 21.4 us -> 19.5 us
    all_to_all x1, waiting for transfers between devices: 0.01 us -> 26.9 us  [shards(): state = lax.all_to_all(state, 'hi', 0, 0, tiled=True)]
    ppermute x3, waiting for transfers between devices: 26 us -> 6.75 us  [shards(): moved.append(lax.ppermute(s, 'lo', [(i, i ^ 2 * m) for i in range(8)]))]
    ppermute x4, waiting for transfers between devices: 25.4 us -> 14.7 us  [shards(): moved.append(lax.ppermute(s, 'hi', [(i, i ^ 4 * m + 2) for i in range(16)]))]
    all_to_all x1, blocking collectives: 37.5 us -> 43.5 us  [shards(): state = lax.all_to_all(state, ('lo', 'hi'), 0, 0, tiled=True)]
    ppermute x4, starting transfers between devices: 9.27 us -> 6.54 us  [shards(): moved.append(lax.ppermute(s, 'hi', [(i, i ^ 4 * m + 2) for i in range(16)]))]
  transfers between devices with their start and end apart: 12 -> 12, of which waited for: 6 -> 4; matrix products, arithmetic and copies ran while one was open for 1% -> 1% of each run, Pallas kernels for 4% -> 4%
where the time goes in v2:
time: 171 us
  waiting for transfers between devices  48.4 us (28%)
  blocking collectives  43.5 us (25%)
  Pallas kernels  29.8 us (17%)
  starting transfers between devices  29.2 us (17%)
  local copies, waits for them, and re-layouts  19.5 us (11%)
    all_to_all x1, blocking collectives, shards(): state = lax.all_to_all(state, ('lo', 'hi'), 0, 0, tiled=True)  43.5 us
    all_to_all x1, waiting for transfers between devices, shards(): state = lax.all_to_all(state, 'hi', 0, 0, tiled=True)  26.9 us
    unnamed x46, local copies, waits for them, and re-layouts  18.1 us
    ppermute x4, waiting for transfers between devices, shards(): moved.append(lax.ppermute(s, 'hi', [(i, i ^ 4 * m + 2) for i in range(16)]))  14.7 us
    pallas_call x1, Pallas kernels, shards(): pl.pallas_call(functools.partial(levels_hi_kernel, nv), out_shape=shape((...  12.4 us
    all_to_all x1, starting transfers between devices, shards(): state = lax.all_to_all(state, 'lo', 0, 0, tiled=True)  7.56 us
    pallas_call x1, Pallas kernels, shards(): pl.pallas_call(functools.partial(levels_lo_kernel, nv), out_shape=shape((...  7 us
    all_to_all x1, starting transfers between devices, shards(): state = lax.all_to_all(state, 'hi', 0, 0, tiled=True)  6.77 us
  transfers between devices with their start and end apart: 12, of which 4 were waited for; matrix products, arithmetic and copies ran while one was open for 1% of the time, Pallas kernels for 4%

profile of v2, /device:TPU:1, one launch (start us, length us, event | category | flops | bytes accessed | tf_op | source)
XLA Modules:
  0.0 170.6 jit_solution(2072189269327172333)
XLA Ops:
  0.0 0.1 pad_add_fusion.pos_ref
  0.1 1.5 copy-done.1
  1.6 1.2 copy-done.3
  2.8 0.7 shard_map.56
  3.4 0.6 copy-done.17
  4.0 0.6 copy-done.18
  4.6 0.6 copy-done.19
  5.3 0.6 copy-done.20
  5.9 3.7 %collective-permute-start.1 = (f32[96,768]{1,0:T(8,128)S(1)}, f32[96,768]{1,0:T(8,128)S(1)}, u32[]{:S(2)}, u32[]{:S(2)}) collective-permute-start(f32[96,768]{1,0:T(8,128)S(1)} %get-tuple-element.30), channel_id=1, source_target_pairs={{0,64},{16,80},{32,96},{48,112},{64,0},{80,16},{96,32},{112,48},{1... | collective-permute-start | bytes 884744 | tf_op jit(solution)/shard_map/ppermute | solution.py:367
  9.6 0.4 collective-permute-start
  10.0 0.5 collective-permute-start.2
  10.5 1.9 %shard_map.55 = f32[8,128,512]{2,1,0:T(8,128)} custom-call(f32[512,1024]{1,0:T(8,128)S(1)} %bitcast.8), custom_call_target="tpu_custom_call" | custom-call | tf_op jit(solution)/shard_map/pallas_call | solution.py:373
  12.4 6.1 %collective-permute-done.y1 = f32[96,256]{1,0:T(8,128)S(1)} collective-permute-done((f32[96,256]{1,0:T(8,128)S(1)}, f32[96,256]{1,0:T(8,128)S(1)}, u32[]{:S(2)}, u32[]{:S(2)}) %collective-permute-start) | collective-permute-done | bytes 98336 | tf_op jit(solution)/shard_map/ppermute | solution.py:367
  18.6 0.6 collective-permute-done.2.y3
  19.2 7.6 %all-to-all-start = ((f32[8,128,512]{2,1,0:T(8,128)}), f32[8,128,512]{2,1,0:T(8,128)S(1)}, u32[]{:S(2)}, u32[]{:S(2)}) async-start(f32[8,128,512]{2,1,0:T(8,128)} %shard_map.55), calls=%async_computation | async-start | bytes 4194304 | tf_op jit(solution)/shard_map/all_to_all | solution.py:382
  26.8 2.8 %collective-permute-start.4 = (f32[96,896]{1,0:T(8,128)}, f32[96,896]{1,0:T(8,128)S(1)}, u32[]{:S(2)}, u32[]{:S(2)}) collective-permute-start(f32[96,896]{1,0:T(8,128)} %copy-done.14), channel_id=1, source_target_pairs={{0,8},{1,9},{2,10},{3,11},{4,12},{5,13},{6,14},{7,15},{8,0},{9,1},... | collective-permute-start | bytes 1032200 | tf_op jit(solution)/shard_map/ppermute | solution.py:369
  29.6 0.3 collective-permute-start.3
  29.9 0.6 collective-permute-start.5
  30.5 0.7 collective-permute-start.6
  31.2 1.3 collective-permute-start.7
  32.5 14.7 %collective-permute-done.6.z0 = f32[96,128]{1,0:T(8,128)S(1)} collective-permute-done((f32[96,128]{1,0:T(8,128)}, f32[96,128]{1,0:T(8,128)S(1)}, u32[]{:S(2)}, u32[]{:S(2)}) %collective-permute-start.6) | collective-permute-done | bytes 49184 | tf_op jit(solution)/shard_map/ppermute | solution.py:371
  47.2 3.2 %collective-permute-start.8 = (f32[96,128]{1,0:T(8,128)}, f32[96,128]{1,0:T(8,128)S(1)}, u32[]{:S(2)}, u32[]{:S(2)}) collective-permute-start(f32[96,128]{1,0:T(8,128)} %copy-done.18), channel_id=1, source_target_pairs={{0,10},{1,11},{2,8},{3,9},{4,14},{5,15},{6,12},{7,13},{8,2},{9,3},... | collective-permute-start | bytes 147464 | tf_op jit(solution)/shard_map/ppermute | solution.py:371
  50.4 0.0 collective-permute-done.7.z1
  50.4 1.3 collective-permute-start.9
  51.7 1.2 slice.18.ain
  52.9 0.0 copy-start.21
  53.0 0.1 slice.21.ain
  53.1 0.7 copy-done.21
  53.8 2.1 %shard_map.57 = (f32[3,1024,128]{2,1,0:T(8,128)S(1)}, f32[3,1024,128]{2,1,0:T(8,128)S(1)}, bf16[3,256,256]{2,1,0:T(8,128)(2,1)S(1)}) custom-call(s32[3]{0:T(128)S(1)} %pad_add_fusion.pos_ref, f32[3,64,1024]{2,1,0:T(8,128)S(1)} %slice.18.ain, f32[3,32,1024]{2,1,0:T(8,128)S(1)} %slice.19.aout, f32[3,32,64]{2,1,0:T(8,128)S(1)} %slice.20.interp, ...), custom_call_target="tpu_custom_call" | custom-call | tf_op jit(solution)/shard_map/pallas_call | solution.py:384
  55.9 1.2 copy-done.10
  57.1 1.1 copy-done.12
  58.2 0.0 collective-permute-done.8.z2
  58.2 0.0 collective-permute-done.9.z3
  58.3 3.5 %shard_map.59 = (f32[4,1024,128]{2,1,0:T(8,128)S(1)}, f32[4,1024,128]{2,1,0:T(8,128)S(1)}, bf16[4,256,256]{2,1,0:T(8,128)(2,1)S(1)}) custom-call(s32[3]{0:T(128)S(1)} %pad_add_fusion.pos_ref, f32[4,64,1024]{2,1,0:T(8,128)S(1)} %slice.21.ain, f32[4,32,1024]{2,1,0:T(8,128)S(1)} %slice.22.aout, f32[4,32,64]{2,1,0:T(8,128)S(1)} %slice.23.interp, ...), custom_call_target="tpu_custom_call" | custom-call | tf_op jit(solution)/shard_map/pallas_call | solution.py:392
  61.8 1.4 copy-done.6
  63.2 1.3 copy-done.8
  64.5 1.4 copy-done.11
  65.9 1.4 copy-done.13
  67.3 7.0 %shard_map.58 = f32[16,64,512]{2,1,0:T(8,128)S(1)} custom-call(f32[8,128,512]{2,1,0:T(8,128)S(1)} %all-to-all-done.x_ref, f32[3,1024,128]{2,1,0:T(8,128)S(1)} %copy-done.11, f32[3,1024,128]{2,1,0:T(8,128)S(1)} %copy-done.13, bf16[3,256,256]{2,1,0:T(8,128)(2,1)S(1)} %get-tuple-element.38.w_ref), custom_call_target="tpu_custom_call" | custom-call | tf_op jit(solution)/shard_map/pallas_call | solution.py:401
  74.3 0.0 copy-start
  74.3 1.3 copy-done
  75.7 6.8 %all-to-all-start.1 = ((f32[16,64,512]{2,1,0:T(8,128)}), f32[16,64,512]{2,1,0:T(8,128)S(1)}, u32[]{:S(2)}, u32[]{:S(2)}) async-start(f32[16,64,512]{2,1,0:T(8,128)} %copy-done), calls=%async_computation.1 | async-start | bytes 4194304 | tf_op jit(solution)/shard_map/all_to_all | solution.py:410
  82.5 26.9 %all-to-all-done.1.x_ref = f32[16,64,512]{2,1,0:T(8,128)S(1)} async-done(((f32[16,64,512]{2,1,0:T(8,128)}), f32[16,64,512]{2,1,0:T(8,128)S(1)}, u32[]{:S(2)}, u32[]{:S(2)}) %all-to-all-start.1) | async-done | bytes 2097184 | tf_op jit(solution)/shard_map/all_to_all | solution.py:410
  109.4 1.6 copy-done.7
  111.0 1.6 copy-done.9
  112.6 12.4 %shard_map.60 = f32[128,32,128]{2,1,0:T(8,128)S(1)} custom-call(s32[1024]{0:T(1024)S(1)} %bitcast.9, f32[16,64,512]{2,1,0:T(8,128)S(1)} %all-to-all-done.1.x_ref, f32[4,1024,128]{2,1,0:T(8,128)S(1)} %copy-done.7, f32[4,1024,128]{2,1,0:T(8,128)S(1)} %copy-done.9, bf16[4,256,256]{2,1,0:T(8,128)(2,1)S(1)} %get-tuple-element.52.w_ref), custom_call_target="tpu_custom_call" | custom-call | tf_op jit(solution)/shard_map/pallas_call | solution.py:414
  125.0 43.5 %all_to_all.15 = f32[128,32,128]{2,1,0:T(8,128)S(1)} all-to-all(f32[128,32,128]{2,1,0:T(8,128)S(1)} %shard_map.60), channel_id=1, replica_groups=mesh['lo'=8,'hi'=16] {'lo','hi'}, dimensions={0} | all-to-all | bytes 4194304 | tf_op jit(solution)/shard_map/all_to_all | solution.py:423
  168.5 2.2 %shard_map.61 = f32[512,1024]{1,0:T(8,128)} custom-call(f32[4096,128]{1,0:T(8,128)S(1)} %bitcast.7), custom_call_target="tpu_custom_call" | custom-call | tf_op jit(solution)/shard_map/pallas_call | solution.py:425
  (38 shorter events, 0.2 us)
Async XLA Ops:
  0.1 1.5 copy-start.1
  1.6 1.2 copy-start.3
  2.8 7.7 %copy-start.5 = (f32[2,32,8,1024]{3,2,1,0:T(8,128)S(1)}, f32[2,32,8,1024]{3,2,1,0:T(8,128)}, u32[]{:S(2)}) copy-start(f32[2,32,8,1024]{3,2,1,0:T(8,128)} %param.5) | copy-start | bytes 6291460
  3.4 0.6 copy-start.17
  4.0 0.6 copy-start.18
  4.6 0.6 copy-start.19
  5.3 0.6 copy-start.20
  5.9 4.2 %copy-start.14 = (f32[96,896]{1,0:T(8,128)}, f32[96,896]{1,0:T(8,128)S(1)}, u32[]{:S(2)}) copy-start(f32[96,896]{1,0:T(8,128)S(1)} %get-tuple-element.40) | copy-start | bytes 1032196
  5.9 4.2 %copy-start.15 = (f32[96,384]{1,0:T(8,128)}, f32[96,384]{1,0:T(8,128)S(1)}, u32[]{:S(2)}) copy-start(f32[96,384]{1,0:T(8,128)S(1)} %get-tuple-element.41) | copy-start | bytes 442372
  5.9 6.6 %copy-start.16 = (f32[96,384]{1,0:T(8,128)}, f32[96,384]{1,0:T(8,128)S(1)}, u32[]{:S(2)}) copy-start(f32[96,384]{1,0:T(8,128)S(1)} %get-tuple-element.39) | copy-start | bytes 442372
  5.9 13.3 %collective-permute-start.1 = (f32[96,768]{1,0:T(8,128)S(1)}, f32[96,768]{1,0:T(8,128)S(1)}, u32[]{:S(2)}, u32[]{:S(2)}) collective-permute-start(f32[96,768]{1,0:T(8,128)S(1)} %get-tuple-element.30), channel_id=1, source_target_pairs={{0,64},{16,80},{32,96},{48,112},{64,0},{80,16},{96,32},{112,48},{1... | collective-permute-start | bytes 884744 | tf_op jit(solution)/shard_map/ppermute | solution.py:367
  9.6 9.0 %collective-permute-start = (f32[96,256]{1,0:T(8,128)S(1)}, f32[96,256]{1,0:T(8,128)S(1)}, u32[]{:S(2)}, u32[]{:S(2)}) collective-permute-start(f32[96,256]{1,0:T(8,128)S(1)} %get-tuple-element.29), channel_id=1, source_target_pairs={{0,32},{16,48},{32,0},{48,16},{64,96},{80,112},{96,64},{112,80},{1... | collective-permute-start | bytes 294920 | tf_op jit(solution)/shard_map/ppermute | solution.py:367
  10.0 9.2 %collective-permute-start.2 = (f32[96,256]{1,0:T(8,128)S(1)}, f32[96,256]{1,0:T(8,128)S(1)}, u32[]{:S(2)}, u32[]{:S(2)}) collective-permute-start(f32[96,256]{1,0:T(8,128)S(1)} %get-tuple-element.31), channel_id=1, source_target_pairs={{0,96},{16,112},{32,64},{48,80},{64,32},{80,48},{96,0},{112,16},{1... | collective-permute-start | bytes 294920 | tf_op jit(solution)/shard_map/ppermute | solution.py:367
  12.4 40.5 %copy-start.4 = (f32[7,32,1024]{2,1,0:T(8,128)S(1)}, f32[7,32,1024]{2,1,0:T(8,128)}, u32[]{:S(2)}) copy-start(f32[7,32,1024]{2,1,0:T(8,128)} %aout.1) | copy-start | bytes 2752516
  19.2 45.3 %all-to-all-start = ((f32[8,128,512]{2,1,0:T(8,128)}), f32[8,128,512]{2,1,0:T(8,128)S(1)}, u32[]{:S(2)}, u32[]{:S(2)}) async-start(f32[8,128,512]{2,1,0:T(8,128)} %shard_map.55), calls=%async_computation | async-start | bytes 4194304 | tf_op jit(solution)/shard_map/all_to_all | solution.py:382
  26.8 26.2 %copy-start.2 = (f32[7,64,1024]{2,1,0:T(8,128)S(1)}, f32[7,64,1024]{2,1,0:T(8,128)}, u32[]{:S(2)}) copy-start(f32[7,64,1024]{2,1,0:T(8,128)} %ain.1) | copy-start | bytes 5505028
  26.8 31.5 %collective-permute-start.4 = (f32[96,896]{1,0:T(8,128)}, f32[96,896]{1,0:T(8,128)S(1)}, u32[]{:S(2)}, u32[]{:S(2)}) collective-permute-start(f32[96,896]{1,0:T(8,128)} %copy-done.14), channel_id=1, source_target_pairs={{0,8},{1,9},{2,10},{3,11},{4,12},{5,13},{6,14},{7,15},{8,0},{9,1},... | collective-permute-start | bytes 1032200 | tf_op jit(solution)/shard_map/ppermute | solution.py:369
  29.6 28.6 %collective-permute-start.3 = (f32[96,384]{1,0:T(8,128)}, f32[96,384]{1,0:T(8,128)S(1)}, u32[]{:S(2)}, u32[]{:S(2)}) collective-permute-start(f32[96,384]{1,0:T(8,128)} %copy-done.16), channel_id=1, source_target_pairs={{0,4},{1,5},{2,6},{3,7},{4,0},{5,1},{6,2},{7,3},{8,12},{9,13},{10,... | collective-permute-start | bytes 442376 | tf_op jit(solution)/shard_map/ppermute | solution.py:369
  29.9 28.3 %collective-permute-start.5 = (f32[96,384]{1,0:T(8,128)}, f32[96,384]{1,0:T(8,128)S(1)}, u32[]{:S(2)}, u32[]{:S(2)}) collective-permute-start(f32[96,384]{1,0:T(8,128)} %copy-done.15), channel_id=1, source_target_pairs={{0,12},{1,13},{2,14},{3,15},{4,8},{5,9},{6,10},{7,11},{8,4},{9,5},... | collective-permute-start | bytes 442376 | tf_op jit(solution)/shard_map/ppermute | solution.py:369
  30.5 16.7 %collective-permute-start.6 = (f32[96,128]{1,0:T(8,128)}, f32[96,128]{1,0:T(8,128)S(1)}, u32[]{:S(2)}, u32[]{:S(2)}) collective-permute-start(f32[96,128]{1,0:T(8,128)} %copy-done.20), channel_id=1, source_target_pairs={{0,2},{1,3},{2,0},{3,1},{4,6},{5,7},{6,4},{7,5},{8,10},{9,11},{10,... | collective-permute-start | bytes 147464 | tf_op jit(solution)/shard_map/ppermute | solution.py:371
  31.2 19.2 %collective-permute-start.7 = (f32[96,128]{1,0:T(8,128)}, f32[96,128]{1,0:T(8,128)S(1)}, u32[]{:S(2)}, u32[]{:S(2)}) collective-permute-start(f32[96,128]{1,0:T(8,128)} %copy-done.19), channel_id=1, source_target_pairs={{0,6},{1,7},{2,4},{3,5},{4,2},{5,3},{6,0},{7,1},{8,14},{9,15},{10,... | collective-permute-start | bytes 147464 | tf_op jit(solution)/shard_map/ppermute | solution.py:371
  47.2 11.0 %collective-permute-start.8 = (f32[96,128]{1,0:T(8,128)}, f32[96,128]{1,0:T(8,128)S(1)}, u32[]{:S(2)}, u32[]{:S(2)}) collective-permute-start(f32[96,128]{1,0:T(8,128)} %copy-done.18), channel_id=1, source_target_pairs={{0,10},{1,11},{2,8},{3,9},{4,14},{5,15},{6,12},{7,13},{8,2},{9,3},... | collective-permute-start | bytes 147464 | tf_op jit(solution)/shard_map/ppermute | solution.py:371
  50.4 7.8 %collective-permute-start.9 = (f32[96,128]{1,0:T(8,128)}, f32[96,128]{1,0:T(8,128)S(1)}, u32[]{:S(2)}, u32[]{:S(2)}) collective-permute-start(f32[96,128]{1,0:T(8,128)} %copy-done.17), channel_id=1, source_target_pairs={{0,14},{1,15},{2,12},{3,13},{4,10},{5,11},{6,8},{7,9},{8,6},{9,7},... | collective-permute-start | bytes 147464 | tf_op jit(solution)/shard_map/ppermute | solution.py:371
  52.9 0.9 copy-start.21
  55.9 1.2 copy-start.10
  57.1 1.1 copy-start.12
  61.8 1.4 copy-start.6
  63.2 1.3 copy-start.8
  64.5 1.4 copy-start.11
  65.9 1.4 copy-start.13
  74.3 1.3 copy-start
  75.7 6.8 %copy-start.22 = (s32[1,1024]{1,0:T(1,128)S(1)}, s32[1,1024]{1,0:T(1,128)}, u32[]{:S(2)}) copy-start(s32[1,1024]{1,0:T(1,128)} %param.9) | copy-start | bytes 12292
  75.7 33.7 %all-to-all-start.1 = ((f32[16,64,512]{2,1,0:T(8,128)}), f32[16,64,512]{2,1,0:T(8,128)S(1)}, u32[]{:S(2)}, u32[]{:S(2)}) async-start(f32[16,64,512]{2,1,0:T(8,128)} %copy-done), calls=%async_computation.1 | async-start | bytes 4194304 | tf_op jit(solution)/shard_map/all_to_all | solution.py:410
  109.4 1.6 copy-start.7
  111.0 1.6 copy-start.9

commit v3 on v2

v3 whole, which is shorter than its diff:
```python
import functools

import jax
import jax.numpy as jnp
from jax import lax
from jax.experimental import pallas as pl
from jax.experimental.pallas import tpu as pltpu
from jax.sharding import PartitionSpec as P

F32 = jnp.float32
BF16 = jnp.bfloat16
VMEM = pl.BlockSpec(memory_space=pltpu.VMEM)
SMEM = pl.BlockSpec(memory_space=pltpu.SMEM)
ANY = pl.BlockSpec(memory_space=pl.ANY)
HBM = pl.BlockSpec(memory_space=pltpu.HBM)
AXES = ("y", "zh", "x", "zl", "c")
PI = 3.141592653589793
TAU = 6.283185307179586

SIN = (
    0.9999996039252741,
    -0.1666655344642713,
    0.008332407591595805,
    -0.00019808739967677424,
    2.699822692004479e-06,
    -2.036622659870151e-08,
)
COS = (
    0.999999989116818,
    -0.49999989185961996,
    0.04166649020175043,
    -0.0013887807832168462,
    2.476996623505445e-05,
    -2.70797756302502e-07,
    1.724760753325688e-09,
)
MIB = 1024 * 1024


def params(mib):
    return pltpu.CompilerParams(vmem_limit_bytes=mib * MIB)


def rev(value, bits):
    out = 0
    for i in range(bits):
        out = out | ((value >> i & 1) << (bits - 1 - i))
    return out


def horner(coefs, u):
    acc = jnp.full_like(u, coefs[-1])
    for c in reversed(coefs[:-1]):
        acc = acc * u + c
    return acc


def sincos(x):
    u = x * x
    return x * horner(SIN, u), horner(COS, u)


def dot(a, b, dims=((1,), (0,))):
    return lax.dot_general(a, b, (dims, ((), ())), preferred_element_type=F32)


def split(x):
    hi = x.astype(BF16)
    return hi, (x - hi.astype(F32)).astype(BF16)


def send_kernel(nv, x_ref, out_ref, columns):
    for kt in range(8):
        columns[kt] = x_ref[:, kt * 128 : kt * 128 + 128]
        for c in range(2):
            for v in range(nv):
                part = columns[kt, pl.ds(c * 256 + v, 128, stride=2), :].T
                lanes = slice((c * nv + v) * 128, (c * nv + v) * 128 + 128)
                for core in range(2):
                    out_ref[rev(kt, 3) * 2 + core, :, lanes] = part[core * 64 : core * 64 + 64]


def final_kernel(nv, x_ref, out_ref, columns):
    ncv = 2 * nv
    for kt in range(8):
        for c in range(2):
            for v in range(nv):
                cv = c * nv + v
                part = x_ref[pl.ds(kt * 128 * ncv + cv, 128, stride=ncv), :]
                columns[kt, pl.ds(c * 256 + v, 128, stride=2), :] = part.T
        out_ref[:, kt * 128 : kt * 128 + 128] = columns[kt]


def fetch(jobs, sems):
    copies = []
    for i, (ain, aout, level, start, width, dst, at) in enumerate(jobs):
        cols = pl.ds(pl.multiple_of(start, 128), width)
        copies.append(
            pltpu.make_async_copy(
                ain.at[level, :, cols], dst.at[0:64, at : at + width], sems.at[0, i]
            )
        )
        copies.append(
            pltpu.make_async_copy(
                aout.at[level, :, cols], dst.at[64:96, at : at + width], sems.at[1, i]
            )
        )
    for copy in copies:
        copy.start()
    for copy in copies:
        copy.wait()


def pack_kernel(pos_ref, ain, aout, y1, y2, y3, x1, x2, x3, sems):
    y = pos_ref[0]
    x = pos_ref[1]
    ry = rev(y, 2)
    rx = rev(x, 2)
    jobs = []
    for m, dst in ((1, y1), (2, y2), (3, y3)):
        jobs.append((ain, aout, 0, (ry ^ rev(m, 2)) * 256, 256, dst, 0))
    jobs.append((ain, aout, 1, ((y >> 1) ^ 1) * 512, 512, y2, 256))
    for m, dst in ((1, x1), (2, x2), (3, x3)):
        jobs.append((ain, aout, 4, (rx ^ rev(m, 2)) * 256, 256, dst, 0))
    jobs.append((ain, aout, 5, ((x >> 1) ^ 1) * 512, 512, x2, 256))
    fetch(jobs, sems)


def core_kernel(pos_ref, ain, aout, y1, y2, y3, kept, sent, sems):
    y = pos_ref[0]
    core = pos_ref[2]
    ry = rev(y, 2)
    jobs = []
    for dst, side in ((kept, core), (sent, 1 - core)):
        jobs.append((ain, aout, 0, ry * 256 + side * 128, 128, dst, 0))
        jobs.append((ain, aout, 1, (y >> 1) * 512 + side * 256, 256, dst, 512))
        jobs.append((ain, aout, 2, side * 512, 512, dst, 1024))
    fetch(jobs, sems)
    for dst, side in ((kept, core), (sent, 1 - core)):
        for m, src in ((1, y1), (2, y2), (3, y3)):
            cols = pl.ds(pl.multiple_of(side * 128, 128), 128)
            dst[:, m * 128 : m * 128 + 128] = src[:, cols]
        cols = pl.ds(pl.multiple_of(256 + side * 256, 128), 256)
        dst[:, 768:1024] = y2[:, cols]


def turned(read, scratch, width):
    for t in range(width // 128):
        part = read(slice(t * 128, t * 128 + 128))
        full = jnp.concatenate([part, jnp.zeros((32, 128), F32)], axis=0)
        scratch[t * 128 : t * 128 + 128, :] = full.T


def got(ref, at):
    return lambda s: ref[:, at + s.start : at + s.stop]


def weights(interp_ref, w_ref, first, count):
    row = lax.broadcasted_iota(jnp.int32, (256, 64), 0)
    col = lax.broadcasted_iota(jnp.int32, (256, 64), 1)
    left = ((row >> 2) == col).astype(F32).astype(BF16)
    row = lax.broadcasted_iota(jnp.int32, (32, 128), 0)
    col = lax.broadcasted_iota(jnp.int32, (32, 128), 1)
    right = (row == (col >> 2)).astype(F32).astype(BF16)
    row = lax.broadcasted_iota(jnp.int32, (256, 128), 0)
    col = lax.broadcasted_iota(jnp.int32, (256, 128), 1)
    keep = (row & 3) == (col & 3)
    for level in range(count):
        for i, part in enumerate(split(interp_ref[first + level])):
            mid = dot(left, part, ((1,), (1,))).astype(BF16)
            full = jnp.where(keep, dot(mid, right), 0.0)
            w_ref[level, :, i * 128 : i * 128 + 128] = full.astype(BF16)


def tables(count, slabs, raw, cos_ref, sin_ref):
    rows = 1024 // slabs
    lane = lax.broadcasted_iota(jnp.int32, (rows, 128), 1)

    def body(m, _):
        low = pl.ds(pl.multiple_of(m * rows, rows), rows)
        high = pl.ds(pl.multiple_of((m + slabs // 2) * rows, rows), rows)
        for level in range(count):
            if level:
                before = jnp.where(
                    lane < 32,
                    pltpu.roll(raw[level - 1, low, :], 64, 1),
                    pltpu.roll(raw[level - 1, high, :], 96, 1),
                )
                before = jnp.where(lane < 64, before, 0.0)
            for t in range(2):
                at = pl.ds(pl.multiple_of((2 * m + t) * rows, rows), rows)
                angle = raw[level, at, :]
                if level:
                    angle = angle + before
                    turn = jnp.where(angle > PI, TAU, jnp.where(angle < -PI, -TAU, 0.0))
                    angle = angle - turn
                s, c = sincos(angle)
                cos_ref[level, at, :] = c
                sin_ref[level, at, :] = s
        return 0

    lax.fori_loop(0, slabs // 2, body, 0)


def table_lo_kernel(
    pos_ref, ain, aout, interp, kept, other, cos_ref, sin_ref, w_ref, raw, scratch, mine, sems
):
    y = pos_ref[0]
    core = pos_ref[2]
    ry = rev(y, 2)
    fetch([(ain, aout, 3, 0, 1024, mine, 0)], sems)
    weights(interp, w_ref, 0, 4)

    def emit(level, base, ts):
        for t in range(ts):
            at = pl.multiple_of((base + t) * 64, 64)
            raw[level, pl.ds(at, 64), :] = scratch[pl.ds(t, 64, stride=ts), :]

    for src, side in ((kept, core), (other, 1 - core)):
        for m in range(4):
            turned(got(src, m * 128), scratch, 128)
            emit(0, ((ry ^ rev(m, 2)) * 2 + side) * 2, 2)
        for m in range(2):
            turned(got(src, 512 + m * 256), scratch, 256)
            emit(1, (((y >> 1) ^ m) * 2 + side) * 4, 4)
        turned(got(src, 1024), scratch, 512)
        emit(2, side * 8, 8)
    turned(got(mine, 0), scratch, 1024)
    emit(3, 0, 16)
    tables(4, 16, raw, cos_ref, sin_ref)


def table_hi_kernel(
    pos_ref, ain, aout, interp, x1, x2, x3, cos_ref, sin_ref, w_ref, raw, scratch, mine, sems
):
    x = pos_ref[1]
    rx = rev(x, 2)
    fetch(
        [
            (ain, aout, 4, rx * 256, 256, mine, 0),
            (ain, aout, 5, (x >> 1) * 512, 512, mine, 256),
            (ain, aout, 6, 0, 1024, mine, 768),
        ],
        sems,
    )
    weights(interp, w_ref, 4, 3)

    def emit(level, base, ts):
        for t in range(ts):
            for T in range(16):
                at = pl.multiple_of((base + t) * 128 + T * 8, 8)
                raw[level, pl.ds(at, 8), :] = scratch[pl.ds(T * ts + t, 8, stride=16 * ts), :]

    for m, src in enumerate((None, x1, x2, x3)):
        read = got(mine, 0) if m == 0 else got(src, 0)
        turned(read, scratch, 256)
        emit(0, (rx ^ rev(m, 2)) * 2, 2)
    turned(got(mine, 256), scratch, 512)
    emit(1, (x >> 1) * 4, 4)
    turned(got(x2, 256), scratch, 512)
    emit(1, (1 - (x >> 1)) * 4, 4)
    turned(got(mine, 768), scratch, 1024)
    emit(2, 0, 8)
    tables(3, 8, raw, cos_ref, sin_ref)


def spread(table, kind):
    lane = lax.broadcasted_iota(jnp.int32, table.shape, 1)
    return jnp.take_along_axis(table, kind * 32 + (lane >> 2), axis=1)


def step(nv, low, high, cos, sin, w, last):
    n = cos.shape[0]
    sides = []
    for kind, src in enumerate((low, high)):
        c = spread(cos, kind)
        s = spread(sin, kind)
        re, im = [], []
        for v in range(nv):
            xr = src(v)
            xi = src(nv + v)
            re.append(xr * c - xi * s)
            im.append(xr * s + xi * c)
        sides.append(jnp.concatenate(re + im, axis=0))
    hi, lo = split(jnp.concatenate(sides, axis=1))
    first = dot(hi, w)
    out = first[:, :128] + first[:, 128:] + dot(lo, w[:, :128])
    out = [out[q * n : q * n + n] for q in range(2 * nv)]
    if not last:
        return out
    c = spread(cos, 2)
    s = spread(sin, 2)
    re = [out[v] * c - out[nv + v] * s for v in range(nv)]
    im = [out[v] * s + out[nv + v] * c for v in range(nv)]
    return re + im


def run_level(nv, level, last, count, rows, load_low, load_high, store, cos_ref, sin_ref, w_ref):
    group = 128 // rows
    w = w_ref[level]

    def body(i, _):
        for t in range(2):
            at = [
                pl.multiple_of((2 * (i * group + g) + t) * rows, rows) for g in range(group)
            ]
            c = jnp.concatenate([cos_ref[level, pl.ds(a, rows), :] for a in at], axis=0)
            s = jnp.concatenate([sin_ref[level, pl.ds(a, rows), :] for a in at], axis=0)
            low = lambda q: jnp.concatenate(
                [load_low(i * group + g, q) for g in range(group)], axis=0
            )
            high = lambda q: jnp.concatenate(
                [load_high(i * group + g, q) for g in range(group)], axis=0
            )
            for q, tile in enumerate(step(nv, low, high, c, s, w, last)):
                for g in range(group):
                    store(2 * (i * group + g) + t, q, tile[g * rows : g * rows + rows])
        return 0

    lax.fori_loop(0, count // group, body, 0)


def levels_kernel(nv, count, slabs, load_first, store_last, sources, held, sems, one, two):
    rows = 1024 // slabs
    lanes = lambda q: slice(q * 128, q * 128 + 128)
    copies = []
    for level in range(count):
        copies.append(
            [
                pltpu.make_async_copy(src.at[level], dst.at[level], sems.at[i, level])
                for i, (src, dst) in enumerate(zip(sources, held))
            ]
        )
        for copy in copies[-1]:
            copy.start()
    bufs = (one, two)
    for level in range(count):
        for copy in copies[level]:
            copy.wait()
        src = bufs[(level + 1) % 2]
        dst = bufs[level % 2]
        if level == 0:
            low, high = load_first
        else:
            low = lambda m, q, src=src: src[m, :, lanes(q)]
            high = lambda m, q, src=src: src[m + slabs // 2, :, lanes(q)]
        last = level == count - 1

        def store(slab, q, tile, dst=dst):
            dst[slab, :, lanes(q)] = tile

        run_level(
            nv, level, last, slabs // 2, rows, low, high,
            store_last if last else store, *held,
        )


def levels_lo_kernel(nv, x_ref, cos, sin, w, out_ref, one, two, cos_v, sin_v, w_v, sems):
    lanes = lambda q: slice(q * 128, q * 128 + 128)

    def at(m):
        return (m >> 1 & 1) * 8 + (m >> 2 & 1) * 4 + (m & 1)

    def put(slab, q, tile):
        for kp in range(8):
            rows = pl.ds(pl.multiple_of(slab * 8, 8), 8)
            out_ref[rev(kp, 3), rows, lanes(q)] = tile[kp * 8 : kp * 8 + 8]

    levels_kernel(
        nv, 4, 16,
        (lambda m, q: x_ref[at(m), :, lanes(q)], lambda m, q: x_ref[at(m) + 2, :, lanes(q)]),
        put, (cos, sin, w), (cos_v, sin_v, w_v), sems, one, two,
    )


def levels_hi_kernel(
    nv, where_ref, x_ref, cos, sin, w, out_ref, one, two, cos_v, sin_v, w_v, sems, done
):
    lanes = lambda q: slice(q * 128, q * 128 + 128)
    ncv = 2 * nv

    def put(slab, q, tile):
        done[pl.ds(pl.multiple_of(slab * 128, 128), 128), q, :] = tile

    levels_kernel(
        nv, 3, 8,
        (
            lambda m, q: x_ref[rev(m, 2) * 2, :, lanes(q)],
            lambda m, q: x_ref[rev(m, 2) * 2 + 1, :, lanes(q)],
        ),
        put, (cos, sin, w), (cos_v, sin_v, w_v), sems, one, two,
    )

    def gather(e, _):
        for r in range(8):
            out_ref[e, r * ncv : r * ncv + ncv, :] = done[where_ref[e * 8 + r]]
        return 0

    lax.fori_loop(0, 128, gather, 0)


def held(count):
    return [
        pltpu.VMEM((count, 1024, 128), F32),
        pltpu.VMEM((count, 1024, 128), F32),
        pltpu.VMEM((count, 256, 256), BF16),
        pltpu.SemaphoreType.DMA((3, count)),
    ]


def table_shapes(count):
    shape = jax.ShapeDtypeStruct
    return [shape((count, 1024, 128), F32)] * 2 + [shape((count, 256, 256), BF16)]


def shards(coefficients, angle_in, angle_out, interp, destination):
    nv = 2
    ncv = 2 * nv
    shape = jax.ShapeDtypeStruct
    pos = jnp.stack([lax.axis_index("y"), lax.axis_index("x"), lax.axis_index("c")])
    pos = pos.astype(jnp.int32)

    sends = pl.pallas_call(
        pack_kernel,
        out_shape=[shape((96, w), F32) for w in (256, 768, 256) * 2],
        in_specs=[SMEM, HBM, HBM],
        out_specs=[VMEM] * 6,
        scratch_shapes=[pltpu.SemaphoreType.DMA((2, 8))],
        compiler_params=params(56),
    )(pos, angle_in, angle_out)
    from_y = [
        lax.ppermute(s, "y", [(i, i ^ m) for i in range(4)]) for m, s in zip((1, 2, 3), sends[:3])
    ]

    state = pl.pallas_call(
        functools.partial(send_kernel, nv),
        out_shape=shape((16, 64, ncv * 128), F32),
        in_specs=[VMEM],
        out_specs=VMEM,
        scratch_shapes=[pltpu.VMEM((8, 512, 128), F32)],
        compiler_params=params(6),
    )(coefficients.reshape(512, 1024))
    state, *from_y = lax.optimization_barrier((state, *from_y))
    state = lax.all_to_all(state, ("y", "zh", "c"), 0, 0, tiled=True)

    from_x = [
        lax.ppermute(s, "x", [(i, i ^ m) for i in range(4)]) for m, s in zip((1, 2, 3), sends[3:])
    ]
    kept, sent = pl.pallas_call(
        core_kernel,
        out_shape=[shape((96, 1536), F32)] * 2,
        in_specs=[SMEM, HBM, HBM] + [VMEM] * 3,
        out_specs=[VMEM] * 2,
        scratch_shapes=[pltpu.SemaphoreType.DMA((2, 6))],
        compiler_params=params(6),
    )(pos, angle_in, angle_out, *from_y)
    other = lax.ppermute(sent, "c", [(0, 1), (1, 0)])

    tables_lo = pl.pallas_call(
        table_lo_kernel,
        out_shape=table_shapes(4),
        in_specs=[SMEM, HBM, HBM] + [VMEM] * 3,
        out_specs=[VMEM] * 3,
        scratch_shapes=[
            pltpu.VMEM((4, 1024, 128), F32),
            pltpu.VMEM((1024, 128), F32),
            pltpu.VMEM((96, 1024), F32),
            pltpu.SemaphoreType.DMA((2, 1)),
        ],
        compiler_params=params(12),
    )(pos, angle_in, angle_out, interp, kept, other)
    tables_hi = pl.pallas_call(
        table_hi_kernel,
        out_shape=table_shapes(3),
        in_specs=[SMEM, HBM, HBM] + [VMEM] * 4,
        out_specs=[VMEM] * 3,
        scratch_shapes=[
            pltpu.VMEM((3, 1024, 128), F32),
            pltpu.VMEM((1024, 128), F32),
            pltpu.VMEM((96, 1792), F32),
            pltpu.SemaphoreType.DMA((2, 3)),
        ],
        compiler_params=params(12),
    )(pos, angle_in, angle_out, interp, *from_x)

    state = pl.pallas_call(
        functools.partial(levels_lo_kernel, nv),
        out_shape=shape((8, 128, ncv * 128), F32),
        in_specs=[VMEM] + [ANY] * 3,
        out_specs=VMEM,
        scratch_shapes=[pltpu.VMEM((16, 64, ncv * 128), F32)] * 2 + held(4),
        compiler_params=params(24),
    )(state, *tables_lo)
    state, *tables_hi = lax.optimization_barrier((state, *tables_hi))
    state = lax.all_to_all(state, ("x", "zl"), 0, 0, tiled=True)

    wanted = destination[0]
    where = (wanted & 7) * 128 + (wanted >> 3 & 15) * 8 + (wanted >> 7)
    state = pl.pallas_call(
        functools.partial(levels_hi_kernel, nv),
        out_shape=shape((128, 8 * ncv, 128), F32),
        in_specs=[SMEM, VMEM] + [ANY] * 3,
        out_specs=VMEM,
        scratch_shapes=[pltpu.VMEM((8, 128, ncv * 128), F32)] * 2
        + held(3)
        + [pltpu.VMEM((1024, ncv, 128), F32)],
        compiler_params=params(24),
    )(where, state, *tables_hi)
    state = lax.all_to_all(state, AXES, 0, 0, tiled=True)

    out = pl.pallas_call(
        functools.partial(final_kernel, nv),
        out_shape=shape((512, 1024), F32),
        in_specs=[VMEM],
        out_specs=VMEM,
        scratch_shapes=[pltpu.VMEM((8, 512, 128), F32)],
        compiler_params=params(6),
    )(state.reshape(1024 * ncv, 128))
    return out.reshape(2, 32, 8, 1024)


def solution(mesh):
    mesh = jax.sharding.Mesh(mesh.devices.reshape(4, 2, 4, 2, 2), AXES)
    placed = (
        P(None, None, None, AXES),
        P(None, None, AXES),
        P(None, None, AXES),
        P(),
        P(AXES, None),
    )
    return jax.shard_map(
        shards,
        mesh=mesh,
        in_specs=placed,
        out_specs=P(None, None, None, AXES),
        check_vma=False,
    )
```

time: 171 us -> 160 us (0.936)
  Pallas kernels: 29.8 us -> 37.9 us
  starting transfers between devices: 29.2 us -> 21.5 us
  local copies, waits for them, and re-layouts: 19.5 us -> 14.5 us
  blocking collectives: 43.5 us -> 38.6 us
    ppermute x10 -> x7, starting transfers between devices: 14.8 us -> 8.52 us  [the longest x3 4.6 us: shards(): lax.ppermute(s, 'y', [(i, i ^ m) for i in range(4)])]
    ppermute x10 -> x7, waiting for transfers between devices: 21.5 us -> 16 us  [the longest x3 8.95 us: shards(): lax.ppermute(s, 'x', [(i, i ^ m) for i in range(4)])]
    pallas_call x1, Pallas kernels: 7 us -> 12 us  [shards(): pl.pallas_call(functools.partial(levels_lo_kernel, nv), out_shape=shape((...]
    all_to_all x1, blocking collectives: 43.5 us -> 38.6 us  [shards(): state = lax.all_to_all(state, AXES, 0, 0, tiled=True)]
    all_to_all x2, waiting for transfers between devices: 26.9 us -> 30.7 us  [the longest x1 30.2 us: shards(): state = lax.all_to_all(state, ('x', 'zl'), 0, 0, tiled=True)]
    unnamed x46 -> x42, local copies, waits for them, and re-layouts: 18.1 us -> 14.5 us
    pallas_call x1, Pallas kernels: 0.65 us -> 3.04 us  [shards(): pl.pallas_call(pack_kernel, out_shape=[shape((96, w), F32) for w in (256,...]
    pallas_call x3 -> x4, Pallas kernels: 7.56 us -> 9.86 us  [the longest x1 4.3 us: shards(): pl.pallas_call(table_lo_kernel, out_shape=table_shapes(4), in_specs=[SMEM...]
  transfers between devices with their start and end apart: 12 -> 9, of which waited for: 4 -> 6; matrix products, arithmetic and copies ran while one was open for 1% -> 0% of each run, Pallas kernels for 4% -> 6%
where the time goes in v3:
time: 160 us
  waiting for transfers between devices  46.7 us (29%)
  blocking collectives  38.6 us (24%)
  Pallas kernels  37.9 us (24%)
  starting transfers between devices  21.5 us (13%)
  local copies, waits for them, and re-layouts  14.5 us (9%)
    all_to_all x1, blocking collectives, shards(): state = lax.all_to_all(state, AXES, 0, 0, tiled=True)  38.6 us
    all_to_all x1, waiting for transfers between devices, shards(): state = lax.all_to_all(state, ('x', 'zl'), 0, 0, tiled=True)  30.2 us
    unnamed x42, local copies, waits for them, and re-layouts  14.5 us
    pallas_call x1, Pallas kernels, shards(): pl.pallas_call(functools.partial(levels_lo_kernel, nv), out_shape=shape((...  12 us
    pallas_call x1, Pallas kernels, shards(): pl.pallas_call(functools.partial(levels_hi_kernel, nv), out_shape=shape((...  10.8 us
    ppermute x3, waiting for transfers between devices, shards(): lax.ppermute(s, 'x', [(i, i ^ m) for i in range(4)])  8.95 us
    all_to_all x1, starting transfers between devices, shards(): state = lax.all_to_all(state, ('y', 'zh', 'c'), 0, 0, tiled=True)  8.34 us
    ppermute x3, waiting for transfers between devices, shards(): lax.ppermute(s, 'y', [(i, i ^ m) for i in range(4)])  7.05 us
  transfers between devices with their start and end apart: 9, of which 6 were waited for; matrix products, arithmetic and copies ran while one was open for 0% of the time, Pallas kernels for 6%

profile of v3, /device:TPU:1, one launch (start us, length us, event | category | flops | bytes accessed | tf_op | source)
XLA Modules:
  0.0 160.0 jit_solution(8285933721977654102)
XLA Ops:
  0.0 0.7 pad_add_fusion.pos_ref
  0.7 3.0 %shard_map.56 = (f32[96,256]{1,0:T(8,128)}, f32[96,768]{1,0:T(8,128)}, f32[96,256]{1,0:T(8,128)}, f32[96,256]{1,0:T(8,128)}, f32[96,768]{1,0:T(8,128)}, /*index=5*/f32[96,256]{1,0:T(8,128)}) custom-call(s32[3]{0:T(128)} %pad_add_fusion.pos_ref, f32[7,64,1024]{2,1,0:T(8,128)} %ain.7, f32[7,32,1024]{2,1,0:T(8,128)} %aout.7), custom_call_target="tpu_custom_call" | custom-call | tf_op jit(solution)/shard_map/pallas_call | solution.py:423
  3.7 3.8 %collective-permute-start.1 = (f32[96,768]{1,0:T(8,128)}, f32[96,768]{1,0:T(8,128)S(1)}, u32[]{:S(2)}, u32[]{:S(2)}) collective-permute-start(f32[96,768]{1,0:T(8,128)} %get-tuple-element.28), channel_id=1, source_target_pairs={{0,64},{32,96},{64,0},{96,32},{1,65},{33,97},{65,1},{97,33},{2,66}... | collective-permute-start | bytes 884744 | tf_op jit(solution)/shard_map/ppermute | solution.py:432
  7.5 0.4 collective-permute-start
  7.9 0.4 collective-permute-start.2
  8.3 0.6 shard_map.55
  8.9 0.0 copy-start.3
  9.0 1.3 copy-done.3
  10.3 6.4 %collective-permute-done.y1 = f32[96,256]{1,0:T(8,128)S(1)} collective-permute-done((f32[96,256]{1,0:T(8,128)}, f32[96,256]{1,0:T(8,128)S(1)}, u32[]{:S(2)}, u32[]{:S(2)}) %collective-permute-start) | collective-permute-done | bytes 98336 | tf_op jit(solution)/shard_map/ppermute | solution.py:432
  16.7 0.6 collective-permute-done.2.y3
  17.3 0.0 collective-permute-done.1.y2
  17.3 8.3 %all-to-all-start = ((f32[16,64,512]{2,1,0:T(8,128)}), f32[16,64,512]{2,1,0:T(8,128)}, u32[]{:S(2)}, u32[]{:S(2)}) async-start(f32[16,64,512]{2,1,0:T(8,128)} %copy-done.3), calls=%async_computation | async-start | bytes 4194304 | tf_op jit(solution)/shard_map/all_to_all | solution.py:444
  25.7 0.0 copy-done
  25.7 0.0 copy-done.1
  25.7 0.0 copy-done.16
  25.7 0.0 copy-start.18
  25.7 0.0 copy-start.20
  25.7 0.0 copy-start.19
  25.7 0.0 copy-start.13
  25.7 0.9 shard_map.57
  26.6 0.2 collective-permute-start.3
  26.9 2.7 %collective-permute-start.5 = (f32[96,768]{1,0:T(8,128)S(1)}, f32[96,768]{1,0:T(8,128)S(1)}, u32[]{:S(2)}, u32[]{:S(2)}) collective-permute-start(f32[96,768]{1,0:T(8,128)S(1)} %copy-done.18), channel_id=1, source_target_pairs={{0,8},{4,12},{8,0},{12,4},{1,9},{5,13},{9,1},{13,5},{2,10},{6,14},... | collective-permute-start | bytes 884744 | tf_op jit(solution)/shard_map/ppermute | solution.py:447
  29.6 0.3 collective-permute-start.4
  29.9 0.6 collective-permute-start.6
  30.6 8.4 %collective-permute-done.4.x1 = f32[96,256]{1,0:T(8,128)S(1)} collective-permute-done((f32[96,256]{1,0:T(8,128)S(1)}, f32[96,256]{1,0:T(8,128)S(1)}, u32[]{:S(2)}, u32[]{:S(2)}) %collective-permute-start.4) | collective-permute-done | bytes 98336 | tf_op jit(solution)/shard_map/ppermute | solution.py:447
  39.0 0.6 collective-permute-done.6.x3
  39.5 0.0 collective-permute-done.5.x2
  39.5 4.1 %shard_map.60 = (f32[3,1024,128]{2,1,0:T(8,128)S(1)}, f32[3,1024,128]{2,1,0:T(8,128)S(1)}, bf16[3,256,256]{2,1,0:T(8,128)(2,1)S(1)}) custom-call(s32[3]{0:T(128)S(1)} %copy-done.16, f32[7,64,1024]{2,1,0:T(8,128)S(1)} %copy-done, f32[7,32,1024]{2,1,0:T(8,128)S(1)} %copy-done.1, f32[7,32,64]{2,1,0:T(8,128)S(1)} %copy-done.13, ...), custom_call_target="tpu_custom_call" | custom-call | tf_op jit(solution)/shard_map/pallas_call | solution.py:472
  43.6 1.1 copy-done.9
  44.8 1.2 copy-done.11
  46.0 0.7 copy-done.14
  46.7 0.0 collective-permute-done.3.other
  46.7 4.3 %shard_map.58 = (f32[4,1024,128]{2,1,0:T(8,128)S(1)}, f32[4,1024,128]{2,1,0:T(8,128)S(1)}, bf16[4,256,256]{2,1,0:T(8,128)(2,1)S(1)}) custom-call(s32[3]{0:T(128)S(1)} %copy-done.16, f32[7,64,1024]{2,1,0:T(8,128)S(1)} %copy-done, f32[7,32,1024]{2,1,0:T(8,128)S(1)} %copy-done.1, f32[7,32,64]{2,1,0:T(8,128)S(1)} %copy-done.13, ...), custom_call_target="tpu_custom_call" | custom-call | tf_op jit(solution)/shard_map/pallas_call | solution.py:459
  51.1 1.3 copy-done.4
  52.4 1.4 copy-done.6
  53.7 0.5 all-to-all-done.x_ref
  54.2 1.6 copy-done.5
  55.8 1.6 copy-done.7
  57.4 12.0 %shard_map.59 = f32[8,128,512]{2,1,0:T(8,128)S(1)} custom-call(f32[16,64,512]{2,1,0:T(8,128)} %all-to-all-done.x_ref, f32[4,1024,128]{2,1,0:T(8,128)S(1)} %copy-done.5, f32[4,1024,128]{2,1,0:T(8,128)S(1)} %copy-done.7, bf16[4,256,256]{2,1,0:T(8,128)(2,1)S(1)} %get-tuple-element.38.w), custom_call_target="tpu_custom_call" | custom-call | tf_op jit(solution)/shard_map/pallas_call | solution.py:486
  69.4 0.0 copy-start.2
  69.5 1.3 copy-done.2
  70.8 4.6 %all-to-all-start.1 = ((f32[8,128,512]{2,1,0:T(8,128)}), f32[8,128,512]{2,1,0:T(8,128)S(1)}, u32[]{:S(2)}, u32[]{:S(2)}) async-start(f32[8,128,512]{2,1,0:T(8,128)} %copy-done.2), calls=%async_computation.1 | async-start | bytes 4194304 | tf_op jit(solution)/shard_map/all_to_all | solution.py:495
  75.4 30.2 %all-to-all-done.1.x_ref = f32[8,128,512]{2,1,0:T(8,128)S(1)} async-done(((f32[8,128,512]{2,1,0:T(8,128)}), f32[8,128,512]{2,1,0:T(8,128)S(1)}, u32[]{:S(2)}, u32[]{:S(2)}) %all-to-all-start.1) | async-done | bytes 2097184 | tf_op jit(solution)/shard_map/all_to_all | solution.py:495
  105.6 1.4 copy-done.10
  107.0 1.4 copy-done.12
  108.4 10.8 %shard_map.61 = f32[128,32,128]{2,1,0:T(8,128)S(1)} custom-call(s32[1024]{0:T(1024)S(1)} %bitcast.9, f32[8,128,512]{2,1,0:T(8,128)S(1)} %all-to-all-done.1.x_ref, f32[3,1024,128]{2,1,0:T(8,128)S(1)} %copy-done.10, f32[3,1024,128]{2,1,0:T(8,128)S(1)} %copy-done.12, bf16[3,256,256]{2,1,0:T(8,128)(2,1)S(1)} %copy-done.15), custom_call_target="tpu_custom_call" | custom-call | tf_op jit(solution)/shard_map/pallas_call | solution.py:499
  119.3 38.6 %all_to_all.15 = f32[128,32,128]{2,1,0:T(8,128)S(1)} all-to-all(f32[128,32,128]{2,1,0:T(8,128)S(1)} %shard_map.61), channel_id=1, replica_groups=mesh['y'=4,'zh'=2,'x'=4,'zl'=2,'c'=2] {'y','zh','x','zl','c'}, dimensions={0} | all-to-all | bytes 4194304 | tf_op jit(solution)/shard_map/all_to_all | solution.py:509
  157.9 2.2 %shard_map.62 = f32[512,1024]{1,0:T(8,128)} custom-call(f32[4096,128]{1,0:T(8,128)S(1)} %bitcast.7), custom_call_target="tpu_custom_call" | custom-call | tf_op jit(solution)/shard_map/pallas_call | solution.py:511
  (23 shorter events, 0.1 us)
Async XLA Ops:
  0.0 8.3 %copy-start.8 = (f32[2,32,8,1024]{3,2,1,0:T(8,128)S(1)}, f32[2,32,8,1024]{3,2,1,0:T(8,128)}, u32[]{:S(2)}) copy-start(f32[2,32,8,1024]{3,2,1,0:T(8,128)} %param.5) | copy-start | bytes 6291460
  3.7 13.6 %collective-permute-start.1 = (f32[96,768]{1,0:T(8,128)}, f32[96,768]{1,0:T(8,128)S(1)}, u32[]{:S(2)}, u32[]{:S(2)}) collective-permute-start(f32[96,768]{1,0:T(8,128)} %get-tuple-element.28), channel_id=1, source_target_pairs={{0,64},{32,96},{64,0},{96,32},{1,65},{33,97},{65,1},{97,33},{2,66}... | collective-permute-start | bytes 884744 | tf_op jit(solution)/shard_map/ppermute | solution.py:432
  7.5 9.2 %collective-permute-start = (f32[96,256]{1,0:T(8,128)}, f32[96,256]{1,0:T(8,128)S(1)}, u32[]{:S(2)}, u32[]{:S(2)}) collective-permute-start(f32[96,256]{1,0:T(8,128)} %get-tuple-element.27), channel_id=1, source_target_pairs={{0,32},{32,0},{64,96},{96,64},{1,33},{33,1},{65,97},{97,65},{2,34}... | collective-permute-start | bytes 294920 | tf_op jit(solution)/shard_map/ppermute | solution.py:432
  7.9 9.4 %collective-permute-start.2 = (f32[96,256]{1,0:T(8,128)}, f32[96,256]{1,0:T(8,128)S(1)}, u32[]{:S(2)}, u32[]{:S(2)}) collective-permute-start(f32[96,256]{1,0:T(8,128)} %get-tuple-element.29), channel_id=1, source_target_pairs={{0,96},{32,64},{64,32},{96,0},{1,97},{33,65},{65,33},{97,1},{2,98}... | collective-permute-start | bytes 294920 | tf_op jit(solution)/shard_map/ppermute | solution.py:432
  8.9 1.3 copy-start.3
  10.3 15.4 %copy-start = (f32[7,64,1024]{2,1,0:T(8,128)S(1)}, f32[7,64,1024]{2,1,0:T(8,128)}, u32[]{:S(2)}) copy-start(f32[7,64,1024]{2,1,0:T(8,128)} %ain.7) | copy-start | bytes 5505028
  10.3 15.4 %copy-start.1 = (f32[7,32,1024]{2,1,0:T(8,128)S(1)}, f32[7,32,1024]{2,1,0:T(8,128)}, u32[]{:S(2)}) copy-start(f32[7,32,1024]{2,1,0:T(8,128)} %aout.7) | copy-start | bytes 2752516
  10.3 15.4 %copy-start.16 = (s32[3]{0:T(128)S(1)}, s32[3]{0:T(128)}, u32[]{:S(2)}) copy-start(s32[3]{0:T(128)} %pad_add_fusion.pos_ref) | copy-start | bytes 40
  17.3 36.9 %all-to-all-start = ((f32[16,64,512]{2,1,0:T(8,128)}), f32[16,64,512]{2,1,0:T(8,128)}, u32[]{:S(2)}, u32[]{:S(2)}) async-start(f32[16,64,512]{2,1,0:T(8,128)} %copy-done.3), calls=%async_computation | async-start | bytes 4194304 | tf_op jit(solution)/shard_map/all_to_all | solution.py:444
  25.7 1.2 copy-start.18
  25.7 3.9 %copy-start.20 = (f32[96,256]{1,0:T(8,128)S(1)}, f32[96,256]{1,0:T(8,128)}, u32[]{:S(2)}) copy-start(f32[96,256]{1,0:T(8,128)} %get-tuple-element.39) | copy-start | bytes 294916
  25.7 4.2 %copy-start.19 = (f32[96,256]{1,0:T(8,128)S(1)}, f32[96,256]{1,0:T(8,128)}, u32[]{:S(2)}) copy-start(f32[96,256]{1,0:T(8,128)} %get-tuple-element.41) | copy-start | bytes 294916
  25.7 13.8 %copy-start.13 = (f32[7,32,64]{2,1,0:T(8,128)S(1)}, f32[7,32,64]{2,1,0:T(8,128)}, u32[]{:S(2)}) copy-start(f32[7,32,64]{2,1,0:T(8,128)} %interp.3) | copy-start | bytes 172036
  26.6 20.1 %collective-permute-start.3 = (f32[96,1536]{1,0:T(8,128)S(1)}, f32[96,1536]{1,0:T(8,128)S(1)}, u32[]{:S(2)}, u32[]{:S(2)}) collective-permute-start(f32[96,1536]{1,0:T(8,128)S(1)} %get-tuple-element.35), channel_id=1, source_target_pairs={{0,1},{1,0},{2,3},{3,2},{4,5},{5,4},{6,7},{7,6},{8,9},{9,8},{10,11... | collective-permute-start | bytes 1769480 | tf_op jit(solution)/shard_map/ppermute | solution.py:457
  26.9 12.6 %collective-permute-start.5 = (f32[96,768]{1,0:T(8,128)S(1)}, f32[96,768]{1,0:T(8,128)S(1)}, u32[]{:S(2)}, u32[]{:S(2)}) collective-permute-start(f32[96,768]{1,0:T(8,128)S(1)} %copy-done.18), channel_id=1, source_target_pairs={{0,8},{4,12},{8,0},{12,4},{1,9},{5,13},{9,1},{13,5},{2,10},{6,14},... | collective-permute-start | bytes 884744 | tf_op jit(solution)/shard_map/ppermute | solution.py:447
  29.6 9.3 %collective-permute-start.4 = (f32[96,256]{1,0:T(8,128)S(1)}, f32[96,256]{1,0:T(8,128)S(1)}, u32[]{:S(2)}, u32[]{:S(2)}) collective-permute-start(f32[96,256]{1,0:T(8,128)S(1)} %copy-done.20), channel_id=1, source_target_pairs={{0,4},{4,0},{8,12},{12,8},{1,5},{5,1},{9,13},{13,9},{2,6},{6,2},{1... | collective-permute-start | bytes 294920 | tf_op jit(solution)/shard_map/ppermute | solution.py:447
  29.9 9.6 %collective-permute-start.6 = (f32[96,256]{1,0:T(8,128)S(1)}, f32[96,256]{1,0:T(8,128)S(1)}, u32[]{:S(2)}, u32[]{:S(2)}) collective-permute-start(f32[96,256]{1,0:T(8,128)S(1)} %copy-done.19), channel_id=1, source_target_pairs={{0,12},{4,8},{8,4},{12,0},{1,13},{5,9},{9,5},{13,1},{2,14},{6,10},... | collective-permute-start | bytes 294920 | tf_op jit(solution)/shard_map/ppermute | solution.py:447
  43.6 1.2 copy-start.9
  44.8 1.2 copy-start.11
  46.0 0.7 copy-start.14
  51.0 1.3 copy-start.4
  52.4 1.4 copy-start.6
  54.2 1.6 copy-start.5
  55.8 1.6 copy-start.7
  69.4 1.3 copy-start.2
  70.8 4.6 %copy-start.17 = (s32[1,1024]{1,0:T(1,128)S(1)}, s32[1,1024]{1,0:T(1,128)}, u32[]{:S(2)}) copy-start(s32[1,1024]{1,0:T(1,128)} %param.9) | copy-start | bytes 12292
  70.8 34.8 %copy-start.15 = (bf16[3,256,256]{2,1,0:T(8,128)(2,1)S(1)}, bf16[3,256,256]{2,1,0:T(8,128)(2,1)}, u32[]{:S(2)}) copy-start(bf16[3,256,256]{2,1,0:T(8,128)(2,1)} %copy-done.14) | copy-start | bytes 1179652
  70.8 34.8 %all-to-all-start.1 = ((f32[8,128,512]{2,1,0:T(8,128)}), f32[8,128,512]{2,1,0:T(8,128)S(1)}, u32[]{:S(2)}, u32[]{:S(2)}) async-start(f32[8,128,512]{2,1,0:T(8,128)} %copy-done.2), calls=%async_computation.1 | async-start | bytes 4194304 | tf_op jit(solution)/shard_map/all_to_all | solution.py:495
  105.6 1.4 copy-start.10
  107.0 1.4 copy-start.12

commit v4 on v3

--- a/solution.py
+++ b/solution.py
@@ -35,6 +35,7 @@
     1.724760753325688e-09,
 )
 MIB = 1024 * 1024
+BIG = 56
 
 
 def params(mib):
@@ -111,24 +112,27 @@
         copy.wait()
 
 
-def pack_kernel(pos_ref, ain, aout, y1, y2, y3, x1, x2, x3, sems):
-    y = pos_ref[0]
-    x = pos_ref[1]
+def pack_y_kernel(ain, aout, y1, y2, y3, sems):
+    y = lax.axis_index("y")
     ry = rev(y, 2)
+    jobs = [(ain, aout, 1, ((y >> 1) ^ 1) * 512, 512, y2, 256)]
+    for m, dst in ((2, y2), (1, y1), (3, y3)):
+        jobs.append((ain, aout, 0, (ry ^ rev(m, 2)) * 256, 256, dst, 0))
+    fetch(jobs, sems)
+
+
+def pack_x_kernel(ain, aout, x1, x2, x3, sems):
+    x = lax.axis_index("x")
     rx = rev(x, 2)
-    jobs = []
-    for m, dst in ((1, y1), (2, y2), (3, y3)):
-        jobs.append((ain, aout, 0, (ry ^ rev(m, 2)) * 256, 256, dst, 0))
-    jobs.append((ain, aout, 1, ((y >> 1) ^ 1) * 512, 512, y2, 256))
-    for m, dst in ((1, x1), (2, x2), (3, x3)):
+    jobs = [(ain, aout, 5, ((x >> 1) ^ 1) * 512, 512, x2, 256)]
+    for m, dst in ((2, x2), (1, x1), (3, x3)):
         jobs.append((ain, aout, 4, (rx ^ rev(m, 2)) * 256, 256, dst, 0))
-    jobs.append((ain, aout, 5, ((x >> 1) ^ 1) * 512, 512, x2, 256))
     fetch(jobs, sems)
 
 
-def core_kernel(pos_ref, ain, aout, y1, y2, y3, kept, sent, sems):
-    y = pos_ref[0]
-    core = pos_ref[2]
+def core_kernel(ain, aout, y1, y2, y3, kept, sent, sems):
+    y = lax.axis_index("y")
+    core = lax.axis_index("c")
     ry = rev(y, 2)
     jobs = []
     for dst, side in ((kept, core), (sent, 1 - core)):
@@ -203,10 +207,10 @@
 
 
 def table_lo_kernel(
-    pos_ref, ain, aout, interp, kept, other, cos_ref, sin_ref, w_ref, raw, scratch, mine, sems
+    ain, aout, interp, kept, other, cos_ref, sin_ref, w_ref, raw, scratch, mine, sems
 ):
-    y = pos_ref[0]
-    core = pos_ref[2]
+    y = lax.axis_index("y")
+    core = lax.axis_index("c")
     ry = rev(y, 2)
     fetch([(ain, aout, 3, 0, 1024, mine, 0)], sems)
     weights(interp, w_ref, 0, 4)
@@ -231,9 +235,9 @@
 
 
 def table_hi_kernel(
-    pos_ref, ain, aout, interp, x1, x2, x3, cos_ref, sin_ref, w_ref, raw, scratch, mine, sems
+    ain, aout, interp, x1, x2, x3, cos_ref, sin_ref, w_ref, raw, scratch, mine, sems
 ):
-    x = pos_ref[1]
+    x = lax.axis_index("x")
     rx = rev(x, 2)
     fetch(
         [
@@ -299,11 +303,9 @@
     group = 128 // rows
     w = w_ref[level]
 
-    def body(i, _):
+    for i in range(count // group):
         for t in range(2):
-            at = [
-                pl.multiple_of((2 * (i * group + g) + t) * rows, rows) for g in range(group)
-            ]
+            at = [(2 * (i * group + g) + t) * rows for g in range(group)]
             c = jnp.concatenate([cos_ref[level, pl.ds(a, rows), :] for a in at], axis=0)
             s = jnp.concatenate([sin_ref[level, pl.ds(a, rows), :] for a in at], axis=0)
             low = lambda q: jnp.concatenate(
@@ -315,9 +317,6 @@
             for q, tile in enumerate(step(nv, low, high, c, s, w, last)):
                 for g in range(group):
                     store(2 * (i * group + g) + t, q, tile[g * rows : g * rows + rows])
-        return 0
-
-    lax.fori_loop(0, count // group, body, 0)
 
 
 def levels_kernel(nv, count, slabs, load_first, store_last, sources, held, sems, one, two):
@@ -363,7 +362,7 @@
 
     def put(slab, q, tile):
         for kp in range(8):
-            rows = pl.ds(pl.multiple_of(slab * 8, 8), 8)
+            rows = slice(slab * 8, slab * 8 + 8)
             out_ref[rev(kp, 3), rows, lanes(q)] = tile[kp * 8 : kp * 8 + 8]
 
     levels_kernel(
@@ -380,7 +379,7 @@
     ncv = 2 * nv
 
     def put(slab, q, tile):
-        done[pl.ds(pl.multiple_of(slab * 128, 128), 128), q, :] = tile
+        done[slab * 128 : slab * 128 + 128, q, :] = tile
 
     levels_kernel(
         nv, 3, 8,
@@ -417,19 +416,16 @@
     nv = 2
     ncv = 2 * nv
     shape = jax.ShapeDtypeStruct
-    pos = jnp.stack([lax.axis_index("y"), lax.axis_index("x"), lax.axis_index("c")])
-    pos = pos.astype(jnp.int32)
-
     sends = pl.pallas_call(
-        pack_kernel,
-        out_shape=[shape((96, w), F32) for w in (256, 768, 256) * 2],
-        in_specs=[SMEM, HBM, HBM],
-        out_specs=[VMEM] * 6,
-        scratch_shapes=[pltpu.SemaphoreType.DMA((2, 8))],
-        compiler_params=params(56),
-    )(pos, angle_in, angle_out)
+        pack_y_kernel,
+        out_shape=[shape((96, w), F32) for w in (256, 768, 256)],
+        in_specs=[HBM, HBM],
+        out_specs=[VMEM] * 3,
+        scratch_shapes=[pltpu.SemaphoreType.DMA((2, 4))],
+        compiler_params=params(BIG),
+    )(angle_in, angle_out)
     from_y = [
-        lax.ppermute(s, "y", [(i, i ^ m) for i in range(4)]) for m, s in zip((1, 2, 3), sends[:3])
+        lax.ppermute(s, "y", [(i, i ^ m) for i in range(4)]) for m, s in zip((1, 2, 3), sends)
     ]
 
     state = pl.pallas_call(
@@ -443,23 +439,31 @@
     state, *from_y = lax.optimization_barrier((state, *from_y))
     state = lax.all_to_all(state, ("y", "zh", "c"), 0, 0, tiled=True)
 
+    sends = pl.pallas_call(
+        pack_x_kernel,
+        out_shape=[shape((96, w), F32) for w in (256, 768, 256)],
+        in_specs=[HBM, HBM],
+        out_specs=[VMEM] * 3,
+        scratch_shapes=[pltpu.SemaphoreType.DMA((2, 4))],
+        compiler_params=params(BIG),
+    )(angle_in, angle_out)
     from_x = [
-        lax.ppermute(s, "x", [(i, i ^ m) for i in range(4)]) for m, s in zip((1, 2, 3), sends[3:])
+        lax.ppermute(s, "x", [(i, i ^ m) for i in range(4)]) for m, s in zip((1, 2, 3), sends)
     ]
     kept, sent = pl.pallas_call(
         core_kernel,
         out_shape=[shape((96, 1536), F32)] * 2,
-        in_specs=[SMEM, HBM, HBM] + [VMEM] * 3,
+        in_specs=[HBM, HBM] + [VMEM] * 3,
         out_specs=[VMEM] * 2,
         scratch_shapes=[pltpu.SemaphoreType.DMA((2, 6))],
-        compiler_params=params(6),
-    )(pos, angle_in, angle_out, *from_y)
+        compiler_params=params(BIG),
+    )(angle_in, angle_out, *from_y)
     other = lax.ppermute(sent, "c", [(0, 1), (1, 0)])
 
     tables_lo = pl.pallas_call(
         table_lo_kernel,
         out_shape=table_shapes(4),
-        in_specs=[SMEM, HBM, HBM] + [VMEM] * 3,
+        in_specs=[HBM, HBM] + [VMEM] * 3,
         out_specs=[VMEM] * 3,
         scratch_shapes=[
             pltpu.VMEM((4, 1024, 128), F32),
@@ -467,12 +471,12 @@
             pltpu.VMEM((96, 1024), F32),
             pltpu.SemaphoreType.DMA((2, 1)),
         ],
-        compiler_params=params(12),
-    )(pos, angle_in, angle_out, interp, kept, other)
+        compiler_params=params(BIG),
+    )(angle_in, angle_out, interp, kept, other)
     tables_hi = pl.pallas_call(
         table_hi_kernel,
         out_shape=table_shapes(3),
-        in_specs=[SMEM, HBM, HBM] + [VMEM] * 4,
+        in_specs=[HBM, HBM] + [VMEM] * 4,
         out_specs=[VMEM] * 3,
         scratch_shapes=[
             pltpu.VMEM((3, 1024, 128), F32),
@@ -480,8 +484,8 @@
             pltpu.VMEM((96, 1792), F32),
             pltpu.SemaphoreType.DMA((2, 3)),
         ],
-        compiler_params=params(12),
-    )(pos, angle_in, angle_out, interp, *from_x)
+        compiler_params=params(BIG),
+    )(angle_in, angle_out, interp, *from_x)
 
     state = pl.pallas_call(
         functools.partial(levels_lo_kernel, nv),
@@ -489,13 +493,13 @@
         in_specs=[VMEM] + [ANY] * 3,
         out_specs=VMEM,
         scratch_shapes=[pltpu.VMEM((16, 64, ncv * 128), F32)] * 2 + held(4),
-        compiler_params=params(24),
+        compiler_params=params(BIG),
     )(state, *tables_lo)
-    state, *tables_hi = lax.optimization_barrier((state, *tables_hi))
-    state = lax.all_to_all(state, ("x", "zl"), 0, 0, tiled=True)
-
     wanted = destination[0]
     where = (wanted & 7) * 128 + (wanted >> 3 & 15) * 8 + (wanted >> 7)
+    state, where, *tables_hi = lax.optimization_barrier((state, where, *tables_hi))
+    state = lax.all_to_all(state, ("x", "zl"), 0, 0, tiled=True)
+
     state = pl.pallas_call(
         functools.partial(levels_hi_kernel, nv),
         out_shape=shape((128, 8 * ncv, 128), F32),
@@ -504,7 +508,7 @@
         scratch_shapes=[pltpu.VMEM((8, 128, ncv * 128), F32)] * 2
         + held(3)
         + [pltpu.VMEM((1024, ncv, 128), F32)],
-        compiler_params=params(24),
+        compiler_params=params(BIG),
     )(where, state, *tables_hi)
     state = lax.all_to_all(state, AXES, 0, 0, tiled=True)
 

time: 160 us -> 157 us (0.981)
  blocking collectives: 38.6 us -> 70.5 us
  waiting for transfers between devices: 46.7 us -> 15.6 us
  Pallas kernels: 37.9 us -> 49 us
  local copies, waits for them, and re-layouts: 14.5 us -> 4.25 us
  starting transfers between devices: 21.5 us -> 16.8 us
    all_to_all x0 -> x1, blocking collectives: none -> 30.5 us  [shards(): state = lax.all_to_all(state, ('x', 'zl'), 0, 0, tiled=True)]
    all_to_all x1 -> x0, waiting for transfers between devices: 30.2 us -> none  [shards(): state = lax.all_to_all(state, ('x', 'zl'), 0, 0, tiled=True)]
    unnamed x42 -> x20, local copies, waits for them, and re-layouts: 14.5 us -> 4.25 us
    pallas_call x3 -> x4, Pallas kernels: 11.4 us -> 19.2 us  [the longest x1 7.94 us: shards(): pl.pallas_call(table_lo_kernel, out_shape=table_shapes(4), in_specs=[HBM,...]
    all_to_all x1 -> x0, starting transfers between devices: 4.61 us -> none  [shards(): state = lax.all_to_all(state, ('x', 'zl'), 0, 0, tiled=True)]
    pallas_call x1, Pallas kernels: 0.88 us -> 3.4 us  [shards(): pl.pallas_call(core_kernel, out_shape=[shape((96, 1536), F32)] * 2, in_sp...]
    pallas_call x1, Pallas kernels: 12 us -> 10.4 us  [shards(): pl.pallas_call(functools.partial(levels_lo_kernel, nv), out_shape=shape((...]
  transfers between devices with their start and end apart: 9 -> 8, of which waited for: 6 -> 4; matrix products, arithmetic and copies ran while one was open for 0% -> 0% of each run, Pallas kernels for 6% -> 14%
where the time goes in v4:
time: 157 us
  blocking collectives  70.5 us (45%)
  Pallas kernels  49 us (31%)
  starting transfers between devices  16.8 us (11%)
  waiting for transfers between devices  15.6 us (10%)
  local copies, waits for them, and re-layouts  4.25 us (3%)
    all_to_all x1, blocking collectives, shards(): state = lax.all_to_all(state, AXES, 0, 0, tiled=True)  40 us
    all_to_all x1, blocking collectives, shards(): state = lax.all_to_all(state, ('x', 'zl'), 0, 0, tiled=True)  30.5 us
    pallas_call x1, Pallas kernels, shards(): pl.pallas_call(functools.partial(levels_hi_kernel, nv), out_shape=shape((...  11.9 us
    pallas_call x1, Pallas kernels, shards(): pl.pallas_call(functools.partial(levels_lo_kernel, nv), out_shape=shape((...  10.4 us
    ppermute x3, waiting for transfers between devices, shards(): lax.ppermute(s, 'x', [(i, i ^ m) for i in range(4)])  8.54 us
    all_to_all x1, starting transfers between devices, shards(): state = lax.all_to_all(state, ('y', 'zh', 'c'), 0, 0, tiled=True)  8.34 us
    pallas_call x1, Pallas kernels, shards(): pl.pallas_call(table_lo_kernel, out_shape=table_shapes(4), in_specs=[HBM,...  7.94 us
    pallas_call x1, Pallas kernels, shards(): pl.pallas_call(table_hi_kernel, out_shape=table_shapes(3), in_specs=[HBM,...  7.36 us
  transfers between devices with their start and end apart: 8, of which 4 were waited for; matrix products, arithmetic and copies ran while one was open for 0% of the time, Pallas kernels for 14%

profile of v4, /device:TPU:1, one launch (start us, length us, event | category | flops | bytes accessed | tf_op | source)
XLA Modules:
  0.0 156.8 jit_solution(15157916257896789769)
XLA Ops:
  0.0 0.0 copy-start
  0.0 2.0 %shard_map.56 = (f32[96,256]{1,0:T(8,128)}, f32[96,768]{1,0:T(8,128)}, f32[96,256]{1,0:T(8,128)}) custom-call(f32[7,64,1024]{2,1,0:T(8,128)} %ain.9, f32[7,32,1024]{2,1,0:T(8,128)} %aout.9), custom_call_target="tpu_custom_call" | custom-call | tf_op jit(solution)/shard_map/pallas_call | solution.py:419
  2.0 3.8 %collective-permute-start.1 = (f32[96,768]{1,0:T(8,128)}, f32[96,768]{1,0:T(8,128)S(1)}, u32[]{:S(2)}, u32[]{:S(2)}) collective-permute-start(f32[96,768]{1,0:T(8,128)} %get-tuple-element.29), channel_id=1, source_target_pairs={{0,64},{32,96},{64,0},{96,32},{1,65},{33,97},{65,1},{97,33},{2,66}... | collective-permute-start | bytes 884744 | tf_op jit(solution)/shard_map/ppermute | solution.py:428
  5.9 0.4 collective-permute-start
  6.3 0.4 collective-permute-start.2
  6.7 0.0 copy-done
  6.7 1.9 %shard_map.55 = f32[16,64,512]{2,1,0:T(8,128)} custom-call(f32[512,1024]{1,0:T(8,128)S(1)} %bitcast.5), custom_call_target="tpu_custom_call" | custom-call | tf_op jit(solution)/shard_map/pallas_call | solution.py:431
  8.6 6.4 %collective-permute-done.y1 = f32[96,256]{1,0:T(8,128)S(1)} collective-permute-done((f32[96,256]{1,0:T(8,128)}, f32[96,256]{1,0:T(8,128)S(1)}, u32[]{:S(2)}, u32[]{:S(2)}) %collective-permute-start) | collective-permute-done | bytes 98336 | tf_op jit(solution)/shard_map/ppermute | solution.py:428
  15.0 0.0 copy-start.5
  15.0 0.6 collective-permute-done.2.y3
  15.7 0.0 copy-start.6
  15.7 0.0 collective-permute-done.1.y2
  15.7 0.0 copy-start.3
  15.7 0.0 copy-done.5
  15.7 0.6 copy-done.6
  16.3 0.1 copy-done.3
  16.4 8.3 %all-to-all-start = ((f32[16,64,512]{2,1,0:T(8,128)}), f32[16,64,512]{2,1,0:T(8,128)S(1)}, u32[]{:S(2)}, u32[]{:S(2)}) async-start(f32[16,64,512]{2,1,0:T(8,128)} %shard_map.55), calls=%async_computation | async-start | bytes 4194304 | tf_op jit(solution)/shard_map/all_to_all | solution.py:440
  24.8 3.4 %shard_map.57 = (f32[96,1536]{1,0:T(8,128)}, f32[96,1536]{1,0:T(8,128)}) custom-call(f32[7,64,1024]{2,1,0:T(8,128)} %ain.9, f32[7,32,1024]{2,1,0:T(8,128)} %aout.9, f32[96,256]{1,0:T(8,128)} %copy-done.5, f32[96,768]{1,0:T(8,128)} %copy-done.3, f32[96,256]{1,0:T(8,128)} %copy-done.6), custom_call_target="tpu_custom_call" | custom-call | tf_op jit(solution)/shard_map/pallas_call | solution.py:453
  28.2 0.0 copy-start.9
  28.2 0.2 collective-permute-start.3
  28.4 1.9 %shard_map.60 = (f32[96,256]{1,0:T(8,128)}, f32[96,768]{1,0:T(8,128)}, f32[96,256]{1,0:T(8,128)}) custom-call(f32[7,64,1024]{2,1,0:T(8,128)} %ain.9, f32[7,32,1024]{2,1,0:T(8,128)} %aout.9), custom_call_target="tpu_custom_call" | custom-call | tf_op jit(solution)/shard_map/pallas_call | solution.py:442
  30.3 2.8 %collective-permute-start.5 = (f32[96,768]{1,0:T(8,128)}, f32[96,768]{1,0:T(8,128)S(1)}, u32[]{:S(2)}, u32[]{:S(2)}) collective-permute-start(f32[96,768]{1,0:T(8,128)} %get-tuple-element.41), channel_id=1, source_target_pairs={{0,8},{4,12},{8,0},{12,4},{1,9},{5,13},{9,1},{13,5},{2,10},{6,14},... | collective-permute-start | bytes 884744 | tf_op jit(solution)/shard_map/ppermute | solution.py:451
  33.1 0.3 collective-permute-start.4
  33.4 0.6 collective-permute-start.6
  33.9 0.0 copy-done.9
  33.9 0.6 shift-right-arithmetic_add_fusion
  34.6 7.9 %collective-permute-done.4.x1 = f32[96,256]{1,0:T(8,128)S(1)} collective-permute-done((f32[96,256]{1,0:T(8,128)}, f32[96,256]{1,0:T(8,128)S(1)}, u32[]{:S(2)}, u32[]{:S(2)}) %collective-permute-start.4) | collective-permute-done | bytes 98336 | tf_op jit(solution)/shard_map/ppermute | solution.py:451
  42.5 0.0 copy-start.7
  42.5 0.6 collective-permute-done.6.x3
  43.1 0.0 copy-start.8
  43.1 0.0 collective-permute-done.5.x2
  43.1 0.0 copy-done.7
  43.1 0.6 copy-done.8
  43.7 0.0 copy-start.4
  43.7 0.7 copy-done.4
  44.4 7.4 %shard_map.61 = (f32[3,1024,128]{2,1,0:T(8,128)}, f32[3,1024,128]{2,1,0:T(8,128)}, bf16[3,256,256]{2,1,0:T(8,128)(2,1)}) custom-call(f32[7,64,1024]{2,1,0:T(8,128)} %ain.9, f32[7,32,1024]{2,1,0:T(8,128)} %aout.9, f32[7,32,64]{2,1,0:T(8,128)} %interp.3, f32[96,256]{1,0:T(8,128)} %copy-done.7, f32[96,768]{1,0:T(8,128)} %copy-done.4, f32[96,256]{1,0:T(8,128)} %copy-done.8), custom_call_target="tpu_custom_call" | custom-call | tf_op jit(solution)/shard_map/pallas_call | solution.py:476
  51.8 0.0 collective-permute-done.3.other
  51.8 0.0 copy-start.2
  51.8 0.8 copy-done.2
  52.7 7.9 %shard_map.58 = (f32[4,1024,128]{2,1,0:T(8,128)}, f32[4,1024,128]{2,1,0:T(8,128)}, bf16[4,256,256]{2,1,0:T(8,128)(2,1)}) custom-call(f32[7,64,1024]{2,1,0:T(8,128)} %ain.9, f32[7,32,1024]{2,1,0:T(8,128)} %aout.9, f32[7,32,64]{2,1,0:T(8,128)} %interp.3, f32[96,1536]{1,0:T(8,128)} %get-tuple-element.35.kept, f32[96,1536]{1,0:T(8,128)} %copy-done.2), custom_call_target="tpu_custom_call" | custom-call | tf_op jit(solution)/shard_map/pallas_call | solution.py:463
  60.6 0.0 all-to-all-done.x_ref
  60.6 0.0 copy-start.1
  60.6 1.3 copy-done.1
  61.9 10.4 %shard_map.59 = f32[8,128,512]{2,1,0:T(8,128)} custom-call(f32[16,64,512]{2,1,0:T(8,128)} %copy-done.1, f32[4,1024,128]{2,1,0:T(8,128)} %get-tuple-element.37.cos, f32[4,1024,128]{2,1,0:T(8,128)} %get-tuple-element.38.sin, bf16[4,256,256]{2,1,0:T(8,128)(2,1)} %get-tuple-element.39.w), custom_call_target="tpu_custom_call" | custom-call | tf_op jit(solution)/shard_map/pallas_call | solution.py:490
  72.3 30.5 %all_to_all.15.x_ref = f32[8,128,512]{2,1,0:T(8,128)} all-to-all(f32[8,128,512]{2,1,0:T(8,128)} %shard_map.59), channel_id=1, replica_groups=mesh['y'=4,'zh'=2,'x'=4,'zl'=2,'c'=2] {'x','zl'}, dimensions={0} | all-to-all | bytes 4194304 | tf_op jit(solution)/shard_map/all_to_all | solution.py:501
  102.8 11.9 %shard_map.62 = f32[128,32,128]{2,1,0:T(8,128)} custom-call(s32[1024]{0:T(1024)} %bitcast.6, f32[8,128,512]{2,1,0:T(8,128)} %all_to_all.15.x_ref, f32[3,1024,128]{2,1,0:T(8,128)} %get-tuple-element.48.cos, f32[3,1024,128]{2,1,0:T(8,128)} %get-tuple-element.49.sin, bf16[3,256,256]{2,1,0:T(8,128)(2,1)} %get-tuple-element.50.w), custom_call_target="tpu_custom_call" | custom-call | tf_op jit(solution)/shard_map/pallas_call | solution.py:503
  114.7 40.0 %all_to_all.16 = f32[128,32,128]{2,1,0:T(8,128)S(1)} all-to-all(f32[128,32,128]{2,1,0:T(8,128)} %shard_map.62), channel_id=1, replica_groups=mesh['y'=4,'zh'=2,'x'=4,'zl'=2,'c'=2] {'y','zh','x','zl','c'}, dimensions={0} | all-to-all | bytes 4194304 | tf_op jit(solution)/shard_map/all_to_all | solution.py:513
  154.7 2.2 %shard_map.63 = f32[512,1024]{1,0:T(8,128)} custom-call(f32[4096,128]{1,0:T(8,128)S(1)} %bitcast.4), custom_call_target="tpu_custom_call" | custom-call | tf_op jit(solution)/shard_map/pallas_call | solution.py:515
Async XLA Ops:
  0.0 6.7 %copy-start = (f32[2,32,8,1024]{3,2,1,0:T(8,128)S(1)}, f32[2,32,8,1024]{3,2,1,0:T(8,128)}, u32[]{:S(2)}) copy-start(f32[2,32,8,1024]{3,2,1,0:T(8,128)} %param.5) | copy-start | bytes 6291460
  2.0 13.6 %collective-permute-start.1 = (f32[96,768]{1,0:T(8,128)}, f32[96,768]{1,0:T(8,128)S(1)}, u32[]{:S(2)}, u32[]{:S(2)}) collective-permute-start(f32[96,768]{1,0:T(8,128)} %get-tuple-element.29), channel_id=1, source_target_pairs={{0,64},{32,96},{64,0},{96,32},{1,65},{33,97},{65,1},{97,33},{2,66}... | collective-permute-start | bytes 884744 | tf_op jit(solution)/shard_map/ppermute | solution.py:428
  5.9 9.2 %collective-permute-start = (f32[96,256]{1,0:T(8,128)}, f32[96,256]{1,0:T(8,128)S(1)}, u32[]{:S(2)}, u32[]{:S(2)}) collective-permute-start(f32[96,256]{1,0:T(8,128)} %get-tuple-element.28), channel_id=1, source_target_pairs={{0,32},{32,0},{64,96},{96,64},{1,33},{33,1},{65,97},{97,65},{2,34}... | collective-permute-start | bytes 294920 | tf_op jit(solution)/shard_map/ppermute | solution.py:428
  6.3 9.4 %collective-permute-start.2 = (f32[96,256]{1,0:T(8,128)}, f32[96,256]{1,0:T(8,128)S(1)}, u32[]{:S(2)}, u32[]{:S(2)}) collective-permute-start(f32[96,256]{1,0:T(8,128)} %get-tuple-element.30), channel_id=1, source_target_pairs={{0,96},{32,64},{64,32},{96,0},{1,97},{33,65},{65,33},{97,1},{2,98}... | collective-permute-start | bytes 294920 | tf_op jit(solution)/shard_map/ppermute | solution.py:428
  15.0 0.6 copy-start.5
  15.7 0.6 copy-start.6
  15.7 0.8 copy-start.3
  16.4 44.2 %all-to-all-start = ((f32[16,64,512]{2,1,0:T(8,128)}), f32[16,64,512]{2,1,0:T(8,128)S(1)}, u32[]{:S(2)}, u32[]{:S(2)}) async-start(f32[16,64,512]{2,1,0:T(8,128)} %shard_map.55), calls=%async_computation | async-start | bytes 4194304 | tf_op jit(solution)/shard_map/all_to_all | solution.py:440
  28.2 5.8 %copy-start.9 = (s32[1,1024]{1,0:T(1,128)S(1)}, s32[1,1024]{1,0:T(1,128)}, u32[]{:S(2)}) copy-start(s32[1,1024]{1,0:T(1,128)} %param.9) | copy-start | bytes 12292
  28.2 23.6 %collective-permute-start.3 = (f32[96,1536]{1,0:T(8,128)}, f32[96,1536]{1,0:T(8,128)S(1)}, u32[]{:S(2)}, u32[]{:S(2)}) collective-permute-start(f32[96,1536]{1,0:T(8,128)} %get-tuple-element.36), channel_id=1, source_target_pairs={{0,1},{1,0},{2,3},{3,2},{4,5},{5,4},{6,7},{7,6},{8,9},{9,8},{10,11... | collective-permute-start | bytes 1769480 | tf_op jit(solution)/shard_map/ppermute | solution.py:461
  30.3 12.8 %collective-permute-start.5 = (f32[96,768]{1,0:T(8,128)}, f32[96,768]{1,0:T(8,128)S(1)}, u32[]{:S(2)}, u32[]{:S(2)}) collective-permute-start(f32[96,768]{1,0:T(8,128)} %get-tuple-element.41), channel_id=1, source_target_pairs={{0,8},{4,12},{8,0},{12,4},{1,9},{5,13},{9,1},{13,5},{2,10},{6,14},... | collective-permute-start | bytes 884744 | tf_op jit(solution)/shard_map/ppermute | solution.py:451
  33.1 9.4 %collective-permute-start.4 = (f32[96,256]{1,0:T(8,128)}, f32[96,256]{1,0:T(8,128)S(1)}, u32[]{:S(2)}, u32[]{:S(2)}) collective-permute-start(f32[96,256]{1,0:T(8,128)} %get-tuple-element.40), channel_id=1, source_target_pairs={{0,4},{4,0},{8,12},{12,8},{1,5},{5,1},{9,13},{13,9},{2,6},{6,2},{1... | collective-permute-start | bytes 294920 | tf_op jit(solution)/shard_map/ppermute | solution.py:451
  33.4 9.7 %collective-permute-start.6 = (f32[96,256]{1,0:T(8,128)}, f32[96,256]{1,0:T(8,128)S(1)}, u32[]{:S(2)}, u32[]{:S(2)}) collective-permute-start(f32[96,256]{1,0:T(8,128)} %get-tuple-element.42), channel_id=1, source_target_pairs={{0,12},{4,8},{8,4},{12,0},{1,13},{5,9},{9,5},{13,1},{2,14},{6,10},... | collective-permute-start | bytes 294920 | tf_op jit(solution)/shard_map/ppermute | solution.py:451
  42.5 0.6 copy-start.7
  43.1 0.6 copy-start.8
  43.7 0.7 copy-start.4
  51.8 0.8 copy-start.2
  60.6 1.3 copy-start.1

commit v5 on v4

--- a/solution.py
+++ b/solution.py
@@ -81,15 +81,22 @@
                     out_ref[rev(kt, 3) * 2 + core, :, lanes] = part[core * 64 : core * 64 + 64]
 
 
-def final_kernel(nv, x_ref, out_ref, columns):
+def final_kernel(nv, x_ref, out_ref, columns, sems):
     ncv = 2 * nv
+
+    def leave(kt):
+        lanes = slice(kt * 128, kt * 128 + 128)
+        return pltpu.make_async_copy(columns.at[kt], out_ref.at[:, lanes], sems.at[kt])
+
     for kt in range(8):
         for c in range(2):
             for v in range(nv):
                 cv = c * nv + v
                 part = x_ref[pl.ds(kt * 128 * ncv + cv, 128, stride=ncv), :]
                 columns[kt, pl.ds(c * 256 + v, 128, stride=2), :] = part.T
-        out_ref[:, kt * 128 : kt * 128 + 128] = columns[kt]
+        leave(kt).start()
+    for kt in range(8):
+        leave(kt).wait()
 
 
 def fetch(jobs, sems):
@@ -176,14 +183,21 @@
             w_ref[level, :, i * 128 : i * 128 + 128] = full.astype(BF16)
 
 
-def tables(count, slabs, raw, cos_ref, sin_ref):
+def tables(count, slabs, raw, cos_ref, sin_ref, cos_v, sin_v, sems):
     rows = 1024 // slabs
     lane = lax.broadcasted_iota(jnp.int32, (rows, 128), 1)
 
-    def body(m, _):
-        low = pl.ds(pl.multiple_of(m * rows, rows), rows)
-        high = pl.ds(pl.multiple_of((m + slabs // 2) * rows, rows), rows)
-        for level in range(count):
+    def leave(level):
+        return [
+            pltpu.make_async_copy(src.at[level], dst.at[level], sems.at[i, level])
+            for i, (src, dst) in enumerate(((cos_v, cos_ref), (sin_v, sin_ref)))
+        ]
+
+    for level in range(count):
+
+        def body(m, _):
+            low = pl.ds(pl.multiple_of(m * rows, rows), rows)
+            high = pl.ds(pl.multiple_of((m + slabs // 2) * rows, rows), rows)
             if level:
                 before = jnp.where(
                     lane < 32,
@@ -199,15 +213,21 @@
                     turn = jnp.where(angle > PI, TAU, jnp.where(angle < -PI, -TAU, 0.0))
                     angle = angle - turn
                 s, c = sincos(angle)
-                cos_ref[level, at, :] = c
-                sin_ref[level, at, :] = s
-        return 0
-
-    lax.fori_loop(0, slabs // 2, body, 0)
+                cos_v[level, at, :] = c
+                sin_v[level, at, :] = s
+            return 0
+
+        lax.fori_loop(0, slabs // 2, body, 0, unroll=2)
+        for copy in leave(level):
+            copy.start()
+    for level in range(count):
+        for copy in leave(level):
+            copy.wait()
 
 
 def table_lo_kernel(
-    ain, aout, interp, kept, other, cos_ref, sin_ref, w_ref, raw, scratch, mine, sems
+    ain, aout, interp, kept, other, cos_ref, sin_ref, w_ref, raw, scratch, mine, sems,
+    cos_v, sin_v, out_sems,
 ):
     y = lax.axis_index("y")
     core = lax.axis_index("c")
@@ -231,11 +251,12 @@
         emit(2, side * 8, 8)
     turned(got(mine, 0), scratch, 1024)
     emit(3, 0, 16)
-    tables(4, 16, raw, cos_ref, sin_ref)
+    tables(4, 16, raw, cos_ref, sin_ref, cos_v, sin_v, out_sems)
 
 
 def table_hi_kernel(
-    ain, aout, interp, x1, x2, x3, cos_ref, sin_ref, w_ref, raw, scratch, mine, sems
+    ain, aout, interp, x1, x2, x3, cos_ref, sin_ref, w_ref, raw, scratch, mine, sems,
+    cos_v, sin_v, out_sems,
 ):
     x = lax.axis_index("x")
     rx = rev(x, 2)
@@ -265,7 +286,7 @@
     emit(1, (1 - (x >> 1)) * 4, 4)
     turned(got(mine, 768), scratch, 1024)
     emit(2, 0, 8)
-    tables(3, 8, raw, cos_ref, sin_ref)
+    tables(3, 8, raw, cos_ref, sin_ref, cos_v, sin_v, out_sems)
 
 
 def spread(table, kind):
@@ -299,103 +320,124 @@
     return re + im
 
 
-def run_level(nv, level, last, count, rows, load_low, load_high, store, cos_ref, sin_ref, w_ref):
+def levels_kernel(nv, count, slabs, first, put, sources, held, sems, x_ref, bufs, x_sems, sent):
+    rows = 1024 // slabs
     group = 128 // rows
-    w = w_ref[level]
-
-    for i in range(count // group):
-        for t in range(2):
-            at = [(2 * (i * group + g) + t) * rows for g in range(group)]
-            c = jnp.concatenate([cos_ref[level, pl.ds(a, rows), :] for a in at], axis=0)
-            s = jnp.concatenate([sin_ref[level, pl.ds(a, rows), :] for a in at], axis=0)
-            low = lambda q: jnp.concatenate(
-                [load_low(i * group + g, q) for g in range(group)], axis=0
-            )
-            high = lambda q: jnp.concatenate(
-                [load_high(i * group + g, q) for g in range(group)], axis=0
-            )
-            for q, tile in enumerate(step(nv, low, high, c, s, w, last)):
-                for g in range(group):
-                    store(2 * (i * group + g) + t, q, tile[g * rows : g * rows + rows])
-
-
-def levels_kernel(nv, count, slabs, load_first, store_last, sources, held, sems, one, two):
-    rows = 1024 // slabs
+    bodies = slabs // 2 // group
     lanes = lambda q: slice(q * 128, q * 128 + 128)
-    copies = []
+    one, two = bufs
+
+    def copies(level):
+        return [
+            pltpu.make_async_copy(src.at[level], dst.at[level], sems.at[i, level])
+            for i, (src, dst) in enumerate(zip(sources, held))
+        ]
+
+    def arrive(i):
+        part = first(i)[0]
+        return pltpu.make_async_copy(x_ref.at[part], two.at[part], x_sems.at[i])
+
+    arrive(0).start()
+    for copy in copies(0):
+        copy.start()
+    for i in range(1, bodies):
+        arrive(i).start()
+    for level in range(1, count):
+        for copy in copies(level):
+            copy.start()
+    cos_ref, sin_ref, w_ref = held
     for level in range(count):
-        copies.append(
-            [
-                pltpu.make_async_copy(src.at[level], dst.at[level], sems.at[i, level])
-                for i, (src, dst) in enumerate(zip(sources, held))
-            ]
-        )
-        for copy in copies[-1]:
-            copy.start()
-    bufs = (one, two)
-    for level in range(count):
-        for copy in copies[level]:
+        for copy in copies(level):
             copy.wait()
+        last = level == count - 1
         src = bufs[(level + 1) % 2]
         dst = bufs[level % 2]
-        if level == 0:
-            low, high = load_first
-        else:
-            low = lambda m, q, src=src: src[m, :, lanes(q)]
-            high = lambda m, q, src=src: src[m + slabs // 2, :, lanes(q)]
-        last = level == count - 1
-
-        def store(slab, q, tile, dst=dst):
-            dst[slab, :, lanes(q)] = tile
-
-        run_level(
-            nv, level, last, slabs // 2, rows, low, high,
-            store_last if last else store, *held,
-        )
-
-
-def levels_lo_kernel(nv, x_ref, cos, sin, w, out_ref, one, two, cos_v, sin_v, w_v, sems):
+        w = w_ref[level]
+        for i in range(bodies):
+            if level == 0:
+                arrive(i).wait()
+                lows, highs = first(i)[1:]
+            else:
+                lows = [i * group + g for g in range(group)]
+                highs = [m + slabs // 2 for m in lows]
+            low = lambda q: jnp.concatenate([src[m, :, lanes(q)] for m in lows], axis=0)
+            high = lambda q: jnp.concatenate([src[m, :, lanes(q)] for m in highs], axis=0)
+            for t in range(2):
+                outs = [2 * (i * group + g) + t for g in range(group)]
+                at = [slice(m * rows, m * rows + rows) for m in outs]
+                c = jnp.concatenate([cos_ref[level, k, :] for k in at], axis=0)
+                s = jnp.concatenate([sin_ref[level, k, :] for k in at], axis=0)
+                for q, tile in enumerate(step(nv, low, high, c, s, w, last)):
+                    for g, m in enumerate(outs):
+                        part = tile[g * rows : g * rows + rows]
+                        if last:
+                            put(m, q, part)
+                        else:
+                            dst[m, :, lanes(q)] = part
+            if last:
+                sent(i)
+
+
+def levels_lo_kernel(
+    nv, x_ref, cos, sin, w, out_ref, one, two, cos_v, sin_v, w_v, sems, x_sems, stage, out_sems
+):
     lanes = lambda q: slice(q * 128, q * 128 + 128)
 
-    def at(m):
-        return (m >> 1 & 1) * 8 + (m >> 2 & 1) * 4 + (m & 1)
+    def first(i):
+        a = (i & 1) * 8 + (i >> 1) * 4
+        return slice(a, a + 4), [a, a + 1], [a + 2, a + 3]
 
     def put(slab, q, tile):
         for kp in range(8):
-            rows = slice(slab * 8, slab * 8 + 8)
-            out_ref[rev(kp, 3), rows, lanes(q)] = tile[kp * 8 : kp * 8 + 8]
+            stage[rev(kp, 3), slab * 8 : slab * 8 + 8, lanes(q)] = tile[kp * 8 : kp * 8 + 8]
+
+    def leave(i):
+        rows = slice(i * 32, i * 32 + 32)
+        return pltpu.make_async_copy(
+            stage.at[:, rows, :], out_ref.at[:, rows, :], out_sems.at[i]
+        )
 
     levels_kernel(
-        nv, 4, 16,
-        (lambda m, q: x_ref[at(m), :, lanes(q)], lambda m, q: x_ref[at(m) + 2, :, lanes(q)]),
-        put, (cos, sin, w), (cos_v, sin_v, w_v), sems, one, two,
+        nv, 4, 16, first, put, (cos, sin, w), (cos_v, sin_v, w_v), sems,
+        x_ref, (one, two), x_sems, lambda i: leave(i).start(),
     )
+    for i in range(4):
+        leave(i).wait()
 
 
 def levels_hi_kernel(
-    nv, where_ref, x_ref, cos, sin, w, out_ref, one, two, cos_v, sin_v, w_v, sems, done
+    nv, where_ref, x_ref, cos, sin, w, out_ref, one, two, cos_v, sin_v, w_v, sems, x_sems,
+    stage, out_sems, done,
 ):
-    lanes = lambda q: slice(q * 128, q * 128 + 128)
     ncv = 2 * nv
+
+    def first(i):
+        a = rev(i, 2) * 2
+        return slice(a, a + 2), [a], [a + 1]
 
     def put(slab, q, tile):
         done[slab * 128 : slab * 128 + 128, q, :] = tile
 
     levels_kernel(
-        nv, 3, 8,
-        (
-            lambda m, q: x_ref[rev(m, 2) * 2, :, lanes(q)],
-            lambda m, q: x_ref[rev(m, 2) * 2 + 1, :, lanes(q)],
-        ),
-        put, (cos, sin, w), (cos_v, sin_v, w_v), sems, one, two,
+        nv, 3, 8, first, put, (cos, sin, w), (cos_v, sin_v, w_v), sems,
+        x_ref, (one, two), x_sems, lambda i: None,
     )
 
-    def gather(e, _):
-        for r in range(8):
-            out_ref[e, r * ncv : r * ncv + ncv, :] = done[where_ref[e * 8 + r]]
-        return 0
-
-    lax.fori_loop(0, 128, gather, 0)
+    def leave(i):
+        part = slice(i * 32, i * 32 + 32)
+        return pltpu.make_async_copy(stage.at[part], out_ref.at[part], out_sems.at[i])
+
+    for i in range(4):
+
+        def gather(e, _):
+            for r in range(8):
+                stage[e, r * ncv : r * ncv + ncv, :] = done[where_ref[e * 8 + r]]
+            return 0
+
+        lax.fori_loop(i * 32, i * 32 + 32, gather, 0)
+        leave(i).start()
+    for i in range(4):
+        leave(i).wait()
 
 
 def held(count):
@@ -404,6 +446,7 @@
         pltpu.VMEM((count, 1024, 128), F32),
         pltpu.VMEM((count, 256, 256), BF16),
         pltpu.SemaphoreType.DMA((3, count)),
+        pltpu.SemaphoreType.DMA((4,)),
     ]
 
 
@@ -464,35 +507,43 @@
         table_lo_kernel,
         out_shape=table_shapes(4),
         in_specs=[HBM, HBM] + [VMEM] * 3,
-        out_specs=[VMEM] * 3,
+        out_specs=[ANY, ANY, VMEM],
         scratch_shapes=[
             pltpu.VMEM((4, 1024, 128), F32),
             pltpu.VMEM((1024, 128), F32),
             pltpu.VMEM((96, 1024), F32),
             pltpu.SemaphoreType.DMA((2, 1)),
-        ],
+        ]
+        + [pltpu.VMEM((4, 1024, 128), F32)] * 2
+        + [pltpu.SemaphoreType.DMA((2, 4))],
         compiler_params=params(BIG),
     )(angle_in, angle_out, interp, kept, other)
+    first, *from_x = lax.optimization_barrier((tables_lo[0], *from_x))
+    tables_lo = [first, *tables_lo[1:]]
     tables_hi = pl.pallas_call(
         table_hi_kernel,
         out_shape=table_shapes(3),
         in_specs=[HBM, HBM] + [VMEM] * 4,
-        out_specs=[VMEM] * 3,
+        out_specs=[ANY, ANY, VMEM],
         scratch_shapes=[
             pltpu.VMEM((3, 1024, 128), F32),
             pltpu.VMEM((1024, 128), F32),
             pltpu.VMEM((96, 1792), F32),
             pltpu.SemaphoreType.DMA((2, 3)),
-        ],
+        ]
+        + [pltpu.VMEM((3, 1024, 128), F32)] * 2
+        + [pltpu.SemaphoreType.DMA((2, 3))],
         compiler_params=params(BIG),
     )(angle_in, angle_out, interp, *from_x)
 
     state = pl.pallas_call(
         functools.partial(levels_lo_kernel, nv),
         out_shape=shape((8, 128, ncv * 128), F32),
-        in_specs=[VMEM] + [ANY] * 3,
-        out_specs=VMEM,
-        scratch_shapes=[pltpu.VMEM((16, 64, ncv * 128), F32)] * 2 + held(4),
+        in_specs=[ANY] * 4,
+        out_specs=ANY,
+        scratch_shapes=[pltpu.VMEM((16, 64, ncv * 128), F32)] * 2
+        + held(4)
+        + [pltpu.VMEM((8, 128, ncv * 128), F32), pltpu.SemaphoreType.DMA((4,))],
         compiler_params=params(BIG),
     )(state, *tables_lo)
     wanted = destination[0]
@@ -503,11 +554,15 @@
     state = pl.pallas_call(
         functools.partial(levels_hi_kernel, nv),
         out_shape=shape((128, 8 * ncv, 128), F32),
-        in_specs=[SMEM, VMEM] + [ANY] * 3,
-        out_specs=VMEM,
+        in_specs=[SMEM] + [ANY] * 4,
+        out_specs=ANY,
         scratch_shapes=[pltpu.VMEM((8, 128, ncv * 128), F32)] * 2
         + held(3)
-        + [pltpu.VMEM((1024, ncv, 128), F32)],
+        + [
+            pltpu.VMEM((128, 8 * ncv, 128), F32),
+            pltpu.SemaphoreType.DMA((4,)),
+            pltpu.VMEM((1024, ncv, 128), F32),
+        ],
         compiler_params=params(BIG),
     )(where, state, *tables_hi)
     state = lax.all_to_all(state, AXES, 0, 0, tiled=True)
@@ -516,8 +571,8 @@
         functools.partial(final_kernel, nv),
         out_shape=shape((512, 1024), F32),
         in_specs=[VMEM],
-        out_specs=VMEM,
-        scratch_shapes=[pltpu.VMEM((8, 512, 128), F32)],
+        out_specs=ANY,
+        scratch_shapes=[pltpu.VMEM((8, 512, 128), F32), pltpu.SemaphoreType.DMA((8,))],
         compiler_params=params(6),
     )(state.reshape(1024 * ncv, 128))
     return out.reshape(2, 32, 8, 1024)

time: 157 us -> 147 us (0.936)
  waiting for transfers between devices: 15.6 us -> 8.63 us
  blocking collectives: 70.5 us -> 68.8 us
    ppermute x3, waiting for transfers between devices: 8.54 us -> 0.01 us  [shards(): lax.ppermute(s, 'x', [(i, i ^ m) for i in range(4)])]
  transfers between devices with their start and end apart: 8 -> 8, of which waited for: 4 -> 3; matrix products, arithmetic and copies ran while one was open for 0% -> 0% of each run, Pallas kernels for 14% -> 15%
where the time goes in v5:
time: 147 us
  blocking collectives  68.8 us (47%)
  Pallas kernels  48 us (33%)
  starting transfers between devices  16.8 us (11%)
  waiting for transfers between devices  8.63 us (6%)
  local copies, waits for them, and re-layouts  3.65 us (2%)
    all_to_all x1, blocking collectives, shards(): state = lax.all_to_all(state, AXES, 0, 0, tiled=True)  39.1 us
    all_to_all x1, blocking collectives, shards(): state = lax.all_to_all(state, ('x', 'zl'), 0, 0, tiled=True)  29.8 us
    pallas_call x1, Pallas kernels, shards(): pl.pallas_call(functools.partial(levels_hi_kernel, nv), out_shape=shape((...  11.8 us
    pallas_call x1, Pallas kernels, shards(): pl.pallas_call(functools.partial(levels_lo_kernel, nv), out_shape=shape((...  9.94 us
    all_to_all x1, starting transfers between devices, shards(): state = lax.all_to_all(state, ('y', 'zh', 'c'), 0, 0, tiled=True)  8.34 us
    pallas_call x1, Pallas kernels, shards(): pl.pallas_call(table_lo_kernel, out_shape=table_shapes(4), in_specs=[HBM,...  8.05 us
    pallas_call x1, Pallas kernels, shards(): pl.pallas_call(table_hi_kernel, out_shape=table_shapes(3), in_specs=[HBM,...  7.43 us
    ppermute x3, waiting for transfers between devices, shards(): lax.ppermute(s, 'y', [(i, i ^ m) for i in range(4)])  7.06 us
  transfers between devices with their start and end apart: 8, of which 3 were waited for; matrix products, arithmetic and copies ran while one was open for 0% of the time, Pallas kernels for 15%

profile of v5, /device:TPU:1, one launch (start us, length us, event | category | flops | bytes accessed | tf_op | source)
XLA Modules:
  0.0 146.8 jit_solution(3793356636892898590)
XLA Ops:
  0.0 0.0 copy-start
  0.0 2.0 %shard_map.56 = (f32[96,256]{1,0:T(8,128)}, f32[96,768]{1,0:T(8,128)}, f32[96,256]{1,0:T(8,128)}) custom-call(f32[7,64,1024]{2,1,0:T(8,128)} %ain.9, f32[7,32,1024]{2,1,0:T(8,128)} %aout.9), custom_call_target="tpu_custom_call" | custom-call | tf_op jit(solution)/shard_map/pallas_call | solution.py:462
  2.0 3.8 %collective-permute-start.1 = (f32[96,768]{1,0:T(8,128)}, f32[96,768]{1,0:T(8,128)S(1)}, u32[]{:S(2)}, u32[]{:S(2)}) collective-permute-start(f32[96,768]{1,0:T(8,128)} %get-tuple-element.33), channel_id=1, source_target_pairs={{0,64},{32,96},{64,0},{96,32},{1,65},{33,97},{65,1},{97,33},{2,66}... | collective-permute-start | bytes 884744 | tf_op jit(solution)/shard_map/ppermute | solution.py:471
  5.9 0.4 collective-permute-start
  6.3 0.4 collective-permute-start.2
  6.7 0.0 copy-done
  6.7 1.9 %shard_map.55 = f32[16,64,512]{2,1,0:T(8,128)} custom-call(f32[512,1024]{1,0:T(8,128)S(1)} %bitcast.5), custom_call_target="tpu_custom_call" | custom-call | tf_op jit(solution)/shard_map/pallas_call | solution.py:474
  8.6 6.4 %collective-permute-done.y1 = f32[96,256]{1,0:T(8,128)S(1)} collective-permute-done((f32[96,256]{1,0:T(8,128)}, f32[96,256]{1,0:T(8,128)S(1)}, u32[]{:S(2)}, u32[]{:S(2)}) %collective-permute-start) | collective-permute-done | bytes 98336 | tf_op jit(solution)/shard_map/ppermute | solution.py:471
  15.0 0.0 copy-start.7
  15.0 0.6 collective-permute-done.2.y3
  15.7 0.0 copy-start.8
  15.7 0.0 collective-permute-done.1.y2
  15.7 0.0 copy-start.4
  15.7 0.0 copy-done.7
  15.7 0.6 copy-done.8
  16.3 0.1 copy-done.4
  16.4 8.3 %all-to-all-start = ((f32[16,64,512]{2,1,0:T(8,128)}), f32[16,64,512]{2,1,0:T(8,128)S(1)}, u32[]{:S(2)}, u32[]{:S(2)}) async-start(f32[16,64,512]{2,1,0:T(8,128)} %shard_map.55), calls=%async_computation | async-start | bytes 4194304 | tf_op jit(solution)/shard_map/all_to_all | solution.py:483
  24.8 3.3 %shard_map.57 = (f32[96,1536]{1,0:T(8,128)}, f32[96,1536]{1,0:T(8,128)}) custom-call(f32[7,64,1024]{2,1,0:T(8,128)} %ain.9, f32[7,32,1024]{2,1,0:T(8,128)} %aout.9, f32[96,256]{1,0:T(8,128)} %copy-done.7, f32[96,768]{1,0:T(8,128)} %copy-done.4, f32[96,256]{1,0:T(8,128)} %copy-done.8), custom_call_target="tpu_custom_call" | custom-call | tf_op jit(solution)/shard_map/pallas_call | solution.py:496
  28.1 0.0 copy-start.9
  28.1 0.2 collective-permute-start.3
  28.3 1.9 %shard_map.59 = (f32[96,256]{1,0:T(8,128)}, f32[96,768]{1,0:T(8,128)}, f32[96,256]{1,0:T(8,128)}) custom-call(f32[7,64,1024]{2,1,0:T(8,128)} %ain.9, f32[7,32,1024]{2,1,0:T(8,128)} %aout.9), custom_call_target="tpu_custom_call" | custom-call | tf_op jit(solution)/shard_map/pallas_call | solution.py:485
  30.2 2.8 %collective-permute-start.5 = (f32[96,768]{1,0:T(8,128)}, f32[96,768]{1,0:T(8,128)S(1)}, u32[]{:S(2)}, u32[]{:S(2)}) collective-permute-start(f32[96,768]{1,0:T(8,128)} %get-tuple-element.43), channel_id=1, source_target_pairs={{0,8},{4,12},{8,0},{12,4},{1,9},{5,13},{9,1},{13,5},{2,10},{6,14},... | collective-permute-start | bytes 884744 | tf_op jit(solution)/shard_map/ppermute | solution.py:494
  33.0 0.3 collective-permute-start.4
  33.3 0.6 collective-permute-start.6
  33.9 0.0 copy-done.9
  33.9 0.6 shift-right-arithmetic_add_fusion
  34.5 0.0 collective-permute-done.3.other
  34.5 0.0 copy-start.2
  34.5 0.8 copy-done.2
  35.3 8.1 %shard_map.58 = (f32[4,1024,128]{2,1,0:T(8,128)}, f32[4,1024,128]{2,1,0:T(8,128)}, bf16[4,256,256]{2,1,0:T(8,128)(2,1)}) custom-call(f32[7,64,1024]{2,1,0:T(8,128)} %ain.9, f32[7,32,1024]{2,1,0:T(8,128)} %aout.9, f32[7,32,64]{2,1,0:T(8,128)} %interp.3, f32[96,1536]{1,0:T(8,128)} %get-tuple-element.39.kept, f32[96,1536]{1,0:T(8,128)} %copy-done.2), custom_call_target="tpu_custom_call" | custom-call | tf_op jit(solution)/shard_map/pallas_call | solution.py:506
  43.4 0.0 collective-permute-done.4.x1
  43.4 0.0 copy-start.5
  43.4 0.0 collective-permute-done.6.x3
  43.4 0.0 copy-start.6
  43.4 0.0 collective-permute-done.5.x2
  43.4 0.0 copy-start.3
  43.5 0.6 copy-done.5
  44.0 0.1 copy-done.6
  44.1 0.1 copy-done.3
  44.2 7.4 %shard_map.61 = (f32[3,1024,128]{2,1,0:T(8,128)}, f32[3,1024,128]{2,1,0:T(8,128)}, bf16[3,256,256]{2,1,0:T(8,128)(2,1)}) custom-call(f32[7,64,1024]{2,1,0:T(8,128)} %ain.9, f32[7,32,1024]{2,1,0:T(8,128)} %aout.9, f32[7,32,64]{2,1,0:T(8,128)} %interp.3, f32[96,256]{1,0:T(8,128)} %copy-done.5, f32[96,768]{1,0:T(8,128)} %copy-done.3, f32[96,256]{1,0:T(8,128)} %copy-done.6), custom_call_target="tpu_custom_call" | custom-call | tf_op jit(solution)/shard_map/pallas_call | solution.py:523
  51.6 1.6 %all-to-all-done.x_ref = f32[16,64,512]{2,1,0:T(8,128)S(1)} async-done(((f32[16,64,512]{2,1,0:T(8,128)}), f32[16,64,512]{2,1,0:T(8,128)S(1)}, u32[]{:S(2)}, u32[]{:S(2)}) %all-to-all-start) | async-done | bytes 2097184 | tf_op jit(solution)/shard_map/all_to_all | solution.py:483
  53.2 0.0 copy-start.1
  53.2 1.3 copy-done.1
  54.5 9.9 %shard_map.60 = f32[8,128,512]{2,1,0:T(8,128)} custom-call(f32[16,64,512]{2,1,0:T(8,128)} %copy-done.1, f32[4,1024,128]{2,1,0:T(8,128)} %get-tuple-element.45.cos, f32[4,1024,128]{2,1,0:T(8,128)} %get-tuple-element.46.sin, bf16[4,256,256]{2,1,0:T(8,128)(2,1)} %get-tuple-element.47.w), custom_call_target="tpu_custom_call" | custom-call | tf_op jit(solution)/shard_map/pallas_call | solution.py:539
  64.5 29.8 %all_to_all.15.x_ref = f32[8,128,512]{2,1,0:T(8,128)} all-to-all(f32[8,128,512]{2,1,0:T(8,128)} %shard_map.60), channel_id=1, replica_groups=mesh['y'=4,'zh'=2,'x'=4,'zl'=2,'c'=2] {'x','zl'}, dimensions={0} | all-to-all | bytes 4194304 | tf_op jit(solution)/shard_map/all_to_all | solution.py:552
  94.2 11.8 %shard_map.62 = f32[128,32,128]{2,1,0:T(8,128)} custom-call(s32[1024]{0:T(1024)} %bitcast.6, f32[8,128,512]{2,1,0:T(8,128)} %all_to_all.15.x_ref, f32[3,1024,128]{2,1,0:T(8,128)} %get-tuple-element.56.cos, f32[3,1024,128]{2,1,0:T(8,128)} %get-tuple-element.57.sin, bf16[3,256,256]{2,1,0:T(8,128)(2,1)} %get-tuple-element.58.w), custom_call_target="tpu_custom_call" | custom-call | tf_op jit(solution)/shard_map/pallas_call | solution.py:554
  106.1 39.1 %all_to_all.16 = f32[128,32,128]{2,1,0:T(8,128)S(1)} all-to-all(f32[128,32,128]{2,1,0:T(8,128)} %shard_map.62), channel_id=1, replica_groups=mesh['y'=4,'zh'=2,'x'=4,'zl'=2,'c'=2] {'y','zh','x','zl','c'}, dimensions={0} | all-to-all | bytes 4194304 | tf_op jit(solution)/shard_map/all_to_all | solution.py:568
  145.1 1.5 %shard_map.63 = f32[512,1024]{1,0:T(8,128)} custom-call(f32[4096,128]{1,0:T(8,128)S(1)} %bitcast.4), custom_call_target="tpu_custom_call" | custom-call | tf_op jit(solution)/shard_map/pallas_call | solution.py:570
Async XLA Ops:
  0.0 6.7 %copy-start = (f32[2,32,8,1024]{3,2,1,0:T(8,128)S(1)}, f32[2,32,8,1024]{3,2,1,0:T(8,128)}, u32[]{:S(2)}) copy-start(f32[2,32,8,1024]{3,2,1,0:T(8,128)} %param.5) | copy-start | bytes 6291460
  2.0 13.6 %collective-permute-start.1 = (f32[96,768]{1,0:T(8,128)}, f32[96,768]{1,0:T(8,128)S(1)}, u32[]{:S(2)}, u32[]{:S(2)}) collective-permute-start(f32[96,768]{1,0:T(8,128)} %get-tuple-element.33), channel_id=1, source_target_pairs={{0,64},{32,96},{64,0},{96,32},{1,65},{33,97},{65,1},{97,33},{2,66}... | collective-permute-start | bytes 884744 | tf_op jit(solution)/shard_map/ppermute | solution.py:471
  5.9 9.2 %collective-permute-start = (f32[96,256]{1,0:T(8,128)}, f32[96,256]{1,0:T(8,128)S(1)}, u32[]{:S(2)}, u32[]{:S(2)}) collective-permute-start(f32[96,256]{1,0:T(8,128)} %get-tuple-element.32), channel_id=1, source_target_pairs={{0,32},{32,0},{64,96},{96,64},{1,33},{33,1},{65,97},{97,65},{2,34}... | collective-permute-start | bytes 294920 | tf_op jit(solution)/shard_map/ppermute | solution.py:471
  6.3 9.4 %collective-permute-start.2 = (f32[96,256]{1,0:T(8,128)}, f32[96,256]{1,0:T(8,128)S(1)}, u32[]{:S(2)}, u32[]{:S(2)}) collective-permute-start(f32[96,256]{1,0:T(8,128)} %get-tuple-element.34), channel_id=1, source_target_pairs={{0,96},{32,64},{64,32},{96,0},{1,97},{33,65},{65,33},{97,1},{2,98}... | collective-permute-start | bytes 294920 | tf_op jit(solution)/shard_map/ppermute | solution.py:471
  15.0 0.6 copy-start.7
  15.7 0.6 copy-start.8
  15.7 0.7 copy-start.4
  16.4 36.8 %all-to-all-start = ((f32[16,64,512]{2,1,0:T(8,128)}), f32[16,64,512]{2,1,0:T(8,128)S(1)}, u32[]{:S(2)}, u32[]{:S(2)}) async-start(f32[16,64,512]{2,1,0:T(8,128)} %shard_map.55), calls=%async_computation | async-start | bytes 4194304 | tf_op jit(solution)/shard_map/all_to_all | solution.py:483
  28.1 5.8 %copy-start.9 = (s32[1,1024]{1,0:T(1,128)S(1)}, s32[1,1024]{1,0:T(1,128)}, u32[]{:S(2)}) copy-start(s32[1,1024]{1,0:T(1,128)} %param.9) | copy-start | bytes 12292
  28.1 6.4 %collective-permute-start.3 = (f32[96,1536]{1,0:T(8,128)}, f32[96,1536]{1,0:T(8,128)S(1)}, u32[]{:S(2)}, u32[]{:S(2)}) collective-permute-start(f32[96,1536]{1,0:T(8,128)} %get-tuple-element.40), channel_id=1, source_target_pairs={{0,1},{1,0},{2,3},{3,2},{4,5},{5,4},{6,7},{7,6},{8,9},{9,8},{10,11... | collective-permute-start | bytes 1769480 | tf_op jit(solution)/shard_map/ppermute | solution.py:504
  30.2 13.2 %collective-permute-start.5 = (f32[96,768]{1,0:T(8,128)}, f32[96,768]{1,0:T(8,128)S(1)}, u32[]{:S(2)}, u32[]{:S(2)}) collective-permute-start(f32[96,768]{1,0:T(8,128)} %get-tuple-element.43), channel_id=1, source_target_pairs={{0,8},{4,12},{8,0},{12,4},{1,9},{5,13},{9,1},{13,5},{2,10},{6,14},... | collective-permute-start | bytes 884744 | tf_op jit(solution)/shard_map/ppermute | solution.py:494
  33.0 10.4 %collective-permute-start.4 = (f32[96,256]{1,0:T(8,128)}, f32[96,256]{1,0:T(8,128)S(1)}, u32[]{:S(2)}, u32[]{:S(2)}) collective-permute-start(f32[96,256]{1,0:T(8,128)} %get-tuple-element.42), channel_id=1, source_target_pairs={{0,4},{4,0},{8,12},{12,8},{1,5},{5,1},{9,13},{13,9},{2,6},{6,2},{1... | collective-permute-start | bytes 294920 | tf_op jit(solution)/shard_map/ppermute | solution.py:494
  33.3 10.1 %collective-permute-start.6 = (f32[96,256]{1,0:T(8,128)}, f32[96,256]{1,0:T(8,128)S(1)}, u32[]{:S(2)}, u32[]{:S(2)}) collective-permute-start(f32[96,256]{1,0:T(8,128)} %get-tuple-element.44), channel_id=1, source_target_pairs={{0,12},{4,8},{8,4},{12,0},{1,13},{5,9},{9,5},{13,1},{2,14},{6,10},... | collective-permute-start | bytes 294920 | tf_op jit(solution)/shard_map/ppermute | solution.py:494
  34.5 0.8 copy-start.2
  43.4 0.6 copy-start.5
  43.4 0.7 copy-start.6
  43.4 0.7 copy-start.3
  53.2 1.3 copy-start.1

commit v6 on v5

--- a/solution.py
+++ b/solution.py
@@ -35,7 +35,8 @@
     1.724760753325688e-09,
 )
 MIB = 1024 * 1024
-BIG = 56
+BIG = 30
+PAD = 72
 
 
 def params(mib):
@@ -183,15 +184,12 @@
             w_ref[level, :, i * 128 : i * 128 + 128] = full.astype(BF16)
 
 
-def tables(count, slabs, raw, cos_ref, sin_ref, cos_v, sin_v, sems):
+def tables(count, slabs, raw, tab_ref, tab_v, sems):
     rows = 1024 // slabs
     lane = lax.broadcasted_iota(jnp.int32, (rows, 128), 1)
 
     def leave(level):
-        return [
-            pltpu.make_async_copy(src.at[level], dst.at[level], sems.at[i, level])
-            for i, (src, dst) in enumerate(((cos_v, cos_ref), (sin_v, sin_ref)))
-        ]
+        return pltpu.make_async_copy(tab_v.at[level], tab_ref.at[level], sems.at[level])
 
     for level in range(count):
 
@@ -213,21 +211,22 @@
                     turn = jnp.where(angle > PI, TAU, jnp.where(angle < -PI, -TAU, 0.0))
                     angle = angle - turn
                 s, c = sincos(angle)
-                cos_v[level, at, :] = c
-                sin_v[level, at, :] = s
+                tab_v[level, at, :] = jnp.where(lane < 64, c, pltpu.roll(s, 64, 1))
+                if level == count - 1:
+                    out = jnp.where(lane < 32, pltpu.roll(c, 64, 1), pltpu.roll(s, 96, 1))
+                    tab_v[count, at, :] = out
             return 0
 
         lax.fori_loop(0, slabs // 2, body, 0, unroll=2)
-        for copy in leave(level):
-            copy.start()
-    for level in range(count):
-        for copy in leave(level):
-            copy.wait()
+        leave(level).start()
+    leave(count).start()
+    for level in range(count + 1):
+        leave(level).wait()
 
 
 def table_lo_kernel(
-    ain, aout, interp, kept, other, cos_ref, sin_ref, w_ref, raw, scratch, mine, sems,
-    cos_v, sin_v, out_sems,
+    ain, aout, interp, kept, other, tab_ref, w_ref, raw, scratch, mine, sems,
+    tab_v, out_sems,
 ):
     y = lax.axis_index("y")
     core = lax.axis_index("c")
@@ -251,12 +250,12 @@
         emit(2, side * 8, 8)
     turned(got(mine, 0), scratch, 1024)
     emit(3, 0, 16)
-    tables(4, 16, raw, cos_ref, sin_ref, cos_v, sin_v, out_sems)
+    tables(4, 16, raw, tab_ref, tab_v, out_sems)
 
 
 def table_hi_kernel(
-    ain, aout, interp, x1, x2, x3, cos_ref, sin_ref, w_ref, raw, scratch, mine, sems,
-    cos_v, sin_v, out_sems,
+    ain, aout, interp, x1, x2, x3, tab_ref, w_ref, raw, scratch, mine, sems,
+    tab_v, out_sems,
 ):
     x = lax.axis_index("x")
     rx = rev(x, 2)
@@ -286,20 +285,20 @@
     emit(1, (1 - (x >> 1)) * 4, 4)
     turned(got(mine, 768), scratch, 1024)
     emit(2, 0, 8)
-    tables(3, 8, raw, cos_ref, sin_ref, cos_v, sin_v, out_sems)
-
-
-def spread(table, kind):
+    tables(3, 8, raw, tab_ref, tab_v, out_sems)
+
+
+def spread(table, first):
     lane = lax.broadcasted_iota(jnp.int32, table.shape, 1)
-    return jnp.take_along_axis(table, kind * 32 + (lane >> 2), axis=1)
-
-
-def step(nv, low, high, cos, sin, w, last):
-    n = cos.shape[0]
+    return jnp.take_along_axis(table, first + (lane >> 2), axis=1)
+
+
+def step(nv, low, high, table, w, after):
+    n = table.shape[0]
     sides = []
     for kind, src in enumerate((low, high)):
-        c = spread(cos, kind)
-        s = spread(sin, kind)
+        c = spread(table, kind * 32)
+        s = spread(table, kind * 32 + 64)
         re, im = [], []
         for v in range(nv):
             xr = src(v)
@@ -311,52 +310,50 @@
     first = dot(hi, w)
     out = first[:, :128] + first[:, 128:] + dot(lo, w[:, :128])
     out = [out[q * n : q * n + n] for q in range(2 * nv)]
-    if not last:
+    if after is None:
         return out
-    c = spread(cos, 2)
-    s = spread(sin, 2)
+    c = spread(after, 0)
+    s = spread(after, 32)
     re = [out[v] * c - out[nv + v] * s for v in range(nv)]
     im = [out[v] * s + out[nv + v] * c for v in range(nv)]
     return re + im
 
 
-def levels_kernel(nv, count, slabs, first, put, sources, held, sems, x_ref, bufs, x_sems, sent):
+def levels_kernel(nv, count, slabs, first, put, sources, held, sems, x_ref, bufs):
     rows = 1024 // slabs
     group = 128 // rows
     bodies = slabs // 2 // group
     lanes = lambda q: slice(q * 128, q * 128 + 128)
     one, two = bufs
 
+    tab_ref, w_ref = held
+
     def copies(level):
+        got = [(0, level), (1, level)] if level < count else [(0, count)]
         return [
-            pltpu.make_async_copy(src.at[level], dst.at[level], sems.at[i, level])
-            for i, (src, dst) in enumerate(zip(sources, held))
+            pltpu.make_async_copy(
+                sources[i].at[k], held[i].at[k], sems.at[i, k]
+            )
+            for i, k in got
         ]
 
-    def arrive(i):
-        part = first(i)[0]
-        return pltpu.make_async_copy(x_ref.at[part], two.at[part], x_sems.at[i])
-
-    arrive(0).start()
     for copy in copies(0):
         copy.start()
-    for i in range(1, bodies):
-        arrive(i).start()
-    for level in range(1, count):
-        for copy in copies(level):
-            copy.start()
-    cos_ref, sin_ref, w_ref = held
     for level in range(count):
         for copy in copies(level):
             copy.wait()
+        for copy in copies(level + 1):
+            copy.start()
+        if level == count - 1:
+            for copy in copies(count):
+                copy.wait()
         last = level == count - 1
-        src = bufs[(level + 1) % 2]
+        src = bufs[(level + 1) % 2] if level else x_ref
         dst = bufs[level % 2]
         w = w_ref[level]
         for i in range(bodies):
             if level == 0:
-                arrive(i).wait()
-                lows, highs = first(i)[1:]
+                lows, highs = first(i)
             else:
                 lows = [i * group + g for g in range(group)]
                 highs = [m + slabs // 2 for m in lows]
@@ -365,94 +362,65 @@
             for t in range(2):
                 outs = [2 * (i * group + g) + t for g in range(group)]
                 at = [slice(m * rows, m * rows + rows) for m in outs]
-                c = jnp.concatenate([cos_ref[level, k, :] for k in at], axis=0)
-                s = jnp.concatenate([sin_ref[level, k, :] for k in at], axis=0)
-                for q, tile in enumerate(step(nv, low, high, c, s, w, last)):
+                read = lambda k: jnp.concatenate([tab_ref[k, r, :] for r in at], axis=0)
+                after = read(count) if last else None
+                for q, tile in enumerate(step(nv, low, high, read(level), w, after)):
                     for g, m in enumerate(outs):
                         part = tile[g * rows : g * rows + rows]
                         if last:
                             put(m, q, part)
                         else:
                             dst[m, :, lanes(q)] = part
-            if last:
-                sent(i)
-
-
-def levels_lo_kernel(
-    nv, x_ref, cos, sin, w, out_ref, one, two, cos_v, sin_v, w_v, sems, x_sems, stage, out_sems
-):
-    lanes = lambda q: slice(q * 128, q * 128 + 128)
-
+
+
+def levels_lo_kernel(nv, x_ref, tab, w, out_ref, one, two, tab_v, w_v, sems):
     def first(i):
         a = (i & 1) * 8 + (i >> 1) * 4
-        return slice(a, a + 4), [a, a + 1], [a + 2, a + 3]
+        return [a, a + 1], [a + 2, a + 3]
 
     def put(slab, q, tile):
         for kp in range(8):
-            stage[rev(kp, 3), slab * 8 : slab * 8 + 8, lanes(q)] = tile[kp * 8 : kp * 8 + 8]
-
-    def leave(i):
-        rows = slice(i * 32, i * 32 + 32)
-        return pltpu.make_async_copy(
-            stage.at[:, rows, :], out_ref.at[:, rows, :], out_sems.at[i]
-        )
+            rows = slice(slab * 8, slab * 8 + 8)
+            out_ref[rev(kp, 3), rows, q * 128 : q * 128 + 128] = tile[kp * 8 : kp * 8 + 8]
 
     levels_kernel(
-        nv, 4, 16, first, put, (cos, sin, w), (cos_v, sin_v, w_v), sems,
-        x_ref, (one, two), x_sems, lambda i: leave(i).start(),
+        nv, 4, 16, first, put, (tab, w), (tab_v, w_v), sems, x_ref, (one, two)
     )
-    for i in range(4):
-        leave(i).wait()
-
-
-def levels_hi_kernel(
-    nv, where_ref, x_ref, cos, sin, w, out_ref, one, two, cos_v, sin_v, w_v, sems, x_sems,
-    stage, out_sems, done,
-):
+
+
+def levels_hi_kernel(nv, where_ref, x_ref, tab, w, out_ref, one, two, tab_v, w_v, sems, done):
     ncv = 2 * nv
 
     def first(i):
         a = rev(i, 2) * 2
-        return slice(a, a + 2), [a], [a + 1]
+        return [a], [a + 1]
 
     def put(slab, q, tile):
         done[slab * 128 : slab * 128 + 128, q, :] = tile
 
     levels_kernel(
-        nv, 3, 8, first, put, (cos, sin, w), (cos_v, sin_v, w_v), sems,
-        x_ref, (one, two), x_sems, lambda i: None,
+        nv, 3, 8, first, put, (tab, w), (tab_v, w_v), sems, x_ref, (one, two)
     )
 
-    def leave(i):
-        part = slice(i * 32, i * 32 + 32)
-        return pltpu.make_async_copy(stage.at[part], out_ref.at[part], out_sems.at[i])
-
-    for i in range(4):
-
-        def gather(e, _):
-            for r in range(8):
-                stage[e, r * ncv : r * ncv + ncv, :] = done[where_ref[e * 8 + r]]
-            return 0
-
-        lax.fori_loop(i * 32, i * 32 + 32, gather, 0)
-        leave(i).start()
-    for i in range(4):
-        leave(i).wait()
+    def gather(e, _):
+        for r in range(8):
+            out_ref[e, r * ncv : r * ncv + ncv, :] = done[where_ref[e * 8 + r]]
+        return 0
+
+    lax.fori_loop(0, 128, gather, 0, unroll=2)
 
 
 def held(count):
     return [
-        pltpu.VMEM((count, 1024, 128), F32),
-        pltpu.VMEM((count, 1024, 128), F32),
+        pltpu.VMEM((count + 1, 1024, 128), F32),
         pltpu.VMEM((count, 256, 256), BF16),
-        pltpu.SemaphoreType.DMA((3, count)),
-        pltpu.SemaphoreType.DMA((4,)),
+        pltpu.SemaphoreType.DMA((2, count + 1)),
     ]
 
 
 def table_shapes(count):
     shape = jax.ShapeDtypeStruct
-    return [shape((count, 1024, 128), F32)] * 2 + [shape((count, 256, 256), BF16)]
+    return [shape((PAD, 1024, 128), F32), shape((count, 256, 256), BF16)]
 
 
 def shards(coefficients, angle_in, angle_out, interp, destination):
@@ -465,7 +433,7 @@
         in_specs=[HBM, HBM],
         out_specs=[VMEM] * 3,
         scratch_shapes=[pltpu.SemaphoreType.DMA((2, 4))],
-        compiler_params=params(BIG),
+        compiler_params=params(56),
     )(angle_in, angle_out)
     from_y = [
         lax.ppermute(s, "y", [(i, i ^ m) for i in range(4)]) for m, s in zip((1, 2, 3), sends)
@@ -507,15 +475,14 @@
         table_lo_kernel,
         out_shape=table_shapes(4),
         in_specs=[HBM, HBM] + [VMEM] * 3,
-        out_specs=[ANY, ANY, VMEM],
+        out_specs=[ANY, VMEM],
         scratch_shapes=[
             pltpu.VMEM((4, 1024, 128), F32),
             pltpu.VMEM((1024, 128), F32),
             pltpu.VMEM((96, 1024), F32),
             pltpu.SemaphoreType.DMA((2, 1)),
         ]
-        + [pltpu.VMEM((4, 1024, 128), F32)] * 2
-        + [pltpu.SemaphoreType.DMA((2, 4))],
+        + [pltpu.VMEM((5, 1024, 128), F32), pltpu.SemaphoreType.DMA((5,))],
         compiler_params=params(BIG),
     )(angle_in, angle_out, interp, kept, other)
     first, *from_x = lax.optimization_barrier((tables_lo[0], *from_x))
@@ -524,26 +491,23 @@
         table_hi_kernel,
         out_shape=table_shapes(3),
         in_specs=[HBM, HBM] + [VMEM] * 4,
-        out_specs=[ANY, ANY, VMEM],
+        out_specs=[ANY, VMEM],
         scratch_shapes=[
             pltpu.VMEM((3, 1024, 128), F32),
             pltpu.VMEM((1024, 128), F32),
             pltpu.VMEM((96, 1792), F32),
             pltpu.SemaphoreType.DMA((2, 3)),
         ]
-        + [pltpu.VMEM((3, 1024, 128), F32)] * 2
-        + [pltpu.SemaphoreType.DMA((2, 3))],
+        + [pltpu.VMEM((4, 1024, 128), F32), pltpu.SemaphoreType.DMA((4,))],
         compiler_params=params(BIG),
     )(angle_in, angle_out, interp, *from_x)
 
     state = pl.pallas_call(
         functools.partial(levels_lo_kernel, nv),
         out_shape=shape((8, 128, ncv * 128), F32),
-        in_specs=[ANY] * 4,
-        out_specs=ANY,
-        scratch_shapes=[pltpu.VMEM((16, 64, ncv * 128), F32)] * 2
-        + held(4)
-        + [pltpu.VMEM((8, 128, ncv * 128), F32), pltpu.SemaphoreType.DMA((4,))],
+        in_specs=[VMEM, ANY, ANY],
+        out_specs=VMEM,
+        scratch_shapes=[pltpu.VMEM((16, 64, ncv * 128), F32)] * 2 + held(4),
         compiler_params=params(BIG),
     )(state, *tables_lo)
     wanted = destination[0]
@@ -554,15 +518,11 @@
     state = pl.pallas_call(
         functools.partial(levels_hi_kernel, nv),
         out_shape=shape((128, 8 * ncv, 128), F32),
-        in_specs=[SMEM] + [ANY] * 4,
-        out_specs=ANY,
+        in_specs=[SMEM, VMEM, ANY, ANY],
+        out_specs=VMEM,
         scratch_shapes=[pltpu.VMEM((8, 128, ncv * 128), F32)] * 2
         + held(3)
-        + [
-            pltpu.VMEM((128, 8 * ncv, 128), F32),
-            pltpu.SemaphoreType.DMA((4,)),
-            pltpu.VMEM((1024, ncv, 128), F32),
-        ],
+        + [pltpu.VMEM((1024, ncv, 128), F32)],
         compiler_params=params(BIG),
     )(where, state, *tables_hi)
     state = lax.all_to_all(state, AXES, 0, 0, tiled=True)

time: 147 us -> 145 us (0.986)
  waiting for transfers between devices: 8.63 us -> 19.6 us
  Pallas kernels: 48 us -> 37.4 us
  local copies, waits for them, and re-layouts: 3.65 us -> 2.08 us
    all_to_all x1, waiting for transfers between devices: 1.56 us -> 9.26 us  [shards(): state = lax.all_to_all(state, ('y', 'zh', 'c'), 0, 0, tiled=True)]
    ppermute x3, waiting for transfers between devices: 0.01 us -> 3.26 us  [shards(): lax.ppermute(s, 'x', [(i, i ^ m) for i in range(4)])]
    pallas_call x1, Pallas kernels: 3.35 us -> 0.35 us  [shards(): pl.pallas_call(core_kernel, out_shape=[shape((96, 1536), F32)] * 2, in_sp...]
    pallas_call x1, Pallas kernels: 7.43 us -> 4.97 us  [shards(): pl.pallas_call(table_hi_kernel, out_shape=table_shapes(3), in_specs=[HBM,...]
    pallas_call x1, Pallas kernels: 8.05 us -> 5.73 us  [shards(): pl.pallas_call(table_lo_kernel, out_shape=table_shapes(4), in_specs=[HBM,...]
    pallas_call x1, Pallas kernels: 1.89 us -> 0.19 us  [shards(): pl.pallas_call(pack_x_kernel, out_shape=[shape((96, w), F32) for w in (25...]
    unnamed x20 -> x16, local copies, waits for them, and re-layouts: 3.65 us -> 2.08 us
  transfers between devices with their start and end apart: 8 -> 8, of which waited for: 3 -> 5; matrix products, arithmetic and copies ran while one was open for 0% -> 0% of each run, Pallas kernels for 15% -> 8%
where the time goes in v6:
time: 145 us; the launch traced here: 144 us
  blocking collectives  68.2 us (47%)
  Pallas kernels  37.4 us (26%)
  waiting for transfers between devices  19.6 us (14%)
  starting transfers between devices  16.9 us (12%)
  local copies, waits for them, and re-layouts  2.08 us (1%)
    all_to_all x1, blocking collectives, shards(): state = lax.all_to_all(state, AXES, 0, 0, tiled=True)  38.6 us
    all_to_all x1, blocking collectives, shards(): state = lax.all_to_all(state, ('x', 'zl'), 0, 0, tiled=True)  29.6 us
    pallas_call x1, Pallas kernels, shards(): pl.pallas_call(functools.partial(levels_lo_kernel, nv), out_shape=shape((...  11.2 us
    pallas_call x1, Pallas kernels, shards(): pl.pallas_call(functools.partial(levels_hi_kernel, nv), out_shape=shape((...  10.8 us
    all_to_all x1, waiting for transfers between devices, shards(): state = lax.all_to_all(state, ('y', 'zh', 'c'), 0, 0, tiled=True)  9.26 us
    all_to_all x1, starting transfers between devices, shards(): state = lax.all_to_all(state, ('y', 'zh', 'c'), 0, 0, tiled=True)  8.34 us
    ppermute x3, waiting for transfers between devices, shards(): lax.ppermute(s, 'y', [(i, i ^ m) for i in range(4)])  7.05 us
    pallas_call x1, Pallas kernels, shards(): pl.pallas_call(table_lo_kernel, out_shape=table_shapes(4), in_specs=[HBM,...  5.73 us
  transfers between devices with their start and end apart: 8, of which 5 were waited for; matrix products, arithmetic and copies ran while one was open for 0% of the time, Pallas kernels for 8%

profile of v6, /device:TPU:1, one launch (start us, length us, event | category | flops | bytes accessed | tf_op | source)
XLA Modules:
  0.0 144.4 jit_solution(7729235049595036857)
XLA Ops:
  0.0 0.0 copy-start.3
  0.0 2.0 %shard_map.56 = (f32[96,256]{1,0:T(8,128)}, f32[96,768]{1,0:T(8,128)}, f32[96,256]{1,0:T(8,128)}) custom-call(f32[7,64,1024]{2,1,0:T(8,128)} %ain.9, f32[7,32,1024]{2,1,0:T(8,128)} %aout.9), custom_call_target="tpu_custom_call" | custom-call | tf_op jit(solution)/shard_map/pallas_call | solution.py:430
  2.0 3.8 %collective-permute-start.1 = (f32[96,768]{1,0:T(8,128)}, f32[96,768]{1,0:T(8,128)S(1)}, u32[]{:S(2)}, u32[]{:S(2)}) collective-permute-start(f32[96,768]{1,0:T(8,128)} %get-tuple-element.30), channel_id=1, source_target_pairs={{0,64},{32,96},{64,0},{96,32},{1,65},{33,97},{65,1},{97,33},{2,66}... | collective-permute-start | bytes 884744 | tf_op jit(solution)/shard_map/ppermute | solution.py:439
  5.9 0.4 collective-permute-start
  6.3 0.4 collective-permute-start.2
  6.6 0.0 copy-done.3
  6.7 0.6 shard_map.55
  7.3 0.0 copy-start.2
  7.3 1.3 copy-done.2
  8.6 0.0 copy-start
  8.6 0.0 copy-start.1
  8.6 6.4 %collective-permute-done.y1 = f32[96,256]{1,0:T(8,128)S(1)} collective-permute-done((f32[96,256]{1,0:T(8,128)}, f32[96,256]{1,0:T(8,128)S(1)}, u32[]{:S(2)}, u32[]{:S(2)}) %collective-permute-start) | collective-permute-done | bytes 98336 | tf_op jit(solution)/shard_map/ppermute | solution.py:439
  15.0 0.6 collective-permute-done.2.y3
  15.7 0.0 collective-permute-done.1.y2
  15.7 8.3 %all-to-all-start = ((f32[16,64,512]{2,1,0:T(8,128)}), f32[16,64,512]{2,1,0:T(8,128)}, u32[]{:S(2)}, u32[]{:S(2)}) async-start(f32[16,64,512]{2,1,0:T(8,128)} %copy-done.2), calls=%async_computation | async-start | bytes 4194304 | tf_op jit(solution)/shard_map/all_to_all | solution.py:451
  24.0 0.0 copy-done
  24.0 0.0 copy-done.1
  24.0 0.3 shard_map.57
  24.4 0.0 copy-start.7
  24.4 0.0 copy-start.4
  24.4 0.2 collective-permute-start.3
  24.6 0.2 shard_map.59
  24.8 2.8 %collective-permute-start.5 = (f32[96,768]{1,0:T(8,128)S(1)}, f32[96,768]{1,0:T(8,128)S(1)}, u32[]{:S(2)}, u32[]{:S(2)}) collective-permute-start(f32[96,768]{1,0:T(8,128)S(1)} %get-tuple-element.40), channel_id=1, source_target_pairs={{0,8},{4,12},{8,0},{12,4},{1,9},{5,13},{9,1},{13,5},{2,10},{6,14},... | collective-permute-start | bytes 884744 | tf_op jit(solution)/shard_map/ppermute | solution.py:462
  27.7 0.3 collective-permute-start.4
  28.0 0.6 collective-permute-start.6
  28.5 0.0 copy-done.7
  28.5 0.0 collective-permute-done.3.other
  28.6 0.0 copy-done.4
  28.6 5.7 %shard_map.58 = (f32[72,1024,128]{2,1,0:T(8,128)}, bf16[4,256,256]{2,1,0:T(8,128)(2,1)S(1)}) custom-call(f32[7,64,1024]{2,1,0:T(8,128)S(1)} %copy-done, f32[7,32,1024]{2,1,0:T(8,128)S(1)} %copy-done.1, f32[7,32,64]{2,1,0:T(8,128)S(1)} %copy-done.4, f32[96,1536]{1,0:T(8,128)S(1)} %get-tuple-element.36.kept, f32[96,1536]{1,0:T(8,128)S(1)} %collective-permute-done.3.other), custom_call_target="tpu_custom_call" | custom-call | tf_op jit(solution)/shard_map/pallas_call | solution.py:474
  34.3 2.7 %collective-permute-done.4.x1 = f32[96,256]{1,0:T(8,128)S(1)} collective-permute-done((f32[96,256]{1,0:T(8,128)S(1)}, f32[96,256]{1,0:T(8,128)S(1)}, u32[]{:S(2)}, u32[]{:S(2)}) %collective-permute-start.4) | collective-permute-done | bytes 98336 | tf_op jit(solution)/shard_map/ppermute | solution.py:462
  37.0 0.6 collective-permute-done.6.x3
  37.6 0.0 collective-permute-done.5.x2
  37.6 5.0 %shard_map.61 = (f32[72,1024,128]{2,1,0:T(8,128)}, bf16[3,256,256]{2,1,0:T(8,128)(2,1)S(1)}) custom-call(f32[7,64,1024]{2,1,0:T(8,128)S(1)} %copy-done, f32[7,32,1024]{2,1,0:T(8,128)S(1)} %copy-done.1, f32[7,32,64]{2,1,0:T(8,128)S(1)} %copy-done.4, f32[96,256]{1,0:T(8,128)S(1)} %collective-permute-done.4.x1, f32[96,768]{1,0:T(8,128)S(1)} %collective-permute-done.5.x2, ...), custom_call_target="tpu_custom_call" | custom-call | tf_op jit(solution)/shard_map/pallas_call | solution.py:490
  42.5 0.0 copy-start.5
  42.5 0.7 copy-done.5
  43.3 9.3 %all-to-all-done.x_ref = f32[16,64,512]{2,1,0:T(8,128)} async-done(((f32[16,64,512]{2,1,0:T(8,128)}), f32[16,64,512]{2,1,0:T(8,128)}, u32[]{:S(2)}, u32[]{:S(2)}) %all-to-all-start) | async-done | bytes 2097184 | tf_op jit(solution)/shard_map/all_to_all | solution.py:451
  52.6 11.2 %shard_map.60 = f32[8,128,512]{2,1,0:T(8,128)S(1)} custom-call(f32[16,64,512]{2,1,0:T(8,128)} %all-to-all-done.x_ref, f32[72,1024,128]{2,1,0:T(8,128)} %get-tuple-element.42.tab, bf16[4,256,256]{2,1,0:T(8,128)(2,1)S(1)} %get-tuple-element.43.w), custom_call_target="tpu_custom_call" | custom-call | tf_op jit(solution)/shard_map/pallas_call | solution.py:505
  63.7 0.0 copy-start.6
  63.7 29.6 %all_to_all.15.x_ref = f32[8,128,512]{2,1,0:T(8,128)S(1)} all-to-all(f32[8,128,512]{2,1,0:T(8,128)S(1)} %shard_map.60), channel_id=1, replica_groups=mesh['y'=4,'zh'=2,'x'=4,'zl'=2,'c'=2] {'x','zl'}, dimensions={0} | all-to-all | bytes 4194304 | tf_op jit(solution)/shard_map/all_to_all | solution.py:516
  93.3 0.0 copy-done.6
  93.3 10.8 %shard_map.62 = f32[128,32,128]{2,1,0:T(8,128)S(1)} custom-call(s32[1024]{0:T(1024)S(1)} %bitcast.6, f32[8,128,512]{2,1,0:T(8,128)S(1)} %all_to_all.15.x_ref, f32[72,1024,128]{2,1,0:T(8,128)} %get-tuple-element.51.tab, bf16[3,256,256]{2,1,0:T(8,128)(2,1)S(1)} %copy-done.6), custom_call_target="tpu_custom_call" | custom-call | tf_op jit(solution)/shard_map/pallas_call | solution.py:518
  104.1 38.6 %all_to_all.16 = f32[128,32,128]{2,1,0:T(8,128)S(1)} all-to-all(f32[128,32,128]{2,1,0:T(8,128)S(1)} %shard_map.62), channel_id=1, replica_groups=mesh['y'=4,'zh'=2,'x'=4,'zl'=2,'c'=2] {'y','zh','x','zl','c'}, dimensions={0} | all-to-all | bytes 4194304 | tf_op jit(solution)/shard_map/all_to_all | solution.py:528
  142.7 1.5 %shard_map.63 = f32[512,1024]{1,0:T(8,128)} custom-call(f32[4096,128]{1,0:T(8,128)S(1)} %bitcast.4), custom_call_target="tpu_custom_call" | custom-call | tf_op jit(solution)/shard_map/pallas_call | solution.py:530
  (1 shorter events, 0.0 us)
Async XLA Ops:
  0.0 6.7 %copy-start.3 = (f32[2,32,8,1024]{3,2,1,0:T(8,128)S(1)}, f32[2,32,8,1024]{3,2,1,0:T(8,128)}, u32[]{:S(2)}) copy-start(f32[2,32,8,1024]{3,2,1,0:T(8,128)} %param.5) | copy-start | bytes 6291460
  2.0 13.6 %collective-permute-start.1 = (f32[96,768]{1,0:T(8,128)}, f32[96,768]{1,0:T(8,128)S(1)}, u32[]{:S(2)}, u32[]{:S(2)}) collective-permute-start(f32[96,768]{1,0:T(8,128)} %get-tuple-element.30), channel_id=1, source_target_pairs={{0,64},{32,96},{64,0},{96,32},{1,65},{33,97},{65,1},{97,33},{2,66}... | collective-permute-start | bytes 884744 | tf_op jit(solution)/shard_map/ppermute | solution.py:439
  5.9 9.2 %collective-permute-start = (f32[96,256]{1,0:T(8,128)}, f32[96,256]{1,0:T(8,128)S(1)}, u32[]{:S(2)}, u32[]{:S(2)}) collective-permute-start(f32[96,256]{1,0:T(8,128)} %get-tuple-element.29), channel_id=1, source_target_pairs={{0,32},{32,0},{64,96},{96,64},{1,33},{33,1},{65,97},{97,65},{2,34}... | collective-permute-start | bytes 294920 | tf_op jit(solution)/shard_map/ppermute | solution.py:439
  6.3 9.4 %collective-permute-start.2 = (f32[96,256]{1,0:T(8,128)}, f32[96,256]{1,0:T(8,128)S(1)}, u32[]{:S(2)}, u32[]{:S(2)}) collective-permute-start(f32[96,256]{1,0:T(8,128)} %get-tuple-element.31), channel_id=1, source_target_pairs={{0,96},{32,64},{64,32},{96,0},{1,97},{33,65},{65,33},{97,1},{2,98}... | collective-permute-start | bytes 294920 | tf_op jit(solution)/shard_map/ppermute | solution.py:439
  7.3 1.3 copy-start.2
  8.6 15.4 %copy-start = (f32[7,64,1024]{2,1,0:T(8,128)S(1)}, f32[7,64,1024]{2,1,0:T(8,128)}, u32[]{:S(2)}) copy-start(f32[7,64,1024]{2,1,0:T(8,128)} %ain.9) | copy-start | bytes 5505028
  8.6 15.4 %copy-start.1 = (f32[7,32,1024]{2,1,0:T(8,128)S(1)}, f32[7,32,1024]{2,1,0:T(8,128)}, u32[]{:S(2)}) copy-start(f32[7,32,1024]{2,1,0:T(8,128)} %aout.9) | copy-start | bytes 2752516
  15.7 36.9 %all-to-all-start = ((f32[16,64,512]{2,1,0:T(8,128)}), f32[16,64,512]{2,1,0:T(8,128)}, u32[]{:S(2)}, u32[]{:S(2)}) async-start(f32[16,64,512]{2,1,0:T(8,128)} %copy-done.2), calls=%async_computation | async-start | bytes 4194304 | tf_op jit(solution)/shard_map/all_to_all | solution.py:451
  24.4 4.2 %copy-start.7 = (s32[1,1024]{1,0:T(1,128)S(1)}, s32[1,1024]{1,0:T(1,128)}, u32[]{:S(2)}) copy-start(s32[1,1024]{1,0:T(1,128)} %param.9) | copy-start | bytes 12292
  24.4 4.2 %copy-start.4 = (f32[7,32,64]{2,1,0:T(8,128)S(1)}, f32[7,32,64]{2,1,0:T(8,128)}, u32[]{:S(2)}) copy-start(f32[7,32,64]{2,1,0:T(8,128)} %interp.3) | copy-start | bytes 172036
  24.4 4.1 %collective-permute-start.3 = (f32[96,1536]{1,0:T(8,128)S(1)}, f32[96,1536]{1,0:T(8,128)S(1)}, u32[]{:S(2)}, u32[]{:S(2)}) collective-permute-start(f32[96,1536]{1,0:T(8,128)S(1)} %get-tuple-element.37), channel_id=1, source_target_pairs={{0,1},{1,0},{2,3},{3,2},{4,5},{5,4},{6,7},{7,6},{8,9},{9,8},{10,11... | collective-permute-start | bytes 1769480 | tf_op jit(solution)/shard_map/ppermute | solution.py:472
  24.8 12.7 %collective-permute-start.5 = (f32[96,768]{1,0:T(8,128)S(1)}, f32[96,768]{1,0:T(8,128)S(1)}, u32[]{:S(2)}, u32[]{:S(2)}) collective-permute-start(f32[96,768]{1,0:T(8,128)S(1)} %get-tuple-element.40), channel_id=1, source_target_pairs={{0,8},{4,12},{8,0},{12,4},{1,9},{5,13},{9,1},{13,5},{2,10},{6,14},... | collective-permute-start | bytes 884744 | tf_op jit(solution)/shard_map/ppermute | solution.py:462
  27.7 9.3 %collective-permute-start.4 = (f32[96,256]{1,0:T(8,128)S(1)}, f32[96,256]{1,0:T(8,128)S(1)}, u32[]{:S(2)}, u32[]{:S(2)}) collective-permute-start(f32[96,256]{1,0:T(8,128)S(1)} %get-tuple-element.39), channel_id=1, source_target_pairs={{0,4},{4,0},{8,12},{12,8},{1,5},{5,1},{9,13},{13,9},{2,6},{6,2},{1... | collective-permute-start | bytes 294920 | tf_op jit(solution)/shard_map/ppermute | solution.py:462
  28.0 9.6 %collective-permute-start.6 = (f32[96,256]{1,0:T(8,128)S(1)}, f32[96,256]{1,0:T(8,128)S(1)}, u32[]{:S(2)}, u32[]{:S(2)}) collective-permute-start(f32[96,256]{1,0:T(8,128)S(1)} %get-tuple-element.41), channel_id=1, source_target_pairs={{0,12},{4,8},{8,4},{12,0},{1,13},{5,9},{9,5},{13,1},{2,14},{6,10},... | collective-permute-start | bytes 294920 | tf_op jit(solution)/shard_map/ppermute | solution.py:462
  42.5 0.7 copy-start.5
  63.7 29.6 %copy-start.6 = (bf16[3,256,256]{2,1,0:T(8,128)(2,1)S(1)}, bf16[3,256,256]{2,1,0:T(8,128)(2,1)}, u32[]{:S(2)}) copy-start(bf16[3,256,256]{2,1,0:T(8,128)(2,1)} %copy-done.5) | copy-start | bytes 1179652

commit v7 on v6

--- a/solution.py
+++ b/solution.py
@@ -319,40 +319,19 @@
     return re + im
 
 
-def levels_kernel(nv, count, slabs, first, put, sources, held, sems, x_ref, bufs):
+def levels_kernel(nv, count, slabs, first, put, x_ref, bufs, tab_ref, w_ref, ready, arrived):
     rows = 1024 // slabs
     group = 128 // rows
-    bodies = slabs // 2 // group
     lanes = lambda q: slice(q * 128, q * 128 + 128)
-    one, two = bufs
-
-    tab_ref, w_ref = held
-
-    def copies(level):
-        got = [(0, level), (1, level)] if level < count else [(0, count)]
-        return [
-            pltpu.make_async_copy(
-                sources[i].at[k], held[i].at[k], sems.at[i, k]
-            )
-            for i, k in got
-        ]
-
-    for copy in copies(0):
-        copy.start()
     for level in range(count):
-        for copy in copies(level):
-            copy.wait()
-        for copy in copies(level + 1):
-            copy.start()
-        if level == count - 1:
-            for copy in copies(count):
-                copy.wait()
+        ready(level)
         last = level == count - 1
         src = bufs[(level + 1) % 2] if level else x_ref
         dst = bufs[level % 2]
         w = w_ref[level]
-        for i in range(bodies):
+        for i in range(slabs // 2 // group):
             if level == 0:
+                arrived(i)
                 lows, highs = first(i)
             else:
                 lows = [i * group + g for g in range(group)]
@@ -373,7 +352,7 @@
                             dst[m, :, lanes(q)] = part
 
 
-def levels_lo_kernel(nv, x_ref, tab, w, out_ref, one, two, tab_v, w_v, sems):
+def levels_lo_kernel(nv, x_ref, tab, w, out_ref, one, two, tab_v, w_v, sems, x_sems):
     def first(i):
         a = (i & 1) * 8 + (i >> 1) * 4
         return [a, a + 1], [a + 2, a + 3]
@@ -383,12 +362,37 @@
             rows = slice(slab * 8, slab * 8 + 8)
             out_ref[rev(kp, 3), rows, q * 128 : q * 128 + 128] = tile[kp * 8 : kp * 8 + 8]
 
+    def arrive(i):
+        at = first(i)[0][0]
+        part = slice(at, at + 4)
+        return pltpu.make_async_copy(x_ref.at[part], two.at[part], x_sems.at[i])
+
+    def copies(level):
+        got = [(tab, tab_v, 0, level)]
+        if level < 4:
+            got.append((w, w_v, 1, level))
+        return [
+            pltpu.make_async_copy(src.at[k], dst.at[k], sems.at[i, k]) for src, dst, i, k in got
+        ]
+
+    def ready(level):
+        for copy in copies(level) + (copies(4) if level == 3 else []):
+            copy.wait()
+
+    arrive(0).start()
+    for copy in copies(0):
+        copy.start()
+    for i in range(1, 4):
+        arrive(i).start()
+    for level in range(1, 5):
+        for copy in copies(level):
+            copy.start()
     levels_kernel(
-        nv, 4, 16, first, put, (tab, w), (tab_v, w_v), sems, x_ref, (one, two)
+        nv, 4, 16, first, put, two, (one, two), tab_v, w_v, ready, lambda i: arrive(i).wait()
     )
 
 
-def levels_hi_kernel(nv, where_ref, x_ref, tab, w, out_ref, one, two, tab_v, w_v, sems, done):
+def levels_hi_kernel(nv, where_ref, x_ref, tab, w, out_ref, one, two, done):
     ncv = 2 * nv
 
     def first(i):
@@ -398,9 +402,8 @@
     def put(slab, q, tile):
         done[slab * 128 : slab * 128 + 128, q, :] = tile
 
-    levels_kernel(
-        nv, 3, 8, first, put, (tab, w), (tab_v, w_v), sems, x_ref, (one, two)
-    )
+    nothing = lambda k: None
+    levels_kernel(nv, 3, 8, first, put, x_ref, (one, two), tab, w, nothing, nothing)
 
     def gather(e, _):
         for r in range(8):
@@ -410,17 +413,9 @@
     lax.fori_loop(0, 128, gather, 0, unroll=2)
 
 
-def held(count):
-    return [
-        pltpu.VMEM((count + 1, 1024, 128), F32),
-        pltpu.VMEM((count, 256, 256), BF16),
-        pltpu.SemaphoreType.DMA((2, count + 1)),
-    ]
-
-
-def table_shapes(count):
+def table_shapes(count, rows):
     shape = jax.ShapeDtypeStruct
-    return [shape((PAD, 1024, 128), F32), shape((count, 256, 256), BF16)]
+    return [shape((rows, 1024, 128), F32), shape((count, 256, 256), BF16)]
 
 
 def shards(coefficients, angle_in, angle_out, interp, destination):
@@ -435,6 +430,7 @@
         scratch_shapes=[pltpu.SemaphoreType.DMA((2, 4))],
         compiler_params=params(56),
     )(angle_in, angle_out)
+    coefficients, *sends = lax.optimization_barrier((coefficients, *sends))
     from_y = [
         lax.ppermute(s, "y", [(i, i ^ m) for i in range(4)]) for m, s in zip((1, 2, 3), sends)
     ]
@@ -447,7 +443,6 @@
         scratch_shapes=[pltpu.VMEM((8, 512, 128), F32)],
         compiler_params=params(6),
     )(coefficients.reshape(512, 1024))
-    state, *from_y = lax.optimization_barrier((state, *from_y))
     state = lax.all_to_all(state, ("y", "zh", "c"), 0, 0, tiled=True)
 
     sends = pl.pallas_call(
@@ -473,7 +468,7 @@
 
     tables_lo = pl.pallas_call(
         table_lo_kernel,
-        out_shape=table_shapes(4),
+        out_shape=table_shapes(4, PAD),
         in_specs=[HBM, HBM] + [VMEM] * 3,
         out_specs=[ANY, VMEM],
         scratch_shapes=[
@@ -489,7 +484,7 @@
     tables_lo = [first, *tables_lo[1:]]
     tables_hi = pl.pallas_call(
         table_hi_kernel,
-        out_shape=table_shapes(3),
+        out_shape=table_shapes(3, 4),
         in_specs=[HBM, HBM] + [VMEM] * 4,
         out_specs=[ANY, VMEM],
         scratch_shapes=[
@@ -505,9 +500,15 @@
     state = pl.pallas_call(
         functools.partial(levels_lo_kernel, nv),
         out_shape=shape((8, 128, ncv * 128), F32),
-        in_specs=[VMEM, ANY, ANY],
+        in_specs=[ANY, ANY, ANY],
         out_specs=VMEM,
-        scratch_shapes=[pltpu.VMEM((16, 64, ncv * 128), F32)] * 2 + held(4),
+        scratch_shapes=[pltpu.VMEM((16, 64, ncv * 128), F32)] * 2
+        + [
+            pltpu.VMEM((5, 1024, 128), F32),
+            pltpu.VMEM((4, 256, 256), BF16),
+            pltpu.SemaphoreType.DMA((2, 5)),
+            pltpu.SemaphoreType.DMA((4,)),
+        ],
         compiler_params=params(BIG),
     )(state, *tables_lo)
     wanted = destination[0]
@@ -518,10 +519,9 @@
     state = pl.pallas_call(
         functools.partial(levels_hi_kernel, nv),
         out_shape=shape((128, 8 * ncv, 128), F32),
-        in_specs=[SMEM, VMEM, ANY, ANY],
+        in_specs=[SMEM] + [VMEM] * 3,
         out_specs=VMEM,
         scratch_shapes=[pltpu.VMEM((8, 128, ncv * 128), F32)] * 2
-        + held(3)
         + [pltpu.VMEM((1024, ncv, 128), F32)],
         compiler_params=params(BIG),
     )(where, state, *tables_hi)

time: 145 us -> 156 us (1.076)
  waiting for transfers between devices: 19.6 us -> 34.2 us
  Pallas kernels: 37.4 us -> 31 us
  starting transfers between devices: 16.9 us -> 18.6 us
    ppermute x3, waiting for transfers between devices: 7.05 us -> 31 us  [shards(): lax.ppermute(s, 'y', [(i, i ^ m) for i in range(4)])]
    all_to_all x1, waiting for transfers between devices: 9.26 us -> 0.01 us  [shards(): state = lax.all_to_all(state, ('y', 'zh', 'c'), 0, 0, tiled=True)]
    pallas_call x1, Pallas kernels: 10.8 us -> 7.36 us  [shards(): pl.pallas_call(functools.partial(levels_hi_kernel, nv), out_shape=shape((...]
    pallas_call x1, Pallas kernels: 11.2 us -> 9.12 us  [shards(): pl.pallas_call(functools.partial(levels_lo_kernel, nv), out_shape=shape((...]
    unnamed x16 -> x26, local copies, waits for them, and re-layouts: 2.08 us -> 3.49 us
  transfers between devices with their start and end apart: 8 -> 8, of which waited for: 5 -> 4; matrix products, arithmetic and copies ran while one was open for 0% -> 0% of each run, Pallas kernels for 8% -> 7%
where the time goes in v7:
time: 156 us; the launch traced here: 155 us
  blocking collectives  67.6 us (43%)
  waiting for transfers between devices  34.2 us (22%)
  Pallas kernels  31 us (20%)
  starting transfers between devices  18.6 us (12%)
  local copies, waits for them, and re-layouts  3.49 us (2%)
    all_to_all x1, blocking collectives, shards(): state = lax.all_to_all(state, AXES, 0, 0, tiled=True)  37.3 us
    ppermute x3, waiting for transfers between devices, shards(): lax.ppermute(s, 'y', [(i, i ^ m) for i in range(4)])  31 us
    all_to_all x1, blocking collectives, shards(): state = lax.all_to_all(state, ('x', 'zl'), 0, 0, tiled=True)  30.3 us
    all_to_all x1, starting transfers between devices, shards(): state = lax.all_to_all(state, ('y', 'zh', 'c'), 0, 0, tiled=True)  9.57 us
    pallas_call x1, Pallas kernels, shards(): pl.pallas_call(functools.partial(levels_lo_kernel, nv), out_shape=shape((...  9.12 us
    pallas_call x1, Pallas kernels, shards(): pl.pallas_call(functools.partial(levels_hi_kernel, nv), out_shape=shape((...  7.36 us
    pallas_call x1, Pallas kernels, shards(): pl.pallas_call(table_lo_kernel, out_shape=table_shapes(4, PAD), in_specs=...  5.69 us
    pallas_call x1, Pallas kernels, shards(): pl.pallas_call(table_hi_kernel, out_shape=table_shapes(3, 4), in_specs=[H...  4.15 us
  transfers between devices with their start and end apart: 8, of which 4 were waited for; matrix products, arithmetic and copies ran while one was open for 0% of the time, Pallas kernels for 7%

profile of v7, /device:TPU:1, one launch (start us, length us, event | category | flops | bytes accessed | tf_op | source)
XLA Modules:
  0.0 155.3 jit_solution(16846746048396969108)
XLA Ops:
  0.0 0.0 copy-start.5
  0.0 2.0 %shard_map.55 = (f32[96,256]{1,0:T(8,128)}, f32[96,768]{1,0:T(8,128)}, f32[96,256]{1,0:T(8,128)}) custom-call(f32[7,64,1024]{2,1,0:T(8,128)} %ain.9, f32[7,32,1024]{2,1,0:T(8,128)} %aout.9), custom_call_target="tpu_custom_call" | custom-call | tf_op jit(solution)/shard_map/pallas_call | solution.py:425
  2.1 0.0 copy-done.5
  2.1 0.6 shard_map.56
  2.7 0.0 copy-start.2
  2.7 1.3 copy-done.2
  4.0 0.0 copy-start.1
  4.0 9.6 %all-to-all-start = ((f32[16,64,512]{2,1,0:T(8,128)}), f32[16,64,512]{2,1,0:T(8,128)}, u32[]{:S(2)}, u32[]{:S(2)}) async-start(f32[16,64,512]{2,1,0:T(8,128)} %copy-done.2), calls=%async_computation | async-start | bytes 4194304 | tf_op jit(solution)/shard_map/all_to_all | solution.py:446
  13.6 0.0 copy-done.10
  13.6 3.0 %collective-permute-start.1 = (f32[96,768]{1,0:T(8,128)S(1)}, f32[96,768]{1,0:T(8,128)S(1)}, u32[]{:S(2)}, u32[]{:S(2)}) collective-permute-start(f32[96,768]{1,0:T(8,128)S(1)} %copy-done.10), channel_id=1, source_target_pairs={{0,64},{32,96},{64,0},{96,32},{1,65},{33,97},{65,1},{97,33},{2,66}... | collective-permute-start | bytes 884744 | tf_op jit(solution)/shard_map/ppermute | solution.py:435
  16.6 0.0 copy-done.12
  16.6 0.3 collective-permute-start
  16.9 0.0 copy-done.11
  16.9 0.7 collective-permute-start.2
  17.6 29.4 %collective-permute-done.y1 = f32[96,256]{1,0:T(8,128)S(1)} collective-permute-done((f32[96,256]{1,0:T(8,128)S(1)}, f32[96,256]{1,0:T(8,128)S(1)}, u32[]{:S(2)}, u32[]{:S(2)}) %collective-permute-start) | collective-permute-done | bytes 98336 | tf_op jit(solution)/shard_map/ppermute | solution.py:435
  47.0 0.0 collective-permute-done.2.y3
  47.0 1.6 %collective-permute-done.1.y2 = f32[96,768]{1,0:T(8,128)S(1)} collective-permute-done((f32[96,768]{1,0:T(8,128)S(1)}, f32[96,768]{1,0:T(8,128)S(1)}, u32[]{:S(2)}, u32[]{:S(2)}) %collective-permute-start.1) | collective-permute-done | bytes 294944 | tf_op jit(solution)/shard_map/ppermute | solution.py:435
  48.6 0.0 copy-done
  48.6 0.0 copy-done.1
  48.6 0.3 shard_map.57
  48.9 0.0 copy-start.9
  48.9 0.0 copy-start.6
  48.9 1.4 collective-permute-start.3
  50.4 0.2 shard_map.59
  50.6 2.8 %collective-permute-start.5 = (f32[96,768]{1,0:T(8,128)S(1)}, f32[96,768]{1,0:T(8,128)S(1)}, u32[]{:S(2)}, u32[]{:S(2)}) collective-permute-start(f32[96,768]{1,0:T(8,128)S(1)} %get-tuple-element.40), channel_id=1, source_target_pairs={{0,8},{4,12},{8,0},{12,4},{1,9},{5,13},{9,1},{13,5},{2,10},{6,14},... | collective-permute-start | bytes 884744 | tf_op jit(solution)/shard_map/ppermute | solution.py:457
  53.4 0.3 collective-permute-start.4
  53.7 0.6 collective-permute-start.6
  54.3 0.0 copy-done.9
  54.3 0.0 collective-permute-done.3.other
  54.3 0.0 copy-done.6
  54.3 5.7 %shard_map.58 = (f32[72,1024,128]{2,1,0:T(8,128)}, bf16[4,256,256]{2,1,0:T(8,128)(2,1)S(1)}) custom-call(f32[7,64,1024]{2,1,0:T(8,128)S(1)} %copy-done, f32[7,32,1024]{2,1,0:T(8,128)S(1)} %copy-done.1, f32[7,32,64]{2,1,0:T(8,128)S(1)} %copy-done.6, f32[96,1536]{1,0:T(8,128)S(1)} %get-tuple-element.36.kept, f32[96,1536]{1,0:T(8,128)S(1)} %collective-permute-done.3.other), custom_call_target="tpu_custom_call" | custom-call | tf_op jit(solution)/shard_map/pallas_call | solution.py:469
  60.0 3.0 %collective-permute-done.4.x1 = f32[96,256]{1,0:T(8,128)S(1)} collective-permute-done((f32[96,256]{1,0:T(8,128)S(1)}, f32[96,256]{1,0:T(8,128)S(1)}, u32[]{:S(2)}, u32[]{:S(2)}) %collective-permute-start.4) | collective-permute-done | bytes 98336 | tf_op jit(solution)/shard_map/ppermute | solution.py:457
  63.0 0.2 collective-permute-done.6.x3
  63.2 0.0 collective-permute-done.5.x2
  63.2 4.2 %shard_map.61 = (f32[4,1024,128]{2,1,0:T(8,128)S(1)}, bf16[3,256,256]{2,1,0:T(8,128)(2,1)S(1)}) custom-call(f32[7,64,1024]{2,1,0:T(8,128)S(1)} %copy-done, f32[7,32,1024]{2,1,0:T(8,128)S(1)} %copy-done.1, f32[7,32,64]{2,1,0:T(8,128)S(1)} %copy-done.6, f32[96,256]{1,0:T(8,128)S(1)} %collective-permute-done.4.x1, f32[96,768]{1,0:T(8,128)S(1)} %collective-permute-done.5.x2, ...), custom_call_target="tpu_custom_call" | custom-call | tf_op jit(solution)/shard_map/pallas_call | solution.py:485
  67.4 0.0 copy-start.3
  67.4 1.4 copy-done.3
  68.7 0.8 copy-done.7
  69.5 0.0 all-to-all-done.x_ref
  69.5 9.1 %shard_map.60 = f32[8,128,512]{2,1,0:T(8,128)S(1)} custom-call(f32[16,64,512]{2,1,0:T(8,128)} %all-to-all-done.x_ref, f32[72,1024,128]{2,1,0:T(8,128)} %get-tuple-element.42.tab, bf16[4,256,256]{2,1,0:T(8,128)(2,1)S(1)} %get-tuple-element.43.w), custom_call_target="tpu_custom_call" | custom-call | tf_op jit(solution)/shard_map/pallas_call | solution.py:500
  78.6 0.0 copy-start.4
  78.6 0.0 copy-start.8
  78.6 30.3 %all_to_all.15.x_ref = f32[8,128,512]{2,1,0:T(8,128)S(1)} all-to-all(f32[8,128,512]{2,1,0:T(8,128)S(1)} %shard_map.60), channel_id=1, replica_groups=mesh['y'=4,'zh'=2,'x'=4,'zl'=2,'c'=2] {'x','zl'}, dimensions={0} | all-to-all | bytes 4194304 | tf_op jit(solution)/shard_map/all_to_all | solution.py:517
  109.0 0.0 copy-done.4
  109.0 0.0 copy-done.8
  109.0 7.4 %shard_map.62 = f32[128,32,128]{2,1,0:T(8,128)S(1)} custom-call(s32[1024]{0:T(1024)S(1)} %bitcast.6, f32[8,128,512]{2,1,0:T(8,128)S(1)} %all_to_all.15.x_ref, f32[4,1024,128]{2,1,0:T(8,128)S(1)} %copy-done.4, bf16[3,256,256]{2,1,0:T(8,128)(2,1)S(1)} %copy-done.8), custom_call_target="tpu_custom_call" | custom-call | tf_op jit(solution)/shard_map/pallas_call | solution.py:519
  116.4 37.3 %all_to_all.16 = f32[128,32,128]{2,1,0:T(8,128)S(1)} all-to-all(f32[128,32,128]{2,1,0:T(8,128)S(1)} %shard_map.62), channel_id=1, replica_groups=mesh['y'=4,'zh'=2,'x'=4,'zl'=2,'c'=2] {'y','zh','x','zl','c'}, dimensions={0} | all-to-all | bytes 4194304 | tf_op jit(solution)/shard_map/all_to_all | solution.py:528
  153.6 1.5 shard_map.63
  (6 shorter events, 0.0 us)
Async XLA Ops:
  0.0 2.1 %copy-start.5 = (f32[2,32,8,1024]{3,2,1,0:T(8,128)S(1)}, f32[2,32,8,1024]{3,2,1,0:T(8,128)}, u32[]{:S(2)}) copy-start(f32[2,32,8,1024]{3,2,1,0:T(8,128)} %param.5) | copy-start | bytes 6291460
  2.7 1.3 copy-start.2
  4.0 9.6 %copy-start.10 = (f32[96,768]{1,0:T(8,128)S(1)}, f32[96,768]{1,0:T(8,128)}, u32[]{:S(2)}) copy-start(f32[96,768]{1,0:T(8,128)} %get-tuple-element.34) | copy-start | bytes 884740
  4.0 12.6 %copy-start.12 = (f32[96,256]{1,0:T(8,128)S(1)}, f32[96,256]{1,0:T(8,128)}, u32[]{:S(2)}) copy-start(f32[96,256]{1,0:T(8,128)} %get-tuple-element.33) | copy-start | bytes 294916
  4.0 12.9 %copy-start.11 = (f32[96,256]{1,0:T(8,128)S(1)}, f32[96,256]{1,0:T(8,128)}, u32[]{:S(2)}) copy-start(f32[96,256]{1,0:T(8,128)} %get-tuple-element.35) | copy-start | bytes 294916
  4.0 44.6 %copy-start = (f32[7,64,1024]{2,1,0:T(8,128)S(1)}, f32[7,64,1024]{2,1,0:T(8,128)}, u32[]{:S(2)}) copy-start(f32[7,64,1024]{2,1,0:T(8,128)} %ain.9) | copy-start | bytes 5505028
  4.0 44.6 %copy-start.1 = (f32[7,32,1024]{2,1,0:T(8,128)S(1)}, f32[7,32,1024]{2,1,0:T(8,128)}, u32[]{:S(2)}) copy-start(f32[7,32,1024]{2,1,0:T(8,128)} %aout.9) | copy-start | bytes 2752516
  4.0 65.5 %all-to-all-start = ((f32[16,64,512]{2,1,0:T(8,128)}), f32[16,64,512]{2,1,0:T(8,128)}, u32[]{:S(2)}, u32[]{:S(2)}) async-start(f32[16,64,512]{2,1,0:T(8,128)} %copy-done.2), calls=%async_computation | async-start | bytes 4194304 | tf_op jit(solution)/shard_map/all_to_all | solution.py:446
  13.6 35.0 %collective-permute-start.1 = (f32[96,768]{1,0:T(8,128)S(1)}, f32[96,768]{1,0:T(8,128)S(1)}, u32[]{:S(2)}, u32[]{:S(2)}) collective-permute-start(f32[96,768]{1,0:T(8,128)S(1)} %copy-done.10), channel_id=1, source_target_pairs={{0,64},{32,96},{64,0},{96,32},{1,65},{33,97},{65,1},{97,33},{2,66}... | collective-permute-start | bytes 884744 | tf_op jit(solution)/shard_map/ppermute | solution.py:435
  16.6 30.4 %collective-permute-start = (f32[96,256]{1,0:T(8,128)S(1)}, f32[96,256]{1,0:T(8,128)S(1)}, u32[]{:S(2)}, u32[]{:S(2)}) collective-permute-start(f32[96,256]{1,0:T(8,128)S(1)} %copy-done.12), channel_id=1, source_target_pairs={{0,32},{32,0},{64,96},{96,64},{1,33},{33,1},{65,97},{97,65},{2,34}... | collective-permute-start | bytes 294920 | tf_op jit(solution)/shard_map/ppermute | solution.py:435
  16.9 30.1 %collective-permute-start.2 = (f32[96,256]{1,0:T(8,128)S(1)}, f32[96,256]{1,0:T(8,128)S(1)}, u32[]{:S(2)}, u32[]{:S(2)}) collective-permute-start(f32[96,256]{1,0:T(8,128)S(1)} %copy-done.11), channel_id=1, source_target_pairs={{0,96},{32,64},{64,32},{96,0},{1,97},{33,65},{65,33},{97,1},{2,98}... | collective-permute-start | bytes 294920 | tf_op jit(solution)/shard_map/ppermute | solution.py:435
  48.9 5.3 %copy-start.9 = (s32[1,1024]{1,0:T(1,128)S(1)}, s32[1,1024]{1,0:T(1,128)}, u32[]{:S(2)}) copy-start(s32[1,1024]{1,0:T(1,128)} %param.9) | copy-start | bytes 12292
  48.9 5.4 %copy-start.6 = (f32[7,32,64]{2,1,0:T(8,128)S(1)}, f32[7,32,64]{2,1,0:T(8,128)}, u32[]{:S(2)}) copy-start(f32[7,32,64]{2,1,0:T(8,128)} %interp.3) | copy-start | bytes 172036
  48.9 5.3 %collective-permute-start.3 = (f32[96,1536]{1,0:T(8,128)S(1)}, f32[96,1536]{1,0:T(8,128)S(1)}, u32[]{:S(2)}, u32[]{:S(2)}) collective-permute-start(f32[96,1536]{1,0:T(8,128)S(1)} %get-tuple-element.37), channel_id=1, source_target_pairs={{0,1},{1,0},{2,3},{3,2},{4,5},{5,4},{6,7},{7,6},{8,9},{9,8},{10,11... | collective-permute-start | bytes 1769480 | tf_op jit(solution)/shard_map/ppermute | solution.py:467
  50.6 12.6 %collective-permute-start.5 = (f32[96,768]{1,0:T(8,128)S(1)}, f32[96,768]{1,0:T(8,128)S(1)}, u32[]{:S(2)}, u32[]{:S(2)}) collective-permute-start(f32[96,768]{1,0:T(8,128)S(1)} %get-tuple-element.40), channel_id=1, source_target_pairs={{0,8},{4,12},{8,0},{12,4},{1,9},{5,13},{9,1},{13,5},{2,10},{6,14},... | collective-permute-start | bytes 884744 | tf_op jit(solution)/shard_map/ppermute | solution.py:457
  53.4 9.6 %collective-permute-start.4 = (f32[96,256]{1,0:T(8,128)S(1)}, f32[96,256]{1,0:T(8,128)S(1)}, u32[]{:S(2)}, u32[]{:S(2)}) collective-permute-start(f32[96,256]{1,0:T(8,128)S(1)} %get-tuple-element.39), channel_id=1, source_target_pairs={{0,4},{4,0},{8,12},{12,8},{1,5},{5,1},{9,13},{13,9},{2,6},{6,2},{1... | collective-permute-start | bytes 294920 | tf_op jit(solution)/shard_map/ppermute | solution.py:457
  53.7 9.5 %collective-permute-start.6 = (f32[96,256]{1,0:T(8,128)S(1)}, f32[96,256]{1,0:T(8,128)S(1)}, u32[]{:S(2)}, u32[]{:S(2)}) collective-permute-start(f32[96,256]{1,0:T(8,128)S(1)} %get-tuple-element.41), channel_id=1, source_target_pairs={{0,12},{4,8},{8,4},{12,0},{1,13},{5,9},{9,5},{13,1},{2,14},{6,10},... | collective-permute-start | bytes 294920 | tf_op jit(solution)/shard_map/ppermute | solution.py:457
  67.4 1.4 copy-start.3
  68.7 0.8 copy-start.7
  78.6 30.4 %copy-start.4 = (f32[4,1024,128]{2,1,0:T(8,128)S(1)}, f32[4,1024,128]{2,1,0:T(8,128)}, u32[]{:S(2)}) copy-start(f32[4,1024,128]{2,1,0:T(8,128)} %copy-done.3) | copy-start | bytes 6291460
  78.6 30.4 %copy-start.8 = (bf16[3,256,256]{2,1,0:T(8,128)(2,1)S(1)}, bf16[3,256,256]{2,1,0:T(8,128)(2,1)}, u32[]{:S(2)}) copy-start(bf16[3,256,256]{2,1,0:T(8,128)(2,1)} %copy-done.7) | copy-start | bytes 1179652

commit v8 on v7

--- a/solution.py
+++ b/solution.py
@@ -319,7 +319,7 @@
     return re + im
 
 
-def levels_kernel(nv, count, slabs, first, put, x_ref, bufs, tab_ref, w_ref, ready, arrived):
+def levels_kernel(nv, count, slabs, first, put, x_ref, bufs, tab_ref, w_ref, ready):
     rows = 1024 // slabs
     group = 128 // rows
     lanes = lambda q: slice(q * 128, q * 128 + 128)
@@ -331,7 +331,6 @@
         w = w_ref[level]
         for i in range(slabs // 2 // group):
             if level == 0:
-                arrived(i)
                 lows, highs = first(i)
             else:
                 lows = [i * group + g for g in range(group)]
@@ -352,7 +351,7 @@
                             dst[m, :, lanes(q)] = part
 
 
-def levels_lo_kernel(nv, x_ref, tab, w, out_ref, one, two, tab_v, w_v, sems, x_sems):
+def levels_lo_kernel(nv, x_ref, tab, w, out_ref, one, two, tab_v, w_v, sems):
     def first(i):
         a = (i & 1) * 8 + (i >> 1) * 4
         return [a, a + 1], [a + 2, a + 3]
@@ -362,33 +361,21 @@
             rows = slice(slab * 8, slab * 8 + 8)
             out_ref[rev(kp, 3), rows, q * 128 : q * 128 + 128] = tile[kp * 8 : kp * 8 + 8]
 
-    def arrive(i):
-        at = first(i)[0][0]
-        part = slice(at, at + 4)
-        return pltpu.make_async_copy(x_ref.at[part], two.at[part], x_sems.at[i])
-
-    def copies(level):
-        got = [(tab, tab_v, 0, level)]
-        if level < 4:
-            got.append((w, w_v, 1, level))
-        return [
-            pltpu.make_async_copy(src.at[k], dst.at[k], sems.at[i, k]) for src, dst, i, k in got
-        ]
+    begin = [
+        pltpu.make_async_copy(tab.at[0], tab_v.at[0], sems.at[0]),
+        pltpu.make_async_copy(w, w_v, sems.at[1]),
+        pltpu.make_async_copy(x_ref, two, sems.at[2]),
+    ]
+    rest = [pltpu.make_async_copy(tab.at[1:5], tab_v.at[1:5], sems.at[3])]
 
     def ready(level):
-        for copy in copies(level) + (copies(4) if level == 3 else []):
+        for copy in (begin, rest, [], [])[level]:
             copy.wait()
 
-    arrive(0).start()
-    for copy in copies(0):
+    for copy in begin + rest:
         copy.start()
-    for i in range(1, 4):
-        arrive(i).start()
-    for level in range(1, 5):
-        for copy in copies(level):
-            copy.start()
     levels_kernel(
-        nv, 4, 16, first, put, two, (one, two), tab_v, w_v, ready, lambda i: arrive(i).wait()
+        nv, 4, 16, first, put, two, (one, two), tab_v, w_v, ready
     )
 
 
@@ -402,8 +389,7 @@
     def put(slab, q, tile):
         done[slab * 128 : slab * 128 + 128, q, :] = tile
 
-    nothing = lambda k: None
-    levels_kernel(nv, 3, 8, first, put, x_ref, (one, two), tab, w, nothing, nothing)
+    levels_kernel(nv, 3, 8, first, put, x_ref, (one, two), tab, w, lambda level: None)
 
     def gather(e, _):
         for r in range(8):
@@ -430,7 +416,6 @@
         scratch_shapes=[pltpu.SemaphoreType.DMA((2, 4))],
         compiler_params=params(56),
     )(angle_in, angle_out)
-    coefficients, *sends = lax.optimization_barrier((coefficients, *sends))
     from_y = [
         lax.ppermute(s, "y", [(i, i ^ m) for i in range(4)]) for m, s in zip((1, 2, 3), sends)
     ]
@@ -443,6 +428,7 @@
         scratch_shapes=[pltpu.VMEM((8, 512, 128), F32)],
         compiler_params=params(6),
     )(coefficients.reshape(512, 1024))
+    state, *from_y = lax.optimization_barrier((state, *from_y))
     state = lax.all_to_all(state, ("y", "zh", "c"), 0, 0, tiled=True)
 
     sends = pl.pallas_call(
@@ -506,7 +492,6 @@
         + [
             pltpu.VMEM((5, 1024, 128), F32),
             pltpu.VMEM((4, 256, 256), BF16),
-            pltpu.SemaphoreType.DMA((2, 5)),
             pltpu.SemaphoreType.DMA((4,)),
         ],
         compiler_params=params(BIG),

time: 156 us -> 138 us (0.88)
  waiting for transfers between devices: 34.2 us -> 19.1 us
  starting transfers between devices: 18.6 us -> 16.9 us
    ppermute x3, waiting for transfers between devices: 31 us -> 7.05 us  [shards(): lax.ppermute(s, 'y', [(i, i ^ m) for i in range(4)])]
    all_to_all x1, waiting for transfers between devices: 0.01 us -> 8.7 us  [shards(): state = lax.all_to_all(state, ('y', 'zh', 'c'), 0, 0, tiled=True)]
    unnamed x26 -> x20, local copies, waits for them, and re-layouts: 3.49 us -> 3.46 us
  transfers between devices with their start and end apart: 8 -> 8, of which waited for: 4 -> 5; matrix products, arithmetic and copies ran while one was open for 0% -> 0% of each run, Pallas kernels for 7% -> 8%
where the time goes in v8:
time: 138 us; the launch traced here: 137 us
  blocking collectives  68.2 us (49%)
  Pallas kernels  29.6 us (21%)
  waiting for transfers between devices  19.1 us (14%)
  starting transfers between devices  16.9 us (12%)
  local copies, waits for them, and re-layouts  3.46 us (3%)
    all_to_all x1, blocking collectives, shards(): state = lax.all_to_all(state, AXES, 0, 0, tiled=True)  38.6 us
    all_to_all x1, blocking collectives, shards(): state = lax.all_to_all(state, ('x', 'zl'), 0, 0, tiled=True)  29.6 us
    all_to_all x1, waiting for transfers between devices, shards(): state = lax.all_to_all(state, ('y', 'zh', 'c'), 0, 0, tiled=True)  8.7 us
    all_to_all x1, starting transfers between devices, shards(): state = lax.all_to_all(state, ('y', 'zh', 'c'), 0, 0, tiled=True)  8.34 us
    pallas_call x1, Pallas kernels, shards(): pl.pallas_call(functools.partial(levels_lo_kernel, nv), out_shape=shape((...  7.66 us
    pallas_call x1, Pallas kernels, shards(): pl.pallas_call(functools.partial(levels_hi_kernel, nv), out_shape=shape((...  7.35 us
    ppermute x3, waiting for transfers between devices, shards(): lax.ppermute(s, 'y', [(i, i ^ m) for i in range(4)])  7.05 us
    pallas_call x1, Pallas kernels, shards(): pl.pallas_call(table_lo_kernel, out_shape=table_shapes(4, PAD), in_specs=...  5.69 us
  transfers between devices with their start and end apart: 8, of which 5 were waited for; matrix products, arithmetic and copies ran while one was open for 0% of the time, Pallas kernels for 8%

profile of v8, /device:TPU:1, one launch (start us, length us, event | category | flops | bytes accessed | tf_op | source)
XLA Modules:
  0.0 137.5 jit_solution(10042265690676727981)
XLA Ops:
  0.0 0.0 copy-start.5
  0.0 2.0 %shard_map.56 = (f32[96,256]{1,0:T(8,128)}, f32[96,768]{1,0:T(8,128)}, f32[96,256]{1,0:T(8,128)}) custom-call(f32[7,64,1024]{2,1,0:T(8,128)} %ain.9, f32[7,32,1024]{2,1,0:T(8,128)} %aout.9), custom_call_target="tpu_custom_call" | custom-call | tf_op jit(solution)/shard_map/pallas_call | solution.py:411
  2.0 3.8 %collective-permute-start.1 = (f32[96,768]{1,0:T(8,128)}, f32[96,768]{1,0:T(8,128)S(1)}, u32[]{:S(2)}, u32[]{:S(2)}) collective-permute-start(f32[96,768]{1,0:T(8,128)} %get-tuple-element.30), channel_id=1, source_target_pairs={{0,64},{32,96},{64,0},{96,32},{1,65},{33,97},{65,1},{97,33},{2,66}... | collective-permute-start | bytes 884744 | tf_op jit(solution)/shard_map/ppermute | solution.py:420
  5.9 0.4 collective-permute-start
  6.3 0.4 collective-permute-start.2
  6.7 0.0 copy-done.5
  6.7 0.6 shard_map.55
  7.3 0.0 copy-start.2
  7.3 1.3 copy-done.2
  8.6 0.0 copy-start
  8.6 0.0 copy-start.1
  8.6 6.4 %collective-permute-done.y1 = f32[96,256]{1,0:T(8,128)S(1)} collective-permute-done((f32[96,256]{1,0:T(8,128)}, f32[96,256]{1,0:T(8,128)S(1)}, u32[]{:S(2)}, u32[]{:S(2)}) %collective-permute-start) | collective-permute-done | bytes 98336 | tf_op jit(solution)/shard_map/ppermute | solution.py:420
  15.0 0.6 collective-permute-done.2.y3
  15.7 0.0 collective-permute-done.1.y2
  15.7 8.3 %all-to-all-start = ((f32[16,64,512]{2,1,0:T(8,128)}), f32[16,64,512]{2,1,0:T(8,128)}, u32[]{:S(2)}, u32[]{:S(2)}) async-start(f32[16,64,512]{2,1,0:T(8,128)} %copy-done.2), calls=%async_computation | async-start | bytes 4194304 | tf_op jit(solution)/shard_map/all_to_all | solution.py:432
  24.0 0.0 copy-done
  24.0 0.0 copy-done.1
  24.0 0.3 shard_map.57
  24.4 0.0 copy-start.9
  24.4 0.0 copy-start.6
  24.4 0.2 collective-permute-start.3
  24.6 0.2 shard_map.59
  24.8 2.8 %collective-permute-start.5 = (f32[96,768]{1,0:T(8,128)S(1)}, f32[96,768]{1,0:T(8,128)S(1)}, u32[]{:S(2)}, u32[]{:S(2)}) collective-permute-start(f32[96,768]{1,0:T(8,128)S(1)} %get-tuple-element.40), channel_id=1, source_target_pairs={{0,8},{4,12},{8,0},{12,4},{1,9},{5,13},{9,1},{13,5},{2,10},{6,14},... | collective-permute-start | bytes 884744 | tf_op jit(solution)/shard_map/ppermute | solution.py:443
  27.7 0.3 collective-permute-start.4
  28.0 0.6 collective-permute-start.6
  28.5 0.0 copy-done.9
  28.5 0.0 collective-permute-done.3.other
  28.6 0.0 copy-done.6
  28.6 5.7 %shard_map.58 = (f32[72,1024,128]{2,1,0:T(8,128)}, bf16[4,256,256]{2,1,0:T(8,128)(2,1)S(1)}) custom-call(f32[7,64,1024]{2,1,0:T(8,128)S(1)} %copy-done, f32[7,32,1024]{2,1,0:T(8,128)S(1)} %copy-done.1, f32[7,32,64]{2,1,0:T(8,128)S(1)} %copy-done.6, f32[96,1536]{1,0:T(8,128)S(1)} %get-tuple-element.36.kept, f32[96,1536]{1,0:T(8,128)S(1)} %collective-permute-done.3.other), custom_call_target="tpu_custom_call" | custom-call | tf_op jit(solution)/shard_map/pallas_call | solution.py:455
  34.3 2.7 %collective-permute-done.4.x1 = f32[96,256]{1,0:T(8,128)S(1)} collective-permute-done((f32[96,256]{1,0:T(8,128)S(1)}, f32[96,256]{1,0:T(8,128)S(1)}, u32[]{:S(2)}, u32[]{:S(2)}) %collective-permute-start.4) | collective-permute-done | bytes 98336 | tf_op jit(solution)/shard_map/ppermute | solution.py:443
  37.0 0.6 collective-permute-done.6.x3
  37.6 0.0 collective-permute-done.5.x2
  37.6 4.2 %shard_map.61 = (f32[4,1024,128]{2,1,0:T(8,128)S(1)}, bf16[3,256,256]{2,1,0:T(8,128)(2,1)S(1)}) custom-call(f32[7,64,1024]{2,1,0:T(8,128)S(1)} %copy-done, f32[7,32,1024]{2,1,0:T(8,128)S(1)} %copy-done.1, f32[7,32,64]{2,1,0:T(8,128)S(1)} %copy-done.6, f32[96,256]{1,0:T(8,128)S(1)} %collective-permute-done.4.x1, f32[96,768]{1,0:T(8,128)S(1)} %collective-permute-done.5.x2, ...), custom_call_target="tpu_custom_call" | custom-call | tf_op jit(solution)/shard_map/pallas_call | solution.py:471
  41.7 0.0 copy-start.3
  41.7 1.4 copy-done.3
  43.1 0.0 copy-start.7
  43.1 0.8 copy-done.7
  43.9 8.7 %all-to-all-done.x_ref = f32[16,64,512]{2,1,0:T(8,128)} async-done(((f32[16,64,512]{2,1,0:T(8,128)}), f32[16,64,512]{2,1,0:T(8,128)}, u32[]{:S(2)}, u32[]{:S(2)}) %all-to-all-start) | async-done | bytes 2097184 | tf_op jit(solution)/shard_map/all_to_all | solution.py:432
  52.6 7.7 %shard_map.60 = f32[8,128,512]{2,1,0:T(8,128)S(1)} custom-call(f32[16,64,512]{2,1,0:T(8,128)} %all-to-all-done.x_ref, f32[72,1024,128]{2,1,0:T(8,128)} %get-tuple-element.42.tab, bf16[4,256,256]{2,1,0:T(8,128)(2,1)S(1)} %get-tuple-element.43.w), custom_call_target="tpu_custom_call" | custom-call | tf_op jit(solution)/shard_map/pallas_call | solution.py:486
  60.2 0.0 copy-start.4
  60.2 0.0 copy-start.8
  60.2 29.6 %all_to_all.15.x_ref = f32[8,128,512]{2,1,0:T(8,128)S(1)} all-to-all(f32[8,128,512]{2,1,0:T(8,128)S(1)} %shard_map.60), channel_id=1, replica_groups=mesh['y'=4,'zh'=2,'x'=4,'zl'=2,'c'=2] {'x','zl'}, dimensions={0} | all-to-all | bytes 4194304 | tf_op jit(solution)/shard_map/all_to_all | solution.py:502
  89.8 0.0 copy-done.4
  89.9 0.0 copy-done.8
  89.9 7.4 %shard_map.62 = f32[128,32,128]{2,1,0:T(8,128)S(1)} custom-call(s32[1024]{0:T(1024)S(1)} %bitcast.6, f32[8,128,512]{2,1,0:T(8,128)S(1)} %all_to_all.15.x_ref, f32[4,1024,128]{2,1,0:T(8,128)S(1)} %copy-done.4, bf16[3,256,256]{2,1,0:T(8,128)(2,1)S(1)} %copy-done.8), custom_call_target="tpu_custom_call" | custom-call | tf_op jit(solution)/shard_map/pallas_call | solution.py:504
  97.2 38.6 %all_to_all.16 = f32[128,32,128]{2,1,0:T(8,128)S(1)} all-to-all(f32[128,32,128]{2,1,0:T(8,128)S(1)} %shard_map.62), channel_id=1, replica_groups=mesh['y'=4,'zh'=2,'x'=4,'zl'=2,'c'=2] {'y','zh','x','zl','c'}, dimensions={0} | all-to-all | bytes 4194304 | tf_op jit(solution)/shard_map/all_to_all | solution.py:513
  135.8 1.5 %shard_map.63 = f32[512,1024]{1,0:T(8,128)} custom-call(f32[4096,128]{1,0:T(8,128)S(1)} %bitcast.4), custom_call_target="tpu_custom_call" | custom-call | tf_op jit(solution)/shard_map/pallas_call | solution.py:515
  (1 shorter events, 0.0 us)
Async XLA Ops:
  0.0 6.7 %copy-start.5 = (f32[2,32,8,1024]{3,2,1,0:T(8,128)S(1)}, f32[2,32,8,1024]{3,2,1,0:T(8,128)}, u32[]{:S(2)}) copy-start(f32[2,32,8,1024]{3,2,1,0:T(8,128)} %param.5) | copy-start | bytes 6291460
  2.0 13.6 %collective-permute-start.1 = (f32[96,768]{1,0:T(8,128)}, f32[96,768]{1,0:T(8,128)S(1)}, u32[]{:S(2)}, u32[]{:S(2)}) collective-permute-start(f32[96,768]{1,0:T(8,128)} %get-tuple-element.30), channel_id=1, source_target_pairs={{0,64},{32,96},{64,0},{96,32},{1,65},{33,97},{65,1},{97,33},{2,66}... | collective-permute-start | bytes 884744 | tf_op jit(solution)/shard_map/ppermute | solution.py:420
  5.9 9.2 %collective-permute-start = (f32[96,256]{1,0:T(8,128)}, f32[96,256]{1,0:T(8,128)S(1)}, u32[]{:S(2)}, u32[]{:S(2)}) collective-permute-start(f32[96,256]{1,0:T(8,128)} %get-tuple-element.29), channel_id=1, source_target_pairs={{0,32},{32,0},{64,96},{96,64},{1,33},{33,1},{65,97},{97,65},{2,34}... | collective-permute-start | bytes 294920 | tf_op jit(solution)/shard_map/ppermute | solution.py:420
  6.3 9.4 %collective-permute-start.2 = (f32[96,256]{1,0:T(8,128)}, f32[96,256]{1,0:T(8,128)S(1)}, u32[]{:S(2)}, u32[]{:S(2)}) collective-permute-start(f32[96,256]{1,0:T(8,128)} %get-tuple-element.31), channel_id=1, source_target_pairs={{0,96},{32,64},{64,32},{96,0},{1,97},{33,65},{65,33},{97,1},{2,98}... | collective-permute-start | bytes 294920 | tf_op jit(solution)/shard_map/ppermute | solution.py:420
  7.3 1.3 copy-start.2
  8.6 15.4 %copy-start = (f32[7,64,1024]{2,1,0:T(8,128)S(1)}, f32[7,64,1024]{2,1,0:T(8,128)}, u32[]{:S(2)}) copy-start(f32[7,64,1024]{2,1,0:T(8,128)} %ain.9) | copy-start | bytes 5505028
  8.6 15.4 %copy-start.1 = (f32[7,32,1024]{2,1,0:T(8,128)S(1)}, f32[7,32,1024]{2,1,0:T(8,128)}, u32[]{:S(2)}) copy-start(f32[7,32,1024]{2,1,0:T(8,128)} %aout.9) | copy-start | bytes 2752516
  15.7 36.9 %all-to-all-start = ((f32[16,64,512]{2,1,0:T(8,128)}), f32[16,64,512]{2,1,0:T(8,128)}, u32[]{:S(2)}, u32[]{:S(2)}) async-start(f32[16,64,512]{2,1,0:T(8,128)} %copy-done.2), calls=%async_computation | async-start | bytes 4194304 | tf_op jit(solution)/shard_map/all_to_all | solution.py:432
  24.4 4.2 %copy-start.9 = (s32[1,1024]{1,0:T(1,128)S(1)}, s32[1,1024]{1,0:T(1,128)}, u32[]{:S(2)}) copy-start(s32[1,1024]{1,0:T(1,128)} %param.9) | copy-start | bytes 12292
  24.4 4.2 %copy-start.6 = (f32[7,32,64]{2,1,0:T(8,128)S(1)}, f32[7,32,64]{2,1,0:T(8,128)}, u32[]{:S(2)}) copy-start(f32[7,32,64]{2,1,0:T(8,128)} %interp.3) | copy-start | bytes 172036
  24.4 4.1 %collective-permute-start.3 = (f32[96,1536]{1,0:T(8,128)S(1)}, f32[96,1536]{1,0:T(8,128)S(1)}, u32[]{:S(2)}, u32[]{:S(2)}) collective-permute-start(f32[96,1536]{1,0:T(8,128)S(1)} %get-tuple-element.37), channel_id=1, source_target_pairs={{0,1},{1,0},{2,3},{3,2},{4,5},{5,4},{6,7},{7,6},{8,9},{9,8},{10,11... | collective-permute-start | bytes 1769480 | tf_op jit(solution)/shard_map/ppermute | solution.py:453
  24.8 12.7 %collective-permute-start.5 = (f32[96,768]{1,0:T(8,128)S(1)}, f32[96,768]{1,0:T(8,128)S(1)}, u32[]{:S(2)}, u32[]{:S(2)}) collective-permute-start(f32[96,768]{1,0:T(8,128)S(1)} %get-tuple-element.40), channel_id=1, source_target_pairs={{0,8},{4,12},{8,0},{12,4},{1,9},{5,13},{9,1},{13,5},{2,10},{6,14},... | collective-permute-start | bytes 884744 | tf_op jit(solution)/shard_map/ppermute | solution.py:443
  27.7 9.3 %collective-permute-start.4 = (f32[96,256]{1,0:T(8,128)S(1)}, f32[96,256]{1,0:T(8,128)S(1)}, u32[]{:S(2)}, u32[]{:S(2)}) collective-permute-start(f32[96,256]{1,0:T(8,128)S(1)} %get-tuple-element.39), channel_id=1, source_target_pairs={{0,4},{4,0},{8,12},{12,8},{1,5},{5,1},{9,13},{13,9},{2,6},{6,2},{1... | collective-permute-start | bytes 294920 | tf_op jit(solution)/shard_map/ppermute | solution.py:443
  28.0 9.6 %collective-permute-start.6 = (f32[96,256]{1,0:T(8,128)S(1)}, f32[96,256]{1,0:T(8,128)S(1)}, u32[]{:S(2)}, u32[]{:S(2)}) collective-permute-start(f32[96,256]{1,0:T(8,128)S(1)} %get-tuple-element.41), channel_id=1, source_target_pairs={{0,12},{4,8},{8,4},{12,0},{1,13},{5,9},{9,5},{13,1},{2,14},{6,10},... | collective-permute-start | bytes 294920 | tf_op jit(solution)/shard_map/ppermute | solution.py:443
  41.7 1.4 copy-start.3
  43.1 0.8 copy-start.7
  60.2 29.6 %copy-start.4 = (f32[4,1024,128]{2,1,0:T(8,128)S(1)}, f32[4,1024,128]{2,1,0:T(8,128)}, u32[]{:S(2)}) copy-start(f32[4,1024,128]{2,1,0:T(8,128)} %copy-done.3) | copy-start | bytes 6291460
  60.2 29.6 %copy-start.8 = (bf16[3,256,256]{2,1,0:T(8,128)(2,1)S(1)}, bf16[3,256,256]{2,1,0:T(8,128)(2,1)}, u32[]{:S(2)}) copy-start(bf16[3,256,256]{2,1,0:T(8,128)(2,1)} %copy-done.7) | copy-start | bytes 1179652

commit v9 on v8

--- a/solution.py
+++ b/solution.py
@@ -414,7 +414,7 @@
         in_specs=[HBM, HBM],
         out_specs=[VMEM] * 3,
         scratch_shapes=[pltpu.SemaphoreType.DMA((2, 4))],
-        compiler_params=params(56),
+        compiler_params=params(60),
     )(angle_in, angle_out)
     from_y = [
         lax.ppermute(s, "y", [(i, i ^ m) for i in range(4)]) for m, s in zip((1, 2, 3), sends)
@@ -428,7 +428,7 @@
         scratch_shapes=[pltpu.VMEM((8, 512, 128), F32)],
         compiler_params=params(6),
     )(coefficients.reshape(512, 1024))
-    state, *from_y = lax.optimization_barrier((state, *from_y))
+    state, from_y[0] = lax.optimization_barrier((state, from_y[0]))
     state = lax.all_to_all(state, ("y", "zh", "c"), 0, 0, tiled=True)
 
     sends = pl.pallas_call(

time: 138 us -> 156 us (1.13)
  waiting for transfers between devices: 19.1 us -> 34.5 us
  starting transfers between devices: 16.9 us -> 20.5 us
    ppermute x3, waiting for transfers between devices: 7.05 us -> 31.4 us  [shards(): lax.ppermute(s, 'y', [(i, i ^ m) for i in range(4)])]
    all_to_all x1, waiting for transfers between devices: 8.7 us -> 0.01 us  [shards(): state = lax.all_to_all(state, ('y', 'zh', 'c'), 0, 0, tiled=True)]
    unnamed x20 -> x24, local copies, waits for them, and re-layouts: 3.46 us -> 3.47 us
  transfers between devices with their start and end apart: 8 -> 8, of which waited for: 5 -> 5; matrix products, arithmetic and copies ran while one was open for 0% -> 0% of each run, Pallas kernels for 8% -> 7%
where the time goes in v9:
time: 156 us
  blocking collectives  67.4 us (43%)
  waiting for transfers between devices  34.5 us (22%)
  Pallas kernels  29.6 us (19%)
  starting transfers between devices  20.5 us (13%)
  local copies, waits for them, and re-layouts  3.47 us (2%)
    all_to_all x1, blocking collectives, shards(): state = lax.all_to_all(state, AXES, 0, 0, tiled=True)  37.1 us
    ppermute x3, waiting for transfers between devices, shards(): lax.ppermute(s, 'y', [(i, i ^ m) for i in range(4)])  31.4 us
    all_to_all x1, blocking collectives, shards(): state = lax.all_to_all(state, ('x', 'zl'), 0, 0, tiled=True)  30.3 us
    all_to_all x1, starting transfers between devices, shards(): state = lax.all_to_all(state, ('y', 'zh', 'c'), 0, 0, tiled=True)  9.78 us
    pallas_call x1, Pallas kernels, shards(): pl.pallas_call(functools.partial(levels_lo_kernel, nv), out_shape=shape((...  7.68 us
    pallas_call x1, Pallas kernels, shards(): pl.pallas_call(functools.partial(levels_hi_kernel, nv), out_shape=shape((...  7.37 us
    ppermute x3, starting transfers between devices, shards(): lax.ppermute(s, 'y', [(i, i ^ m) for i in range(4)])  6.06 us
    pallas_call x1, Pallas kernels, shards(): pl.pallas_call(table_lo_kernel, out_shape=table_shapes(4, PAD), in_specs=...  5.7 us
  transfers between devices with their start and end apart: 8, of which 5 were waited for; matrix products, arithmetic and copies ran while one was open for 0% of the time, Pallas kernels for 7%

profile of v9, /device:TPU:1, one launch (start us, length us, event | category | flops | bytes accessed | tf_op | source)
XLA Modules:
  0.0 155.9 jit_solution(4858069317374766684)
XLA Ops:
  0.0 0.0 copy-start.5
  0.0 2.0 %shard_map.56 = (f32[96,256]{1,0:T(8,128)}, f32[96,768]{1,0:T(8,128)}, f32[96,256]{1,0:T(8,128)}) custom-call(f32[7,64,1024]{2,1,0:T(8,128)} %ain.9, f32[7,32,1024]{2,1,0:T(8,128)} %aout.9), custom_call_target="tpu_custom_call" | custom-call | tf_op jit(solution)/shard_map/pallas_call | solution.py:411
  2.1 2.2 %collective-permute-start = (f32[96,256]{1,0:T(8,128)}, f32[96,256]{1,0:T(8,128)S(1)}, u32[]{:S(2)}, u32[]{:S(2)}) collective-permute-start(f32[96,256]{1,0:T(8,128)} %get-tuple-element.27), channel_id=1, source_target_pairs={{0,32},{32,0},{64,96},{96,64},{1,33},{33,1},{65,97},{97,65},{2,34}... | collective-permute-start | bytes 294920 | tf_op jit(solution)/shard_map/ppermute | solution.py:420
  4.3 0.0 copy-done.5
  4.3 0.6 shard_map.55
  4.9 0.0 copy-start.2
  4.9 1.3 copy-done.2
  6.2 0.0 copy-start.11
  6.2 0.0 copy-start
  6.2 0.3 collective-permute-done.y1
  6.5 9.8 %all-to-all-start = ((f32[16,64,512]{2,1,0:T(8,128)}), f32[16,64,512]{2,1,0:T(8,128)}, u32[]{:S(2)}, u32[]{:S(2)}) async-start(f32[16,64,512]{2,1,0:T(8,128)} %copy-done.2), calls=%async_computation | async-start | bytes 4194304 | tf_op jit(solution)/shard_map/all_to_all | solution.py:432
  16.3 0.0 copy-done.10
  16.3 3.0 %collective-permute-start.1 = (f32[96,768]{1,0:T(8,128)S(1)}, f32[96,768]{1,0:T(8,128)S(1)}, u32[]{:S(2)}, u32[]{:S(2)}) collective-permute-start(f32[96,768]{1,0:T(8,128)S(1)} %copy-done.10), channel_id=1, source_target_pairs={{0,64},{32,96},{64,0},{96,32},{1,65},{33,97},{65,1},{97,33},{2,66}... | collective-permute-start | bytes 884744 | tf_op jit(solution)/shard_map/ppermute | solution.py:420
  19.2 0.0 copy-done.11
  19.2 0.9 collective-permute-start.2
  20.1 28.4 %collective-permute-done.2.y3 = f32[96,256]{1,0:T(8,128)S(1)} collective-permute-done((f32[96,256]{1,0:T(8,128)S(1)}, f32[96,256]{1,0:T(8,128)S(1)}, u32[]{:S(2)}, u32[]{:S(2)}) %collective-permute-start.2) | collective-permute-done | bytes 98336 | tf_op jit(solution)/shard_map/ppermute | solution.py:420
  48.5 2.7 %collective-permute-done.1.y2 = f32[96,768]{1,0:T(8,128)S(1)} collective-permute-done((f32[96,768]{1,0:T(8,128)S(1)}, f32[96,768]{1,0:T(8,128)S(1)}, u32[]{:S(2)}, u32[]{:S(2)}) %collective-permute-start.1) | collective-permute-done | bytes 294944 | tf_op jit(solution)/shard_map/ppermute | solution.py:420
  51.2 0.0 copy-done
  51.2 0.0 copy-done.1
  51.2 0.3 shard_map.57
  51.6 0.0 copy-start.9
  51.6 0.0 copy-start.6
  51.6 1.0 collective-permute-start.3
  52.5 0.2 shard_map.59
  52.7 2.8 %collective-permute-start.5 = (f32[96,768]{1,0:T(8,128)S(1)}, f32[96,768]{1,0:T(8,128)S(1)}, u32[]{:S(2)}, u32[]{:S(2)}) collective-permute-start(f32[96,768]{1,0:T(8,128)S(1)} %get-tuple-element.36), channel_id=1, source_target_pairs={{0,8},{4,12},{8,0},{12,4},{1,9},{5,13},{9,1},{13,5},{2,10},{6,14},... | collective-permute-start | bytes 884744 | tf_op jit(solution)/shard_map/ppermute | solution.py:443
  55.6 0.3 collective-permute-start.4
  55.9 0.6 collective-permute-start.6
  56.4 0.0 copy-done.9
  56.4 0.0 collective-permute-done.3.other
  56.5 0.0 copy-done.6
  56.5 5.7 %shard_map.58 = (f32[72,1024,128]{2,1,0:T(8,128)}, bf16[4,256,256]{2,1,0:T(8,128)(2,1)S(1)}) custom-call(f32[7,64,1024]{2,1,0:T(8,128)S(1)} %copy-done, f32[7,32,1024]{2,1,0:T(8,128)S(1)} %copy-done.1, f32[7,32,64]{2,1,0:T(8,128)S(1)} %copy-done.6, f32[96,1536]{1,0:T(8,128)S(1)} %get-tuple-element.32.kept, f32[96,1536]{1,0:T(8,128)S(1)} %collective-permute-done.3.other), custom_call_target="tpu_custom_call" | custom-call | tf_op jit(solution)/shard_map/pallas_call | solution.py:455
  62.2 3.0 %collective-permute-done.4.x1 = f32[96,256]{1,0:T(8,128)S(1)} collective-permute-done((f32[96,256]{1,0:T(8,128)S(1)}, f32[96,256]{1,0:T(8,128)S(1)}, u32[]{:S(2)}, u32[]{:S(2)}) %collective-permute-start.4) | collective-permute-done | bytes 98336 | tf_op jit(solution)/shard_map/ppermute | solution.py:443
  65.2 0.2 collective-permute-done.6.x3
  65.4 0.0 collective-permute-done.5.x2
  65.4 4.2 %shard_map.61 = (f32[4,1024,128]{2,1,0:T(8,128)S(1)}, bf16[3,256,256]{2,1,0:T(8,128)(2,1)S(1)}) custom-call(f32[7,64,1024]{2,1,0:T(8,128)S(1)} %copy-done, f32[7,32,1024]{2,1,0:T(8,128)S(1)} %copy-done.1, f32[7,32,64]{2,1,0:T(8,128)S(1)} %copy-done.6, f32[96,256]{1,0:T(8,128)S(1)} %collective-permute-done.4.x1, f32[96,768]{1,0:T(8,128)S(1)} %collective-permute-done.5.x2, ...), custom_call_target="tpu_custom_call" | custom-call | tf_op jit(solution)/shard_map/pallas_call | solution.py:471
  69.5 0.0 copy-start.3
  69.5 1.4 copy-done.3
  70.9 0.8 copy-done.7
  71.6 0.0 all-to-all-done.x_ref
  71.7 7.7 %shard_map.60 = f32[8,128,512]{2,1,0:T(8,128)S(1)} custom-call(f32[16,64,512]{2,1,0:T(8,128)} %all-to-all-done.x_ref, f32[72,1024,128]{2,1,0:T(8,128)} %get-tuple-element.38.tab, bf16[4,256,256]{2,1,0:T(8,128)(2,1)S(1)} %get-tuple-element.39.w), custom_call_target="tpu_custom_call" | custom-call | tf_op jit(solution)/shard_map/pallas_call | solution.py:486
  79.3 0.0 copy-start.4
  79.3 0.0 copy-start.8
  79.4 30.3 %all_to_all.15.x_ref = f32[8,128,512]{2,1,0:T(8,128)S(1)} all-to-all(f32[8,128,512]{2,1,0:T(8,128)S(1)} %shard_map.60), channel_id=1, replica_groups=mesh['y'=4,'zh'=2,'x'=4,'zl'=2,'c'=2] {'x','zl'}, dimensions={0} | all-to-all | bytes 4194304 | tf_op jit(solution)/shard_map/all_to_all | solution.py:502
  109.7 0.0 copy-done.4
  109.7 0.0 copy-done.8
  109.7 7.4 %shard_map.62 = f32[128,32,128]{2,1,0:T(8,128)S(1)} custom-call(s32[1024]{0:T(1024)S(1)} %bitcast.6, f32[8,128,512]{2,1,0:T(8,128)S(1)} %all_to_all.15.x_ref, f32[4,1024,128]{2,1,0:T(8,128)S(1)} %copy-done.4, bf16[3,256,256]{2,1,0:T(8,128)(2,1)S(1)} %copy-done.8), custom_call_target="tpu_custom_call" | custom-call | tf_op jit(solution)/shard_map/pallas_call | solution.py:504
  117.0 37.1 %all_to_all.16 = f32[128,32,128]{2,1,0:T(8,128)S(1)} all-to-all(f32[128,32,128]{2,1,0:T(8,128)S(1)} %shard_map.62), channel_id=1, replica_groups=mesh['y'=4,'zh'=2,'x'=4,'zl'=2,'c'=2] {'y','zh','x','zl','c'}, dimensions={0} | all-to-all | bytes 4194304 | tf_op jit(solution)/shard_map/all_to_all | solution.py:513
  154.2 1.5 shard_map.63
  (4 shorter events, 0.0 us)
Async XLA Ops:
  0.0 4.3 %copy-start.5 = (f32[2,32,8,1024]{3,2,1,0:T(8,128)S(1)}, f32[2,32,8,1024]{3,2,1,0:T(8,128)}, u32[]{:S(2)}) copy-start(f32[2,32,8,1024]{3,2,1,0:T(8,128)} %param.5) | copy-start | bytes 6291460
  2.1 4.4 %collective-permute-start = (f32[96,256]{1,0:T(8,128)}, f32[96,256]{1,0:T(8,128)S(1)}, u32[]{:S(2)}, u32[]{:S(2)}) collective-permute-start(f32[96,256]{1,0:T(8,128)} %get-tuple-element.27), channel_id=1, source_target_pairs={{0,32},{32,0},{64,96},{96,64},{1,33},{33,1},{65,97},{97,65},{2,34}... | collective-permute-start | bytes 294920 | tf_op jit(solution)/shard_map/ppermute | solution.py:420
  4.9 1.3 copy-start.2
  6.2 10.1 %copy-start.10 = (f32[96,768]{1,0:T(8,128)S(1)}, f32[96,768]{1,0:T(8,128)}, u32[]{:S(2)}) copy-start(f32[96,768]{1,0:T(8,128)} %get-tuple-element.30) | copy-start | bytes 884740
  6.2 13.0 %copy-start.11 = (f32[96,256]{1,0:T(8,128)S(1)}, f32[96,256]{1,0:T(8,128)}, u32[]{:S(2)}) copy-start(f32[96,256]{1,0:T(8,128)} %get-tuple-element.31) | copy-start | bytes 294916
  6.2 45.0 %copy-start = (f32[7,64,1024]{2,1,0:T(8,128)S(1)}, f32[7,64,1024]{2,1,0:T(8,128)}, u32[]{:S(2)}) copy-start(f32[7,64,1024]{2,1,0:T(8,128)} %ain.9) | copy-start | bytes 5505028
  6.2 45.0 %copy-start.1 = (f32[7,32,1024]{2,1,0:T(8,128)S(1)}, f32[7,32,1024]{2,1,0:T(8,128)}, u32[]{:S(2)}) copy-start(f32[7,32,1024]{2,1,0:T(8,128)} %aout.9) | copy-start | bytes 2752516
  6.5 65.2 %all-to-all-start = ((f32[16,64,512]{2,1,0:T(8,128)}), f32[16,64,512]{2,1,0:T(8,128)}, u32[]{:S(2)}, u32[]{:S(2)}) async-start(f32[16,64,512]{2,1,0:T(8,128)} %copy-done.2), calls=%async_computation | async-start | bytes 4194304 | tf_op jit(solution)/shard_map/all_to_all | solution.py:432
  16.3 35.0 %collective-permute-start.1 = (f32[96,768]{1,0:T(8,128)S(1)}, f32[96,768]{1,0:T(8,128)S(1)}, u32[]{:S(2)}, u32[]{:S(2)}) collective-permute-start(f32[96,768]{1,0:T(8,128)S(1)} %copy-done.10), channel_id=1, source_target_pairs={{0,64},{32,96},{64,0},{96,32},{1,65},{33,97},{65,1},{97,33},{2,66}... | collective-permute-start | bytes 884744 | tf_op jit(solution)/shard_map/ppermute | solution.py:420
  19.2 29.2 %collective-permute-start.2 = (f32[96,256]{1,0:T(8,128)S(1)}, f32[96,256]{1,0:T(8,128)S(1)}, u32[]{:S(2)}, u32[]{:S(2)}) collective-permute-start(f32[96,256]{1,0:T(8,128)S(1)} %copy-done.11), channel_id=1, source_target_pairs={{0,96},{32,64},{64,32},{96,0},{1,97},{33,65},{65,33},{97,1},{2,98}... | collective-permute-start | bytes 294920 | tf_op jit(solution)/shard_map/ppermute | solution.py:420
  51.6 4.9 %copy-start.9 = (s32[1,1024]{1,0:T(1,128)S(1)}, s32[1,1024]{1,0:T(1,128)}, u32[]{:S(2)}) copy-start(s32[1,1024]{1,0:T(1,128)} %param.9) | copy-start | bytes 12292
  51.6 4.9 %copy-start.6 = (f32[7,32,64]{2,1,0:T(8,128)S(1)}, f32[7,32,64]{2,1,0:T(8,128)}, u32[]{:S(2)}) copy-start(f32[7,32,64]{2,1,0:T(8,128)} %interp.3) | copy-start | bytes 172036
  51.6 4.9 %collective-permute-start.3 = (f32[96,1536]{1,0:T(8,128)S(1)}, f32[96,1536]{1,0:T(8,128)S(1)}, u32[]{:S(2)}, u32[]{:S(2)}) collective-permute-start(f32[96,1536]{1,0:T(8,128)S(1)} %get-tuple-element.33), channel_id=1, source_target_pairs={{0,1},{1,0},{2,3},{3,2},{4,5},{5,4},{6,7},{7,6},{8,9},{9,8},{10,11... | collective-permute-start | bytes 1769480 | tf_op jit(solution)/shard_map/ppermute | solution.py:453
  52.7 12.6 %collective-permute-start.5 = (f32[96,768]{1,0:T(8,128)S(1)}, f32[96,768]{1,0:T(8,128)S(1)}, u32[]{:S(2)}, u32[]{:S(2)}) collective-permute-start(f32[96,768]{1,0:T(8,128)S(1)} %get-tuple-element.36), channel_id=1, source_target_pairs={{0,8},{4,12},{8,0},{12,4},{1,9},{5,13},{9,1},{13,5},{2,10},{6,14},... | collective-permute-start | bytes 884744 | tf_op jit(solution)/shard_map/ppermute | solution.py:443
  55.6 9.6 %collective-permute-start.4 = (f32[96,256]{1,0:T(8,128)S(1)}, f32[96,256]{1,0:T(8,128)S(1)}, u32[]{:S(2)}, u32[]{:S(2)}) collective-permute-start(f32[96,256]{1,0:T(8,128)S(1)} %get-tuple-element.35), channel_id=1, source_target_pairs={{0,4},{4,0},{8,12},{12,8},{1,5},{5,1},{9,13},{13,9},{2,6},{6,2},{1... | collective-permute-start | bytes 294920 | tf_op jit(solution)/shard_map/ppermute | solution.py:443
  55.9 9.5 %collective-permute-start.6 = (f32[96,256]{1,0:T(8,128)S(1)}, f32[96,256]{1,0:T(8,128)S(1)}, u32[]{:S(2)}, u32[]{:S(2)}) collective-permute-start(f32[96,256]{1,0:T(8,128)S(1)} %get-tuple-element.37), channel_id=1, source_target_pairs={{0,12},{4,8},{8,4},{12,0},{1,13},{5,9},{9,5},{13,1},{2,14},{6,10},... | collective-permute-start | bytes 294920 | tf_op jit(solution)/shard_map/ppermute | solution.py:443
  69.5 1.4 copy-start.3
  70.9 0.8 copy-start.7
  79.3 30.3 %copy-start.4 = (f32[4,1024,128]{2,1,0:T(8,128)S(1)}, f32[4,1024,128]{2,1,0:T(8,128)}, u32[]{:S(2)}) copy-start(f32[4,1024,128]{2,1,0:T(8,128)} %copy-done.3) | copy-start | bytes 6291460
  79.3 30.3 %copy-start.8 = (bf16[3,256,256]{2,1,0:T(8,128)(2,1)S(1)}, bf16[3,256,256]{2,1,0:T(8,128)(2,1)}, u32[]{:S(2)}) copy-start(bf16[3,256,256]{2,1,0:T(8,128)(2,1)} %copy-done.7) | copy-start | bytes 1179652

commit v10 on v8

--- a/solution.py
+++ b/solution.py
@@ -13,7 +13,12 @@
 SMEM = pl.BlockSpec(memory_space=pltpu.SMEM)
 ANY = pl.BlockSpec(memory_space=pl.ANY)
 HBM = pl.BlockSpec(memory_space=pltpu.HBM)
-AXES = ("y", "zh", "x", "zl", "c")
+AXES = ("y1", "y0", "zh", "x1", "x0", "zl", "c")
+Y = ("y1", "y0")
+X = ("x1", "x0")
+FIRST = ("y1", "y0", "zh", "c")
+SECOND = ("zl", "x0", "x1")
+LAST = ("x1", "x0", "zl", "y1", "y0", "zh", "c")
 PI = 3.141592653589793
 TAU = 6.283185307179586
 
@@ -50,6 +55,13 @@
     return out
 
 
+def place(names):
+    index = 0
+    for name in names:
+        index = index * 2 + lax.axis_index(name)
+    return index
+
+
 def horner(coefs, u):
     acc = jnp.full_like(u, coefs[-1])
     for c in reversed(coefs[:-1]):
@@ -93,7 +105,13 @@
         for c in range(2):
             for v in range(nv):
                 cv = c * nv + v
-                part = x_ref[pl.ds(kt * 128 * ncv + cv, 128, stride=ncv), :]
+                part = jnp.concatenate(
+                    [
+                        x_ref[pl.ds((xz * 16 + kt * 2) * 8 * ncv + cv, 16, stride=ncv), :]
+                        for xz in range(8)
+                    ],
+                    axis=0,
+                )
                 columns[kt, pl.ds(c * 256 + v, 128, stride=2), :] = part.T
         leave(kt).start()
     for kt in range(8):
@@ -121,7 +139,7 @@
 
 
 def pack_y_kernel(ain, aout, y1, y2, y3, sems):
-    y = lax.axis_index("y")
+    y = place(Y)
     ry = rev(y, 2)
     jobs = [(ain, aout, 1, ((y >> 1) ^ 1) * 512, 512, y2, 256)]
     for m, dst in ((2, y2), (1, y1), (3, y3)):
@@ -130,7 +148,7 @@
 
 
 def pack_x_kernel(ain, aout, x1, x2, x3, sems):
-    x = lax.axis_index("x")
+    x = place(X)
     rx = rev(x, 2)
     jobs = [(ain, aout, 5, ((x >> 1) ^ 1) * 512, 512, x2, 256)]
     for m, dst in ((2, x2), (1, x1), (3, x3)):
@@ -139,7 +157,7 @@
 
 
 def core_kernel(ain, aout, y1, y2, y3, kept, sent, sems):
-    y = lax.axis_index("y")
+    y = place(Y)
     core = lax.axis_index("c")
     ry = rev(y, 2)
     jobs = []
@@ -228,7 +246,7 @@
     ain, aout, interp, kept, other, tab_ref, w_ref, raw, scratch, mine, sems,
     tab_v, out_sems,
 ):
-    y = lax.axis_index("y")
+    y = place(Y)
     core = lax.axis_index("c")
     ry = rev(y, 2)
     fetch([(ain, aout, 3, 0, 1024, mine, 0)], sems)
@@ -257,7 +275,7 @@
     ain, aout, interp, x1, x2, x3, tab_ref, w_ref, raw, scratch, mine, sems,
     tab_v, out_sems,
 ):
-    x = lax.axis_index("x")
+    x = place(X)
     rx = rev(x, 2)
     fetch(
         [
@@ -359,7 +377,7 @@
     def put(slab, q, tile):
         for kp in range(8):
             rows = slice(slab * 8, slab * 8 + 8)
-            out_ref[rev(kp, 3), rows, q * 128 : q * 128 + 128] = tile[kp * 8 : kp * 8 + 8]
+            out_ref[kp, rows, q * 128 : q * 128 + 128] = tile[kp * 8 : kp * 8 + 8]
 
     begin = [
         pltpu.make_async_copy(tab.at[0], tab_v.at[0], sems.at[0]),
@@ -383,20 +401,20 @@
     ncv = 2 * nv
 
     def first(i):
-        a = rev(i, 2) * 2
-        return [a], [a + 1]
+        return [i], [i + 4]
 
     def put(slab, q, tile):
-        done[slab * 128 : slab * 128 + 128, q, :] = tile
+        done[pl.ds(slab * 128 * ncv + q, 128, stride=ncv), :] = tile
 
     levels_kernel(nv, 3, 8, first, put, x_ref, (one, two), tab, w, lambda level: None)
 
     def gather(e, _):
         for r in range(8):
-            out_ref[e, r * ncv : r * ncv + ncv, :] = done[where_ref[e * 8 + r]]
+            row = pl.multiple_of(where_ref[e * 8 + r], ncv)
+            out_ref[e, r * ncv : r * ncv + ncv, :] = done[pl.ds(row, ncv), :]
         return 0
 
-    lax.fori_loop(0, 128, gather, 0, unroll=2)
+    lax.fori_loop(0, 128, gather, 0, unroll=4)
 
 
 def table_shapes(count, rows):
@@ -414,10 +432,10 @@
         in_specs=[HBM, HBM],
         out_specs=[VMEM] * 3,
         scratch_shapes=[pltpu.SemaphoreType.DMA((2, 4))],
-        compiler_params=params(56),
+        compiler_params=params(53),
     )(angle_in, angle_out)
     from_y = [
-        lax.ppermute(s, "y", [(i, i ^ m) for i in range(4)]) for m, s in zip((1, 2, 3), sends)
+        lax.ppermute(s, Y, [(i, i ^ m) for i in range(4)]) for m, s in zip((1, 2, 3), sends)
     ]
 
     state = pl.pallas_call(
@@ -429,7 +447,7 @@
         compiler_params=params(6),
     )(coefficients.reshape(512, 1024))
     state, *from_y = lax.optimization_barrier((state, *from_y))
-    state = lax.all_to_all(state, ("y", "zh", "c"), 0, 0, tiled=True)
+    state = lax.all_to_all(state, FIRST, 0, 0, tiled=True)
 
     sends = pl.pallas_call(
         pack_x_kernel,
@@ -440,7 +458,7 @@
         compiler_params=params(BIG),
     )(angle_in, angle_out)
     from_x = [
-        lax.ppermute(s, "x", [(i, i ^ m) for i in range(4)]) for m, s in zip((1, 2, 3), sends)
+        lax.ppermute(s, X, [(i, i ^ m) for i in range(4)]) for m, s in zip((1, 2, 3), sends)
     ]
     kept, sent = pl.pallas_call(
         core_kernel,
@@ -498,8 +516,9 @@
     )(state, *tables_lo)
     wanted = destination[0]
     where = (wanted & 7) * 128 + (wanted >> 3 & 15) * 8 + (wanted >> 7)
+    where = (where * ncv).reshape(8, 8, 16).swapaxes(0, 1).reshape(1024)
     state, where, *tables_hi = lax.optimization_barrier((state, where, *tables_hi))
-    state = lax.all_to_all(state, ("x", "zl"), 0, 0, tiled=True)
+    state = lax.all_to_all(state, SECOND, 0, 0, tiled=True)
 
     state = pl.pallas_call(
         functools.partial(levels_hi_kernel, nv),
@@ -507,10 +526,10 @@
         in_specs=[SMEM] + [VMEM] * 3,
         out_specs=VMEM,
         scratch_shapes=[pltpu.VMEM((8, 128, ncv * 128), F32)] * 2
-        + [pltpu.VMEM((1024, ncv, 128), F32)],
+        + [pltpu.VMEM((1024 * ncv, 128), F32)],
         compiler_params=params(BIG),
     )(where, state, *tables_hi)
-    state = lax.all_to_all(state, AXES, 0, 0, tiled=True)
+    state = lax.all_to_all(state, LAST, 0, 0, tiled=True)
 
     out = pl.pallas_call(
         functools.partial(final_kernel, nv),
@@ -524,7 +543,7 @@
 
 
 def solution(mesh):
-    mesh = jax.sharding.Mesh(mesh.devices.reshape(4, 2, 4, 2, 2), AXES)
+    mesh = jax.sharding.Mesh(mesh.devices.reshape((2,) * 7), AXES)
     placed = (
         P(None, None, None, AXES),
         P(None, None, AXES),

time: 138 us -> 136 us (0.986)
  waiting for transfers between devices: 19.1 us -> 8.62 us
  local copies, waits for them, and re-layouts: 3.46 us -> 10.1 us
    all_to_all x1, waiting for transfers between devices: 8.7 us -> 1.76 us  [shards(): state = lax.all_to_all(state, FIRST, 0, 0, tiled=True)]
    ppermute x6, waiting for transfers between devices: 10.4 us -> 6.85 us  [the longest x3 6.84 us: shards(): lax.ppermute(s, Y, [(i, i ^ m) for i in range(4)])]
    mul x0 -> x2, local copies, waits for them, and re-layouts: none -> 2.74 us  [shards(): where = (where * ncv).reshape(8, 8, 16).swapaxes(0, 1).reshape(1024)]
    unnamed x20 -> x30, local copies, waits for them, and re-layouts: 3.46 us -> 5.92 us
    pallas_call x1, Pallas kernels: 7.35 us -> 5.8 us  [shards(): pl.pallas_call(functools.partial(levels_hi_kernel, nv), out_shape=shape((...]
    reshape x0 -> x1, local copies, waits for them, and re-layouts: none -> 1.43 us  [shards(): where = (where * ncv).reshape(8, 8, 16).swapaxes(0, 1).reshape(1024)]
  transfers between devices with their start and end apart: 8 -> 8, of which waited for: 5 -> 3; matrix products, arithmetic and copies ran while one was open for 0% -> 4% of each run, Pallas kernels for 8% -> 11%
where the time goes in v10:
time: 136 us
  blocking collectives  68.4 us (50%)
  Pallas kernels  30.9 us (23%)
  starting transfers between devices  16.9 us (12%)
  local copies, waits for them, and re-layouts  10.1 us (7%)
  waiting for transfers between devices  8.62 us (6%)
    all_to_all x1, blocking collectives, shards(): state = lax.all_to_all(state, LAST, 0, 0, tiled=True)  38.2 us
    all_to_all x1, blocking collectives, shards(): state = lax.all_to_all(state, SECOND, 0, 0, tiled=True)  30.2 us
    all_to_all x1, starting transfers between devices, shards(): state = lax.all_to_all(state, FIRST, 0, 0, tiled=True)  8.34 us
    pallas_call x1, Pallas kernels, shards(): pl.pallas_call(functools.partial(levels_lo_kernel, nv), out_shape=shape((...  7.67 us
    ppermute x3, waiting for transfers between devices, shards(): lax.ppermute(s, Y, [(i, i ^ m) for i in range(4)])  6.84 us
    pallas_call x1, Pallas kernels, shards(): pl.pallas_call(table_lo_kernel, out_shape=table_shapes(4, PAD), in_specs=...  6.75 us
    unnamed x30, local copies, waits for them, and re-layouts  5.92 us
    pallas_call x1, Pallas kernels, shards(): pl.pallas_call(functools.partial(levels_hi_kernel, nv), out_shape=shape((...  5.8 us
  transfers between devices with their start and end apart: 8, of which 3 were waited for; matrix products, arithmetic and copies ran while one was open for 4% of the time, Pallas kernels for 11%

profile of v10, /device:TPU:1, one launch (start us, length us, event | category | flops | bytes accessed | tf_op | source)
XLA Modules:
  0.0 135.9 jit_solution(5081667035892701862)
XLA Ops:
  0.0 1.2 shard_map.56
  1.3 3.8 %collective-permute-start.1 = (f32[96,768]{1,0:T(8,128)S(1)}, f32[96,768]{1,0:T(8,128)S(1)}, u32[]{:S(2)}, u32[]{:S(2)}) collective-permute-start(f32[96,768]{1,0:T(8,128)S(1)} %get-tuple-element.30), channel_id=1, source_target_pairs={{0,64},{32,96},{64,0},{96,32},{1,65},{33,97},{65,1},{97,33},{2,66}... | collective-permute-start | bytes 884744 | tf_op jit(solution)/shard_map/ppermute | solution.py:438
  5.1 0.4 collective-permute-start
  5.5 0.4 collective-permute-start.2
  5.9 0.0 copy-done.5
  5.9 0.6 shard_map.55
  6.5 0.0 copy-start.2
  6.5 1.3 copy-done.2
  7.8 6.2 %collective-permute-done.y1 = f32[96,256]{1,0:T(8,128)S(1)} collective-permute-done((f32[96,256]{1,0:T(8,128)S(1)}, f32[96,256]{1,0:T(8,128)S(1)}, u32[]{:S(2)}, u32[]{:S(2)}) %collective-permute-start) | collective-permute-done | bytes 98336 | tf_op jit(solution)/shard_map/ppermute | solution.py:438
  14.0 0.6 collective-permute-done.2.y3
  14.7 0.0 collective-permute-done.1.y2
  14.7 0.7 copy-done.11
  15.4 8.3 %all-to-all-start = ((f32[16,64,512]{2,1,0:T(8,128)}), f32[16,64,512]{2,1,0:T(8,128)}, u32[]{:S(2)}, u32[]{:S(2)}) async-start(f32[16,64,512]{2,1,0:T(8,128)} %copy-done.2), calls=%async_computation | async-start | bytes 4194304 | tf_op jit(solution)/shard_map/all_to_all | solution.py:450
  23.7 0.0 copy-done
  23.7 1.0 copy-done.12
  24.7 1.2 shard_map.57
  25.9 0.0 copy-start.14
  25.9 0.0 copy-start.8
  25.9 0.2 collective-permute-start.3
  26.1 1.0 shard_map.59
  27.1 2.8 %collective-permute-start.5 = (f32[96,768]{1,0:T(8,128)}, f32[96,768]{1,0:T(8,128)}, u32[]{:S(2)}, u32[]{:S(2)}) collective-permute-start(f32[96,768]{1,0:T(8,128)} %get-tuple-element.40), channel_id=1, source_target_pairs={{0,8},{4,12},{8,0},{12,4},{1,9},{5,13},{9,1},{13,5},{2,10},{6,14},... | collective-permute-start | bytes 884744 | tf_op jit(solution)/shard_map/ppermute | solution.py:461
  30.0 0.3 collective-permute-start.4
  30.3 0.6 collective-permute-start.6
  30.8 0.6 multiply_reduce_fusion
  31.4 1.4 reshape.33
  32.8 1.4 %copy.8 = s32[8,8,16]{2,0,1:T(8,128)} copy(s32[8,8,16]{2,1,0:T(8,128)} %reshape.33) | data formatting | bytes 8192 | tf_op jit(solution)/shard_map/mul | solution.py:519
  34.2 1.4 %reshape.28.where_ref = s32[1024]{0:T(1024)} reshape(s32[8,8,16]{2,1,0:T(8,128)} %bitcast.8) | data formatting | bytes 8192 | tf_op jit(solution)/shard_map/reshape | solution.py:519
  35.6 0.0 collective-permute-done.3.other
  35.6 0.0 copy-done.8
  35.6 6.7 %shard_map.58 = (f32[72,1024,128]{2,1,0:T(8,128)}, bf16[4,256,256]{2,1,0:T(8,128)(2,1)S(1)}) custom-call(f32[7,64,1024]{2,1,0:T(8,128)S(1)} %copy-done, f32[7,32,1024]{2,1,0:T(8,128)S(1)} %copy-done.1, f32[7,32,64]{2,1,0:T(8,128)S(1)} %copy-done.8, f32[96,1536]{1,0:T(8,128)S(1)} %get-tuple-element.36.kept, f32[96,1536]{1,0:T(8,128)} %collective-permute-done.3.other), custom_call_target="tpu_custom_call" | custom-call | tf_op jit(solution)/shard_map/pallas_call | solution.py:473
  42.4 0.0 copy-start.6
  42.4 0.8 copy-done.6
  43.2 0.0 collective-permute-done.4.x1
  43.2 0.0 collective-permute-done.6.x3
  43.2 0.0 collective-permute-done.5.x2
  43.2 5.2 %shard_map.61 = (f32[4,1024,128]{2,1,0:T(8,128)S(1)}, bf16[3,256,256]{2,1,0:T(8,128)(2,1)S(1)}) custom-call(f32[7,64,1024]{2,1,0:T(8,128)S(1)} %copy-done, f32[7,32,1024]{2,1,0:T(8,128)S(1)} %copy-done.1, f32[7,32,64]{2,1,0:T(8,128)S(1)} %copy-done.8, f32[96,256]{1,0:T(8,128)S(1)} %collective-permute-done.4.x1, f32[96,768]{1,0:T(8,128)} %collective-permute-done.5.x2, ...), custom_call_target="tpu_custom_call" | custom-call | tf_op jit(solution)/shard_map/pallas_call | solution.py:489
  48.4 1.4 %copy-done.3 = f32[4,1024,128]{2,1,0:T(8,128)} copy-done((f32[4,1024,128]{2,1,0:T(8,128)}, f32[4,1024,128]{2,1,0:T(8,128)S(1)}, u32[]{:S(2)}) %copy-start.3) | copy-done | bytes 2097176
  49.8 0.7 copy-done.9
  50.5 1.8 %all-to-all-done.x_ref = f32[16,64,512]{2,1,0:T(8,128)} async-done(((f32[16,64,512]{2,1,0:T(8,128)}), f32[16,64,512]{2,1,0:T(8,128)}, u32[]{:S(2)}, u32[]{:S(2)}) %all-to-all-start) | async-done | bytes 2097184 | tf_op jit(solution)/shard_map/all_to_all | solution.py:450
  52.3 0.0 copy-done.7
  52.3 7.7 %shard_map.60 = f32[8,128,512]{2,1,0:T(8,128)S(1)} custom-call(f32[16,64,512]{2,1,0:T(8,128)} %all-to-all-done.x_ref, f32[72,1024,128]{2,1,0:T(8,128)} %get-tuple-element.42.tab, bf16[4,256,256]{2,1,0:T(8,128)(2,1)S(1)} %copy-done.7), custom_call_target="tpu_custom_call" | custom-call | tf_op jit(solution)/shard_map/pallas_call | solution.py:504
  59.9 0.0 copy-start.4
  60.0 0.0 copy-start.10
  60.0 0.0 copy-start.13
  60.0 30.2 %all_to_all.15.x_ref = f32[8,128,512]{2,1,0:T(8,128)S(1)} all-to-all(f32[8,128,512]{2,1,0:T(8,128)S(1)} %shard_map.60), channel_id=1, replica_groups=mesh['y1'=2,'y0'=2,'zh'=2,'x1'=2,'x0'=2,'zl'=2,'c'=2] {'zl','x0','x1'}, dimensions={0} | all-to-all | bytes 4194304 | tf_op jit(solution)/shard_map/all_to_all | solution.py:521
  90.2 5.8 %shard_map.62 = f32[128,32,128]{2,1,0:T(8,128)S(1)} custom-call(s32[1024]{0:T(1024)S(1)} %copy-done.13, f32[8,128,512]{2,1,0:T(8,128)S(1)} %all_to_all.15.x_ref, f32[4,1024,128]{2,1,0:T(8,128)S(1)} %copy-done.4, bf16[3,256,256]{2,1,0:T(8,128)(2,1)S(1)} %copy-done.10), custom_call_target="tpu_custom_call" | custom-call | tf_op jit(solution)/shard_map/pallas_call | solution.py:523
  96.0 38.2 %all_to_all.16 = f32[128,32,128]{2,1,0:T(8,128)S(1)} all-to-all(f32[128,32,128]{2,1,0:T(8,128)S(1)} %shard_map.62), channel_id=1, replica_groups=mesh['y1'=2,'y0'=2,'zh'=2,'x1'=2,'x0'=2,'zl'=2,'c'=2] {'x1','x0','zl','y..., dimensions={0} | all-to-all | bytes 4194304 | tf_op jit(solution)/shard_map/all_to_all | solution.py:532
  134.2 1.5 %shard_map.63 = f32[512,1024]{1,0:T(8,128)} custom-call(f32[4096,128]{1,0:T(8,128)S(1)} %bitcast.6), custom_call_target="tpu_custom_call" | custom-call | tf_op jit(solution)/shard_map/pallas_call | solution.py:534
  (13 shorter events, 0.0 us)
Async XLA Ops:
  0.0 5.9 %copy-start.5 = (f32[2,32,8,1024]{3,2,1,0:T(8,128)S(1)}, f32[2,32,8,1024]{3,2,1,0:T(8,128)}, u32[]{:S(2)}) copy-start(f32[2,32,8,1024]{3,2,1,0:T(8,128)} %param.5) | copy-start | bytes 6291460
  1.3 13.4 %collective-permute-start.1 = (f32[96,768]{1,0:T(8,128)S(1)}, f32[96,768]{1,0:T(8,128)S(1)}, u32[]{:S(2)}, u32[]{:S(2)}) collective-permute-start(f32[96,768]{1,0:T(8,128)S(1)} %get-tuple-element.30), channel_id=1, source_target_pairs={{0,64},{32,96},{64,0},{96,32},{1,65},{33,97},{65,1},{97,33},{2,66}... | collective-permute-start | bytes 884744 | tf_op jit(solution)/shard_map/ppermute | solution.py:438
  5.1 9.0 %collective-permute-start = (f32[96,256]{1,0:T(8,128)S(1)}, f32[96,256]{1,0:T(8,128)S(1)}, u32[]{:S(2)}, u32[]{:S(2)}) collective-permute-start(f32[96,256]{1,0:T(8,128)S(1)} %get-tuple-element.29), channel_id=1, source_target_pairs={{0,32},{32,0},{64,96},{96,64},{1,33},{33,1},{65,97},{97,65},{2,34}... | collective-permute-start | bytes 294920 | tf_op jit(solution)/shard_map/ppermute | solution.py:438
  5.5 9.2 %collective-permute-start.2 = (f32[96,256]{1,0:T(8,128)S(1)}, f32[96,256]{1,0:T(8,128)S(1)}, u32[]{:S(2)}, u32[]{:S(2)}) collective-permute-start(f32[96,256]{1,0:T(8,128)S(1)} %get-tuple-element.31), channel_id=1, source_target_pairs={{0,96},{32,64},{64,32},{96,0},{1,97},{33,65},{65,33},{97,1},{2,98}... | collective-permute-start | bytes 294920 | tf_op jit(solution)/shard_map/ppermute | solution.py:438
  6.5 1.3 copy-start.2
  7.8 15.9 %copy-start = (f32[7,64,1024]{2,1,0:T(8,128)S(1)}, f32[7,64,1024]{2,1,0:T(8,128)}, u32[]{:S(2)}) copy-start(f32[7,64,1024]{2,1,0:T(8,128)} %ain.9) | copy-start | bytes 5505028
  7.8 15.9 %copy-start.1 = (f32[7,32,1024]{2,1,0:T(8,128)S(1)}, f32[7,32,1024]{2,1,0:T(8,128)}, u32[]{:S(2)}) copy-start(f32[7,32,1024]{2,1,0:T(8,128)} %aout.9) | copy-start | bytes 2752516
  14.7 0.7 copy-start.11
  15.4 36.9 %all-to-all-start = ((f32[16,64,512]{2,1,0:T(8,128)}), f32[16,64,512]{2,1,0:T(8,128)}, u32[]{:S(2)}, u32[]{:S(2)}) async-start(f32[16,64,512]{2,1,0:T(8,128)} %copy-done.2), calls=%async_computation | async-start | bytes 4194304 | tf_op jit(solution)/shard_map/all_to_all | solution.py:450
  23.7 1.0 copy-start.12
  25.9 4.9 %copy-start.14 = (s32[1,1024]{1,0:T(1,128)S(1)}, s32[1,1024]{1,0:T(1,128)}, u32[]{:S(2)}) copy-start(s32[1,1024]{1,0:T(1,128)} %param.9) | copy-start | bytes 12292
  25.9 9.7 %copy-start.8 = (f32[7,32,64]{2,1,0:T(8,128)S(1)}, f32[7,32,64]{2,1,0:T(8,128)}, u32[]{:S(2)}) copy-start(f32[7,32,64]{2,1,0:T(8,128)} %interp.3) | copy-start | bytes 172036
  25.9 9.7 %collective-permute-start.3 = (f32[96,1536]{1,0:T(8,128)}, f32[96,1536]{1,0:T(8,128)}, u32[]{:S(2)}, u32[]{:S(2)}) collective-permute-start(f32[96,1536]{1,0:T(8,128)} %get-tuple-element.37), channel_id=1, source_target_pairs={{0,1},{1,0},{2,3},{3,2},{4,5},{5,4},{6,7},{7,6},{8,9},{9,8},{10,11... | collective-permute-start | bytes 1769480 | tf_op jit(solution)/shard_map/ppermute | solution.py:471
  27.1 16.0 %collective-permute-start.5 = (f32[96,768]{1,0:T(8,128)}, f32[96,768]{1,0:T(8,128)}, u32[]{:S(2)}, u32[]{:S(2)}) collective-permute-start(f32[96,768]{1,0:T(8,128)} %get-tuple-element.40), channel_id=1, source_target_pairs={{0,8},{4,12},{8,0},{12,4},{1,9},{5,13},{9,1},{13,5},{2,10},{6,14},... | collective-permute-start | bytes 884744 | tf_op jit(solution)/shard_map/ppermute | solution.py:461
  30.0 13.2 %collective-permute-start.4 = (f32[96,256]{1,0:T(8,128)}, f32[96,256]{1,0:T(8,128)S(1)}, u32[]{:S(2)}, u32[]{:S(2)}) collective-permute-start(f32[96,256]{1,0:T(8,128)} %get-tuple-element.39), channel_id=1, source_target_pairs={{0,4},{4,0},{8,12},{12,8},{1,5},{5,1},{9,13},{13,9},{2,6},{6,2},{1... | collective-permute-start | bytes 294920 | tf_op jit(solution)/shard_map/ppermute | solution.py:461
  30.3 12.9 %collective-permute-start.6 = (f32[96,256]{1,0:T(8,128)}, f32[96,256]{1,0:T(8,128)}, u32[]{:S(2)}, u32[]{:S(2)}) collective-permute-start(f32[96,256]{1,0:T(8,128)} %get-tuple-element.41), channel_id=1, source_target_pairs={{0,12},{4,8},{8,4},{12,0},{1,13},{5,9},{9,5},{13,1},{2,14},{6,10},... | collective-permute-start | bytes 294920 | tf_op jit(solution)/shard_map/ppermute | solution.py:461
  42.4 0.8 copy-start.6
  43.2 9.1 %copy-start.7 = (bf16[4,256,256]{2,1,0:T(8,128)(2,1)S(1)}, bf16[4,256,256]{2,1,0:T(8,128)(2,1)}, u32[]{:S(2)}) copy-start(bf16[4,256,256]{2,1,0:T(8,128)(2,1)} %copy-done.6) | copy-start | bytes 1572868
  48.4 1.4 %copy-start.3 = (f32[4,1024,128]{2,1,0:T(8,128)}, f32[4,1024,128]{2,1,0:T(8,128)S(1)}, u32[]{:S(2)}) copy-start(f32[4,1024,128]{2,1,0:T(8,128)S(1)} %get-tuple-element.51.tab) | copy-start | bytes 6291460
  49.8 0.7 copy-start.9
  59.9 30.2 %copy-start.4 = (f32[4,1024,128]{2,1,0:T(8,128)S(1)}, f32[4,1024,128]{2,1,0:T(8,128)}, u32[]{:S(2)}) copy-start(f32[4,1024,128]{2,1,0:T(8,128)} %copy-done.3) | copy-start | bytes 6291460
  60.0 30.2 %copy-start.10 = (bf16[3,256,256]{2,1,0:T(8,128)(2,1)S(1)}, bf16[3,256,256]{2,1,0:T(8,128)(2,1)}, u32[]{:S(2)}) copy-start(bf16[3,256,256]{2,1,0:T(8,128)(2,1)} %copy-done.9) | copy-start | bytes 1179652
  60.0 30.2 %copy-start.13 = (s32[1024]{0:T(1024)S(1)}, s32[1024]{0:T(1024)}, u32[]{:S(2)}) copy-start(s32[1024]{0:T(1024)} %reshape.28.where_ref) | copy-start | bytes 12292

commit v11 on v10

--- a/solution.py
+++ b/solution.py
@@ -243,14 +243,13 @@
 
 
 def table_lo_kernel(
-    ain, aout, interp, kept, other, tab_ref, w_ref, raw, scratch, mine, sems,
+    ain, aout, kept, other, tab_ref, raw, scratch, mine, sems,
     tab_v, out_sems,
 ):
     y = place(Y)
     core = lax.axis_index("c")
     ry = rev(y, 2)
     fetch([(ain, aout, 3, 0, 1024, mine, 0)], sems)
-    weights(interp, w_ref, 0, 4)
 
     def emit(level, base, ts):
         for t in range(ts):
@@ -369,7 +368,7 @@
                             dst[m, :, lanes(q)] = part
 
 
-def levels_lo_kernel(nv, x_ref, tab, w, out_ref, one, two, tab_v, w_v, sems):
+def levels_lo_kernel(nv, x_ref, tab, interp, out_ref, one, two, tab_v, w_v, interp_v, sems):
     def first(i):
         a = (i & 1) * 8 + (i >> 1) * 4
         return [a, a + 1], [a + 2, a + 3]
@@ -381,7 +380,6 @@
 
     begin = [
         pltpu.make_async_copy(tab.at[0], tab_v.at[0], sems.at[0]),
-        pltpu.make_async_copy(w, w_v, sems.at[1]),
         pltpu.make_async_copy(x_ref, two, sems.at[2]),
     ]
     rest = [pltpu.make_async_copy(tab.at[1:5], tab_v.at[1:5], sems.at[3])]
@@ -390,8 +388,12 @@
         for copy in (begin, rest, [], [])[level]:
             copy.wait()
 
+    small = pltpu.make_async_copy(interp, interp_v, sems.at[1])
+    small.start()
     for copy in begin + rest:
         copy.start()
+    small.wait()
+    weights(interp_v, w_v, 0, 4)
     levels_kernel(
         nv, 4, 16, first, put, two, (one, two), tab_v, w_v, ready
     )
@@ -409,8 +411,9 @@
     levels_kernel(nv, 3, 8, first, put, x_ref, (one, two), tab, w, lambda level: None)
 
     def gather(e, _):
+        slot = (e >> 1 & 7) * 128 + (e >> 4) * 16 + (e & 1) * 8
         for r in range(8):
-            row = pl.multiple_of(where_ref[e * 8 + r], ncv)
+            row = pl.multiple_of(where_ref[slot + r], ncv)
             out_ref[e, r * ncv : r * ncv + ncv, :] = done[pl.ds(row, ncv), :]
         return 0
 
@@ -472,9 +475,9 @@
 
     tables_lo = pl.pallas_call(
         table_lo_kernel,
-        out_shape=table_shapes(4, PAD),
-        in_specs=[HBM, HBM] + [VMEM] * 3,
-        out_specs=[ANY, VMEM],
+        out_shape=shape((PAD, 1024, 128), F32),
+        in_specs=[HBM, HBM] + [VMEM] * 2,
+        out_specs=ANY,
         scratch_shapes=[
             pltpu.VMEM((4, 1024, 128), F32),
             pltpu.VMEM((1024, 128), F32),
@@ -483,9 +486,8 @@
         ]
         + [pltpu.VMEM((5, 1024, 128), F32), pltpu.SemaphoreType.DMA((5,))],
         compiler_params=params(BIG),
-    )(angle_in, angle_out, interp, kept, other)
-    first, *from_x = lax.optimization_barrier((tables_lo[0], *from_x))
-    tables_lo = [first, *tables_lo[1:]]
+    )(angle_in, angle_out, kept, other)
+    tables_lo, *from_x = lax.optimization_barrier((tables_lo, *from_x))
     tables_hi = pl.pallas_call(
         table_hi_kernel,
         out_shape=table_shapes(3, 4),
@@ -510,13 +512,14 @@
         + [
             pltpu.VMEM((5, 1024, 128), F32),
             pltpu.VMEM((4, 256, 256), BF16),
+            pltpu.VMEM((7, 32, 64), F32),
             pltpu.SemaphoreType.DMA((4,)),
         ],
         compiler_params=params(BIG),
-    )(state, *tables_lo)
+    )(state, tables_lo, interp)
     wanted = destination[0]
     where = (wanted & 7) * 128 + (wanted >> 3 & 15) * 8 + (wanted >> 7)
-    where = (where * ncv).reshape(8, 8, 16).swapaxes(0, 1).reshape(1024)
+    where = where * ncv
     state, where, *tables_hi = lax.optimization_barrier((state, where, *tables_hi))
     state = lax.all_to_all(state, SECOND, 0, 0, tiled=True)
 

time: 136 us -> 135 us (level)
  waiting for transfers between devices: 8.62 us -> 19.7 us
  local copies, waits for them, and re-layouts: 10.1 us -> 2.69 us
  Pallas kernels: 30.9 us -> 27.6 us
    all_to_all x1, waiting for transfers between devices: 1.76 us -> 9.49 us  [shards(): state = lax.all_to_all(state, FIRST, 0, 0, tiled=True)]
    ppermute x3, waiting for transfers between devices: 0.01 us -> 3.35 us  [shards(): lax.ppermute(s, X, [(i, i ^ m) for i in range(4)])]
    unnamed x30 -> x16, local copies, waits for them, and re-layouts: 5.92 us -> 2.69 us
    mul x2 -> x0, local copies, waits for them, and re-layouts: 2.74 us -> none  [shards(): where = (where * ncv).reshape(8, 8, 16).swapaxes(0, 1).reshape(1024)]
    reshape x1 -> x0, local copies, waits for them, and re-layouts: 1.43 us -> none  [shards(): where = (where * ncv).reshape(8, 8, 16).swapaxes(0, 1).reshape(1024)]
  transfers between devices with their start and end apart: 8 -> 8, of which waited for: 3 -> 5; matrix products, arithmetic and copies ran while one was open for 4% -> 0% of each run, Pallas kernels for 11% -> 8%
where the time goes in v11:
time: 135 us
  blocking collectives  68.1 us (50%)
  Pallas kernels  27.6 us (20%)
  waiting for transfers between devices  19.7 us (15%)
  starting transfers between devices  16.9 us (13%)
  local copies, waits for them, and re-layouts  2.69 us (2%)
    all_to_all x1, blocking collectives, shards(): state = lax.all_to_all(state, LAST, 0, 0, tiled=True)  37.9 us
    all_to_all x1, blocking collectives, shards(): state = lax.all_to_all(state, SECOND, 0, 0, tiled=True)  30.2 us
    all_to_all x1, waiting for transfers between devices, shards(): state = lax.all_to_all(state, FIRST, 0, 0, tiled=True)  9.49 us
    all_to_all x1, starting transfers between devices, shards(): state = lax.all_to_all(state, FIRST, 0, 0, tiled=True)  8.34 us
    pallas_call x1, Pallas kernels, shards(): pl.pallas_call(functools.partial(levels_lo_kernel, nv), out_shape=shape((...  7.78 us
    ppermute x3, waiting for transfers between devices, shards(): lax.ppermute(s, Y, [(i, i ^ m) for i in range(4)])  6.84 us
    pallas_call x1, Pallas kernels, shards(): pl.pallas_call(functools.partial(levels_hi_kernel, nv), out_shape=shape((...  6.06 us
    pallas_call x1, Pallas kernels, shards(): pl.pallas_call(table_lo_kernel, out_shape=shape((PAD, 1024, 128), F32), i...  5.64 us
  transfers between devices with their start and end apart: 8, of which 5 were waited for; matrix products, arithmetic and copies ran while one was open for 0% of the time, Pallas kernels for 8%

profile of v11, /device:TPU:1, one launch (start us, length us, event | category | flops | bytes accessed | tf_op | source)
XLA Modules:
  0.0 135.2 jit_solution(957956447433410198)
XLA Ops:
  0.0 0.0 copy-start.5
  0.0 1.2 shard_map.56
  1.3 3.8 %collective-permute-start.1 = (f32[96,768]{1,0:T(8,128)S(1)}, f32[96,768]{1,0:T(8,128)S(1)}, u32[]{:S(2)}, u32[]{:S(2)}) collective-permute-start(f32[96,768]{1,0:T(8,128)S(1)} %get-tuple-element.28), channel_id=1, source_target_pairs={{0,64},{32,96},{64,0},{96,32},{1,65},{33,97},{65,1},{97,33},{2,66}... | collective-permute-start | bytes 884744 | tf_op jit(solution)/shard_map/ppermute | solution.py:441
  5.1 0.4 collective-permute-start
  5.5 0.4 collective-permute-start.2
  5.9 0.0 copy-done.5
  5.9 0.6 shard_map.55
  6.5 0.0 copy-start.2
  6.5 1.3 copy-done.2
  7.8 0.0 copy-start
  7.8 0.0 copy-start.1
  7.8 6.2 %collective-permute-done.y1 = f32[96,256]{1,0:T(8,128)S(1)} collective-permute-done((f32[96,256]{1,0:T(8,128)S(1)}, f32[96,256]{1,0:T(8,128)S(1)}, u32[]{:S(2)}, u32[]{:S(2)}) %collective-permute-start) | collective-permute-done | bytes 98336 | tf_op jit(solution)/shard_map/ppermute | solution.py:441
  14.0 0.6 collective-permute-done.2.y3
  14.7 0.0 collective-permute-done.1.y2
  14.7 8.3 %all-to-all-start = ((f32[16,64,512]{2,1,0:T(8,128)}), f32[16,64,512]{2,1,0:T(8,128)}, u32[]{:S(2)}, u32[]{:S(2)}) async-start(f32[16,64,512]{2,1,0:T(8,128)} %copy-done.2), calls=%async_computation | async-start | bytes 4194304 | tf_op jit(solution)/shard_map/all_to_all | solution.py:453
  23.0 0.0 copy-done
  23.0 0.0 copy-done.1
  23.0 0.3 shard_map.57
  23.4 0.0 copy-start.7
  23.4 0.2 collective-permute-start.3
  23.6 0.2 shard_map.59
  23.8 2.8 %collective-permute-start.5 = (f32[96,768]{1,0:T(8,128)S(1)}, f32[96,768]{1,0:T(8,128)S(1)}, u32[]{:S(2)}, u32[]{:S(2)}) collective-permute-start(f32[96,768]{1,0:T(8,128)S(1)} %get-tuple-element.37), channel_id=1, source_target_pairs={{0,8},{4,12},{8,0},{12,4},{1,9},{5,13},{9,1},{13,5},{2,10},{6,14},... | collective-permute-start | bytes 884744 | tf_op jit(solution)/shard_map/ppermute | solution.py:464
  26.6 0.3 collective-permute-start.4
  27.0 0.6 collective-permute-start.6
  27.5 0.0 copy-done.7
  27.5 0.0 collective-permute-done.3.other
  27.5 0.0 copy-start.6
  27.6 5.6 %shard_map.58.tab = f32[72,1024,128]{2,1,0:T(8,128)} custom-call(f32[7,64,1024]{2,1,0:T(8,128)S(1)} %copy-done, f32[7,32,1024]{2,1,0:T(8,128)S(1)} %copy-done.1, f32[96,1536]{1,0:T(8,128)S(1)} %get-tuple-element.34.kept, f32[96,1536]{1,0:T(8,128)S(1)} %collective-permute-done.3.other), custom_call_target="tpu_custom_call" | custom-call | tf_op jit(solution)/shard_map/pallas_call | solution.py:476
  33.2 2.8 %collective-permute-done.4.x1 = f32[96,256]{1,0:T(8,128)S(1)} collective-permute-done((f32[96,256]{1,0:T(8,128)S(1)}, f32[96,256]{1,0:T(8,128)S(1)}, u32[]{:S(2)}, u32[]{:S(2)}) %collective-permute-start.4) | collective-permute-done | bytes 98336 | tf_op jit(solution)/shard_map/ppermute | solution.py:464
  36.0 0.6 collective-permute-done.6.x3
  36.6 0.0 collective-permute-done.5.x2
  36.6 0.0 copy-done.6
  36.6 4.2 %shard_map.61 = (f32[4,1024,128]{2,1,0:T(8,128)S(1)}, bf16[3,256,256]{2,1,0:T(8,128)(2,1)S(1)}) custom-call(f32[7,64,1024]{2,1,0:T(8,128)S(1)} %copy-done, f32[7,32,1024]{2,1,0:T(8,128)S(1)} %copy-done.1, f32[7,32,64]{2,1,0:T(8,128)S(1)} %copy-done.6, f32[96,256]{1,0:T(8,128)S(1)} %collective-permute-done.4.x1, f32[96,768]{1,0:T(8,128)S(1)} %collective-permute-done.5.x2, ...), custom_call_target="tpu_custom_call" | custom-call | tf_op jit(solution)/shard_map/pallas_call | solution.py:491
  40.7 0.0 copy-start.3
  40.7 1.3 copy-done.3
  42.1 9.5 %all-to-all-done.x_ref = f32[16,64,512]{2,1,0:T(8,128)} async-done(((f32[16,64,512]{2,1,0:T(8,128)}), f32[16,64,512]{2,1,0:T(8,128)}, u32[]{:S(2)}, u32[]{:S(2)}) %all-to-all-start) | async-done | bytes 2097184 | tf_op jit(solution)/shard_map/all_to_all | solution.py:453
  51.6 7.8 %shard_map.60 = f32[8,128,512]{2,1,0:T(8,128)S(1)} custom-call(f32[16,64,512]{2,1,0:T(8,128)} %all-to-all-done.x_ref, f32[72,1024,128]{2,1,0:T(8,128)} %shard_map.58.tab, f32[7,32,64]{2,1,0:T(8,128)S(1)} %copy-done.6), custom_call_target="tpu_custom_call" | custom-call | tf_op jit(solution)/shard_map/pallas_call | solution.py:506
  59.3 0.0 copy-start.4
  59.4 30.2 %all_to_all.15.x_ref = f32[8,128,512]{2,1,0:T(8,128)S(1)} all-to-all(f32[8,128,512]{2,1,0:T(8,128)S(1)} %shard_map.60), channel_id=1, replica_groups=mesh['y1'=2,'y0'=2,'zh'=2,'x1'=2,'x0'=2,'zl'=2,'c'=2] {'zl','x0','x1'}, dimensions={0} | all-to-all | bytes 4194304 | tf_op jit(solution)/shard_map/all_to_all | solution.py:524
  89.6 0.0 copy-done.4
  89.6 6.1 %shard_map.62 = f32[128,32,128]{2,1,0:T(8,128)S(1)} custom-call(s32[1024]{0:T(1024)S(1)} %bitcast.6, f32[8,128,512]{2,1,0:T(8,128)S(1)} %all_to_all.15.x_ref, f32[4,1024,128]{2,1,0:T(8,128)S(1)} %copy-done.4, bf16[3,256,256]{2,1,0:T(8,128)(2,1)S(1)} %get-tuple-element.48.w), custom_call_target="tpu_custom_call" | custom-call | tf_op jit(solution)/shard_map/pallas_call | solution.py:526
  95.6 37.9 %all_to_all.16 = f32[128,32,128]{2,1,0:T(8,128)S(1)} all-to-all(f32[128,32,128]{2,1,0:T(8,128)S(1)} %shard_map.62), channel_id=1, replica_groups=mesh['y1'=2,'y0'=2,'zh'=2,'x1'=2,'x0'=2,'zl'=2,'c'=2] {'x1','x0','zl','y..., dimensions={0} | all-to-all | bytes 4194304 | tf_op jit(solution)/shard_map/all_to_all | solution.py:535
  133.6 1.5 %shard_map.63 = f32[512,1024]{1,0:T(8,128)} custom-call(f32[4096,128]{1,0:T(8,128)S(1)} %bitcast.4), custom_call_target="tpu_custom_call" | custom-call | tf_op jit(solution)/shard_map/pallas_call | solution.py:537
  (1 shorter events, 0.0 us)
Async XLA Ops:
  0.0 5.9 %copy-start.5 = (f32[2,32,8,1024]{3,2,1,0:T(8,128)S(1)}, f32[2,32,8,1024]{3,2,1,0:T(8,128)}, u32[]{:S(2)}) copy-start(f32[2,32,8,1024]{3,2,1,0:T(8,128)} %param.5) | copy-start | bytes 6291460
  1.3 13.4 %collective-permute-start.1 = (f32[96,768]{1,0:T(8,128)S(1)}, f32[96,768]{1,0:T(8,128)S(1)}, u32[]{:S(2)}, u32[]{:S(2)}) collective-permute-start(f32[96,768]{1,0:T(8,128)S(1)} %get-tuple-element.28), channel_id=1, source_target_pairs={{0,64},{32,96},{64,0},{96,32},{1,65},{33,97},{65,1},{97,33},{2,66}... | collective-permute-start | bytes 884744 | tf_op jit(solution)/shard_map/ppermute | solution.py:441
  5.1 9.0 %collective-permute-start = (f32[96,256]{1,0:T(8,128)S(1)}, f32[96,256]{1,0:T(8,128)S(1)}, u32[]{:S(2)}, u32[]{:S(2)}) collective-permute-start(f32[96,256]{1,0:T(8,128)S(1)} %get-tuple-element.27), channel_id=1, source_target_pairs={{0,32},{32,0},{64,96},{96,64},{1,33},{33,1},{65,97},{97,65},{2,34}... | collective-permute-start | bytes 294920 | tf_op jit(solution)/shard_map/ppermute | solution.py:441
  5.5 9.2 %collective-permute-start.2 = (f32[96,256]{1,0:T(8,128)S(1)}, f32[96,256]{1,0:T(8,128)S(1)}, u32[]{:S(2)}, u32[]{:S(2)}) collective-permute-start(f32[96,256]{1,0:T(8,128)S(1)} %get-tuple-element.29), channel_id=1, source_target_pairs={{0,96},{32,64},{64,32},{96,0},{1,97},{33,65},{65,33},{97,1},{2,98}... | collective-permute-start | bytes 294920 | tf_op jit(solution)/shard_map/ppermute | solution.py:441
  6.5 1.3 copy-start.2
  7.8 15.2 %copy-start = (f32[7,64,1024]{2,1,0:T(8,128)S(1)}, f32[7,64,1024]{2,1,0:T(8,128)}, u32[]{:S(2)}) copy-start(f32[7,64,1024]{2,1,0:T(8,128)} %ain.9) | copy-start | bytes 5505028
  7.8 15.2 %copy-start.1 = (f32[7,32,1024]{2,1,0:T(8,128)S(1)}, f32[7,32,1024]{2,1,0:T(8,128)}, u32[]{:S(2)}) copy-start(f32[7,32,1024]{2,1,0:T(8,128)} %aout.9) | copy-start | bytes 2752516
  14.7 36.9 %all-to-all-start = ((f32[16,64,512]{2,1,0:T(8,128)}), f32[16,64,512]{2,1,0:T(8,128)}, u32[]{:S(2)}, u32[]{:S(2)}) async-start(f32[16,64,512]{2,1,0:T(8,128)} %copy-done.2), calls=%async_computation | async-start | bytes 4194304 | tf_op jit(solution)/shard_map/all_to_all | solution.py:453
  23.4 4.1 %copy-start.7 = (s32[1,1024]{1,0:T(1,128)S(1)}, s32[1,1024]{1,0:T(1,128)}, u32[]{:S(2)}) copy-start(s32[1,1024]{1,0:T(1,128)} %param.9) | copy-start | bytes 12292
  23.4 4.1 %collective-permute-start.3 = (f32[96,1536]{1,0:T(8,128)S(1)}, f32[96,1536]{1,0:T(8,128)S(1)}, u32[]{:S(2)}, u32[]{:S(2)}) collective-permute-start(f32[96,1536]{1,0:T(8,128)S(1)} %get-tuple-element.35), channel_id=1, source_target_pairs={{0,1},{1,0},{2,3},{3,2},{4,5},{5,4},{6,7},{7,6},{8,9},{9,8},{10,11... | collective-permute-start | bytes 1769480 | tf_op jit(solution)/shard_map/ppermute | solution.py:474
  23.8 12.7 %collective-permute-start.5 = (f32[96,768]{1,0:T(8,128)S(1)}, f32[96,768]{1,0:T(8,128)S(1)}, u32[]{:S(2)}, u32[]{:S(2)}) collective-permute-start(f32[96,768]{1,0:T(8,128)S(1)} %get-tuple-element.37), channel_id=1, source_target_pairs={{0,8},{4,12},{8,0},{12,4},{1,9},{5,13},{9,1},{13,5},{2,10},{6,14},... | collective-permute-start | bytes 884744 | tf_op jit(solution)/shard_map/ppermute | solution.py:464
  26.6 9.3 %collective-permute-start.4 = (f32[96,256]{1,0:T(8,128)S(1)}, f32[96,256]{1,0:T(8,128)S(1)}, u32[]{:S(2)}, u32[]{:S(2)}) collective-permute-start(f32[96,256]{1,0:T(8,128)S(1)} %get-tuple-element.36), channel_id=1, source_target_pairs={{0,4},{4,0},{8,12},{12,8},{1,5},{5,1},{9,13},{13,9},{2,6},{6,2},{1... | collective-permute-start | bytes 294920 | tf_op jit(solution)/shard_map/ppermute | solution.py:464
  27.0 9.6 %collective-permute-start.6 = (f32[96,256]{1,0:T(8,128)S(1)}, f32[96,256]{1,0:T(8,128)S(1)}, u32[]{:S(2)}, u32[]{:S(2)}) collective-permute-start(f32[96,256]{1,0:T(8,128)S(1)} %get-tuple-element.38), channel_id=1, source_target_pairs={{0,12},{4,8},{8,4},{12,0},{1,13},{5,9},{9,5},{13,1},{2,14},{6,10},... | collective-permute-start | bytes 294920 | tf_op jit(solution)/shard_map/ppermute | solution.py:464
  27.5 9.0 %copy-start.6 = (f32[7,32,64]{2,1,0:T(8,128)S(1)}, f32[7,32,64]{2,1,0:T(8,128)}, u32[]{:S(2)}) copy-start(f32[7,32,64]{2,1,0:T(8,128)} %interp.3) | copy-start | bytes 172036
  40.7 1.3 copy-start.3
  59.3 30.2 %copy-start.4 = (f32[4,1024,128]{2,1,0:T(8,128)S(1)}, f32[4,1024,128]{2,1,0:T(8,128)}, u32[]{:S(2)}) copy-start(f32[4,1024,128]{2,1,0:T(8,128)} %copy-done.3) | copy-start | bytes 6291460

commit v12 on v11

--- a/solution.py
+++ b/solution.py
@@ -16,7 +16,7 @@
 AXES = ("y1", "y0", "zh", "x1", "x0", "zl", "c")
 Y = ("y1", "y0")
 X = ("x1", "x0")
-FIRST = ("y1", "y0", "zh", "c")
+FIRST = ("zh", "c", "y1", "y0")
 SECOND = ("zl", "x0", "x1")
 LAST = ("x1", "x0", "zl", "y1", "y0", "zh", "c")
 PI = 3.141592653589793
@@ -91,7 +91,8 @@
                 part = columns[kt, pl.ds(c * 256 + v, 128, stride=2), :].T
                 lanes = slice((c * nv + v) * 128, (c * nv + v) * 128 + 128)
                 for core in range(2):
-                    out_ref[rev(kt, 3) * 2 + core, :, lanes] = part[core * 64 : core * 64 + 64]
+                    owner = (kt >> 2) * 8 + core * 4 + rev(kt & 3, 2)
+                    out_ref[owner, :, lanes] = part[core * 64 : core * 64 + 64]
 
 
 def final_kernel(nv, x_ref, out_ref, columns, sems):
@@ -370,8 +371,8 @@
 
 def levels_lo_kernel(nv, x_ref, tab, interp, out_ref, one, two, tab_v, w_v, interp_v, sems):
     def first(i):
-        a = (i & 1) * 8 + (i >> 1) * 4
-        return [a, a + 1], [a + 2, a + 3]
+        a = rev(i, 2)
+        return [a, a + 4], [a + 8, a + 12]
 
     def put(slab, q, tile):
         for kp in range(8):

time: 135 us -> 134 us (level)
  blocking collectives: 68.1 us -> 66.5 us
where the time goes in v12:
time: 134 us
  blocking collectives  66.5 us (50%)
  Pallas kernels  27.6 us (21%)
  waiting for transfers between devices  20.3 us (15%)
  starting transfers between devices  16.9 us (13%)
  local copies, waits for them, and re-layouts  2.69 us (2%)
    all_to_all x1, blocking collectives, shards(): state = lax.all_to_all(state, LAST, 0, 0, tiled=True)  37.4 us
    all_to_all x1, blocking collectives, shards(): state = lax.all_to_all(state, SECOND, 0, 0, tiled=True)  29 us
    all_to_all x1, waiting for transfers between devices, shards(): state = lax.all_to_all(state, FIRST, 0, 0, tiled=True)  10.1 us
    all_to_all x1, starting transfers between devices, shards(): state = lax.all_to_all(state, FIRST, 0, 0, tiled=True)  8.34 us
    pallas_call x1, Pallas kernels, shards(): pl.pallas_call(functools.partial(levels_lo_kernel, nv), out_shape=shape((...  7.78 us
    ppermute x3, waiting for transfers between devices, shards(): lax.ppermute(s, Y, [(i, i ^ m) for i in range(4)])  6.84 us
    pallas_call x1, Pallas kernels, shards(): pl.pallas_call(functools.partial(levels_hi_kernel, nv), out_shape=shape((...  6.06 us
    pallas_call x1, Pallas kernels, shards(): pl.pallas_call(table_lo_kernel, out_shape=shape((PAD, 1024, 128), F32), i...  5.64 us
  transfers between devices with their start and end apart: 8, of which 5 were waited for; matrix products, arithmetic and copies ran while one was open for 0% of the time, Pallas kernels for 8%

profile of v12, /device:TPU:1, one launch (start us, length us, event | category | flops | bytes accessed | tf_op | source)
XLA Modules:
  0.0 134.2 jit_solution(3053918624132702154)
XLA Ops:
  0.0 0.0 copy-start.5
  0.0 1.2 shard_map.56
  1.3 3.8 %collective-permute-start.1 = (f32[96,768]{1,0:T(8,128)S(1)}, f32[96,768]{1,0:T(8,128)S(1)}, u32[]{:S(2)}, u32[]{:S(2)}) collective-permute-start(f32[96,768]{1,0:T(8,128)S(1)} %get-tuple-element.28), channel_id=1, source_target_pairs={{0,64},{32,96},{64,0},{96,32},{1,65},{33,97},{65,1},{97,33},{2,66}... | collective-permute-start | bytes 884744 | tf_op jit(solution)/shard_map/ppermute | solution.py:442
  5.1 0.4 collective-permute-start
  5.5 0.4 collective-permute-start.2
  5.9 0.0 copy-done.5
  5.9 0.6 shard_map.55
  6.5 0.0 copy-start.2
  6.5 1.3 copy-done.2
  7.8 0.0 copy-start
  7.8 0.0 copy-start.1
  7.8 6.2 %collective-permute-done.y1 = f32[96,256]{1,0:T(8,128)S(1)} collective-permute-done((f32[96,256]{1,0:T(8,128)S(1)}, f32[96,256]{1,0:T(8,128)S(1)}, u32[]{:S(2)}, u32[]{:S(2)}) %collective-permute-start) | collective-permute-done | bytes 98336 | tf_op jit(solution)/shard_map/ppermute | solution.py:442
  14.0 0.6 collective-permute-done.2.y3
  14.7 0.0 collective-permute-done.1.y2
  14.7 8.3 %all-to-all-start = ((f32[16,64,512]{2,1,0:T(8,128)}), f32[16,64,512]{2,1,0:T(8,128)}, u32[]{:S(2)}, u32[]{:S(2)}) async-start(f32[16,64,512]{2,1,0:T(8,128)} %copy-done.2), calls=%async_computation | async-start | bytes 4194304 | tf_op jit(solution)/shard_map/all_to_all | solution.py:454
  23.0 0.0 copy-done
  23.0 0.0 copy-done.1
  23.0 0.3 shard_map.57
  23.4 0.0 copy-start.7
  23.4 0.2 collective-permute-start.3
  23.6 0.2 shard_map.59
  23.8 2.8 %collective-permute-start.5 = (f32[96,768]{1,0:T(8,128)S(1)}, f32[96,768]{1,0:T(8,128)S(1)}, u32[]{:S(2)}, u32[]{:S(2)}) collective-permute-start(f32[96,768]{1,0:T(8,128)S(1)} %get-tuple-element.37), channel_id=1, source_target_pairs={{0,8},{4,12},{8,0},{12,4},{1,9},{5,13},{9,1},{13,5},{2,10},{6,14},... | collective-permute-start | bytes 884744 | tf_op jit(solution)/shard_map/ppermute | solution.py:465
  26.6 0.3 collective-permute-start.4
  27.0 0.6 collective-permute-start.6
  27.5 0.0 copy-done.7
  27.5 0.0 collective-permute-done.3.other
  27.5 0.0 copy-start.6
  27.6 5.6 %shard_map.58.tab = f32[72,1024,128]{2,1,0:T(8,128)} custom-call(f32[7,64,1024]{2,1,0:T(8,128)S(1)} %copy-done, f32[7,32,1024]{2,1,0:T(8,128)S(1)} %copy-done.1, f32[96,1536]{1,0:T(8,128)S(1)} %get-tuple-element.34.kept, f32[96,1536]{1,0:T(8,128)S(1)} %collective-permute-done.3.other), custom_call_target="tpu_custom_call" | custom-call | tf_op jit(solution)/shard_map/pallas_call | solution.py:477
  33.2 2.8 %collective-permute-done.4.x1 = f32[96,256]{1,0:T(8,128)S(1)} collective-permute-done((f32[96,256]{1,0:T(8,128)S(1)}, f32[96,256]{1,0:T(8,128)S(1)}, u32[]{:S(2)}, u32[]{:S(2)}) %collective-permute-start.4) | collective-permute-done | bytes 98336 | tf_op jit(solution)/shard_map/ppermute | solution.py:465
  36.0 0.6 collective-permute-done.6.x3
  36.6 0.0 collective-permute-done.5.x2
  36.6 0.0 copy-done.6
  36.6 4.2 %shard_map.61 = (f32[4,1024,128]{2,1,0:T(8,128)S(1)}, bf16[3,256,256]{2,1,0:T(8,128)(2,1)S(1)}) custom-call(f32[7,64,1024]{2,1,0:T(8,128)S(1)} %copy-done, f32[7,32,1024]{2,1,0:T(8,128)S(1)} %copy-done.1, f32[7,32,64]{2,1,0:T(8,128)S(1)} %copy-done.6, f32[96,256]{1,0:T(8,128)S(1)} %collective-permute-done.4.x1, f32[96,768]{1,0:T(8,128)S(1)} %collective-permute-done.5.x2, ...), custom_call_target="tpu_custom_call" | custom-call | tf_op jit(solution)/shard_map/pallas_call | solution.py:492
  40.7 0.0 copy-start.3
  40.7 1.3 copy-done.3
  42.1 10.1 %all-to-all-done.x_ref = f32[16,64,512]{2,1,0:T(8,128)} async-done(((f32[16,64,512]{2,1,0:T(8,128)}), f32[16,64,512]{2,1,0:T(8,128)}, u32[]{:S(2)}, u32[]{:S(2)}) %all-to-all-start) | async-done | bytes 2097184 | tf_op jit(solution)/shard_map/all_to_all | solution.py:454
  52.1 7.8 %shard_map.60 = f32[8,128,512]{2,1,0:T(8,128)S(1)} custom-call(f32[16,64,512]{2,1,0:T(8,128)} %all-to-all-done.x_ref, f32[72,1024,128]{2,1,0:T(8,128)} %shard_map.58.tab, f32[7,32,64]{2,1,0:T(8,128)S(1)} %copy-done.6), custom_call_target="tpu_custom_call" | custom-call | tf_op jit(solution)/shard_map/pallas_call | solution.py:507
  59.9 0.0 copy-start.4
  59.9 29.0 %all_to_all.15.x_ref = f32[8,128,512]{2,1,0:T(8,128)S(1)} all-to-all(f32[8,128,512]{2,1,0:T(8,128)S(1)} %shard_map.60), channel_id=1, replica_groups=mesh['y1'=2,'y0'=2,'zh'=2,'x1'=2,'x0'=2,'zl'=2,'c'=2] {'zl','x0','x1'}, dimensions={0} | all-to-all | bytes 4194304 | tf_op jit(solution)/shard_map/all_to_all | solution.py:525
  89.0 0.0 copy-done.4
  89.0 6.1 %shard_map.62 = f32[128,32,128]{2,1,0:T(8,128)S(1)} custom-call(s32[1024]{0:T(1024)S(1)} %bitcast.6, f32[8,128,512]{2,1,0:T(8,128)S(1)} %all_to_all.15.x_ref, f32[4,1024,128]{2,1,0:T(8,128)S(1)} %copy-done.4, bf16[3,256,256]{2,1,0:T(8,128)(2,1)S(1)} %get-tuple-element.48.w), custom_call_target="tpu_custom_call" | custom-call | tf_op jit(solution)/shard_map/pallas_call | solution.py:527
  95.0 37.4 %all_to_all.16 = f32[128,32,128]{2,1,0:T(8,128)S(1)} all-to-all(f32[128,32,128]{2,1,0:T(8,128)S(1)} %shard_map.62), channel_id=1, replica_groups=mesh['y1'=2,'y0'=2,'zh'=2,'x1'=2,'x0'=2,'zl'=2,'c'=2] {'x1','x0','zl','y..., dimensions={0} | all-to-all | bytes 4194304 | tf_op jit(solution)/shard_map/all_to_all | solution.py:536
  132.5 1.5 %shard_map.63 = f32[512,1024]{1,0:T(8,128)} custom-call(f32[4096,128]{1,0:T(8,128)S(1)} %bitcast.4), custom_call_target="tpu_custom_call" | custom-call | tf_op jit(solution)/shard_map/pallas_call | solution.py:538
  (1 shorter events, 0.0 us)
Async XLA Ops:
  0.0 5.9 %copy-start.5 = (f32[2,32,8,1024]{3,2,1,0:T(8,128)S(1)}, f32[2,32,8,1024]{3,2,1,0:T(8,128)}, u32[]{:S(2)}) copy-start(f32[2,32,8,1024]{3,2,1,0:T(8,128)} %param.5) | copy-start | bytes 6291460
  1.3 13.4 %collective-permute-start.1 = (f32[96,768]{1,0:T(8,128)S(1)}, f32[96,768]{1,0:T(8,128)S(1)}, u32[]{:S(2)}, u32[]{:S(2)}) collective-permute-start(f32[96,768]{1,0:T(8,128)S(1)} %get-tuple-element.28), channel_id=1, source_target_pairs={{0,64},{32,96},{64,0},{96,32},{1,65},{33,97},{65,1},{97,33},{2,66}... | collective-permute-start | bytes 884744 | tf_op jit(solution)/shard_map/ppermute | solution.py:442
  5.1 9.0 %collective-permute-start = (f32[96,256]{1,0:T(8,128)S(1)}, f32[96,256]{1,0:T(8,128)S(1)}, u32[]{:S(2)}, u32[]{:S(2)}) collective-permute-start(f32[96,256]{1,0:T(8,128)S(1)} %get-tuple-element.27), channel_id=1, source_target_pairs={{0,32},{32,0},{64,96},{96,64},{1,33},{33,1},{65,97},{97,65},{2,34}... | collective-permute-start | bytes 294920 | tf_op jit(solution)/shard_map/ppermute | solution.py:442
  5.5 9.2 %collective-permute-start.2 = (f32[96,256]{1,0:T(8,128)S(1)}, f32[96,256]{1,0:T(8,128)S(1)}, u32[]{:S(2)}, u32[]{:S(2)}) collective-permute-start(f32[96,256]{1,0:T(8,128)S(1)} %get-tuple-element.29), channel_id=1, source_target_pairs={{0,96},{32,64},{64,32},{96,0},{1,97},{33,65},{65,33},{97,1},{2,98}... | collective-permute-start | bytes 294920 | tf_op jit(solution)/shard_map/ppermute | solution.py:442
  6.5 1.3 copy-start.2
  7.8 15.2 %copy-start = (f32[7,64,1024]{2,1,0:T(8,128)S(1)}, f32[7,64,1024]{2,1,0:T(8,128)}, u32[]{:S(2)}) copy-start(f32[7,64,1024]{2,1,0:T(8,128)} %ain.9) | copy-start | bytes 5505028
  7.8 15.2 %copy-start.1 = (f32[7,32,1024]{2,1,0:T(8,128)S(1)}, f32[7,32,1024]{2,1,0:T(8,128)}, u32[]{:S(2)}) copy-start(f32[7,32,1024]{2,1,0:T(8,128)} %aout.9) | copy-start | bytes 2752516
  14.7 37.5 %all-to-all-start = ((f32[16,64,512]{2,1,0:T(8,128)}), f32[16,64,512]{2,1,0:T(8,128)}, u32[]{:S(2)}, u32[]{:S(2)}) async-start(f32[16,64,512]{2,1,0:T(8,128)} %copy-done.2), calls=%async_computation | async-start | bytes 4194304 | tf_op jit(solution)/shard_map/all_to_all | solution.py:454
  23.4 4.1 %copy-start.7 = (s32[1,1024]{1,0:T(1,128)S(1)}, s32[1,1024]{1,0:T(1,128)}, u32[]{:S(2)}) copy-start(s32[1,1024]{1,0:T(1,128)} %param.9) | copy-start | bytes 12292
  23.4 4.1 %collective-permute-start.3 = (f32[96,1536]{1,0:T(8,128)S(1)}, f32[96,1536]{1,0:T(8,128)S(1)}, u32[]{:S(2)}, u32[]{:S(2)}) collective-permute-start(f32[96,1536]{1,0:T(8,128)S(1)} %get-tuple-element.35), channel_id=1, source_target_pairs={{0,1},{1,0},{2,3},{3,2},{4,5},{5,4},{6,7},{7,6},{8,9},{9,8},{10,11... | collective-permute-start | bytes 1769480 | tf_op jit(solution)/shard_map/ppermute | solution.py:475
  23.8 12.7 %collective-permute-start.5 = (f32[96,768]{1,0:T(8,128)S(1)}, f32[96,768]{1,0:T(8,128)S(1)}, u32[]{:S(2)}, u32[]{:S(2)}) collective-permute-start(f32[96,768]{1,0:T(8,128)S(1)} %get-tuple-element.37), channel_id=1, source_target_pairs={{0,8},{4,12},{8,0},{12,4},{1,9},{5,13},{9,1},{13,5},{2,10},{6,14},... | collective-permute-start | bytes 884744 | tf_op jit(solution)/shard_map/ppermute | solution.py:465
  26.6 9.3 %collective-permute-start.4 = (f32[96,256]{1,0:T(8,128)S(1)}, f32[96,256]{1,0:T(8,128)S(1)}, u32[]{:S(2)}, u32[]{:S(2)}) collective-permute-start(f32[96,256]{1,0:T(8,128)S(1)} %get-tuple-element.36), channel_id=1, source_target_pairs={{0,4},{4,0},{8,12},{12,8},{1,5},{5,1},{9,13},{13,9},{2,6},{6,2},{1... | collective-permute-start | bytes 294920 | tf_op jit(solution)/shard_map/ppermute | solution.py:465
  27.0 9.6 %collective-permute-start.6 = (f32[96,256]{1,0:T(8,128)S(1)}, f32[96,256]{1,0:T(8,128)S(1)}, u32[]{:S(2)}, u32[]{:S(2)}) collective-permute-start(f32[96,256]{1,0:T(8,128)S(1)} %get-tuple-element.38), channel_id=1, source_target_pairs={{0,12},{4,8},{8,4},{12,0},{1,13},{5,9},{9,5},{13,1},{2,14},{6,10},... | collective-permute-start | bytes 294920 | tf_op jit(solution)/shard_map/ppermute | solution.py:465
  27.5 9.0 %copy-start.6 = (f32[7,32,64]{2,1,0:T(8,128)S(1)}, f32[7,32,64]{2,1,0:T(8,128)}, u32[]{:S(2)}) copy-start(f32[7,32,64]{2,1,0:T(8,128)} %interp.3) | copy-start | bytes 172036
  40.7 1.3 %copy-start.3 = (f32[4,1024,128]{2,1,0:T(8,128)}, f32[4,1024,128]{2,1,0:T(8,128)S(1)}, u32[]{:S(2)}) copy-start(f32[4,1024,128]{2,1,0:T(8,128)S(1)} %get-tuple-element.47.tab) | copy-start | bytes 6291460
  59.9 29.0 %copy-start.4 = (f32[4,1024,128]{2,1,0:T(8,128)S(1)}, f32[4,1024,128]{2,1,0:T(8,128)}, u32[]{:S(2)}) copy-start(f32[4,1024,128]{2,1,0:T(8,128)} %copy-done.3) | copy-start | bytes 6291460

commit v13 on v12

--- a/solution.py
+++ b/solution.py
@@ -139,12 +139,20 @@
         copy.wait()
 
 
-def pack_y_kernel(ain, aout, y1, y2, y3, sems):
+def pack_far_kernel(ain, aout, y2, sems):
     y = place(Y)
-    ry = rev(y, 2)
-    jobs = [(ain, aout, 1, ((y >> 1) ^ 1) * 512, 512, y2, 256)]
-    for m, dst in ((2, y2), (1, y1), (3, y3)):
-        jobs.append((ain, aout, 0, (ry ^ rev(m, 2)) * 256, 256, dst, 0))
+    jobs = [
+        (ain, aout, 1, ((y >> 1) ^ 1) * 512, 512, y2, 256),
+        (ain, aout, 0, (rev(y, 2) ^ rev(2, 2)) * 256, 256, y2, 0),
+    ]
+    fetch(jobs, sems)
+
+
+def pack_near_kernel(ain, aout, y1, y3, sems):
+    ry = rev(place(Y), 2)
+    jobs = [
+        (ain, aout, 0, (ry ^ rev(m, 2)) * 256, 256, dst, 0) for m, dst in ((1, y1), (3, y3))
+    ]
     fetch(jobs, sems)
 
 
@@ -430,16 +438,22 @@
     nv = 2
     ncv = 2 * nv
     shape = jax.ShapeDtypeStruct
-    sends = pl.pallas_call(
-        pack_y_kernel,
-        out_shape=[shape((96, w), F32) for w in (256, 768, 256)],
-        in_specs=[HBM, HBM],
-        out_specs=[VMEM] * 3,
-        scratch_shapes=[pltpu.SemaphoreType.DMA((2, 4))],
-        compiler_params=params(53),
-    )(angle_in, angle_out)
+    def pack(kernel, widths):
+        return pl.pallas_call(
+            kernel,
+            out_shape=[shape((96, w), F32) for w in widths],
+            in_specs=[HBM, HBM],
+            out_specs=[VMEM] * len(widths),
+            scratch_shapes=[pltpu.SemaphoreType.DMA((2, 2))],
+            compiler_params=params(53),
+        )
+
+    far = pack(pack_far_kernel, (768,))(angle_in, angle_out)[0]
+    ain, aout, far = lax.optimization_barrier((angle_in, angle_out, far))
+    near = pack(pack_near_kernel, (256, 256))(ain, aout)
     from_y = [
-        lax.ppermute(s, Y, [(i, i ^ m) for i in range(4)]) for m, s in zip((1, 2, 3), sends)
+        lax.ppermute(s, Y, [(i, i ^ m) for i in range(4)])
+        for m, s in zip((1, 2, 3), (near[0], far, near[1]))
     ]
 
     state = pl.pallas_call(

time: 134 us -> 134 us (level)
  transfers between devices with their start and end apart: 8 -> 8, of which waited for: 5 -> 5; matrix products, arithmetic and copies ran while one was open for 0% -> 0% of each run, Pallas kernels for 8% -> 9%
where the time goes in v13:
time: 134 us
  blocking collectives  66.5 us (50%)
  Pallas kernels  28.2 us (21%)
  waiting for transfers between devices  19 us (14%)
  starting transfers between devices  17.2 us (13%)
  local copies, waits for them, and re-layouts  2.69 us (2%)
    all_to_all x1, blocking collectives, shards(): state = lax.all_to_all(state, LAST, 0, 0, tiled=True)  37.5 us
    all_to_all x1, blocking collectives, shards(): state = lax.all_to_all(state, SECOND, 0, 0, tiled=True)  29 us
    all_to_all x1, waiting for transfers between devices, shards(): state = lax.all_to_all(state, FIRST, 0, 0, tiled=True)  10.1 us
    all_to_all x1, starting transfers between devices, shards(): state = lax.all_to_all(state, FIRST, 0, 0, tiled=True)  8.53 us
    pallas_call x1, Pallas kernels, shards(): pl.pallas_call(functools.partial(levels_lo_kernel, nv), out_shape=shape((...  7.79 us
    pallas_call x1, Pallas kernels, shards(): pl.pallas_call(functools.partial(levels_hi_kernel, nv), out_shape=shape((...  6.06 us
    pallas_call x1, Pallas kernels, shards(): pl.pallas_call(table_lo_kernel, out_shape=shape((PAD, 1024, 128), F32), i...  5.64 us
    ppermute x3, waiting for transfers between devices, shards(): lax.ppermute(s, Y, [(i, i ^ m) for i in range(4)])  5.55 us
  transfers between devices with their start and end apart: 8, of which 5 were waited for; matrix products, arithmetic and copies ran while one was open for 0% of the time, Pallas kernels for 9%

profile of v13, /device:TPU:1, one launch (start us, length us, event | category | flops | bytes accessed | tf_op | source)
XLA Modules:
  0.0 133.9 jit_solution(44139521580315431)
XLA Ops:
  0.0 1.0 shard_map.56
  1.0 0.0 copy-start.5
  1.0 3.8 %collective-permute-start.1 = (f32[96,768]{1,0:T(8,128)S(1)}, f32[96,768]{1,0:T(8,128)S(1)}, u32[]{:S(2)}, u32[]{:S(2)}) collective-permute-start(f32[96,768]{1,0:T(8,128)S(1)} %shard_map.56), channel_id=1, source_target_pairs={{0,64},{32,96},{64,0},{96,32},{1,65},{33,97},{65,1},{97,33},{2,66}... | collective-permute-start | bytes 884744 | tf_op jit(solution)/shard_map/ppermute | solution.py:455
  4.8 0.9 shard_map.57
  5.7 0.5 collective-permute-start
  6.2 0.5 collective-permute-start.2
  6.7 0.0 copy-done.5
  6.7 0.6 shard_map.55
  7.3 0.0 copy-start.2
  7.3 1.3 copy-done.2
  8.6 0.0 copy-start
  8.6 0.0 copy-start.1
  8.7 5.1 %collective-permute-done.y1 = f32[96,256]{1,0:T(8,128)S(1)} collective-permute-done((f32[96,256]{1,0:T(8,128)S(1)}, f32[96,256]{1,0:T(8,128)S(1)}, u32[]{:S(2)}, u32[]{:S(2)}) %collective-permute-start) | collective-permute-done | bytes 98336 | tf_op jit(solution)/shard_map/ppermute | solution.py:455
  13.8 0.4 collective-permute-done.2.y3
  14.2 0.0 collective-permute-done.1.y2
  14.2 8.5 %all-to-all-start = ((f32[16,64,512]{2,1,0:T(8,128)}), f32[16,64,512]{2,1,0:T(8,128)}, u32[]{:S(2)}, u32[]{:S(2)}) async-start(f32[16,64,512]{2,1,0:T(8,128)} %copy-done.2), calls=%async_computation | async-start | bytes 4194304 | tf_op jit(solution)/shard_map/all_to_all | solution.py:468
  22.7 0.0 copy-done
  22.7 0.0 copy-done.1
  22.8 0.3 shard_map.58
  23.1 0.0 copy-start.7
  23.1 0.2 collective-permute-start.3
  23.4 0.2 shard_map.60
  23.6 2.8 %collective-permute-start.5 = (f32[96,768]{1,0:T(8,128)S(1)}, f32[96,768]{1,0:T(8,128)S(1)}, u32[]{:S(2)}, u32[]{:S(2)}) collective-permute-start(f32[96,768]{1,0:T(8,128)S(1)} %get-tuple-element.41), channel_id=1, source_target_pairs={{0,8},{4,12},{8,0},{12,4},{1,9},{5,13},{9,1},{13,5},{2,10},{6,14},... | collective-permute-start | bytes 884744 | tf_op jit(solution)/shard_map/ppermute | solution.py:479
  26.4 0.3 collective-permute-start.4
  26.7 0.6 collective-permute-start.6
  27.2 0.0 copy-done.7
  27.3 0.0 collective-permute-done.3.other
  27.3 0.0 copy-start.6
  27.3 5.6 %shard_map.59.tab = f32[72,1024,128]{2,1,0:T(8,128)} custom-call(f32[7,64,1024]{2,1,0:T(8,128)S(1)} %copy-done, f32[7,32,1024]{2,1,0:T(8,128)S(1)} %copy-done.1, f32[96,1536]{1,0:T(8,128)S(1)} %get-tuple-element.38.kept, f32[96,1536]{1,0:T(8,128)S(1)} %collective-permute-done.3.other), custom_call_target="tpu_custom_call" | custom-call | tf_op jit(solution)/shard_map/pallas_call | solution.py:491
  32.9 2.8 %collective-permute-done.4.x1 = f32[96,256]{1,0:T(8,128)S(1)} collective-permute-done((f32[96,256]{1,0:T(8,128)S(1)}, f32[96,256]{1,0:T(8,128)S(1)}, u32[]{:S(2)}, u32[]{:S(2)}) %collective-permute-start.4) | collective-permute-done | bytes 98336 | tf_op jit(solution)/shard_map/ppermute | solution.py:479
  35.7 0.6 collective-permute-done.6.x3
  36.3 0.0 collective-permute-done.5.x2
  36.3 0.0 copy-done.6
  36.3 4.2 %shard_map.62 = (f32[4,1024,128]{2,1,0:T(8,128)S(1)}, bf16[3,256,256]{2,1,0:T(8,128)(2,1)S(1)}) custom-call(f32[7,64,1024]{2,1,0:T(8,128)S(1)} %copy-done, f32[7,32,1024]{2,1,0:T(8,128)S(1)} %copy-done.1, f32[7,32,64]{2,1,0:T(8,128)S(1)} %copy-done.6, f32[96,256]{1,0:T(8,128)S(1)} %collective-permute-done.4.x1, f32[96,768]{1,0:T(8,128)S(1)} %collective-permute-done.5.x2, ...), custom_call_target="tpu_custom_call" | custom-call | tf_op jit(solution)/shard_map/pallas_call | solution.py:506
  40.4 0.0 copy-start.3
  40.5 1.3 copy-done.3
  41.8 10.1 %all-to-all-done.x_ref = f32[16,64,512]{2,1,0:T(8,128)} async-done(((f32[16,64,512]{2,1,0:T(8,128)}), f32[16,64,512]{2,1,0:T(8,128)}, u32[]{:S(2)}, u32[]{:S(2)}) %all-to-all-start) | async-done | bytes 2097184 | tf_op jit(solution)/shard_map/all_to_all | solution.py:468
  51.9 7.8 %shard_map.61 = f32[8,128,512]{2,1,0:T(8,128)S(1)} custom-call(f32[16,64,512]{2,1,0:T(8,128)} %all-to-all-done.x_ref, f32[72,1024,128]{2,1,0:T(8,128)} %shard_map.59.tab, f32[7,32,64]{2,1,0:T(8,128)S(1)} %copy-done.6), custom_call_target="tpu_custom_call" | custom-call | tf_op jit(solution)/shard_map/pallas_call | solution.py:521
  59.7 0.0 copy-start.4
  59.7 29.0 %all_to_all.15.x_ref = f32[8,128,512]{2,1,0:T(8,128)S(1)} all-to-all(f32[8,128,512]{2,1,0:T(8,128)S(1)} %shard_map.61), channel_id=1, replica_groups=mesh['y1'=2,'y0'=2,'zh'=2,'x1'=2,'x0'=2,'zl'=2,'c'=2] {'zl','x0','x1'}, dimensions={0} | all-to-all | bytes 4194304 | tf_op jit(solution)/shard_map/all_to_all | solution.py:539
  88.7 0.0 copy-done.4
  88.7 6.1 %shard_map.63 = f32[128,32,128]{2,1,0:T(8,128)S(1)} custom-call(s32[1024]{0:T(1024)S(1)} %bitcast.6, f32[8,128,512]{2,1,0:T(8,128)S(1)} %all_to_all.15.x_ref, f32[4,1024,128]{2,1,0:T(8,128)S(1)} %copy-done.4, bf16[3,256,256]{2,1,0:T(8,128)(2,1)S(1)} %get-tuple-element.52.w), custom_call_target="tpu_custom_call" | custom-call | tf_op jit(solution)/shard_map/pallas_call | solution.py:541
  94.7 37.5 %all_to_all.16 = f32[128,32,128]{2,1,0:T(8,128)S(1)} all-to-all(f32[128,32,128]{2,1,0:T(8,128)S(1)} %shard_map.63), channel_id=1, replica_groups=mesh['y1'=2,'y0'=2,'zh'=2,'x1'=2,'x0'=2,'zl'=2,'c'=2] {'x1','x0','zl','y..., dimensions={0} | all-to-all | bytes 4194304 | tf_op jit(solution)/shard_map/all_to_all | solution.py:550
  132.2 1.5 %shard_map.64 = f32[512,1024]{1,0:T(8,128)} custom-call(f32[4096,128]{1,0:T(8,128)S(1)} %bitcast.4), custom_call_target="tpu_custom_call" | custom-call | tf_op jit(solution)/shard_map/pallas_call | solution.py:552
  (1 shorter events, 0.0 us)
Async XLA Ops:
  1.0 5.7 %copy-start.5 = (f32[2,32,8,1024]{3,2,1,0:T(8,128)S(1)}, f32[2,32,8,1024]{3,2,1,0:T(8,128)}, u32[]{:S(2)}) copy-start(f32[2,32,8,1024]{3,2,1,0:T(8,128)} %param.5) | copy-start | bytes 6291460
  1.0 13.2 %collective-permute-start.1 = (f32[96,768]{1,0:T(8,128)S(1)}, f32[96,768]{1,0:T(8,128)S(1)}, u32[]{:S(2)}, u32[]{:S(2)}) collective-permute-start(f32[96,768]{1,0:T(8,128)S(1)} %shard_map.56), channel_id=1, source_target_pairs={{0,64},{32,96},{64,0},{96,32},{1,65},{33,97},{65,1},{97,33},{2,66}... | collective-permute-start | bytes 884744 | tf_op jit(solution)/shard_map/ppermute | solution.py:455
  5.7 8.0 %collective-permute-start = (f32[96,256]{1,0:T(8,128)S(1)}, f32[96,256]{1,0:T(8,128)S(1)}, u32[]{:S(2)}, u32[]{:S(2)}) collective-permute-start(f32[96,256]{1,0:T(8,128)S(1)} %get-tuple-element.31), channel_id=1, source_target_pairs={{0,32},{32,0},{64,96},{96,64},{1,33},{33,1},{65,97},{97,65},{2,34}... | collective-permute-start | bytes 294920 | tf_op jit(solution)/shard_map/ppermute | solution.py:455
  6.2 8.0 %collective-permute-start.2 = (f32[96,256]{1,0:T(8,128)S(1)}, f32[96,256]{1,0:T(8,128)S(1)}, u32[]{:S(2)}, u32[]{:S(2)}) collective-permute-start(f32[96,256]{1,0:T(8,128)S(1)} %get-tuple-element.33), channel_id=1, source_target_pairs={{0,96},{32,64},{64,32},{96,0},{1,97},{33,65},{65,33},{97,1},{2,98}... | collective-permute-start | bytes 294920 | tf_op jit(solution)/shard_map/ppermute | solution.py:455
  7.3 1.3 copy-start.2
  8.6 14.1 %copy-start = (f32[7,64,1024]{2,1,0:T(8,128)S(1)}, f32[7,64,1024]{2,1,0:T(8,128)}, u32[]{:S(2)}) copy-start(f32[7,64,1024]{2,1,0:T(8,128)} %ain.10) | copy-start | bytes 5505028
  8.6 14.1 %copy-start.1 = (f32[7,32,1024]{2,1,0:T(8,128)S(1)}, f32[7,32,1024]{2,1,0:T(8,128)}, u32[]{:S(2)}) copy-start(f32[7,32,1024]{2,1,0:T(8,128)} %aout.10) | copy-start | bytes 2752516
  14.2 37.7 %all-to-all-start = ((f32[16,64,512]{2,1,0:T(8,128)}), f32[16,64,512]{2,1,0:T(8,128)}, u32[]{:S(2)}, u32[]{:S(2)}) async-start(f32[16,64,512]{2,1,0:T(8,128)} %copy-done.2), calls=%async_computation | async-start | bytes 4194304 | tf_op jit(solution)/shard_map/all_to_all | solution.py:468
  23.1 4.1 %copy-start.7 = (s32[1,1024]{1,0:T(1,128)S(1)}, s32[1,1024]{1,0:T(1,128)}, u32[]{:S(2)}) copy-start(s32[1,1024]{1,0:T(1,128)} %param.9) | copy-start | bytes 12292
  23.1 4.1 %collective-permute-start.3 = (f32[96,1536]{1,0:T(8,128)S(1)}, f32[96,1536]{1,0:T(8,128)S(1)}, u32[]{:S(2)}, u32[]{:S(2)}) collective-permute-start(f32[96,1536]{1,0:T(8,128)S(1)} %get-tuple-element.39), channel_id=1, source_target_pairs={{0,1},{1,0},{2,3},{3,2},{4,5},{5,4},{6,7},{7,6},{8,9},{9,8},{10,11... | collective-permute-start | bytes 1769480 | tf_op jit(solution)/shard_map/ppermute | solution.py:489
  23.6 12.7 %collective-permute-start.5 = (f32[96,768]{1,0:T(8,128)S(1)}, f32[96,768]{1,0:T(8,128)S(1)}, u32[]{:S(2)}, u32[]{:S(2)}) collective-permute-start(f32[96,768]{1,0:T(8,128)S(1)} %get-tuple-element.41), channel_id=1, source_target_pairs={{0,8},{4,12},{8,0},{12,4},{1,9},{5,13},{9,1},{13,5},{2,10},{6,14},... | collective-permute-start | bytes 884744 | tf_op jit(solution)/shard_map/ppermute | solution.py:479
  26.4 9.3 %collective-permute-start.4 = (f32[96,256]{1,0:T(8,128)S(1)}, f32[96,256]{1,0:T(8,128)S(1)}, u32[]{:S(2)}, u32[]{:S(2)}) collective-permute-start(f32[96,256]{1,0:T(8,128)S(1)} %get-tuple-element.40), channel_id=1, source_target_pairs={{0,4},{4,0},{8,12},{12,8},{1,5},{5,1},{9,13},{13,9},{2,6},{6,2},{1... | collective-permute-start | bytes 294920 | tf_op jit(solution)/shard_map/ppermute | solution.py:479
  26.7 9.6 %collective-permute-start.6 = (f32[96,256]{1,0:T(8,128)S(1)}, f32[96,256]{1,0:T(8,128)S(1)}, u32[]{:S(2)}, u32[]{:S(2)}) collective-permute-start(f32[96,256]{1,0:T(8,128)S(1)} %get-tuple-element.42), channel_id=1, source_target_pairs={{0,12},{4,8},{8,4},{12,0},{1,13},{5,9},{9,5},{13,1},{2,14},{6,10},... | collective-permute-start | bytes 294920 | tf_op jit(solution)/shard_map/ppermute | solution.py:479
  27.3 9.0 %copy-start.6 = (f32[7,32,64]{2,1,0:T(8,128)S(1)}, f32[7,32,64]{2,1,0:T(8,128)}, u32[]{:S(2)}) copy-start(f32[7,32,64]{2,1,0:T(8,128)} %interp.3) | copy-start | bytes 172036
  40.4 1.3 %copy-start.3 = (f32[4,1024,128]{2,1,0:T(8,128)}, f32[4,1024,128]{2,1,0:T(8,128)S(1)}, u32[]{:S(2)}) copy-start(f32[4,1024,128]{2,1,0:T(8,128)S(1)} %get-tuple-element.51.tab) | copy-start | bytes 6291460
  59.7 29.0 %copy-start.4 = (f32[4,1024,128]{2,1,0:T(8,128)S(1)}, f32[4,1024,128]{2,1,0:T(8,128)}, u32[]{:S(2)}) copy-start(f32[4,1024,128]{2,1,0:T(8,128)} %copy-done.3) | copy-start | bytes 6291460

commit v14 on v13

--- a/solution.py
+++ b/solution.py
@@ -426,7 +426,7 @@
             out_ref[e, r * ncv : r * ncv + ncv, :] = done[pl.ds(row, ncv), :]
         return 0
 
-    lax.fori_loop(0, 128, gather, 0, unroll=4)
+    lax.fori_loop(0, 128, gather, 0, unroll=8)
 
 
 def table_shapes(count, rows):

time: 134 us -> 134 us (level)
  no operation moved by 1% of the time
where the time goes in v14:
time: 134 us
  blocking collectives  66.5 us (50%)
  Pallas kernels  28.2 us (21%)
  waiting for transfers between devices  19 us (14%)
  starting transfers between devices  17.2 us (13%)
  local copies, waits for them, and re-layouts  2.69 us (2%)
    all_to_all x1, blocking collectives, shards(): state = lax.all_to_all(state, LAST, 0, 0, tiled=True)  37.5 us
    all_to_all x1, blocking collectives, shards(): state = lax.all_to_all(state, SECOND, 0, 0, tiled=True)  29 us
    all_to_all x1, waiting for transfers between devices, shards(): state = lax.all_to_all(state, FIRST, 0, 0, tiled=True)  10.1 us
    all_to_all x1, starting transfers between devices, shards(): state = lax.all_to_all(state, FIRST, 0, 0, tiled=True)  8.53 us
    pallas_call x1, Pallas kernels, shards(): pl.pallas_call(functools.partial(levels_lo_kernel, nv), out_shape=shape((...  7.79 us
    pallas_call x1, Pallas kernels, shards(): pl.pallas_call(functools.partial(levels_hi_kernel, nv), out_shape=shape((...  6.01 us
    pallas_call x1, Pallas kernels, shards(): pl.pallas_call(table_lo_kernel, out_shape=shape((PAD, 1024, 128), F32), i...  5.64 us
    ppermute x3, waiting for transfers between devices, shards(): lax.ppermute(s, Y, [(i, i ^ m) for i in range(4)])  5.55 us
  transfers between devices with their start and end apart: 8, of which 5 were waited for; matrix products, arithmetic and copies ran while one was open for 0% of the time, Pallas kernels for 9%

profile of v14, /device:TPU:1, one launch (start us, length us, event | category | flops | bytes accessed | tf_op | source)
XLA Modules:
  0.0 133.8 jit_solution(379062865915680178)
XLA Ops:
  0.0 1.0 shard_map.56
  1.0 0.0 copy-start.5
  1.0 3.8 %collective-permute-start.1 = (f32[96,768]{1,0:T(8,128)S(1)}, f32[96,768]{1,0:T(8,128)S(1)}, u32[]{:S(2)}, u32[]{:S(2)}) collective-permute-start(f32[96,768]{1,0:T(8,128)S(1)} %shard_map.56), channel_id=1, source_target_pairs={{0,64},{32,96},{64,0},{96,32},{1,65},{33,97},{65,1},{97,33},{2,66}... | collective-permute-start | bytes 884744 | tf_op jit(solution)/shard_map/ppermute | solution.py:455
  4.8 0.9 shard_map.57
  5.7 0.5 collective-permute-start
  6.2 0.5 collective-permute-start.2
  6.7 0.0 copy-done.5
  6.7 0.6 shard_map.55
  7.3 0.0 copy-start.2
  7.3 1.3 copy-done.2
  8.6 0.0 copy-start
  8.6 0.0 copy-start.1
  8.7 5.1 %collective-permute-done.y1 = f32[96,256]{1,0:T(8,128)S(1)} collective-permute-done((f32[96,256]{1,0:T(8,128)S(1)}, f32[96,256]{1,0:T(8,128)S(1)}, u32[]{:S(2)}, u32[]{:S(2)}) %collective-permute-start) | collective-permute-done | bytes 98336 | tf_op jit(solution)/shard_map/ppermute | solution.py:455
  13.8 0.4 collective-permute-done.2.y3
  14.2 0.0 collective-permute-done.1.y2
  14.2 8.5 %all-to-all-start = ((f32[16,64,512]{2,1,0:T(8,128)}), f32[16,64,512]{2,1,0:T(8,128)}, u32[]{:S(2)}, u32[]{:S(2)}) async-start(f32[16,64,512]{2,1,0:T(8,128)} %copy-done.2), calls=%async_computation | async-start | bytes 4194304 | tf_op jit(solution)/shard_map/all_to_all | solution.py:468
  22.7 0.0 copy-done
  22.7 0.0 copy-done.1
  22.8 0.3 shard_map.58
  23.1 0.0 copy-start.7
  23.1 0.2 collective-permute-start.3
  23.4 0.2 shard_map.60
  23.6 2.8 %collective-permute-start.5 = (f32[96,768]{1,0:T(8,128)S(1)}, f32[96,768]{1,0:T(8,128)S(1)}, u32[]{:S(2)}, u32[]{:S(2)}) collective-permute-start(f32[96,768]{1,0:T(8,128)S(1)} %get-tuple-element.41), channel_id=1, source_target_pairs={{0,8},{4,12},{8,0},{12,4},{1,9},{5,13},{9,1},{13,5},{2,10},{6,14},... | collective-permute-start | bytes 884744 | tf_op jit(solution)/shard_map/ppermute | solution.py:479
  26.4 0.3 collective-permute-start.4
  26.7 0.6 collective-permute-start.6
  27.2 0.0 copy-done.7
  27.3 0.0 collective-permute-done.3.other
  27.3 0.0 copy-start.6
  27.3 5.6 %shard_map.59.tab = f32[72,1024,128]{2,1,0:T(8,128)} custom-call(f32[7,64,1024]{2,1,0:T(8,128)S(1)} %copy-done, f32[7,32,1024]{2,1,0:T(8,128)S(1)} %copy-done.1, f32[96,1536]{1,0:T(8,128)S(1)} %get-tuple-element.38.kept, f32[96,1536]{1,0:T(8,128)S(1)} %collective-permute-done.3.other), custom_call_target="tpu_custom_call" | custom-call | tf_op jit(solution)/shard_map/pallas_call | solution.py:491
  32.9 2.8 %collective-permute-done.4.x1 = f32[96,256]{1,0:T(8,128)S(1)} collective-permute-done((f32[96,256]{1,0:T(8,128)S(1)}, f32[96,256]{1,0:T(8,128)S(1)}, u32[]{:S(2)}, u32[]{:S(2)}) %collective-permute-start.4) | collective-permute-done | bytes 98336 | tf_op jit(solution)/shard_map/ppermute | solution.py:479
  35.7 0.6 collective-permute-done.6.x3
  36.3 0.0 collective-permute-done.5.x2
  36.3 0.0 copy-done.6
  36.3 4.2 %shard_map.62 = (f32[4,1024,128]{2,1,0:T(8,128)S(1)}, bf16[3,256,256]{2,1,0:T(8,128)(2,1)S(1)}) custom-call(f32[7,64,1024]{2,1,0:T(8,128)S(1)} %copy-done, f32[7,32,1024]{2,1,0:T(8,128)S(1)} %copy-done.1, f32[7,32,64]{2,1,0:T(8,128)S(1)} %copy-done.6, f32[96,256]{1,0:T(8,128)S(1)} %collective-permute-done.4.x1, f32[96,768]{1,0:T(8,128)S(1)} %collective-permute-done.5.x2, ...), custom_call_target="tpu_custom_call" | custom-call | tf_op jit(solution)/shard_map/pallas_call | solution.py:506
  40.4 0.0 copy-start.3
  40.5 1.3 copy-done.3
  41.8 10.1 %all-to-all-done.x_ref = f32[16,64,512]{2,1,0:T(8,128)} async-done(((f32[16,64,512]{2,1,0:T(8,128)}), f32[16,64,512]{2,1,0:T(8,128)}, u32[]{:S(2)}, u32[]{:S(2)}) %all-to-all-start) | async-done | bytes 2097184 | tf_op jit(solution)/shard_map/all_to_all | solution.py:468
  51.9 7.8 %shard_map.61 = f32[8,128,512]{2,1,0:T(8,128)S(1)} custom-call(f32[16,64,512]{2,1,0:T(8,128)} %all-to-all-done.x_ref, f32[72,1024,128]{2,1,0:T(8,128)} %shard_map.59.tab, f32[7,32,64]{2,1,0:T(8,128)S(1)} %copy-done.6), custom_call_target="tpu_custom_call" | custom-call | tf_op jit(solution)/shard_map/pallas_call | solution.py:521
  59.7 0.0 copy-start.4
  59.7 29.0 %all_to_all.15.x_ref = f32[8,128,512]{2,1,0:T(8,128)S(1)} all-to-all(f32[8,128,512]{2,1,0:T(8,128)S(1)} %shard_map.61), channel_id=1, replica_groups=mesh['y1'=2,'y0'=2,'zh'=2,'x1'=2,'x0'=2,'zl'=2,'c'=2] {'zl','x0','x1'}, dimensions={0} | all-to-all | bytes 4194304 | tf_op jit(solution)/shard_map/all_to_all | solution.py:539
  88.7 0.0 copy-done.4
  88.7 6.0 %shard_map.63 = f32[128,32,128]{2,1,0:T(8,128)S(1)} custom-call(s32[1024]{0:T(1024)S(1)} %bitcast.6, f32[8,128,512]{2,1,0:T(8,128)S(1)} %all_to_all.15.x_ref, f32[4,1024,128]{2,1,0:T(8,128)S(1)} %copy-done.4, bf16[3,256,256]{2,1,0:T(8,128)(2,1)S(1)} %get-tuple-element.52.w), custom_call_target="tpu_custom_call" | custom-call | tf_op jit(solution)/shard_map/pallas_call | solution.py:541
  94.7 37.5 %all_to_all.16 = f32[128,32,128]{2,1,0:T(8,128)S(1)} all-to-all(f32[128,32,128]{2,1,0:T(8,128)S(1)} %shard_map.63), channel_id=1, replica_groups=mesh['y1'=2,'y0'=2,'zh'=2,'x1'=2,'x0'=2,'zl'=2,'c'=2] {'x1','x0','zl','y..., dimensions={0} | all-to-all | bytes 4194304 | tf_op jit(solution)/shard_map/all_to_all | solution.py:550
  132.2 1.5 %shard_map.64 = f32[512,1024]{1,0:T(8,128)} custom-call(f32[4096,128]{1,0:T(8,128)S(1)} %bitcast.4), custom_call_target="tpu_custom_call" | custom-call | tf_op jit(solution)/shard_map/pallas_call | solution.py:552
  (1 shorter events, 0.0 us)
Async XLA Ops:
  1.0 5.7 %copy-start.5 = (f32[2,32,8,1024]{3,2,1,0:T(8,128)S(1)}, f32[2,32,8,1024]{3,2,1,0:T(8,128)}, u32[]{:S(2)}) copy-start(f32[2,32,8,1024]{3,2,1,0:T(8,128)} %param.5) | copy-start | bytes 6291460
  1.0 13.2 %collective-permute-start.1 = (f32[96,768]{1,0:T(8,128)S(1)}, f32[96,768]{1,0:T(8,128)S(1)}, u32[]{:S(2)}, u32[]{:S(2)}) collective-permute-start(f32[96,768]{1,0:T(8,128)S(1)} %shard_map.56), channel_id=1, source_target_pairs={{0,64},{32,96},{64,0},{96,32},{1,65},{33,97},{65,1},{97,33},{2,66}... | collective-permute-start | bytes 884744 | tf_op jit(solution)/shard_map/ppermute | solution.py:455
  5.7 8.0 %collective-permute-start = (f32[96,256]{1,0:T(8,128)S(1)}, f32[96,256]{1,0:T(8,128)S(1)}, u32[]{:S(2)}, u32[]{:S(2)}) collective-permute-start(f32[96,256]{1,0:T(8,128)S(1)} %get-tuple-element.31), channel_id=1, source_target_pairs={{0,32},{32,0},{64,96},{96,64},{1,33},{33,1},{65,97},{97,65},{2,34}... | collective-permute-start | bytes 294920 | tf_op jit(solution)/shard_map/ppermute | solution.py:455
  6.2 8.0 %collective-permute-start.2 = (f32[96,256]{1,0:T(8,128)S(1)}, f32[96,256]{1,0:T(8,128)S(1)}, u32[]{:S(2)}, u32[]{:S(2)}) collective-permute-start(f32[96,256]{1,0:T(8,128)S(1)} %get-tuple-element.33), channel_id=1, source_target_pairs={{0,96},{32,64},{64,32},{96,0},{1,97},{33,65},{65,33},{97,1},{2,98}... | collective-permute-start | bytes 294920 | tf_op jit(solution)/shard_map/ppermute | solution.py:455
  7.3 1.3 copy-start.2
  8.6 14.1 %copy-start = (f32[7,64,1024]{2,1,0:T(8,128)S(1)}, f32[7,64,1024]{2,1,0:T(8,128)}, u32[]{:S(2)}) copy-start(f32[7,64,1024]{2,1,0:T(8,128)} %ain.10) | copy-start | bytes 5505028
  8.6 14.1 %copy-start.1 = (f32[7,32,1024]{2,1,0:T(8,128)S(1)}, f32[7,32,1024]{2,1,0:T(8,128)}, u32[]{:S(2)}) copy-start(f32[7,32,1024]{2,1,0:T(8,128)} %aout.10) | copy-start | bytes 2752516
  14.2 37.7 %all-to-all-start = ((f32[16,64,512]{2,1,0:T(8,128)}), f32[16,64,512]{2,1,0:T(8,128)}, u32[]{:S(2)}, u32[]{:S(2)}) async-start(f32[16,64,512]{2,1,0:T(8,128)} %copy-done.2), calls=%async_computation | async-start | bytes 4194304 | tf_op jit(solution)/shard_map/all_to_all | solution.py:468
  23.1 4.1 %copy-start.7 = (s32[1,1024]{1,0:T(1,128)S(1)}, s32[1,1024]{1,0:T(1,128)}, u32[]{:S(2)}) copy-start(s32[1,1024]{1,0:T(1,128)} %param.9) | copy-start | bytes 12292
  23.1 4.1 %collective-permute-start.3 = (f32[96,1536]{1,0:T(8,128)S(1)}, f32[96,1536]{1,0:T(8,128)S(1)}, u32[]{:S(2)}, u32[]{:S(2)}) collective-permute-start(f32[96,1536]{1,0:T(8,128)S(1)} %get-tuple-element.39), channel_id=1, source_target_pairs={{0,1},{1,0},{2,3},{3,2},{4,5},{5,4},{6,7},{7,6},{8,9},{9,8},{10,11... | collective-permute-start | bytes 1769480 | tf_op jit(solution)/shard_map/ppermute | solution.py:489
  23.6 12.7 %collective-permute-start.5 = (f32[96,768]{1,0:T(8,128)S(1)}, f32[96,768]{1,0:T(8,128)S(1)}, u32[]{:S(2)}, u32[]{:S(2)}) collective-permute-start(f32[96,768]{1,0:T(8,128)S(1)} %get-tuple-element.41), channel_id=1, source_target_pairs={{0,8},{4,12},{8,0},{12,4},{1,9},{5,13},{9,1},{13,5},{2,10},{6,14},... | collective-permute-start | bytes 884744 | tf_op jit(solution)/shard_map/ppermute | solution.py:479
  26.4 9.3 %collective-permute-start.4 = (f32[96,256]{1,0:T(8,128)S(1)}, f32[96,256]{1,0:T(8,128)S(1)}, u32[]{:S(2)}, u32[]{:S(2)}) collective-permute-start(f32[96,256]{1,0:T(8,128)S(1)} %get-tuple-element.40), channel_id=1, source_target_pairs={{0,4},{4,0},{8,12},{12,8},{1,5},{5,1},{9,13},{13,9},{2,6},{6,2},{1... | collective-permute-start | bytes 294920 | tf_op jit(solution)/shard_map/ppermute | solution.py:479
  26.7 9.6 %collective-permute-start.6 = (f32[96,256]{1,0:T(8,128)S(1)}, f32[96,256]{1,0:T(8,128)S(1)}, u32[]{:S(2)}, u32[]{:S(2)}) collective-permute-start(f32[96,256]{1,0:T(8,128)S(1)} %get-tuple-element.42), channel_id=1, source_target_pairs={{0,12},{4,8},{8,4},{12,0},{1,13},{5,9},{9,5},{13,1},{2,14},{6,10},... | collective-permute-start | bytes 294920 | tf_op jit(solution)/shard_map/ppermute | solution.py:479
  27.3 9.0 %copy-start.6 = (f32[7,32,64]{2,1,0:T(8,128)S(1)}, f32[7,32,64]{2,1,0:T(8,128)}, u32[]{:S(2)}) copy-start(f32[7,32,64]{2,1,0:T(8,128)} %interp.3) | copy-start | bytes 172036
  40.4 1.3 %copy-start.3 = (f32[4,1024,128]{2,1,0:T(8,128)}, f32[4,1024,128]{2,1,0:T(8,128)S(1)}, u32[]{:S(2)}) copy-start(f32[4,1024,128]{2,1,0:T(8,128)S(1)} %get-tuple-element.51.tab) | copy-start | bytes 6291460
  59.7 29.0 %copy-start.4 = (f32[4,1024,128]{2,1,0:T(8,128)S(1)}, f32[4,1024,128]{2,1,0:T(8,128)}, u32[]{:S(2)}) copy-start(f32[4,1024,128]{2,1,0:T(8,128)} %copy-done.3) | copy-start | bytes 6291460
